TPU v7x, 512 devices: a whole 4x4x16 slice. The times are simulated.
512 devices in a mesh: seq: 2 (over y_lo), head: 8 (over x, y_hi), dp: 32 (over z, core).
Axes of the slice: x: 4, y: 4 (y_hi: 2, y_lo: 2; y = y_hi * 2 + y_lo), z: 16, core: 2. Of those that a mesh axis runs over, the one named last changes fastest.
Arguments:
- latents: bfloat16 [32, 4, 512, 1152], P('dp', 'seq', 'head'), may hold values from -6 to 6
- cotangent: bfloat16 [32, 4, 512, 1152], P('dp', 'seq', 'head'), may hold values from -6 to 6
- w_qkv: bfloat16 [2, 8, 3, 72, 1152], P(None, 'head'), may hold values from -0.1875 to 0.1875
- w_out: bfloat16 [2, 8, 72, 1152], P(None, 'head'), may hold values from -0.25 to 0.25
Outputs:
- output: bfloat16 [32, 4, 512, 1152], P('dp', 'seq', 'head')
- latent_grads: bfloat16 [32, 4, 512, 1152], P('dp', 'seq', 'head')
- grad_w_qkv: float32 [2, 8, 3, 72, 1152], P(None, 'head')
- grad_w_out: float32 [2, 8, 72, 1152], P(None, 'head')
All inputs are finite; a program needn't handle non-finite values.
Results may differ from a plain program's by a relative error of at most 0.022.
Values may be sent and summed in bfloat16 or wider, within the bound.
No kernel may reach another device: no remote copies, remote signals or barrier semaphores. Data moves between devices by JAX's collectives and lax.ppermute only.
A program may use at most 64 MiB of HBM per device.

v0:
```python
import jax
import jax.numpy as jnp
from jax import lax
from jax.sharding import PartitionSpec as P

EPSILON = 1e-06
SPATIAL_FORM = (
    ("hfeq,hfek->hfqk", "hfqk,hfek->hfeq", "hfqk,hfeq->hfek", "hfqk,hfek->hfeq", "hfqk,hfeq->hfek"),
    3,
)
TEMPORAL_FORM = (
    ("hqea,hkea->hqka", "hqka,hkea->hqea", "hqka,hqea->hkea", "hqka,hkea->hqea", "hqka,hqea->hkea"),
    2,
)


def product(pattern, first_op, second_op):
    return jnp.einsum(pattern, first_op, second_op, preferred_element_type=jnp.float32)


def normalize(inputs):
    widened = inputs.astype(jnp.float32)
    centered = widened - jnp.mean(widened, axis=-1, keepdims=True)
    inverse = lax.rsqrt(jnp.mean(centered * centered, axis=-1, keepdims=True) + EPSILON)
    return (centered * inverse, inverse)


def attend(queries, key_rows, value_rows, form):
    patterns, key_axis = form
    score_scale = queries.shape[-2] ** (-0.5)
    exponent = jnp.exp(product(patterns[0], queries, key_rows) * score_scale)
    attn_probs = exponent / jnp.sum(exponent, axis=key_axis, keepdims=True)
    rounded = attn_probs.astype(jnp.bfloat16)
    heads_out = product(patterns[1], rounded, value_rows).astype(jnp.bfloat16)
    return (heads_out, attn_probs, rounded)


def attend_back(queries, key_rows, value_rows, attn_probs, rounded, grad_heads, form):
    patterns, key_axis = form
    score_scale = queries.shape[-2] ** (-0.5)
    grad_values = product(patterns[2], rounded, grad_heads)
    grad_probs = product(patterns[0], grad_heads, value_rows)
    centered = grad_probs - jnp.sum(attn_probs * grad_probs, axis=key_axis, keepdims=True)
    score_grads = (attn_probs * centered * score_scale).astype(jnp.bfloat16)
    grad_queries = product(patterns[3], score_grads, key_rows)
    grad_keys = product(patterns[4], score_grads, queries)
    return jnp.stack([grad_queries, grad_keys, grad_values], axis=0).astype(jnp.bfloat16)


def collect_rows(local_rows):
    return lax.all_gather(local_rows, "head", axis=1, tiled=True)


def block_forward(inputs, w_qkv, form):
    normed, inverse = normalize(inputs)
    gathered = collect_rows(normed.astype(jnp.bfloat16))
    projected = product("fad,hced->chfea", gathered, w_qkv).astype(jnp.bfloat16)
    heads_out, attn_probs, rounded = attend(projected[0], projected[1], projected[2], form)
    return (normed, inverse, gathered, projected, attn_probs, rounded, heads_out)


def project_heads(heads_out, w_rows):
    return product(
        "hfea,hed->fad",
        lax.all_to_all(heads_out, "head", split_axis=3, concat_axis=0, tiled=True),
        w_rows,
    )


def block_backward(grad_in, saved, w_qkv, w_out, form):
    normed, inverse, gathered, projected, attn_probs, rounded, heads_out = saved
    cotangent_rows = collect_rows(grad_in)
    grad_w_out = product("hfea,fad->hed", heads_out, cotangent_rows)
    grad_heads = product("fad,hed->hfea", cotangent_rows, w_out).astype(jnp.bfloat16)
    qkv_grads = attend_back(
        projected[0], projected[1], projected[2], attn_probs, rounded, grad_heads, form
    )
    grad_w_qkv = product("chfea,fad->hced", qkv_grads, gathered)
    scattered = lax.psum_scatter(
        product("chfea,hced->afd", qkv_grads, w_qkv).astype(jnp.bfloat16),
        "head",
        scatter_dimension=0,
        tiled=True,
    ).astype(jnp.float32)
    normed_grads = jnp.transpose(scattered, (1, 0, 2))
    mean_grad = jnp.mean(normed_grads, axis=-1, keepdims=True)
    mean_cross = jnp.mean(normed_grads * normed, axis=-1, keepdims=True)
    total_grad = grad_in.astype(jnp.float32) + inverse * (
        normed_grads - mean_grad - normed * mean_cross
    )
    return (total_grad, grad_w_qkv, grad_w_out)


def to_positions(frames_major):
    return lax.all_to_all(frames_major, "seq", split_axis=1, concat_axis=0, tiled=True)


def to_frames(positions_major):
    return lax.all_to_all(positions_major, "seq", split_axis=0, concat_axis=1, tiled=True)


def on_device(latents, cotangent, w_qkv, w_out):
    w_full = lax.all_gather(w_out, "head", axis=1, tiled=True)
    first_in = latents[0]
    saved_one = block_forward(first_in, w_qkv[0], SPATIAL_FORM)
    first_out = (first_in.astype(jnp.float32) + project_heads(saved_one[6], w_full[0])).astype(
        jnp.bfloat16
    )
    second_in = to_positions(first_out)
    saved_two = block_forward(second_in, w_qkv[1], TEMPORAL_FORM)
    second_out = (second_in.astype(jnp.float32) + project_heads(saved_two[6], w_full[1])).astype(
        jnp.bfloat16
    )
    result = to_frames(second_out)
    grad_two = to_positions(cotangent[0])
    total_two, qkv_two, out_two = block_backward(
        grad_two, saved_two, w_qkv[1], w_out[1], TEMPORAL_FORM
    )
    grad_one = to_frames(total_two.astype(jnp.bfloat16))
    total_one, qkv_one, out_one = block_backward(
        grad_one, saved_one, w_qkv[0], w_out[0], SPATIAL_FORM
    )
    qkv_one, out_one, qkv_two, out_two = lax.psum(
        (qkv_one, out_one, qkv_two, out_two), ("seq", "dp")
    )
    grad_qkv = jnp.stack([qkv_one, qkv_two])
    grad_out = jnp.stack([out_one, out_two])
    return (result[None], total_one.astype(jnp.bfloat16)[None], grad_qkv, grad_out)


def solution(mesh):
    in_specs = (
        P("dp", "seq", "head", None),
        P("dp", "seq", "head", None),
        P(None, "head", None, None, None),
        P(None, "head", None, None),
    )
    out_specs = (
        P("dp", "seq", "head", None),
        P("dp", "seq", "head", None),
        P(None, "head", None, None, None),
        P(None, "head", None, None),
    )
    return jax.shard_map(
        on_device, mesh=mesh, in_specs=in_specs, out_specs=out_specs, check_vma=False
    )
```

profile of v0, /device:TPU:7, one launch (start us, length us, event | category | flops | bytes accessed | tf_op | source)
XLA Modules:
  0.0 1045.0 jit_solution(10019753942540927601)
XLA Ops:
  13.6 7.0 all_to_all.96
  21.4 64.9 %all-gather.6.cloned.1.call-done = bf16[2,512,1152]{2,1,0:T(8,128)(2,1)} async-done(((bf16[2,64,1152]{2,1,0:T(8,128)(2,1)}), bf16[2,512,1152]{2,1,0:T(8,128)(2,1)}) %all-gather.6.cloned.1.call-update) | async-done | bytes 2359312 | tf_op jit(solution)/shard_map/all_gather | solution.py:51
  86.2 2.6 fusion.35
  90.9 9.3 all_to_all.97
  100.3 62.4 %all-gather.8.cloned.1.call-done = bf16[2,8,72,1152]{3,2,1,0:T(8,128)(2,1)} async-done(((bf16[2,1,72,1152]{3,2,1,0:T(8,128)(2,1)}), bf16[2,8,72,1152]{3,2,1,0:T(8,128)(2,1)}) %all-gather.8.cloned.1.call-update) | async-done | bytes 2654224 | tf_op jit(solution)/shard_map/all_gather | solution.py:103
  164.8 6.6 all_to_all.98
  172.9 64.8 %all-gather.12.cloned.1.call-done = bf16[4,256,1152]{2,1,0:T(8,128)(2,1)} async-done(((bf16[4,32,1152]{2,1,0:T(8,128)(2,1)}), bf16[4,256,1152]{2,1,0:T(8,128)(2,1)}) %all-gather.12.cloned.1.call-update) | async-done | bytes 2359312 | tf_op jit(solution)/shard_map/all_gather | solution.py:51
  237.6 2.6 fusion.54
  240.4 72.0 %all-gather.10.cloned.1.call-done = bf16[4,256,1152]{2,1,0:T(8,128)(2,1)} async-done(((bf16[4,32,1152]{2,1,0:T(8,128)(2,1)}), bf16[4,256,1152]{2,1,0:T(8,128)(2,1)}) %all-gather.10.cloned.1.call-update) | async-done | bytes 2359312 | tf_op jit(solution)/shard_map/all_gather | solution.py:51
  312.4 2.7 fusion.32
  320.6 2.4 fusion.2
  323.0 91.5 %reduce-scatter.3.cloned.1.call-done = bf16[32,4,1152]{2,0,1:T(8,128)(2,1)} async-done(((bf16[256,4,1152]{2,0,1:T(8,128)(2,1)}), bf16[32,4,1152]{2,0,1:T(8,128)(2,1)}) %reduce-scatter.3.cloned.1.call-update) | async-done | bytes 294928 | tf_op jit(solution)/shard_map/reduce_scatter | solution.py:79
  416.9 6.6 all_to_all.99
  429.4 67.4 %all-gather.14.cloned.1.call-done = bf16[2,512,1152]{2,1,0:T(8,128)(2,1)} async-done(((bf16[2,64,1152]{2,1,0:T(8,128)(2,1)}), bf16[2,512,1152]{2,1,0:T(8,128)(2,1)}) %all-gather.14.cloned.1.call-update) | async-done | bytes 2359312 | tf_op jit(solution)/shard_map/all_gather | solution.py:51
  496.9 2.6 fusion.55
  500.6 2.8 fusion.102
  503.4 4.2 fusion.50
  507.5 5.5 fusion.47
  517.9 2.4 fusion.1
  521.2 9.3 all_to_all.100
  532.3 6.6 all_to_all.101
  539.7 406.8 %all-reduce.3.cloned.1.call-done = (f32[1,1,3,72,1152]{4,3,2,1,0:T(8,128)}, f32[1,1,3,72,1152]{4,3,2,1,0:T(8,128)}, f32[1,1,72,1152]{3,2,1,0:T(8,128)}, f32[1,1,72,1152]{3,2,1,0:T(8,128)}) async-done(((f32[1,1,3,72,1152]{4,3,2,1,0:T(8,128)}, f32[1,1,3,72,1152]{4,3,2,1,0:T(8,128)}, f32[1,1,72,1152]{3,2,1,0:T(8,128)}, f32[1,1,72,1152]{3,2,1,0:T(8,128)}), (f32[1,1,3,72,1152]{4,3,2,1,0:T(8,128)}, ...) | async-done | bytes 2654224 | tf_op jit(solution)/shard_map/psum | solution.py:123
  948.4 3.0 pad_maximum_fusion
  951.4 83.5 %reduce-scatter.5.cloned.1.call-done = bf16[64,2,1152]{2,0,1:T(8,128)(2,1)} async-done(((bf16[512,2,1152]{2,0,1:T(8,128)(2,1)}), bf16[64,2,1152]{2,0,1:T(8,128)(2,1)}) %reduce-scatter.5.cloned.1.call-update) | async-done | bytes 294928 | tf_op jit(solution)/shard_map/reduce_scatter | solution.py:79
  (126 shorter events, 41.3 us)
Async XLA Ops:
  7.2 79.1 %copy-start.21 = (bf16[2,1,3,72,1152]{4,3,2,1,0:T(8,128)(2,1)S(1)}, bf16[2,1,3,72,1152]{4,3,2,1,0:T(8,128)(2,1)}, u32[]{:S(2)}) copy-start(bf16[2,1,3,72,1152]{4,3,2,1,0:T(8,128)(2,1)} %param.6) | copy-start | bytes 2985988
  7.2 79.1 %all-gather.6.cloned.1.call-start = ((), (), s32[]{:S(2)}) async-start(), calls=%async_computation.8 | async-start | bytes 2654208 | tf_op jit(solution)/shard_map/all_gather | solution.py:51
  11.5 151.2 %all-gather.8.cloned.1.call-start = ((), (), s32[]{:S(2)}) async-start(), calls=%async_computation.9 | async-start | bytes 2985984 | tf_op jit(solution)/shard_map/all_gather | solution.py:103
  12.2 225.4 %all-gather.12.cloned.1.call-start = ((), (), s32[]{:S(2)}) async-start(), calls=%async_computation.11 | async-start | bytes 2654208 | tf_op jit(solution)/shard_map/all_gather | solution.py:51
  21.3 291.1 %all-gather.10.cloned.1.call-start = ((), (), s32[]{:S(2)}) async-start(), calls=%async_computation.10 | async-start | bytes 2654208 | tf_op jit(solution)/shard_map/all_gather | solution.py:51
  89.4 73.3 %copy-start.2 = (bf16[1,2,64,1152]{3,2,1,0:T(8,128)(2,1)S(1)}, bf16[1,2,64,1152]{3,2,1,0:T(8,128)(2,1)}, u32[]{:S(2)}) copy-start(bf16[1,2,64,1152]{3,2,1,0:T(8,128)(2,1)} %param.4) | copy-start | bytes 884740
  171.4 66.3 %copy-start.7 = (bf16[2,1,72,1152]{3,2,1,0:T(8,128)(2,1)S(1)}, bf16[2,1,72,1152]{3,2,1,0:T(8,128)(2,1)}, u32[]{:S(2)}) copy-start(bf16[2,1,72,1152]{3,2,1,0:T(8,128)(2,1)} %param.7) | copy-start | bytes 995332
  172.8 241.7 %reduce-scatter.3.cloned.1.call-start = ((), (), s32[]{:S(2)}) async-start(), calls=%async_computation.12 | async-start | bytes 2654208 | tf_op jit(solution)/shard_map/reduce_scatter | solution.py:79
  317.9 2.7 copy-start.22
  323.0 92.7 %copy-start.3 = (bf16[2,2,32,1152]{3,2,0,1:T(8,128)(2,1)S(1)}, bf16[2,2,32,1152]{3,2,0,1:T(8,128)(2,1)}, u32[]{:S(2)}) copy-start(bf16[2,2,32,1152]{3,2,0,1:T(8,128)(2,1)} %copy.75) | copy-start | bytes 884740
  323.0 173.9 %all-gather.14.cloned.1.call-start = ((), (), s32[]{:S(2)}) async-start(), calls=%async_computation.13 | async-start | bytes 2654208 | tf_op jit(solution)/shard_map/all_gather | solution.py:51
  424.3 2.1 copy-start
  424.3 522.2 %all-reduce.3.cloned.1.call-start = ((), (), s32[]{:S(2)}) async-start(), calls=%async_computation.15 | async-start | bytes 5308416 | tf_op jit(solution)/shard_map/psum | solution.py:123
  424.5 3.1 copy-start.20
  426.3 1.4 copy-start.12
  427.7 69.2 %copy-start.8 = (bf16[2,1,72,1152]{3,2,1,0:T(8,128)(2,1)S(1)}, bf16[2,1,72,1152]{3,2,1,0:T(8,128)(2,1)}, u32[]{:S(2)}) copy-start(bf16[2,1,72,1152]{3,2,1,0:T(8,128)(2,1)} %param.7) | copy-start | bytes 995332
  429.4 70.0 %copy-start.6 = (f32[2,512,512]{1,2,0:T(8,128)S(1)}, f32[2,512,512]{1,2,0:T(8,128)}, u32[]{:S(2)}) copy-start(f32[2,512,512]{1,2,0:T(8,128)} %copy-done.5) | copy-start | bytes 6291460
  507.5 5.5 copy-start.1
  513.1 1.8 copy-start.19
  513.1 1.8 copy-start.24
  513.1 1.8 copy-start.26
  513.1 1.8 copy-start.28
  516.6 518.3 %reduce-scatter.5.cloned.1.call-start = ((), (), s32[]{:S(2)}) async-start(), calls=%async_computation.14 | async-start | bytes 2654208 | tf_op jit(solution)/shard_map/reduce_scatter | solution.py:79
  948.4 87.7 %copy-start.4 = (bf16[2,2,32,1152]{3,2,0,1:T(8,128)(2,1)S(1)}, bf16[2,2,32,1152]{3,2,0,1:T(8,128)(2,1)}, u32[]{:S(2)}) copy-start(bf16[2,2,32,1152]{3,2,0,1:T(8,128)(2,1)} %copy.83) | copy-start | bytes 884740
  (14 other events, 15.7 us)
Sparse Core Ops, SparseCore 0:
  11.8 74.3 all-gather.5
  89.4 73.2 all-gather.7
  166.5 71.1 all-gather.11
  241.3 71.0 all-gather.9
  323.1 91.3 reduce-scatter.2
  424.4 72.4 all-gather.13
  516.7 429.6 all-reduce.2
  951.1 83.6 reduce-scatter.4
where the time goes:
time: 1050 us; the launch traced here: 1040 us
  waiting for transfers between devices  914 us (87%)
  blocking collectives  45.4 us (4%)
  matrix products  43.7 us (4%)
  other arithmetic  17.3 us (2%)
  between operations  14.6 us (1%)
    psum x1, waiting for transfers between devices, on_device(): lax.psum((qkv_one, out_one, qkv_two, out_two), ('seq', 'dp'))  407 us
    all_gather x4, waiting for transfers between devices, collect_rows(): return lax.all_gather(local_rows, 'head', axis=1, tiled=True)  269 us
    reduce_scatter x2, waiting for transfers between devices, block_backward(): lax.psum_scatter(product('chfea,hced->afd', qkv_grads, w_qkv).astype(jnp....  175 us
    all_gather x1, waiting for transfers between devices, on_device(): w_full = lax.all_gather(w_out, 'head', axis=1, tiled=True)  62.4 us
    dot_general x24, matrix products, product(): jnp.einsum(pattern, first_op, second_op, preferred_element_type=jnp.float32)  43.7 us
  transfers between devices with their start and end apart: 8, of which 8 were waited for; matrix products, arithmetic and copies ran while one was open for 3% of the time, Pallas kernels for 0%

commit v1 on v0

v1 whole, which is shorter than its diff:
```python
import functools

import jax
import jax.numpy as jnp
from jax import lax
from jax.experimental import pallas as pl
from jax.experimental.pallas import tpu as pltpu
from jax.sharding import PartitionSpec as P

EPSILON = 1e-06
E = 72
SCALE = E ** (-0.5)
RING = [[0, 2, 4, 6, 7, 5, 3, 1]]
BF = jnp.bfloat16
F32 = jnp.float32


def nn(a, b):
    return lax.dot_general(a, b, (((1,), (0,)), ((), ())), preferred_element_type=F32)


def nt(a, b):
    return lax.dot_general(a, b, (((1,), (1,)), ((), ())), preferred_element_type=F32)


def tn(a, b):
    return lax.dot_general(a, b, (((0,), (0,)), ((), ())), preferred_element_type=F32)


def normalize(rows):
    wide = rows.astype(F32)
    centered = wide - jnp.mean(wide, axis=-1, keepdims=True)
    inverse = lax.rsqrt(jnp.mean(centered * centered, axis=-1, keepdims=True) + EPSILON)
    return centered * inverse, inverse


def normalize_back(grad, inverse, normed, normed_grads):
    mean_grad = jnp.mean(normed_grads, axis=-1, keepdims=True)
    mean_cross = jnp.mean(normed_grads * normed, axis=-1, keepdims=True)
    return grad.astype(F32) + inverse * (normed_grads - mean_grad - normed * mean_cross)


def regroup(first, second):
    low = lax.broadcasted_iota(jnp.int32, first.shape, 1) < 64
    return (
        jnp.where(low, first, pltpu.roll(second, 64, 1)),
        jnp.where(low, pltpu.roll(first, 64, 1), second),
    )


def norm_kernel(x_ref, out_ref):
    hidden = normalize(x_ref[...])[0].astype(BF)
    for j in range(8):
        out_ref[j] = hidden


def frame_rows(hidden_ref, f):
    return hidden_ref[:, f * 64 : (f + 1) * 64, :].reshape(512, hidden_ref.shape[2])


def softmax(queries, key_rows):
    exponent = jnp.exp(tn(queries, key_rows) * SCALE)
    return exponent / jnp.sum(exponent, axis=1, keepdims=True)


def split3(stacked):
    return tuple(stacked[i * E : (i + 1) * E].astype(BF) for i in range(3))


def spatial_kernel(hidden_ref, w_ref, heads_ref, qkv_ref):
    outs = []
    for f in range(2):
        qkv = nt(w_ref[...], frame_rows(hidden_ref, f))
        qkv_ref[f] = qkv.astype(BF)
        q, k, v = split3(qkv)
        weights = softmax(q, k).astype(BF)
        outs.append(nt(v, weights))
    for m in range(4):
        lanes = slice(m * 128, (m + 1) * 128)
        a, b = regroup(outs[0][:, lanes], outs[1][:, lanes])
        heads_ref[2 * m] = a.astype(BF)
        heads_ref[2 * m + 1] = b.astype(BF)


def middle_kernel(x_ref, g_ref, heads_ref, wo_ref, out_ref):
    y = (x_ref[...].astype(F32) + tn(heads_ref[...], wo_ref[...])).astype(BF)
    g = g_ref[...]
    for s in range(2):
        for f in range(2):
            rows = slice((2 * f + s) * 32, (2 * f + s + 1) * 32)
            out_ref[s, 0, f] = y[rows]
            out_ref[s, 1, f] = g[rows]


def temporal_kernel(
    core_ref, pair_ref, mine_ref, other_ref,
    back_ref, keep_ref, send_ref,
    w_ref, gw_ref, qk_ref, vg_ref, g0_ref, g1_ref, sems,
):
    core = core_ref[0]
    loads = (
        pltpu.make_async_copy(mine_ref, w_ref.at[core], sems.at[0]),
        pltpu.make_async_copy(other_ref, w_ref.at[1 - core], sems.at[1]),
    )
    for load in loads:
        load.start()
    depth = pair_ref.shape[-1]
    rows = jnp.concatenate([pair_ref[s, 0, f] for s in range(2) for f in range(2)], axis=0)
    grad = jnp.concatenate([pair_ref[s, 1, f] for s in range(2) for f in range(2)], axis=0)
    normed, inverse = normalize(rows)
    hidden = normed.astype(BF)
    both = jnp.concatenate([hidden, grad], axis=0)
    for load in loads:
        load.wait()
    qk_ref[...] = nt(w_ref[0], hidden)
    vg_ref[...] = nt(w_ref[1], both)

    def rounded(value):
        return value.astype(BF).astype(F32)

    def ahead(value, r):
        return pltpu.roll(value, 128 - 32 * r, 1) if r else value

    def behind(value, r):
        return pltpu.roll(value, 32 * r, 1) if r else value

    zeros = jnp.zeros((E, 128), F32)
    for h in range(8):
        base = h * 2 * E
        q = rounded(qk_ref[base : base + E])
        k = rounded(qk_ref[base + E : base + 2 * E])
        v = rounded(vg_ref[base : base + E, :128])
        gh = rounded(vg_ref[base + E : base + 2 * E, 128:])
        ks = [ahead(k, r) for r in range(4)]
        vs = [ahead(v, r) for r in range(4)]
        exps = [jnp.exp(jnp.sum(q * kr, axis=0, keepdims=True) * SCALE) for kr in ks]
        total = exps[0] + exps[1] + exps[2] + exps[3]
        probs = [e / total for e in exps]
        weights = [rounded(p) for p in probs]
        heads = sum(w * vr for w, vr in zip(weights, vs))
        gps = [jnp.sum(gh * vr, axis=0, keepdims=True) for vr in vs]
        inner = sum(p * gp for p, gp in zip(probs, gps))
        sgs = [rounded(p * (gp - inner) * SCALE) for p, gp in zip(probs, gps)]
        gq = sum(sg * kr for sg, kr in zip(sgs, ks))
        gk = sum(behind(sg * q, r) for r, sg in enumerate(sgs))
        gv = sum(behind(w * gh, r) for r, w in enumerate(weights))
        g0_ref[base : base + 2 * E] = jnp.concatenate([gq, gk], axis=0).astype(BF)
        g1_ref[base : base + 2 * E, :128] = jnp.concatenate([gv, zeros], axis=0).astype(BF)
        g1_ref[base : base + 2 * E, 128:] = jnp.concatenate([zeros, heads], axis=0).astype(BF)
    for h in range(8):
        span = slice(h * 2 * E, (h + 1) * 2 * E)
        gw_ref[0, span] = nn(g0_ref[span], hidden).astype(BF)
        gw_ref[1, span] = nn(g1_ref[span], both).astype(BF)
    stores = (
        pltpu.make_async_copy(gw_ref.at[core], keep_ref, sems.at[0]),
        pltpu.make_async_copy(gw_ref.at[1 - core], send_ref, sems.at[1]),
    )
    for store in stores:
        store.start()
    mixed = tn(g1_ref[...], w_ref[1])
    normed_grads = tn(g0_ref[...], w_ref[0]) + mixed[:128]
    result = (rows.astype(F32) + mixed[128:]).astype(BF)
    total_grad = normalize_back(grad, inverse, normed, normed_grads).astype(BF)
    for s in range(2):
        for f in range(2):
            at = slice((2 * s + f) * 32, (2 * s + f + 1) * 32)
            back_ref[s, 0, f] = result[at]
            back_ref[s, 1, f] = total_grad[at]
    for store in stores:
        store.wait()


def local_rows(pair_ref, which):
    return jnp.concatenate([pair_ref[s, which, f] for f in range(2) for s in range(2)], axis=0)


def turn_kernel(back_ref, heads_ref, wo_ref, gh_ref, gw_ref, out_ref, grad_ref):
    out_ref[...] = local_rows(back_ref, 0)
    grad = local_rows(back_ref, 1)
    grad_ref[...] = grad
    gh_ref[...] = nt(wo_ref[...], grad).astype(BF)
    gw_ref[...] = nn(heads_ref[...], grad).astype(BF)


def spatial_back_kernel(qkv_ref, gh_ref, hidden_ref, w_ref, terms_ref, gw_ref):
    frames = ([], [])
    for m in range(4):
        pair = regroup(gh_ref[2 * m].astype(F32), gh_ref[2 * m + 1].astype(F32))
        for f in range(2):
            frames[f].append(pair[f])
    total = None
    for f in range(2):
        q, k, v = split3(qkv_ref[f].astype(F32))
        gh = jnp.concatenate(frames[f], axis=1).astype(BF)
        probs = softmax(q, k)
        gv = nn(gh, probs.astype(BF))
        gp = tn(gh, v)
        inner = jnp.sum(probs * gp, axis=1, keepdims=True)
        sg = (probs * (gp - inner) * SCALE).astype(BF)
        grads = jnp.concatenate([nt(k, sg), nn(q, sg), gv], axis=0).astype(BF)
        gw = nn(grads, frame_rows(hidden_ref, f))
        total = gw if total is None else total + gw
        terms = tn(grads, w_ref[...]).astype(BF)
        for j in range(8):
            terms_ref[j, f * 64 : (f + 1) * 64, :] = terms[j * 64 : (j + 1) * 64]
    gw_ref[...] = total.astype(BF)


def last_kernel(terms_ref, x_ref, g_ref, out_ref):
    normed, inverse = normalize(x_ref[...])
    normed_grads = terms_ref[0].astype(F32)
    for j in range(1, 8):
        normed_grads = normed_grads + terms_ref[j].astype(F32)
    out_ref[...] = normalize_back(g_ref[...], inverse, normed, normed_grads).astype(BF)


VMEM = pl.BlockSpec(memory_space=pltpu.VMEM)
SMEM = pl.BlockSpec(memory_space=pltpu.SMEM)
ANY = pl.BlockSpec(memory_space=pl.ANY)
PARAMS = pltpu.CompilerParams(vmem_limit_bytes=48 * 1024 * 1024)


def shape(*dims):
    return jax.ShapeDtypeStruct(dims, BF)


def call(kernel, outs, *args, **more):
    return pl.pallas_call(
        kernel,
        out_shape=outs,
        in_specs=more.pop("in_specs", [VMEM] * len(args)),
        out_specs=more.pop("out_specs", jax.tree.map(lambda _: VMEM, outs)),
        compiler_params=PARAMS,
        **more,
    )(*args)


def over_head(blocks):
    return lax.all_to_all(blocks, "head", 0, 0, tiled=True, axis_index_groups=RING)


def over_seq(blocks):
    return lax.all_to_all(blocks, "seq", 0, 0, tiled=True)


def swap_cores(value, n_dp):
    return lax.ppermute(value, "dp", [(i, i ^ 1) for i in range(n_dp)])


def in_order(core, mine, other):
    return jnp.where(core == 0, jnp.stack([mine, other]), jnp.stack([other, mine]))


def pick(stacked, at):
    return lax.dynamic_index_in_dim(stacked, at, 0, keepdims=False)


def sum_all(grads, n_dp):
    n_z = n_dp // 2
    low = min(4, n_z)
    high = n_z // low
    rows, depth = grads.shape
    near = [
        [s * n_dp + 2 * (b * low + a) + c for s in range(2) for a in range(low)]
        for b in range(high)
        for c in range(2)
    ]
    far = [
        [2 * (b * low + a) + c for b in range(high)] for a in range(low) for c in range(2)
    ]
    parts = lax.all_to_all(
        grads.reshape(2 * low, rows // (2 * low), depth), ("seq", "dp"), 0, 0,
        tiled=True, axis_index_groups=near,
    )
    part = jnp.sum(parts.astype(F32), axis=0).astype(BF)
    if high > 1:
        copies = jnp.broadcast_to(part[None], (high, *part.shape))
        parts = lax.all_to_all(copies, "dp", 0, 0, tiled=True, axis_index_groups=far)
        part = jnp.sum(parts.astype(F32), axis=0).astype(BF)
    copies = jnp.broadcast_to(part[None], (2 * low, *part.shape))
    whole = lax.all_to_all(
        copies, ("seq", "dp"), 0, 0, tiled=True, axis_index_groups=near
    )
    return whole.reshape(rows, depth)


def on_device(n_dp, latents, cotangent, w_qkv, w_out):
    depth = latents.shape[-1]
    core = lax.axis_index("dp") % 2
    x = latents.reshape(128, depth)
    g = cotangent.reshape(128, depth)
    w_own = w_qkv[0].reshape(3 * E, depth)

    half_out = pick(w_out[0].reshape(2, E // 2, depth), core)
    half_two = pick(
        jnp.concatenate([w_qkv[1].reshape(3 * E, depth), w_out[1].reshape(E, depth)]).reshape(
            2, 2 * E, depth
        ),
        core,
    )
    mine_out = lax.all_gather(half_out, "head", axis_index_groups=RING)
    mine_two = lax.all_gather(half_two, "head", axis_index_groups=RING).reshape(16 * E, depth)
    other_out = swap_cores(mine_out, n_dp)
    wo = in_order(core, mine_out, other_out).transpose(1, 0, 2, 3).reshape(8 * E, depth)

    hidden = over_head(call(norm_kernel, shape(8, 128, depth), x))
    heads, qkv = call(spatial_kernel, (shape(8, E, 128), shape(2, 3 * E, 512)), hidden, w_own)
    heads = over_head(heads).reshape(8 * E, 128)
    pair = over_seq(call(middle_kernel, shape(2, 2, 2, 32, depth), x, g, heads, wo))
    other_two = swap_cores(mine_two, n_dp)
    big = shape(16 * E, depth)
    back, keep, send = call(
        temporal_kernel,
        (shape(2, 2, 2, 32, depth), big, big),
        core.reshape(1).astype(jnp.int32), pair, mine_two, other_two,
        in_specs=[SMEM, VMEM, ANY, ANY],
        out_specs=(VMEM, ANY, ANY),
        scratch_shapes=[
            pltpu.VMEM((2, 16 * E, depth), BF),
            pltpu.VMEM((2, 16 * E, depth), BF),
            pltpu.VMEM((16 * E, 128), F32),
            pltpu.VMEM((16 * E, 256), F32),
            pltpu.VMEM((16 * E, 128), BF),
            pltpu.VMEM((16 * E, 256), BF),
            pltpu.SemaphoreType.DMA((2,)),
        ],
    )
    back = over_seq(back)
    two = (keep.astype(F32) + swap_cores(send, n_dp).astype(F32)).astype(BF)
    two = lax.psum_scatter(
        two, "head", scatter_dimension=0, tiled=True, axis_index_groups=RING
    )
    gh, out_one, output, grad_one = call(
        turn_kernel,
        (shape(8 * E, 128), shape(8 * E, depth), shape(128, depth), shape(128, depth)),
        back, heads, wo,
    )
    out_one = lax.psum_scatter(
        out_one, "head", scatter_dimension=0, tiled=True, axis_index_groups=RING
    )
    gh = over_head(gh.reshape(8, E, 128))
    terms, qkv_one = call(
        spatial_back_kernel, (shape(8, 128, depth), shape(3 * E, depth)), qkv, gh, hidden, w_own
    )
    latent_grads = call(last_kernel, shape(128, depth), over_head(terms), x, grad_one)

    one = jnp.concatenate([qkv_one, out_one]).reshape(2, 2 * E, depth)
    one = pick(one, core).astype(F32) + swap_cores(pick(one, 1 - core), n_dp).astype(F32)
    sums = sum_all(jnp.concatenate([one.astype(BF), two]), n_dp)
    sums = in_order(core, sums, swap_cores(sums, n_dp)).astype(F32)
    sums = sums.reshape(2, 2, 2 * E, depth).transpose(1, 0, 2, 3).reshape(2, 4, E, depth)
    return (
        output.reshape(latents.shape),
        latent_grads.reshape(latents.shape),
        sums[:, None, :3],
        sums[:, 3:],
    )


def solution(mesh):
    rows = P("dp", "seq", "head", None)
    specs = (rows, rows, P(None, "head", None, None, None), P(None, "head", None, None))
    return jax.shard_map(
        functools.partial(on_device, mesh.shape["dp"]),
        mesh=mesh, in_specs=specs, out_specs=specs, check_vma=False,
    )
```

time: 1050 us -> 419 us (0.40)
  waiting for transfers between devices: 914 us -> 142 us
  blocking collectives: 45.4 us -> 144 us
  starting transfers between devices: 0.51 us -> 54.5 us
  matrix products: 43.7 us -> 0 us
  Pallas kernels: 0 us -> 21.1 us
  local copies, waits for them, and re-layouts: 9.45 us -> 23.9 us
    psum x1 -> x0, waiting for transfers between devices: 407 us -> none  [on_device(): lax.psum((qkv_one, out_one, qkv_two, out_two), ('seq', 'dp'))]
    all_gather x5 -> x1, waiting for transfers between devices: 331 us -> 50 us  [on_device(): lax.all_gather(half_two, 'head', axis_index_groups=RING)]
    reduce_scatter x2 -> x1, waiting for transfers between devices: 175 us -> 43.7 us  [on_device(): lax.psum_scatter(two, 'head', scatter_dimension=0, tiled=True, axis_index...]
    all_gather x0 -> x1, blocking collectives: none -> 51.7 us  [on_device(): mine_out = lax.all_gather(half_out, 'head', axis_index_groups=RING)]
    all_to_all x6 -> x5, blocking collectives: 45.4 us -> 92.7 us  [the longest x1 28.6 us: sum_all(): lax.all_to_all(copies, 'dp', 0, 0, tiled=True, axis_index_groups=far)]
    dot_general x24 -> x0, matrix products: 43.7 us -> none  [product(): jnp.einsum(pattern, first_op, second_op, preferred_element_type=jnp.float32)]
    ppermute x0 -> x5, starting transfers between devices: none -> 31.6 us  [swap_cores(): return lax.ppermute(value, 'dp', [(i, i ^ 1) for i in range(n_dp)])]
    all_to_all x0 -> x4, waiting for transfers between devices: none -> 26.2 us  [over_head(): lax.all_to_all(blocks, 'head', 0, 0, tiled=True, axis_index_groups=RING)]
  transfers between devices with their start and end apart: 8 -> 12, of which waited for: 8 -> 7; matrix products, arithmetic and copies ran while one was open for 3% -> 5% of each run, Pallas kernels for 0% -> 3%
where the time goes in v1:
time: 419 us; the launch traced here: 411 us
  blocking collectives  144 us (34%)
  waiting for transfers between devices  142 us (34%)
  starting transfers between devices  54.5 us (13%)
  local copies, waits for them, and re-layouts  23.9 us (6%)
  Pallas kernels  21.1 us (5%)
  between operations  14 us (3%)
  other arithmetic  10.9 us (3%)
    all_gather x1, blocking collectives, on_device(): mine_out = lax.all_gather(half_out, 'head', axis_index_groups=RING)  51.7 us
    all_gather x1, waiting for transfers between devices, on_device(): lax.all_gather(half_two, 'head', axis_index_groups=RING)  50 us
    reduce_scatter x1, waiting for transfers between devices, on_device(): lax.psum_scatter(two, 'head', scatter_dimension=0, tiled=True, axis_index...  43.7 us
    ppermute x5, starting transfers between devices, swap_cores(): return lax.ppermute(value, 'dp', [(i, i ^ 1) for i in range(n_dp)])  31.6 us
    all_to_all x1, blocking collectives, sum_all(): lax.all_to_all(copies, 'dp', 0, 0, tiled=True, axis_index_groups=far)  28.6 us
    all_to_all x4, waiting for transfers between devices, over_head(): lax.all_to_all(blocks, 'head', 0, 0, tiled=True, axis_index_groups=RING)  26.2 us
    all_to_all x4, starting transfers between devices, over_head(): lax.all_to_all(blocks, 'head', 0, 0, tiled=True, axis_index_groups=RING)  22.8 us
    all_to_all x1, blocking collectives, sum_all(): lax.all_to_all(grads.reshape(2 * low, rows // (2 * low), depth), ('seq',...  22.4 us
  transfers between devices with their start and end apart: 12, of which 7 were waited for; matrix products, arithmetic and copies ran while one was open for 5% of the time, Pallas kernels for 3%

profile of v1, /device:TPU:7, one launch (start us, length us, event | category | flops | bytes accessed | tf_op | source)
XLA Modules:
  0.0 410.9 jit_solution(11272928529611484535)
XLA Ops:
  10.4 50.0 %all-gather.2.cloned.1.call-done = bf16[8,144,1152]{2,1,0:T(8,128)(2,1)} async-done(((bf16[1,144,1152]{2,1,0:T(8,128)(2,1)}), bf16[8,144,1152]{2,1,0:T(8,128)(2,1)}) %all-gather.2.cloned.1.call-update) | async-done | bytes 2654224 | tf_op jit(solution)/shard_map/all_gather | solution.py:302
  60.3 5.1 %collective-permute-start.1 = (bf16[1152,1152]{1,0:T(8,128)(2,1)}, bf16[1152,1152]{1,0:T(8,128)(2,1)}, u32[]{:S(2)}, u32[]{:S(2)}) collective-permute-start(bf16[1152,1152]{1,0:T(8,128)(2,1)} %bitcast.48), channel_id=1, source_target_pairs={{0,1},{1,0},{2,3},{3,2},{4,5},{5,4},{6,7},{7,6},{8,9},{9,8},{10,11... | collective-permute-start | bytes 7962632 | tf_op jit(solution)/shard_map/ppermute | solution.py:247
  67.2 4.8 %all-to-all-start = ((bf16[8,128,1152]{2,1,0:T(8,128)(2,1)}), bf16[8,128,1152]{2,1,0:T(8,128)(2,1)S(1)}, u32[]{:S(2)}, u32[]{:S(2)}) async-start(bf16[8,128,1152]{2,1,0:T(8,128)(2,1)} %copy-done.1), calls=%async_computation | async-start | bytes 4718592 | tf_op jit(solution)/shard_map/all_to_all | solution.py:239
  73.6 51.7 %all_gather.8 = bf16[8,36,1152]{2,1,0:T(8,128)(2,1)S(1)} all-gather(bf16[1,36,1152]{2,1,0:T(8,128)(2,1)S(1)} %constant_dynamic-slice_fusion.1), channel_id=1, replica_groups={{0,64,128,192,224,160,96,32},{1,65,129,193,225,161,97,33},{2,66,130,194..., dimensions={0}, use_global_device_ids=true | all-gather | bytes 746496 | tf_op jit(solution)/shard_map/all_gather | solution.py:301
  127.2 8.3 %collective-permute-start = (bf16[8,36,1152]{2,0,1:T(8,128)(2,1)}, bf16[8,36,1152]{2,0,1:T(8,128)(2,1)}, u32[]{:S(2)}, u32[]{:S(2)}) collective-permute-start(bf16[8,36,1152]{2,0,1:T(8,128)(2,1)} %copy.22), channel_id=1, source_target_pairs={{0,1},{1,0},{2,3},{3,2},{4,5},{5,4},{6,7},{7,6},{8,9},{9,8},{10,11... | collective-permute-start | bytes 1990664 | tf_op jit(solution)/shard_map/ppermute | solution.py:247
  139.5 2.9 shard_map.76
  143.2 6.0 %all-to-all-start.1 = ((bf16[8,72,128]{2,1,0:T(8,128)(2,1)}), bf16[8,72,128]{2,1,0:T(8,128)(2,1)S(1)}, u32[]{:S(2)}, u32[]{:S(2)}) async-start(bf16[8,72,128]{2,1,0:T(8,128)(2,1)} %get-tuple-element.15), calls=%async_computation.1 | async-start | bytes 294912 | tf_op jit(solution)/shard_map/all_to_all | solution.py:239
  155.4 9.8 %all_to_all.45.pair_ref = bf16[2,2,2,32,1152]{4,3,2,1,0:T(8,128)(2,1)S(1)} all-to-all(bf16[2,2,2,32,1152]{4,3,2,1,0:T(8,128)(2,1)S(1)} %shard_map.77), channel_id=1, replica_groups=mesh['seq'=2,'head'=8,'dp'=32] {'seq'}, dimensions={0} | all-to-all | bytes 1179648 | tf_op jit(solution)/shard_map/all_to_all | solution.py:243
  165.2 8.5 %shard_map.78 = (bf16[2,2,2,32,1152]{4,3,2,1,0:T(8,128)(2,1)S(1)}, bf16[1152,1152]{1,0:T(8,128)(2,1)S(1)}, bf16[1152,1152]{1,0:T(8,128)(2,1)}) custom-call(s32[1]{0:T(128)} %bitcast.core_ref, bf16[2,2,2,32,1152]{4,3,2,1,0:T(8,128)(2,1)S(1)} %all_to_all.45.pair_ref, bf16[1152,1152]{1,0:T(8,128)(2,1)} %bitcast.49, ...), custom_call_target="tpu_custom_call" | custom-call | tf_op jit(solution)/shard_map/pallas_call | solution.py:228
  175.3 4.2 %collective-permute-start.3 = (bf16[1152,1152]{1,0:T(8,128)(2,1)}, bf16[1152,1152]{1,0:T(8,128)(2,1)}, u32[]{:S(2)}, u32[]{:S(2)}) collective-permute-start(bf16[1152,1152]{1,0:T(8,128)(2,1)} %get-tuple-element.25), channel_id=1, source_target_pairs={{0,1},{1,0},{2,3},{3,2},{4,5},{5,4},{6,7},{7,6},{8,9},{9,8},{10,11... | collective-permute-start | bytes 7962632 | tf_op jit(solution)/shard_map/ppermute | solution.py:247
  179.4 11.3 %all_to_all.46.back_ref = bf16[2,2,2,32,1152]{4,3,2,1,0:T(8,128)(2,1)S(1)} all-to-all(bf16[2,2,2,32,1152]{4,3,2,1,0:T(8,128)(2,1)S(1)} %get-tuple-element.16), channel_id=1, replica_groups=mesh['seq'=2,'head'=8,'dp'=32] {'seq'}, dimensions={0} | all-to-all | bytes 1179648 | tf_op jit(solution)/shard_map/all_to_all | solution.py:243
  193.5 4.8 %add_convert_fusion = bf16[1152,1152]{1,0:T(8,128)(2,1)} fusion(bf16[1152,1152]{1,0:T(8,128)(2,1)} %collective-permute-done.3, bf16[1152,1152]{1,0:T(8,128)(2,1)} %copy-done.3), kind=kLoop, calls=%fused_computation | loop fusion | flops 5308416 | bytes 7962624 | tf_op jit(solution)/shard_map/convert_element_type | solution.py:329
  198.3 6.8 %all-to-all-start.4 = ((bf16[8,72,128]{2,1,0:T(8,128)(2,1)}), bf16[8,72,128]{2,1,0:T(8,128)(2,1)S(1)}, u32[]{:S(2)}, u32[]{:S(2)}) async-start(bf16[8,72,128]{2,1,0:T(8,128)(2,1)} %bitcast.13), calls=%async_computation.4 | async-start | bytes 294912 | tf_op jit(solution)/shard_map/all_to_all | solution.py:239
  205.1 5.3 %all-to-all-done.4.gh_ref = bf16[8,72,128]{2,1,0:T(8,128)(2,1)S(1)} async-done(((bf16[8,72,128]{2,1,0:T(8,128)(2,1)}), bf16[8,72,128]{2,1,0:T(8,128)(2,1)S(1)}, u32[]{:S(2)}, u32[]{:S(2)}) %all-to-all-start.4) | async-done | bytes 147488 | tf_op jit(solution)/shard_map/all_to_all | solution.py:239
  210.4 5.5 %shard_map.80 = (bf16[8,128,1152]{2,1,0:T(8,128)(2,1)S(1)}, bf16[216,1152]{1,0:T(8,128)(2,1)S(1)}) custom-call(bf16[2,216,512]{2,1,0:T(8,128)(2,1)S(1)} %copy-done.6, bf16[8,72,128]{2,1,0:T(8,128)(2,1)S(1)} %all-to-all-done.4.gh_ref, bf16[8,128,1152]{2,1,0:T(8,128)(2,1)} %copy-done, bf16[216,1152]{1,0:T(8,128)(2,1)S(1)} %bitcast.37), custom_call_target="tpu_custom_call" | custom-call | tf_op jit(solution)/shard_map/pallas_call | solution.py:228
  217.4 18.9 %reduce-scatter.8.cloned.1.call-done = bf16[72,1152]{1,0:T(8,128)(2,1)} async-done(((bf16[576,1152]{1,0:T(8,128)(2,1)}), bf16[72,1152]{1,0:T(8,128)(2,1)}) %reduce-scatter.8.cloned.1.call-update) | async-done | bytes 165904
  237.2 7.2 %collective-permute-start.2 = (bf16[144,1152]{1,0:T(8,128)(2,1)S(1)}, bf16[144,1152]{1,0:T(8,128)(2,1)S(1)}, u32[]{:S(2)}, u32[]{:S(2)}) collective-permute-start(bf16[144,1152]{1,0:T(8,128)(2,1)S(1)} %dynamic-slice_bitcast_fusion), channel_id=1, source_target_pairs={{0,1},{1,0},{2,3},{3,2},{4,5},{5,4},{6,7},{7,6},{8,9},{9,8},{10,11... | collective-permute-start | bytes 995336 | tf_op jit(solution)/shard_map/ppermute | solution.py:247
  245.8 43.7 %reduce-scatter.6.cloned.1.call-done = bf16[144,1152]{1,0:T(8,128)(2,1)} async-done(((bf16[1152,1152]{1,0:T(8,128)(2,1)}), bf16[144,1152]{1,0:T(8,128)(2,1)}) %reduce-scatter.6.cloned.1.call-update) | async-done | bytes 331792 | tf_op jit(solution)/shard_map/reduce_scatter | solution.py:330
  290.6 22.4 %all_to_all.47 = bf16[8,36,1152]{2,1,0:T(8,128)(2,1)S(1)} all-to-all(bf16[8,36,1152]{2,1,0:T(8,128)(2,1)S(1)} %reshape.77), channel_id=1, replica_groups={{0,2,4,6,256,258,260,262},{1,3,5,7,257,259,261,263},{8,10,12,14,264,266..., dimensions={0} | all-to-all | bytes 1327104 | tf_op jit(solution)/shard_map/all_to_all | solution.py:271
  313.2 28.6 %all_to_all.48 = bf16[4,36,1152]{2,1,0:T(8,128)(2,1)S(1)} all-to-all(bf16[4,36,1152]{2,1,0:T(8,128)(2,1)S(1)} %broadcast_in_dim.6), channel_id=1, replica_groups={{0,8,16,24},{1,9,17,25},{2,10,18,26},{3,11,19,27},{4,12,20,28},{5,13,21..., dimensions={0} | all-to-all | bytes 663552 | tf_op jit(solution)/shard_map/all_to_all | solution.py:278
  341.9 20.7 %all_to_all.49 = bf16[8,36,1152]{2,1,0:T(8,128)(2,1)} all-to-all(bf16[8,36,1152]{2,1,0:T(8,128)(2,1)S(1)} %broadcast_in_dim.7), channel_id=1, replica_groups={{0,2,4,6,256,258,260,262},{1,3,5,7,257,259,261,263},{8,10,12,14,264,266..., dimensions={0} | all-to-all | bytes 1327104 | tf_op jit(solution)/shard_map/all_to_all | solution.py:281
  362.6 5.2 %all-to-all-start.5 = ((bf16[8,128,1152]{2,1,0:T(8,128)(2,1)}), bf16[8,128,1152]{2,1,0:T(8,128)(2,1)S(1)}, u32[]{:S(2)}, u32[]{:S(2)}) async-start(bf16[8,128,1152]{2,1,0:T(8,128)(2,1)} %copy-done.4), calls=%async_computation.5 | async-start | bytes 4718592 | tf_op jit(solution)/shard_map/all_to_all | solution.py:239
  369.8 7.0 %collective-permute-start.4 = (bf16[288,1152]{1,0:T(8,128)(2,1)}, bf16[288,1152]{1,0:T(8,128)(2,1)}, u32[]{:S(2)}, u32[]{:S(2)}) collective-permute-start(bf16[288,1152]{1,0:T(8,128)(2,1)} %reshape.78), channel_id=1, source_target_pairs={{0,1},{1,0},{2,3},{3,2},{4,5},{5,4},{6,7},{7,6},{8,9},{9,8},{10,11... | collective-permute-start | bytes 1990664 | tf_op jit(solution)/shard_map/ppermute | solution.py:247
  376.8 20.9 %all-to-all-done.5.terms_ref = bf16[8,128,1152]{2,1,0:T(8,128)(2,1)S(1)} async-done(((bf16[8,128,1152]{2,1,0:T(8,128)(2,1)}), bf16[8,128,1152]{2,1,0:T(8,128)(2,1)S(1)}, u32[]{:S(2)}, u32[]{:S(2)}) %all-to-all-start.5) | async-done | bytes 2359328 | tf_op jit(solution)/shard_map/all_to_all | solution.py:239
  (65 shorter events, 37.7 us)
Async XLA Ops:
  7.2 53.2 %all-gather.2.cloned.1.call-start = ((), (), s32[]{:S(2)}) async-start(), calls=%async_computation.11 | async-start | bytes 2985984 | tf_op jit(solution)/shard_map/all_gather | solution.py:302
  9.5 55.9 %copy-start.2 = (bf16[1,2,64,1152]{3,2,1,0:T(8,128)(2,1)S(1)}, bf16[1,2,64,1152]{3,2,1,0:T(8,128)(2,1)}, u32[]{:S(2)}) copy-start(bf16[1,2,64,1152]{3,2,1,0:T(8,128)(2,1)} %param.4) | copy-start | bytes 884740
  60.3 104.9 %collective-permute-start.1 = (bf16[1152,1152]{1,0:T(8,128)(2,1)}, bf16[1152,1152]{1,0:T(8,128)(2,1)}, u32[]{:S(2)}, u32[]{:S(2)}) collective-permute-start(bf16[1152,1152]{1,0:T(8,128)(2,1)} %bitcast.48), channel_id=1, source_target_pairs={{0,1},{1,0},{2,3},{3,2},{4,5},{5,4},{6,7},{7,6},{8,9},{9,8},{10,11... | collective-permute-start | bytes 7962632 | tf_op jit(solution)/shard_map/ppermute | solution.py:247
  65.8 1.4 copy-start.1
  67.2 72.3 %all-to-all-start = ((bf16[8,128,1152]{2,1,0:T(8,128)(2,1)}), bf16[8,128,1152]{2,1,0:T(8,128)(2,1)S(1)}, u32[]{:S(2)}, u32[]{:S(2)}) async-start(bf16[8,128,1152]{2,1,0:T(8,128)(2,1)} %copy-done.1), calls=%async_computation | async-start | bytes 4718592 | tf_op jit(solution)/shard_map/all_to_all | solution.py:239
  125.3 1.0 copy-start.10
  127.2 10.3 %collective-permute-start = (bf16[8,36,1152]{2,0,1:T(8,128)(2,1)}, bf16[8,36,1152]{2,0,1:T(8,128)(2,1)}, u32[]{:S(2)}, u32[]{:S(2)}) collective-permute-start(bf16[8,36,1152]{2,0,1:T(8,128)(2,1)} %copy.22), channel_id=1, source_target_pairs={{0,1},{1,0},{2,3},{3,2},{4,5},{5,4},{6,7},{7,6},{8,9},{9,8},{10,11... | collective-permute-start | bytes 1990664 | tf_op jit(solution)/shard_map/ppermute | solution.py:247
  139.5 3.7 copy-start
  142.4 0.8 copy-start.5
  143.2 11.8 %all-to-all-start.1 = ((bf16[8,72,128]{2,1,0:T(8,128)(2,1)}), bf16[8,72,128]{2,1,0:T(8,128)(2,1)S(1)}, u32[]{:S(2)}, u32[]{:S(2)}) async-start(bf16[8,72,128]{2,1,0:T(8,128)(2,1)} %get-tuple-element.15), calls=%async_computation.1 | async-start | bytes 294912 | tf_op jit(solution)/shard_map/all_to_all | solution.py:239
  149.2 87.0 %reduce-scatter.8.cloned.1.call-start = ((), (), s32[]{:S(2)}) async-start(), calls=%async_computation.13 | async-start | bytes 1492992
  152.6 2.3 copy-start.9
  173.7 1.6 copy-start.3
  175.3 18.2 %collective-permute-start.3 = (bf16[1152,1152]{1,0:T(8,128)(2,1)}, bf16[1152,1152]{1,0:T(8,128)(2,1)}, u32[]{:S(2)}, u32[]{:S(2)}) collective-permute-start(bf16[1152,1152]{1,0:T(8,128)(2,1)} %get-tuple-element.25), channel_id=1, source_target_pairs={{0,1},{1,0},{2,3},{3,2},{4,5},{5,4},{6,7},{7,6},{8,9},{9,8},{10,11... | collective-permute-start | bytes 7962632 | tf_op jit(solution)/shard_map/ppermute | solution.py:247
  192.7 0.7 copy-start.7
  193.4 96.0 %reduce-scatter.6.cloned.1.call-start = ((), (), s32[]{:S(2)}) async-start(), calls=%async_computation.12 | async-start | bytes 2985984 | tf_op jit(solution)/shard_map/reduce_scatter | solution.py:330
  198.3 12.2 %copy-start.6 = (bf16[2,216,512]{2,1,0:T(8,128)(2,1)S(1)}, bf16[2,216,512]{2,1,0:T(8,128)(2,1)}, u32[]{:S(2)}) copy-start(bf16[2,216,512]{2,1,0:T(8,128)(2,1)} %copy-done.5) | copy-start | bytes 1327108
  198.3 12.1 %all-to-all-start.4 = ((bf16[8,72,128]{2,1,0:T(8,128)(2,1)}), bf16[8,72,128]{2,1,0:T(8,128)(2,1)S(1)}, u32[]{:S(2)}, u32[]{:S(2)}) async-start(bf16[8,72,128]{2,1,0:T(8,128)(2,1)} %bitcast.13), calls=%async_computation.4 | async-start | bytes 294912 | tf_op jit(solution)/shard_map/all_to_all | solution.py:239
  215.9 1.4 copy-start.4
  237.2 8.5 %collective-permute-start.2 = (bf16[144,1152]{1,0:T(8,128)(2,1)S(1)}, bf16[144,1152]{1,0:T(8,128)(2,1)S(1)}, u32[]{:S(2)}, u32[]{:S(2)}) collective-permute-start(bf16[144,1152]{1,0:T(8,128)(2,1)S(1)} %dynamic-slice_bitcast_fusion), channel_id=1, source_target_pairs={{0,1},{1,0},{2,3},{3,2},{4,5},{5,4},{6,7},{7,6},{8,9},{9,8},{10,11... | collective-permute-start | bytes 995336 | tf_op jit(solution)/shard_map/ppermute | solution.py:247
  362.6 35.1 %all-to-all-start.5 = ((bf16[8,128,1152]{2,1,0:T(8,128)(2,1)}), bf16[8,128,1152]{2,1,0:T(8,128)(2,1)S(1)}, u32[]{:S(2)}, u32[]{:S(2)}) async-start(bf16[8,128,1152]{2,1,0:T(8,128)(2,1)} %copy-done.4), calls=%async_computation.5 | async-start | bytes 4718592 | tf_op jit(solution)/shard_map/all_to_all | solution.py:239
  367.8 29.9 %copy-start.8 = (bf16[128,1152]{1,0:T(8,128)(2,1)S(1)}, bf16[128,1152]{1,0:T(8,128)(2,1)}, u32[]{:S(2)}) copy-start(bf16[128,1152]{1,0:T(8,128)(2,1)} %copy-done.7) | copy-start | bytes 884740
  369.8 30.5 %collective-permute-start.4 = (bf16[288,1152]{1,0:T(8,128)(2,1)}, bf16[288,1152]{1,0:T(8,128)(2,1)}, u32[]{:S(2)}, u32[]{:S(2)}) collective-permute-start(bf16[288,1152]{1,0:T(8,128)(2,1)} %reshape.78), channel_id=1, source_target_pairs={{0,1},{1,0},{2,3},{3,2},{4,5},{5,4},{6,7},{7,6},{8,9},{9,8},{10,11... | collective-permute-start | bytes 1990664 | tf_op jit(solution)/shard_map/ppermute | solution.py:247
Sparse Core Ops, SparseCore 0:
  10.7 49.6 all-gather.1
  193.6 42.6 reduce-scatter.7
  239.3 50.1 reduce-scatter.5

commit v2 on v1

--- a/solution.py
+++ b/solution.py
@@ -48,10 +48,11 @@
     )
 
 
-def norm_kernel(x_ref, out_ref):
+def norm_kernel(x_ref, wo_ref, out_ref, copies_ref):
     hidden = normalize(x_ref[...])[0].astype(BF)
     for j in range(8):
         out_ref[j] = hidden
+        copies_ref[j] = wo_ref[...]
 
 
 def frame_rows(hidden_ref, f):
@@ -82,7 +83,7 @@
         heads_ref[2 * m + 1] = b.astype(BF)
 
 
-def middle_kernel(x_ref, g_ref, heads_ref, wo_ref, out_ref):
+def middle_kernel(x_ref, g_ref, heads_ref, wo_ref, pass_ref, out_ref, same_ref):
     y = (x_ref[...].astype(F32) + tn(heads_ref[...], wo_ref[...])).astype(BF)
     g = g_ref[...]
     for s in range(2):
@@ -174,12 +175,18 @@
     return jnp.concatenate([pair_ref[s, which, f] for f in range(2) for s in range(2)], axis=0)
 
 
-def turn_kernel(back_ref, heads_ref, wo_ref, gh_ref, gw_ref, out_ref, grad_ref):
+def turn_kernel(
+    back_ref, heads_ref, wo_ref, keep_ref, recv_ref, gh_ref, parts_ref, out_ref, grad_ref
+):
     out_ref[...] = local_rows(back_ref, 0)
     grad = local_rows(back_ref, 1)
     grad_ref[...] = grad
     gh_ref[...] = nt(wo_ref[...], grad).astype(BF)
-    gw_ref[...] = nn(heads_ref[...], grad).astype(BF)
+    gw = nn(heads_ref[...], grad)
+    for h in range(8):
+        span = slice(h * 2 * E, (h + 1) * 2 * E)
+        two = keep_ref[span].astype(F32) + recv_ref[span].astype(F32)
+        parts_ref[h] = jnp.concatenate([two, gw[h * E : (h + 1) * E]], axis=0).astype(BF)
 
 
 def spatial_back_kernel(qkv_ref, gh_ref, hidden_ref, w_ref, terms_ref, gw_ref):
@@ -206,7 +213,32 @@
     gw_ref[...] = total.astype(BF)
 
 
-def last_kernel(terms_ref, x_ref, g_ref, out_ref):
+def gather_kernel(core_ref, parts_ref, qkv_ref, two_ref, keep_ref, send_ref, halves_ref):
+    core = core_ref[0]
+    total = parts_ref[0].astype(F32)
+    for j in range(1, 8):
+        total = total + parts_ref[j].astype(F32)
+    two_ref[...] = total[: 2 * E].astype(BF)
+    qkv = qkv_ref[...].astype(F32)
+    halves_ref[0] = qkv[: 2 * E]
+    halves_ref[1] = jnp.concatenate([qkv[2 * E :], total[2 * E :]], axis=0)
+    keep_ref[...] = halves_ref[core].astype(BF)
+    send_ref[...] = halves_ref[1 - core].astype(BF)
+
+
+def result_kernel(core_ref, mine_ref, other_ref, qkv_ref, out_ref, halves_ref):
+    core = core_ref[0]
+    halves_ref[core] = mine_ref[...].astype(F32)
+    halves_ref[1 - core] = other_ref[...].astype(F32)
+    for b in range(2):
+        at = b * 2 * E
+        qkv_ref[b, 0] = halves_ref[0, at : at + E]
+        qkv_ref[b, 1] = halves_ref[0, at + E : at + 2 * E]
+        qkv_ref[b, 2] = halves_ref[1, at : at + E]
+        out_ref[b] = halves_ref[1, at + E : at + 2 * E]
+
+
+def last_kernel(terms_ref, x_ref, g_ref, pass_ref, out_ref, same_ref):
     normed, inverse = normalize(x_ref[...])
     normed_grads = terms_ref[0].astype(F32)
     for j in range(1, 8):
@@ -247,19 +279,14 @@
     return lax.ppermute(value, "dp", [(i, i ^ 1) for i in range(n_dp)])
 
 
-def in_order(core, mine, other):
-    return jnp.where(core == 0, jnp.stack([mine, other]), jnp.stack([other, mine]))
-
-
 def pick(stacked, at):
     return lax.dynamic_index_in_dim(stacked, at, 0, keepdims=False)
 
 
-def sum_all(grads, n_dp):
+def groups_of(n_dp):
     n_z = n_dp // 2
     low = min(4, n_z)
     high = n_z // low
-    rows, depth = grads.shape
     near = [
         [s * n_dp + 2 * (b * low + a) + c for s in range(2) for a in range(low)]
         for b in range(high)
@@ -268,51 +295,72 @@
     far = [
         [2 * (b * low + a) + c for b in range(high)] for a in range(low) for c in range(2)
     ]
+    return near, far
+
+
+def sum_near(grads, near):
+    rows, depth = grads.shape
+    n = len(near[0])
     parts = lax.all_to_all(
-        grads.reshape(2 * low, rows // (2 * low), depth), ("seq", "dp"), 0, 0,
+        grads.reshape(n, rows // n, depth), ("seq", "dp"), 0, 0,
         tiled=True, axis_index_groups=near,
     )
-    part = jnp.sum(parts.astype(F32), axis=0).astype(BF)
-    if high > 1:
-        copies = jnp.broadcast_to(part[None], (high, *part.shape))
-        parts = lax.all_to_all(copies, "dp", 0, 0, tiled=True, axis_index_groups=far)
-        part = jnp.sum(parts.astype(F32), axis=0).astype(BF)
-    copies = jnp.broadcast_to(part[None], (2 * low, *part.shape))
+    return jnp.sum(parts.astype(F32), axis=0).astype(BF)
+
+
+def sum_far(part, far):
+    if len(far[0]) == 1:
+        return part
+    copies = jnp.broadcast_to(part[None], (len(far[0]), *part.shape))
+    parts = lax.all_to_all(copies, "dp", 0, 0, tiled=True, axis_index_groups=far)
+    return jnp.sum(parts.astype(F32), axis=0).astype(BF)
+
+
+def spread(part, near):
+    copies = jnp.broadcast_to(part[None], (len(near[0]), *part.shape))
     whole = lax.all_to_all(
         copies, ("seq", "dp"), 0, 0, tiled=True, axis_index_groups=near
     )
-    return whole.reshape(rows, depth)
+    return whole.reshape(len(near[0]) * part.shape[0], part.shape[1])
 
 
 def on_device(n_dp, latents, cotangent, w_qkv, w_out):
     depth = latents.shape[-1]
     core = lax.axis_index("dp") % 2
+    core_arg = core.reshape(1).astype(jnp.int32)
+    near, far = groups_of(n_dp)
     x = latents.reshape(128, depth)
     g = cotangent.reshape(128, depth)
     w_own = w_qkv[0].reshape(3 * E, depth)
 
-    half_out = pick(w_out[0].reshape(2, E // 2, depth), core)
     half_two = pick(
         jnp.concatenate([w_qkv[1].reshape(3 * E, depth), w_out[1].reshape(E, depth)]).reshape(
             2, 2 * E, depth
         ),
         core,
     )
-    mine_out = lax.all_gather(half_out, "head", axis_index_groups=RING)
     mine_two = lax.all_gather(half_two, "head", axis_index_groups=RING).reshape(16 * E, depth)
-    other_out = swap_cores(mine_out, n_dp)
-    wo = in_order(core, mine_out, other_out).transpose(1, 0, 2, 3).reshape(8 * E, depth)
-
-    hidden = over_head(call(norm_kernel, shape(8, 128, depth), x))
+
+    hidden, wo = call(
+        norm_kernel, (shape(8, 128, depth), shape(8, E, depth)), x, w_out[0].reshape(E, depth)
+    )
+    hidden = over_head(hidden)
+    wo = over_head(wo).reshape(8 * E, depth)
     heads, qkv = call(spatial_kernel, (shape(8, E, 128), shape(2, 3 * E, 512)), hidden, w_own)
     heads = over_head(heads).reshape(8 * E, 128)
-    pair = over_seq(call(middle_kernel, shape(2, 2, 2, 32, depth), x, g, heads, wo))
+    big = shape(16 * E, depth)
+    pair, mine_two = call(
+        middle_kernel, (shape(2, 2, 2, 32, depth), big), x, g, heads, wo, mine_two,
+        in_specs=[VMEM] * 4 + [ANY],
+        out_specs=(VMEM, ANY),
+        input_output_aliases={4: 1},
+    )
+    pair = over_seq(pair)
     other_two = swap_cores(mine_two, n_dp)
-    big = shape(16 * E, depth)
     back, keep, send = call(
         temporal_kernel,
         (shape(2, 2, 2, 32, depth), big, big),
-        core.reshape(1).astype(jnp.int32), pair, mine_two, other_two,
+        core_arg, pair, mine_two, other_two,
         in_specs=[SMEM, VMEM, ANY, ANY],
         out_specs=(VMEM, ANY, ANY),
         scratch_shapes=[
@@ -326,34 +374,46 @@
         ],
     )
     back = over_seq(back)
-    two = (keep.astype(F32) + swap_cores(send, n_dp).astype(F32)).astype(BF)
-    two = lax.psum_scatter(
-        two, "head", scatter_dimension=0, tiled=True, axis_index_groups=RING
-    )
-    gh, out_one, output, grad_one = call(
+    gh, parts, output, grad_one = call(
         turn_kernel,
-        (shape(8 * E, 128), shape(8 * E, depth), shape(128, depth), shape(128, depth)),
-        back, heads, wo,
-    )
-    out_one = lax.psum_scatter(
-        out_one, "head", scatter_dimension=0, tiled=True, axis_index_groups=RING
+        (shape(8 * E, 128), shape(8, 3 * E, depth), shape(128, depth), shape(128, depth)),
+        back, heads, wo, keep, swap_cores(send, n_dp),
     )
     gh = over_head(gh.reshape(8, E, 128))
+    parts = over_head(parts)
     terms, qkv_one = call(
         spatial_back_kernel, (shape(8, 128, depth), shape(3 * E, depth)), qkv, gh, hidden, w_own
     )
-    latent_grads = call(last_kernel, shape(128, depth), over_head(terms), x, grad_one)
-
-    one = jnp.concatenate([qkv_one, out_one]).reshape(2, 2 * E, depth)
-    one = pick(one, core).astype(F32) + swap_cores(pick(one, 1 - core), n_dp).astype(F32)
-    sums = sum_all(jnp.concatenate([one.astype(BF), two]), n_dp)
-    sums = in_order(core, sums, swap_cores(sums, n_dp)).astype(F32)
-    sums = sums.reshape(2, 2, 2 * E, depth).transpose(1, 0, 2, 3).reshape(2, 4, E, depth)
+    half = shape(2 * E, depth)
+    two, keep, send = call(
+        gather_kernel, (half, half, half), core_arg, parts, qkv_one,
+        in_specs=[SMEM, VMEM, VMEM],
+        scratch_shapes=[pltpu.VMEM((2, 2 * E, depth), F32)],
+    )
+    one = (keep.astype(F32) + swap_cores(send, n_dp).astype(F32)).astype(BF)
+    part = sum_near(jnp.concatenate([one, two]), near)
+    latent_grads, part = call(
+        last_kernel, (shape(128, depth), shape(*part.shape)), over_head(terms), x, grad_one, part,
+        in_specs=[VMEM] * 3 + [ANY],
+        out_specs=(VMEM, ANY),
+        input_output_aliases={3: 1},
+    )
+    mine = spread(sum_far(part, far), near)
+    grad_qkv, grad_out = call(
+        result_kernel,
+        (
+            jax.ShapeDtypeStruct((2, 3, E, depth), F32),
+            jax.ShapeDtypeStruct((2, E, depth), F32),
+        ),
+        core_arg, mine, swap_cores(mine, n_dp),
+        in_specs=[SMEM, VMEM, VMEM],
+        scratch_shapes=[pltpu.VMEM((2, 4 * E, depth), F32)],
+    )
     return (
         output.reshape(latents.shape),
         latent_grads.reshape(latents.shape),
-        sums[:, None, :3],
-        sums[:, 3:],
+        grad_qkv[:, None],
+        grad_out[:, None],
     )
 
 

time: 419 us -> 373 us (0.89); the launches traced: 411 us -> 372 us
  waiting for transfers between devices: 142 us -> 105 us
  blocking collectives: 144 us -> 170 us
  starting transfers between devices: 54.5 us -> 37.6 us
  local copies, waits for them, and re-layouts: 23.9 us -> 12.7 us
  Pallas kernels: 21.1 us -> 30.8 us
  other arithmetic: 10.9 us -> 1.49 us
    all_to_all x3 -> x6, blocking collectives: 71.7 us -> 148 us  [the longest x3 62.8 us: over_head(): lax.all_to_all(blocks, 'head', 0, 0, tiled=True, axis_index_groups=RING)]
    all_to_all x4 -> x3, waiting for transfers between devices: 26.2 us -> 102 us  [over_head(): lax.all_to_all(blocks, 'head', 0, 0, tiled=True, axis_index_groups=RING)]
    all_gather x1 -> x0, blocking collectives: 51.7 us -> none  [on_device(): mine_out = lax.all_gather(half_out, 'head', axis_index_groups=RING)]
    all_gather x1, waiting for transfers between devices: 50 us -> 0.01 us  [on_device(): lax.all_gather(half_two, 'head', axis_index_groups=RING)]
    reduce_scatter x1 -> x0, waiting for transfers between devices: 43.7 us -> none  [on_device(): lax.psum_scatter(two, 'head', scatter_dimension=0, tiled=True, axis_index...]
    unnamed x4 -> x1, waiting for transfers between devices: 18.9 us -> 0.02 us
    ppermute x5 -> x4, starting transfers between devices: 31.6 us -> 19.1 us  [swap_cores(): return lax.ppermute(value, 'dp', [(i, i ^ 1) for i in range(n_dp)])]
    pallas_call x7 -> x9, Pallas kernels: 21.1 us -> 30.8 us  [call(): pl.pallas_call(kernel, out_shape=outs, in_specs=more.pop('in_specs', [VME...]
  transfers between devices with their start and end apart: 12 -> 8, of which waited for: 7 -> 5; matrix products, arithmetic and copies ran while one was open for 5% -> 0% of each run, Pallas kernels for 3% -> 2%
where the time goes in v2:
time: 373 us; the launch traced here: 372 us
  blocking collectives  170 us (46%)
  waiting for transfers between devices  105 us (28%)
  starting transfers between devices  37.6 us (10%)
  Pallas kernels  30.8 us (8%)
  between operations  14.2 us (4%)
  local copies, waits for them, and re-layouts  12.7 us (3%)
    all_to_all x3, waiting for transfers between devices, over_head(): lax.all_to_all(blocks, 'head', 0, 0, tiled=True, axis_index_groups=RING)  102 us
    all_to_all x3, blocking collectives, over_head(): lax.all_to_all(blocks, 'head', 0, 0, tiled=True, axis_index_groups=RING)  62.8 us
    pallas_call x9, Pallas kernels, call(): pl.pallas_call(kernel, out_shape=outs, in_specs=more.pop('in_specs', [VME...  30.8 us
    all_to_all x1, blocking collectives, sum_far(): lax.all_to_all(copies, 'dp', 0, 0, tiled=True, axis_index_groups=far)  30.2 us
    all_to_all x1, blocking collectives, spread(): lax.all_to_all(copies, ('seq', 'dp'), 0, 0, tiled=True, axis_index_groups...  28.2 us
    all_to_all x1, blocking collectives, sum_near(): lax.all_to_all(grads.reshape(n, rows // n, depth), ('seq', 'dp'), 0, 0, t...  26.6 us
    all_to_all x2, blocking collectives, over_seq(): return lax.all_to_all(blocks, 'seq', 0, 0, tiled=True)  22.3 us
    ppermute x4, starting transfers between devices, swap_cores(): return lax.ppermute(value, 'dp', [(i, i ^ 1) for i in range(n_dp)])  19.1 us
  transfers between devices with their start and end apart: 8, of which 5 were waited for; matrix products, arithmetic and copies ran while one was open for 0% of the time, Pallas kernels for 2%

profile of v2, /device:TPU:7, one launch (start us, length us, event | category | flops | bytes accessed | tf_op | source)
XLA Modules:
  0.0 371.7 jit_solution(10187101104401628954)
XLA Ops:
  10.9 41.1 %all_to_all.55.hidden_ref = bf16[8,128,1152]{2,1,0:T(8,128)(2,1)S(1)} all-to-all(bf16[8,128,1152]{2,1,0:T(8,128)(2,1)S(1)} %get-tuple-element.26), channel_id=1, replica_groups={{0,64,128,192,224,160,96,32},{1,65,129,193,225,161,97,33},{2,66,130,194..., dimensions={0} | all-to-all | bytes 4718592 | tf_op jit(solution)/shard_map/all_to_all | solution.py:271
  52.0 5.5 %all-to-all-start.2 = ((bf16[8,72,1152]{2,1,0:T(8,128)(2,1)}), bf16[8,72,1152]{2,1,0:T(8,128)(2,1)}, u32[]{:S(2)}, u32[]{:S(2)}) async-start(bf16[8,72,1152]{2,1,0:T(8,128)(2,1)} %copy-done.5), calls=%async_computation.2 | async-start | bytes 2654208 | tf_op jit(solution)/shard_map/all_to_all | solution.py:271
  57.5 2.2 shard_map.76
  61.2 20.6 %all-to-all-done.2 = bf16[8,72,1152]{2,1,0:T(8,128)(2,1)} async-done(((bf16[8,72,1152]{2,1,0:T(8,128)(2,1)}), bf16[8,72,1152]{2,1,0:T(8,128)(2,1)}, u32[]{:S(2)}, u32[]{:S(2)}) %all-to-all-start.2) | async-done | bytes 1327136 | tf_op jit(solution)/shard_map/all_to_all | solution.py:271
  81.7 11.9 %all_to_all.56 = bf16[8,72,128]{2,1,0:T(8,128)(2,1)S(1)} all-to-all(bf16[8,72,128]{2,1,0:T(8,128)(2,1)} %copy-done.9), channel_id=1, replica_groups={{0,64,128,192,224,160,96,32},{1,65,129,193,225,161,97,33},{2,66,130,194..., dimensions={0} | all-to-all | bytes 294912 | tf_op jit(solution)/shard_map/all_to_all | solution.py:271
  98.7 7.7 %collective-permute-start = (bf16[1152,1152]{1,0:T(8,128)(2,1)S(1)}, bf16[1152,1152]{1,0:T(8,128)(2,1)S(1)}, u32[]{:S(2)}, u32[]{:S(2)}) collective-permute-start(bf16[1152,1152]{1,0:T(8,128)(2,1)S(1)} %get-tuple-element.30.mine_ref), channel_id=1, source_target_pairs={{0,1},{1,0},{2,3},{3,2},{4,5},{5,4},{6,7},{7,6},{8,9},{9,8},{10,11... | collective-permute-start | bytes 7962632 | tf_op jit(solution)/shard_map/ppermute | solution.py:279
  106.4 11.0 %all_to_all.57.pair_ref = bf16[2,2,2,32,1152]{4,3,2,1,0:T(8,128)(2,1)S(1)} all-to-all(bf16[2,2,2,32,1152]{4,3,2,1,0:T(8,128)(2,1)S(1)} %get-tuple-element.29), channel_id=1, replica_groups=mesh['seq'=2,'head'=8,'dp'=32] {'seq'}, dimensions={0} | all-to-all | bytes 1179648 | tf_op jit(solution)/shard_map/all_to_all | solution.py:275
  118.9 8.5 %shard_map.78 = (bf16[2,2,2,32,1152]{4,3,2,1,0:T(8,128)(2,1)S(1)}, bf16[1152,1152]{1,0:T(8,128)(2,1)S(1)}, bf16[1152,1152]{1,0:T(8,128)(2,1)}) custom-call(s32[1]{0:T(128)} %bitcast.core_ref, bf16[2,2,2,32,1152]{4,3,2,1,0:T(8,128)(2,1)S(1)} %all_to_all.57.pair_ref, bf16[1152,1152]{1,0:T(8,128)(2,1)} %copy-done.2, bf16[1152,1152]{1,0:T(8,128)(2,1)} %copy-done.11), custom_call_target="tpu_custom_call" | custom-call | tf_op jit(solution)/shard_map/pallas_call | solution.py:260
  127.4 2.9 collective-permute-start.1
  130.4 11.3 %all_to_all.58.back_ref = bf16[2,2,2,32,1152]{4,3,2,1,0:T(8,128)(2,1)S(1)} all-to-all(bf16[2,2,2,32,1152]{4,3,2,1,0:T(8,128)(2,1)S(1)} %get-tuple-element.31), channel_id=1, replica_groups=mesh['seq'=2,'head'=8,'dp'=32] {'seq'}, dimensions={0} | all-to-all | bytes 1179648 | tf_op jit(solution)/shard_map/all_to_all | solution.py:275
  143.2 6.0 %shard_map.79 = (bf16[576,128]{1,0:T(8,128)(2,1)S(1)}, bf16[8,216,1152]{2,1,0:T(8,128)(2,1)}, bf16[128,1152]{1,0:T(8,128)(2,1)}, bf16[128,1152]{1,0:T(8,128)(2,1)S(1)}) custom-call(bf16[2,2,2,32,1152]{4,3,2,1,0:T(8,128)(2,1)S(1)} %all_to_all.58.back_ref, bf16[576,128]{1,0:T(8,128)(2,1)S(1)} %bitcast.29, bf16[576,1152]{1,0:T(8,128)(2,1)} %bitcast.6.wo_ref, ...), custom_call_target="tpu_custom_call" | custom-call | tf_op jit(solution)/shard_map/pallas_call | solution.py:260
  149.2 9.8 %all_to_all.59.gh_ref = bf16[8,72,128]{2,1,0:T(8,128)(2,1)S(1)} all-to-all(bf16[8,72,128]{2,1,0:T(8,128)(2,1)S(1)} %bitcast.31), channel_id=1, replica_groups={{0,64,128,192,224,160,96,32},{1,65,129,193,225,161,97,33},{2,66,130,194..., dimensions={0} | all-to-all | bytes 294912 | tf_op jit(solution)/shard_map/all_to_all | solution.py:271
  159.0 6.3 %all-to-all-start.7 = ((bf16[8,216,1152]{2,1,0:T(8,128)(2,1)}), bf16[8,216,1152]{2,1,0:T(8,128)(2,1)}, u32[]{:S(2)}, u32[]{:S(2)}) async-start(bf16[8,216,1152]{2,1,0:T(8,128)(2,1)} %get-tuple-element.39), calls=%async_computation.7 | async-start | bytes 7962624 | tf_op jit(solution)/shard_map/all_to_all | solution.py:271
  165.3 5.5 %shard_map.80 = (bf16[8,128,1152]{2,1,0:T(8,128)(2,1)S(1)}, bf16[216,1152]{1,0:T(8,128)(2,1)S(1)}) custom-call(bf16[2,216,512]{2,1,0:T(8,128)(2,1)S(1)} %copy-done.7, bf16[8,72,128]{2,1,0:T(8,128)(2,1)S(1)} %all_to_all.59.gh_ref, bf16[8,128,1152]{2,1,0:T(8,128)(2,1)} %copy-done, bf16[216,1152]{1,0:T(8,128)(2,1)S(1)} %bitcast.24), custom_call_target="tpu_custom_call" | custom-call | tf_op jit(solution)/shard_map/pallas_call | solution.py:260
  172.2 49.3 %all-to-all-done.7.parts_ref = bf16[8,216,1152]{2,1,0:T(8,128)(2,1)} async-done(((bf16[8,216,1152]{2,1,0:T(8,128)(2,1)}), bf16[8,216,1152]{2,1,0:T(8,128)(2,1)}, u32[]{:S(2)}, u32[]{:S(2)}) %all-to-all-start.7) | async-done | bytes 3981344 | tf_op jit(solution)/shard_map/all_to_all | solution.py:271
  221.5 3.2 shard_map.81
  224.7 4.4 %collective-permute-start.2 = (bf16[144,1152]{1,0:T(8,128)(2,1)S(1)}, bf16[144,1152]{1,0:T(8,128)(2,1)S(1)}, u32[]{:S(2)}, u32[]{:S(2)}) collective-permute-start(bf16[144,1152]{1,0:T(8,128)(2,1)S(1)} %get-tuple-element.42), channel_id=1, source_target_pairs={{0,1},{1,0},{2,3},{3,2},{4,5},{5,4},{6,7},{7,6},{8,9},{9,8},{10,11... | collective-permute-start | bytes 995336 | tf_op jit(solution)/shard_map/ppermute | solution.py:279
  230.6 26.6 %all_to_all.60 = bf16[8,36,1152]{2,1,0:T(8,128)(2,1)} all-to-all(bf16[8,36,1152]{2,1,0:T(8,128)(2,1)S(1)} %reshape.55), channel_id=1, replica_groups={{0,2,4,6,256,258,260,262},{1,3,5,7,257,259,261,263},{8,10,12,14,264,266..., dimensions={0} | all-to-all | bytes 1327104 | tf_op jit(solution)/shard_map/all_to_all | solution.py:304
  257.1 6.7 %all-to-all-start.6 = ((bf16[8,128,1152]{2,1,0:T(8,128)(2,1)}), bf16[8,128,1152]{2,1,0:T(8,128)(2,1)S(1)}, u32[]{:S(2)}, u32[]{:S(2)}) async-start(bf16[8,128,1152]{2,1,0:T(8,128)(2,1)} %copy-done.4), calls=%async_computation.6 | async-start | bytes 4718592 | tf_op jit(solution)/shard_map/all_to_all | solution.py:271
  265.1 31.9 %all-to-all-done.6.terms_ref = bf16[8,128,1152]{2,1,0:T(8,128)(2,1)S(1)} async-done(((bf16[8,128,1152]{2,1,0:T(8,128)(2,1)}), bf16[8,128,1152]{2,1,0:T(8,128)(2,1)S(1)}, u32[]{:S(2)}, u32[]{:S(2)}) %all-to-all-start.6) | async-done | bytes 2359328 | tf_op jit(solution)/shard_map/all_to_all | solution.py:271
  298.4 30.2 %all_to_all.61 = bf16[4,36,1152]{2,1,0:T(8,128)(2,1)S(1)} all-to-all(bf16[4,36,1152]{2,1,0:T(8,128)(2,1)S(1)} %broadcast_in_dim.8), channel_id=1, replica_groups={{0,8,16,24},{1,9,17,25},{2,10,18,26},{3,11,19,27},{4,12,20,28},{5,13,21..., dimensions={0} | all-to-all | bytes 663552 | tf_op jit(solution)/shard_map/all_to_all | solution.py:315
  328.8 28.2 %all_to_all.62 = bf16[8,36,1152]{2,1,0:T(8,128)(2,1)S(1)} all-to-all(bf16[8,36,1152]{2,1,0:T(8,128)(2,1)S(1)} %broadcast_in_dim.9), channel_id=1, replica_groups={{0,2,4,6,256,258,260,262},{1,3,5,7,257,259,261,263},{8,10,12,14,264,266..., dimensions={0} | all-to-all | bytes 1327104 | tf_op jit(solution)/shard_map/all_to_all | solution.py:321
  357.2 4.1 %collective-permute-start.3 = (bf16[288,1152]{1,0:T(8,128)(2,1)S(1)}, bf16[288,1152]{1,0:T(8,128)(2,1)S(1)}, u32[]{:S(2)}, u32[]{:S(2)}) collective-permute-start(bf16[288,1152]{1,0:T(8,128)(2,1)S(1)} %reshape.57.mine_ref), channel_id=1, source_target_pairs={{0,1},{1,0},{2,3},{3,2},{4,5},{5,4},{6,7},{7,6},{8,9},{9,8},{10,11... | collective-permute-start | bytes 1990664 | tf_op jit(solution)/shard_map/ppermute | solution.py:279
  363.0 1.8 shard_map.83
  (46 shorter events, 20.8 us)
Async XLA Ops:
  7.2 86.4 %all-gather.2.cloned.1.call-start = ((), (), s32[]{:S(2)}) async-start(), calls=%async_computation.11 | async-start | bytes 2985984 | tf_op jit(solution)/shard_map/all_gather | solution.py:342
  7.2 3.2 copy-start.3
  10.9 41.2 %copy-start.5 = (bf16[8,72,1152]{2,1,0:T(8,128)(2,1)}, bf16[8,72,1152]{2,1,0:T(8,128)(2,1)S(1)}, u32[]{:S(2)}) copy-start(bf16[8,72,1152]{2,1,0:T(8,128)(2,1)S(1)} %get-tuple-element.28) | copy-start | bytes 3981316
  52.0 7.7 %copy-start = (bf16[8,128,1152]{2,1,0:T(8,128)(2,1)}, bf16[8,128,1152]{2,1,0:T(8,128)(2,1)S(1)}, u32[]{:S(2)}) copy-start(bf16[8,128,1152]{2,1,0:T(8,128)(2,1)S(1)} %all_to_all.55.hidden_ref) | copy-start | bytes 7077892
  52.0 41.6 %copy-start.8 = (bf16[1,2,64,1152]{3,2,1,0:T(8,128)(2,1)S(1)}, bf16[1,2,64,1152]{3,2,1,0:T(8,128)(2,1)}, u32[]{:S(2)}) copy-start(bf16[1,2,64,1152]{3,2,1,0:T(8,128)(2,1)} %param.5) | copy-start | bytes 884740
  52.0 29.7 %all-to-all-start.2 = ((bf16[8,72,1152]{2,1,0:T(8,128)(2,1)}), bf16[8,72,1152]{2,1,0:T(8,128)(2,1)}, u32[]{:S(2)}, u32[]{:S(2)}) async-start(bf16[8,72,1152]{2,1,0:T(8,128)(2,1)} %copy-done.5), calls=%async_computation.2 | async-start | bytes 2654208 | tf_op jit(solution)/shard_map/all_to_all | solution.py:271
  59.8 0.8 copy-start.6
  60.5 0.7 copy-start.9
  93.6 1.8 copy-start.1
  97.2 1.5 copy-start.2
  98.7 18.7 %collective-permute-start = (bf16[1152,1152]{1,0:T(8,128)(2,1)S(1)}, bf16[1152,1152]{1,0:T(8,128)(2,1)S(1)}, u32[]{:S(2)}, u32[]{:S(2)}) collective-permute-start(bf16[1152,1152]{1,0:T(8,128)(2,1)S(1)} %get-tuple-element.30.mine_ref), channel_id=1, source_target_pairs={{0,1},{1,0},{2,3},{3,2},{4,5},{5,4},{6,7},{7,6},{8,9},{9,8},{10,11... | collective-permute-start | bytes 7962632 | tf_op jit(solution)/shard_map/ppermute | solution.py:279
  117.4 1.5 copy-start.11
  127.4 14.2 %collective-permute-start.1 = (bf16[1152,1152]{1,0:T(8,128)(2,1)}, bf16[1152,1152]{1,0:T(8,128)(2,1)S(1)}, u32[]{:S(2)}, u32[]{:S(2)}) collective-permute-start(bf16[1152,1152]{1,0:T(8,128)(2,1)} %get-tuple-element.33), channel_id=1, source_target_pairs={{0,1},{1,0},{2,3},{3,2},{4,5},{5,4},{6,7},{7,6},{8,9},{9,8},{10,11... | collective-permute-start | bytes 7962632 | tf_op jit(solution)/shard_map/ppermute | solution.py:279
  141.6 1.5 copy-start.10
  159.0 6.3 %copy-start.7 = (bf16[2,216,512]{2,1,0:T(8,128)(2,1)S(1)}, bf16[2,216,512]{2,1,0:T(8,128)(2,1)}, u32[]{:S(2)}) copy-start(bf16[2,216,512]{2,1,0:T(8,128)(2,1)} %copy-done.6) | copy-start | bytes 1327108
  159.0 62.5 %all-to-all-start.7 = ((bf16[8,216,1152]{2,1,0:T(8,128)(2,1)}), bf16[8,216,1152]{2,1,0:T(8,128)(2,1)}, u32[]{:S(2)}, u32[]{:S(2)}) async-start(bf16[8,216,1152]{2,1,0:T(8,128)(2,1)} %get-tuple-element.39), calls=%async_computation.7 | async-start | bytes 7962624 | tf_op jit(solution)/shard_map/all_to_all | solution.py:271
  170.7 1.5 copy-start.4
  224.7 5.6 %collective-permute-start.2 = (bf16[144,1152]{1,0:T(8,128)(2,1)S(1)}, bf16[144,1152]{1,0:T(8,128)(2,1)S(1)}, u32[]{:S(2)}, u32[]{:S(2)}) collective-permute-start(bf16[144,1152]{1,0:T(8,128)(2,1)S(1)} %get-tuple-element.42), channel_id=1, source_target_pairs={{0,1},{1,0},{2,3},{3,2},{4,5},{5,4},{6,7},{7,6},{8,9},{9,8},{10,11... | collective-permute-start | bytes 995336 | tf_op jit(solution)/shard_map/ppermute | solution.py:279
  257.1 39.9 %all-to-all-start.6 = ((bf16[8,128,1152]{2,1,0:T(8,128)(2,1)}), bf16[8,128,1152]{2,1,0:T(8,128)(2,1)S(1)}, u32[]{:S(2)}, u32[]{:S(2)}) async-start(bf16[8,128,1152]{2,1,0:T(8,128)(2,1)} %copy-done.4), calls=%async_computation.6 | async-start | bytes 4718592 | tf_op jit(solution)/shard_map/all_to_all | solution.py:271
  357.2 5.8 %collective-permute-start.3 = (bf16[288,1152]{1,0:T(8,128)(2,1)S(1)}, bf16[288,1152]{1,0:T(8,128)(2,1)S(1)}, u32[]{:S(2)}, u32[]{:S(2)}) collective-permute-start(bf16[288,1152]{1,0:T(8,128)(2,1)S(1)} %reshape.57.mine_ref), channel_id=1, source_target_pairs={{0,1},{1,0},{2,3},{3,2},{4,5},{5,4},{6,7},{7,6},{8,9},{9,8},{10,11... | collective-permute-start | bytes 1990664 | tf_op jit(solution)/shard_map/ppermute | solution.py:279
Sparse Core Ops, SparseCore 0:
  10.5 72.2 all-gather.1

commit v3 on v2

--- a/solution.py
+++ b/solution.py
@@ -48,11 +48,17 @@
     )
 
 
-def norm_kernel(x_ref, wo_ref, out_ref, copies_ref):
+def norm_kernel(at_ref, x_ref, wq_ref, wo_ref, out_ref, own_ref, parts_ref):
     hidden = normalize(x_ref[...])[0].astype(BF)
     for j in range(8):
         out_ref[j] = hidden
-        copies_ref[j] = wo_ref[...]
+    for i in range(3):
+        parts_ref[i] = wq_ref[1, i].astype(F32)
+    parts_ref[3] = wo_ref[1].astype(F32)
+    first = wo_ref[0].astype(F32)
+    half = jnp.where(at_ref[0] == 0, first[:40], first[32:])
+    part = parts_ref[2 * at_ref[0] + at_ref[1]]
+    own_ref[...] = jnp.concatenate([part, half], axis=0).astype(BF)
 
 
 def frame_rows(hidden_ref, f):
@@ -68,7 +74,11 @@
     return tuple(stacked[i * E : (i + 1) * E].astype(BF) for i in range(3))
 
 
-def spatial_kernel(hidden_ref, w_ref, heads_ref, qkv_ref):
+def spatial_kernel(hidden_ref, w_ref, all_ref, heads_ref, qkv_ref, two_ref, one_ref):
+    for h in range(8):
+        both = all_ref[h].astype(F32)
+        two_ref[h] = both[:E].astype(BF)
+        one_ref[h] = both[E:].astype(BF)
     outs = []
     for f in range(2):
         qkv = nt(w_ref[...], frame_rows(hidden_ref, f))
@@ -83,8 +93,15 @@
         heads_ref[2 * m + 1] = b.astype(BF)
 
 
-def middle_kernel(x_ref, g_ref, heads_ref, wo_ref, pass_ref, out_ref, same_ref):
-    y = (x_ref[...].astype(F32) + tn(heads_ref[...], wo_ref[...])).astype(BF)
+def middle_kernel(core_ref, x_ref, g_ref, heads_ref, mine_ref, other_ref, out_ref, split_ref):
+    core = core_ref[0]
+    for h in range(8):
+        heads = heads_ref[h].astype(F32)
+        split_ref[0, h * 40 : (h + 1) * 40] = heads[:40]
+        low = jnp.zeros((8, 128), F32)
+        split_ref[1, h * 40 : (h + 1) * 40] = jnp.concatenate([low, heads[40:]], axis=0)
+    y = x_ref[...].astype(F32) + tn(split_ref[core].astype(BF), mine_ref[...])
+    y = (y + tn(split_ref[1 - core].astype(BF), other_ref[...])).astype(BF)
     g = g_ref[...]
     for s in range(2):
         for f in range(2):
@@ -94,14 +111,17 @@
 
 
 def temporal_kernel(
-    core_ref, pair_ref, mine_ref, other_ref,
+    at_ref, pair_ref, own_ref, z_ref, core_ref, both_ref,
     back_ref, keep_ref, send_ref,
-    w_ref, gw_ref, qk_ref, vg_ref, g0_ref, g1_ref, sems,
+    w_ref, gw_ref, in_ref, grads_ref, sems,
 ):
-    core = core_ref[0]
+    core, odd = at_ref[0], at_ref[1]
+    here, there = 2 * core, 2 * (1 - core)
     loads = (
-        pltpu.make_async_copy(mine_ref, w_ref.at[core], sems.at[0]),
-        pltpu.make_async_copy(other_ref, w_ref.at[1 - core], sems.at[1]),
+        pltpu.make_async_copy(own_ref, w_ref.at[here + odd], sems.at[0]),
+        pltpu.make_async_copy(z_ref, w_ref.at[here + 1 - odd], sems.at[1]),
+        pltpu.make_async_copy(core_ref, w_ref.at[there + odd], sems.at[2]),
+        pltpu.make_async_copy(both_ref, w_ref.at[there + 1 - odd], sems.at[3]),
     )
     for load in loads:
         load.start()
@@ -110,11 +130,10 @@
     grad = jnp.concatenate([pair_ref[s, 1, f] for s in range(2) for f in range(2)], axis=0)
     normed, inverse = normalize(rows)
     hidden = normed.astype(BF)
-    both = jnp.concatenate([hidden, grad], axis=0)
     for load in loads:
         load.wait()
-    qk_ref[...] = nt(w_ref[0], hidden)
-    vg_ref[...] = nt(w_ref[1], both)
+    for i in range(4):
+        in_ref[i] = nt(w_ref[i], grad if i == 3 else hidden)
 
     def rounded(value):
         return value.astype(BF).astype(F32)
@@ -125,13 +144,9 @@
     def behind(value, r):
         return pltpu.roll(value, 32 * r, 1) if r else value
 
-    zeros = jnp.zeros((E, 128), F32)
     for h in range(8):
-        base = h * 2 * E
-        q = rounded(qk_ref[base : base + E])
-        k = rounded(qk_ref[base + E : base + 2 * E])
-        v = rounded(vg_ref[base : base + E, :128])
-        gh = rounded(vg_ref[base + E : base + 2 * E, 128:])
+        span = slice(h * E, (h + 1) * E)
+        q, k, v, gh = (rounded(in_ref[i, span]) for i in range(4))
         ks = [ahead(k, r) for r in range(4)]
         vs = [ahead(v, r) for r in range(4)]
         exps = [jnp.exp(jnp.sum(q * kr, axis=0, keepdims=True) * SCALE) for kr in ks]
@@ -145,22 +160,22 @@
         gq = sum(sg * kr for sg, kr in zip(sgs, ks))
         gk = sum(behind(sg * q, r) for r, sg in enumerate(sgs))
         gv = sum(behind(w * gh, r) for r, w in enumerate(weights))
-        g0_ref[base : base + 2 * E] = jnp.concatenate([gq, gk], axis=0).astype(BF)
-        g1_ref[base : base + 2 * E, :128] = jnp.concatenate([gv, zeros], axis=0).astype(BF)
-        g1_ref[base : base + 2 * E, 128:] = jnp.concatenate([zeros, heads], axis=0).astype(BF)
-    for h in range(8):
-        span = slice(h * 2 * E, (h + 1) * 2 * E)
-        gw_ref[0, span] = nn(g0_ref[span], hidden).astype(BF)
-        gw_ref[1, span] = nn(g1_ref[span], both).astype(BF)
+        for i, grads in enumerate((gq, gk, gv, heads)):
+            grads_ref[i, span] = grads
+        wide = slice(h * 2 * E, (h + 1) * 2 * E)
+        qk_grads = jnp.concatenate([gq, gk], axis=0).astype(BF)
+        gw_ref[0, wide] = nn(qk_grads, hidden).astype(BF)
+        vo_grads = [nn(gv.astype(BF), hidden), nn(heads.astype(BF), grad)]
+        gw_ref[1, wide] = jnp.concatenate(vo_grads, axis=0).astype(BF)
     stores = (
         pltpu.make_async_copy(gw_ref.at[core], keep_ref, sems.at[0]),
         pltpu.make_async_copy(gw_ref.at[1 - core], send_ref, sems.at[1]),
     )
     for store in stores:
         store.start()
-    mixed = tn(g1_ref[...], w_ref[1])
-    normed_grads = tn(g0_ref[...], w_ref[0]) + mixed[:128]
-    result = (rows.astype(F32) + mixed[128:]).astype(BF)
+    sums = [tn(grads_ref[i].astype(BF), w_ref[i]) for i in range(4)]
+    normed_grads = sums[0] + sums[1] + sums[2]
+    result = (rows.astype(F32) + sums[3]).astype(BF)
     total_grad = normalize_back(grad, inverse, normed, normed_grads).astype(BF)
     for s in range(2):
         for f in range(2):
@@ -176,17 +191,20 @@
 
 
 def turn_kernel(
-    back_ref, heads_ref, wo_ref, keep_ref, recv_ref, gh_ref, parts_ref, out_ref, grad_ref
+    core_ref, back_ref, heads_ref, mine_ref, other_ref,
+    gh_ref, gw_ref, out_ref, grad_ref, split_ref,
 ):
+    core = core_ref[0]
     out_ref[...] = local_rows(back_ref, 0)
     grad = local_rows(back_ref, 1)
     grad_ref[...] = grad
-    gh_ref[...] = nt(wo_ref[...], grad).astype(BF)
-    gw = nn(heads_ref[...], grad)
+    split_ref[core] = nt(mine_ref[...], grad)
+    split_ref[1 - core] = nt(other_ref[...], grad)
     for h in range(8):
-        span = slice(h * 2 * E, (h + 1) * 2 * E)
-        two = keep_ref[span].astype(F32) + recv_ref[span].astype(F32)
-        parts_ref[h] = jnp.concatenate([two, gw[h * E : (h + 1) * E]], axis=0).astype(BF)
+        at = h * 40
+        pieces = [split_ref[0, at : at + 40], split_ref[1, at + 8 : at + 40]]
+        gh_ref[h] = jnp.concatenate(pieces, axis=0).astype(BF)
+        gw_ref[h] = nn(heads_ref[h], grad).astype(BF)
 
 
 def spatial_back_kernel(qkv_ref, gh_ref, hidden_ref, w_ref, terms_ref, gw_ref):
@@ -213,15 +231,14 @@
     gw_ref[...] = total.astype(BF)
 
 
-def gather_kernel(core_ref, parts_ref, qkv_ref, two_ref, keep_ref, send_ref, halves_ref):
+def gather_kernel(core_ref, parts_ref, qkv_ref, keep_ref, send_ref, halves_ref):
     core = core_ref[0]
     total = parts_ref[0].astype(F32)
     for j in range(1, 8):
         total = total + parts_ref[j].astype(F32)
-    two_ref[...] = total[: 2 * E].astype(BF)
     qkv = qkv_ref[...].astype(F32)
     halves_ref[0] = qkv[: 2 * E]
-    halves_ref[1] = jnp.concatenate([qkv[2 * E :], total[2 * E :]], axis=0)
+    halves_ref[1] = jnp.concatenate([qkv[2 * E :], total], axis=0)
     keep_ref[...] = halves_ref[core].astype(BF)
     send_ref[...] = halves_ref[1 - core].astype(BF)
 
@@ -238,7 +255,14 @@
         out_ref[b] = halves_ref[1, at + E : at + 2 * E]
 
 
-def last_kernel(terms_ref, x_ref, g_ref, pass_ref, out_ref, same_ref):
+def last_kernel(
+    terms_ref, x_ref, g_ref, keep_ref, recv_ref, two_ref, out_ref, chain_ref, rows_ref
+):
+    rows_ref[: 2 * E] = keep_ref[...].astype(F32) + recv_ref[...].astype(F32)
+    rows_ref[2 * E : 4 * E] = two_ref[...].astype(F32)
+    rows_ref[4 * E :] = jnp.zeros_like(rows_ref[4 * E :])
+    for i in range(8):
+        chain_ref[i] = rows_ref[i * 40 : (i + 1) * 40].astype(BF)
     normed, inverse = normalize(x_ref[...])
     normed_grads = terms_ref[0].astype(F32)
     for j in range(1, 8):
@@ -275,12 +299,8 @@
     return lax.all_to_all(blocks, "seq", 0, 0, tiled=True)
 
 
-def swap_cores(value, n_dp):
-    return lax.ppermute(value, "dp", [(i, i ^ 1) for i in range(n_dp)])
-
-
-def pick(stacked, at):
-    return lax.dynamic_index_in_dim(stacked, at, 0, keepdims=False)
+def swap_cores(value, n_dp, bit=1):
+    return lax.ppermute(value, "dp", [(i, i ^ bit) for i in range(n_dp)])
 
 
 def groups_of(n_dp):
@@ -299,12 +319,7 @@
 
 
 def sum_near(grads, near):
-    rows, depth = grads.shape
-    n = len(near[0])
-    parts = lax.all_to_all(
-        grads.reshape(n, rows // n, depth), ("seq", "dp"), 0, 0,
-        tiled=True, axis_index_groups=near,
-    )
+    parts = lax.all_to_all(grads, ("seq", "dp"), 0, 0, tiled=True, axis_index_groups=near)
     return jnp.sum(parts.astype(F32), axis=0).astype(BF)
 
 
@@ -326,78 +341,84 @@
 
 def on_device(n_dp, latents, cotangent, w_qkv, w_out):
     depth = latents.shape[-1]
-    core = lax.axis_index("dp") % 2
-    core_arg = core.reshape(1).astype(jnp.int32)
+    index = lax.axis_index("dp")
+    at = jnp.stack([index % 2, index // 2 % 2]).astype(jnp.int32)
     near, far = groups_of(n_dp)
     x = latents.reshape(128, depth)
     g = cotangent.reshape(128, depth)
     w_own = w_qkv[0].reshape(3 * E, depth)
 
-    half_two = pick(
-        jnp.concatenate([w_qkv[1].reshape(3 * E, depth), w_out[1].reshape(E, depth)]).reshape(
-            2, 2 * E, depth
-        ),
-        core,
-    )
-    mine_two = lax.all_gather(half_two, "head", axis_index_groups=RING).reshape(16 * E, depth)
-
-    hidden, wo = call(
-        norm_kernel, (shape(8, 128, depth), shape(8, E, depth)), x, w_out[0].reshape(E, depth)
-    )
+    hidden, own = call(
+        norm_kernel, (shape(8, 128, depth), shape(E + 40, depth)),
+        at, x, w_qkv.reshape(2, 3, E, depth), w_out.reshape(2, E, depth),
+        in_specs=[SMEM] + [VMEM] * 3,
+        scratch_shapes=[pltpu.VMEM((4, E, depth), F32)],
+    )
+    parts = lax.all_gather(own, "head", axis_index_groups=RING)
     hidden = over_head(hidden)
-    wo = over_head(wo).reshape(8 * E, depth)
-    heads, qkv = call(spatial_kernel, (shape(8, E, 128), shape(2, 3 * E, 512)), hidden, w_own)
-    heads = over_head(heads).reshape(8 * E, 128)
+    heads, qkv, own, mine_one = call(
+        spatial_kernel,
+        (shape(8, E, 128), shape(2, 3 * E, 512), shape(8, E, depth), shape(8, 40, depth)),
+        hidden, w_own, parts,
+    )
+    heads = over_head(heads)
+    mine_one = mine_one.reshape(320, depth)
+    other_one = swap_cores(mine_one, n_dp)
+    own = own.reshape(8 * E, depth)
+    from_z = swap_cores(own, n_dp, 2)
+    from_core = swap_cores(own, n_dp)
+    from_both = swap_cores(from_z, n_dp)
+    pair = call(
+        middle_kernel, shape(2, 2, 2, 32, depth), at, x, g, heads, mine_one, other_one,
+        in_specs=[SMEM] + [VMEM] * 5,
+        scratch_shapes=[pltpu.VMEM((2, 320, 128), F32)],
+    )
+    pair = over_seq(pair)
     big = shape(16 * E, depth)
-    pair, mine_two = call(
-        middle_kernel, (shape(2, 2, 2, 32, depth), big), x, g, heads, wo, mine_two,
-        in_specs=[VMEM] * 4 + [ANY],
-        out_specs=(VMEM, ANY),
-        input_output_aliases={4: 1},
-    )
-    pair = over_seq(pair)
-    other_two = swap_cores(mine_two, n_dp)
     back, keep, send = call(
         temporal_kernel,
         (shape(2, 2, 2, 32, depth), big, big),
-        core_arg, pair, mine_two, other_two,
-        in_specs=[SMEM, VMEM, ANY, ANY],
+        at, pair, own, from_z, from_core, from_both,
+        in_specs=[SMEM, VMEM] + [ANY] * 4,
         out_specs=(VMEM, ANY, ANY),
         scratch_shapes=[
+            pltpu.VMEM((4, 8 * E, depth), BF),
             pltpu.VMEM((2, 16 * E, depth), BF),
-            pltpu.VMEM((2, 16 * E, depth), BF),
-            pltpu.VMEM((16 * E, 128), F32),
-            pltpu.VMEM((16 * E, 256), F32),
-            pltpu.VMEM((16 * E, 128), BF),
-            pltpu.VMEM((16 * E, 256), BF),
-            pltpu.SemaphoreType.DMA((2,)),
+            pltpu.VMEM((4, 8 * E, 128), F32),
+            pltpu.VMEM((4, 8 * E, 128), F32),
+            pltpu.SemaphoreType.DMA((4,)),
         ],
     )
     back = over_seq(back)
+    two = (keep.astype(F32) + swap_cores(send, n_dp).astype(F32)).astype(BF)
+    two = lax.psum_scatter(
+        two, "head", scatter_dimension=0, tiled=True, axis_index_groups=RING
+    )
     gh, parts, output, grad_one = call(
         turn_kernel,
-        (shape(8 * E, 128), shape(8, 3 * E, depth), shape(128, depth), shape(128, depth)),
-        back, heads, wo, keep, swap_cores(send, n_dp),
-    )
-    gh = over_head(gh.reshape(8, E, 128))
+        (shape(8, E, 128), shape(8, E, depth), shape(128, depth), shape(128, depth)),
+        at, back, heads, mine_one, other_one,
+        in_specs=[SMEM] + [VMEM] * 4,
+        scratch_shapes=[pltpu.VMEM((2, 320, 128), F32)],
+    )
+    gh = over_head(gh)
     parts = over_head(parts)
     terms, qkv_one = call(
         spatial_back_kernel, (shape(8, 128, depth), shape(3 * E, depth)), qkv, gh, hidden, w_own
     )
     half = shape(2 * E, depth)
-    two, keep, send = call(
-        gather_kernel, (half, half, half), core_arg, parts, qkv_one,
+    keep, send = call(
+        gather_kernel, (half, half), at, parts, qkv_one,
         in_specs=[SMEM, VMEM, VMEM],
         scratch_shapes=[pltpu.VMEM((2, 2 * E, depth), F32)],
     )
-    one = (keep.astype(F32) + swap_cores(send, n_dp).astype(F32)).astype(BF)
-    part = sum_near(jnp.concatenate([one, two]), near)
-    latent_grads, part = call(
-        last_kernel, (shape(128, depth), shape(*part.shape)), over_head(terms), x, grad_one, part,
-        in_specs=[VMEM] * 3 + [ANY],
-        out_specs=(VMEM, ANY),
-        input_output_aliases={3: 1},
-    )
+    n_near = len(near[0])
+    latent_grads, chain = call(
+        last_kernel, (shape(128, depth), shape(n_near, 320 // n_near, depth)),
+        over_head(terms), x, grad_one, keep, swap_cores(send, n_dp), two,
+        scratch_shapes=[pltpu.VMEM((320, depth), F32)],
+    )
+    part = sum_near(chain, near)
     mine = spread(sum_far(part, far), near)
     grad_qkv, grad_out = call(
         result_kernel,
@@ -405,9 +426,9 @@
             jax.ShapeDtypeStruct((2, 3, E, depth), F32),
             jax.ShapeDtypeStruct((2, E, depth), F32),
         ),
-        core_arg, mine, swap_cores(mine, n_dp),
+        at, mine, swap_cores(mine, n_dp),
         in_specs=[SMEM, VMEM, VMEM],
-        scratch_shapes=[pltpu.VMEM((2, 4 * E, depth), F32)],
+        scratch_shapes=[pltpu.VMEM((2, 320, depth), F32)],
     )
     return (
         output.reshape(latents.shape),

time: 373 us -> 358 us (0.960); the launches traced: 372 us -> 353 us
  blocking collectives: 170 us -> 117 us
  starting transfers between devices: 37.6 us -> 55.6 us
  waiting for transfers between devices: 105 us -> 119 us
    all_to_all x3 -> x2, blocking collectives: 62.8 us -> 20.6 us  [over_head(): lax.all_to_all(blocks, 'head', 0, 0, tiled=True, axis_index_groups=RING)]
    all_to_all x3, waiting for transfers between devices: 102 us -> 69.3 us  [over_head(): lax.all_to_all(blocks, 'head', 0, 0, tiled=True, axis_index_groups=RING)]
    all_gather x1, waiting for transfers between devices: 0.01 us -> 24.9 us  [on_device(): parts = lax.all_gather(own, 'head', axis_index_groups=RING)]
    ppermute x4 -> x7, waiting for transfers between devices: 2.96 us -> 25 us  [swap_cores(): return lax.ppermute(value, 'dp', [(i, i ^ bit) for i in range(n_dp)])]
    ppermute x4 -> x7, starting transfers between devices: 19.1 us -> 38.1 us  [swap_cores(): return lax.ppermute(value, 'dp', [(i, i ^ bit) for i in range(n_dp)])]
    all_to_all x1, blocking collectives: 28.2 us -> 23 us  [spread(): lax.all_to_all(copies, ('seq', 'dp'), 0, 0, tiled=True, axis_index_groups...]
    unnamed x24 -> x34, local copies, waits for them, and re-layouts: 9.23 us -> 14.3 us
    convert_element_type x1, other arithmetic: 0.09 us -> 4.01 us  [on_device(): two = (keep.astype(F32) + swap_cores(send, n_dp).astype(F32)).astype(BF)]
  transfers between devices with their start and end apart: 8 -> 12, of which waited for: 5 -> 8; matrix products, arithmetic and copies ran while one was open for 0% -> 0% of each run, Pallas kernels for 2% -> 3%
where the time goes in v3:
time: 358 us; the launch traced here: 353 us
  waiting for transfers between devices  119 us (33%)
  blocking collectives  117 us (33%)
  starting transfers between devices  55.6 us (16%)
  Pallas kernels  28 us (8%)
  local copies, waits for them, and re-layouts  14.5 us (4%)
  between operations  14.2 us (4%)
  other arithmetic  4.25 us (1%)
    all_to_all x3, waiting for transfers between devices, over_head(): lax.all_to_all(blocks, 'head', 0, 0, tiled=True, axis_index_groups=RING)  69.3 us
    ppermute x7, starting transfers between devices, swap_cores(): return lax.ppermute(value, 'dp', [(i, i ^ bit) for i in range(n_dp)])  38.1 us
    all_to_all x1, blocking collectives, sum_far(): lax.all_to_all(copies, 'dp', 0, 0, tiled=True, axis_index_groups=far)  29.2 us
    pallas_call x9, Pallas kernels, call(): pl.pallas_call(kernel, out_shape=outs, in_specs=more.pop('in_specs', [VME...  28 us
    ppermute x7, waiting for transfers between devices, swap_cores(): return lax.ppermute(value, 'dp', [(i, i ^ bit) for i in range(n_dp)])  25 us
    all_gather x1, waiting for transfers between devices, on_device(): parts = lax.all_gather(own, 'head', axis_index_groups=RING)  24.9 us
    all_to_all x1, blocking collectives, sum_near(): lax.all_to_all(grads, ('seq', 'dp'), 0, 0, tiled=True, axis_index_groups=...  23.9 us
    all_to_all x1, blocking collectives, spread(): lax.all_to_all(copies, ('seq', 'dp'), 0, 0, tiled=True, axis_index_groups...  23 us
  transfers between devices with their start and end apart: 12, of which 8 were waited for; matrix products, arithmetic and copies ran while one was open for 0% of the time, Pallas kernels for 3%

profile of v3, /device:TPU:7, one launch (start us, length us, event | category | flops | bytes accessed | tf_op | source)
XLA Modules:
  0.0 352.7 jit_solution(14322187979864183252)
XLA Ops:
  12.9 7.0 %all-to-all-start = ((bf16[8,128,1152]{2,1,0:T(8,128)(2,1)}), bf16[8,128,1152]{2,1,0:T(8,128)(2,1)}, u32[]{:S(2)}, u32[]{:S(2)}) async-start(bf16[8,128,1152]{2,1,0:T(8,128)(2,1)} %get-tuple-element.25), calls=%async_computation | async-start | bytes 4718592 | tf_op jit(solution)/shard_map/all_to_all | solution.py:295
  20.0 29.4 %all-to-all-done.hidden_ref = bf16[8,128,1152]{2,1,0:T(8,128)(2,1)} async-done(((bf16[8,128,1152]{2,1,0:T(8,128)(2,1)}), bf16[8,128,1152]{2,1,0:T(8,128)(2,1)}, u32[]{:S(2)}, u32[]{:S(2)}) %all-to-all-start) | async-done | bytes 2359328 | tf_op jit(solution)/shard_map/all_to_all | solution.py:295
  49.4 24.9 %all-gather.3.cloned.1.call-done = bf16[896,1152]{1,0:T(8,128)(2,1)} async-done(((bf16[112,1152]{1,0:T(8,128)(2,1)}), bf16[896,1152]{1,0:T(8,128)(2,1)}) %all-gather.3.cloned.1.call-update) | async-done | bytes 2064400 | tf_op jit(solution)/shard_map/all_gather | solution.py:357
  80.0 6.6 %collective-permute-start.1 = (bf16[576,1152]{1,0:T(8,128)(2,1)S(1)}, bf16[576,1152]{1,0:T(8,128)(2,1)S(1)}, u32[]{:S(2)}, u32[]{:S(2)}) collective-permute-start(bf16[576,1152]{1,0:T(8,128)(2,1)S(1)} %bitcast.31), channel_id=1, source_target_pairs={{0,2},{1,3},{2,0},{3,1},{4,6},{5,7},{6,4},{7,5},{8,10},{9,11},{10,... | collective-permute-start | bytes 3981320 | tf_op jit(solution)/shard_map/ppermute | solution.py:303
  86.6 7.2 %collective-permute-start.2 = (bf16[576,1152]{1,0:T(8,128)(2,1)S(1)}, bf16[576,1152]{1,0:T(8,128)(2,1)S(1)}, u32[]{:S(2)}, u32[]{:S(2)}) collective-permute-start(bf16[576,1152]{1,0:T(8,128)(2,1)S(1)} %bitcast.32), channel_id=1, source_target_pairs={{0,1},{1,0},{2,3},{3,2},{4,5},{5,4},{6,7},{7,6},{8,9},{9,8},{10,11... | collective-permute-start | bytes 3981320 | tf_op jit(solution)/shard_map/ppermute | solution.py:303
  93.8 17.2 %collective-permute-done.1.z_ref = bf16[576,1152]{1,0:T(8,128)(2,1)S(1)} collective-permute-done((bf16[576,1152]{1,0:T(8,128)(2,1)S(1)}, bf16[576,1152]{1,0:T(8,128)(2,1)S(1)}, u32[]{:S(2)}, u32[]{:S(2)}) %collective-permute-start.1) | collective-permute-done | bytes 1327136 | tf_op jit(solution)/shard_map/ppermute | solution.py:303
  111.0 7.6 %collective-permute-start.3 = (bf16[576,1152]{1,0:T(8,128)(2,1)S(1)}, bf16[576,1152]{1,0:T(8,128)(2,1)S(1)}, u32[]{:S(2)}, u32[]{:S(2)}) collective-permute-start(bf16[576,1152]{1,0:T(8,128)(2,1)S(1)} %collective-permute-done.1.z_ref), channel_id=1, source_target_pairs={{0,1},{1,0},{2,3},{3,2},{4,5},{5,4},{6,7},{7,6},{8,9},{9,8},{10,11... | collective-permute-start | bytes 3981320 | tf_op jit(solution)/shard_map/ppermute | solution.py:303
  120.5 10.2 %all_to_all.50.heads_ref = bf16[8,72,128]{2,1,0:T(8,128)(2,1)S(1)} all-to-all(bf16[8,72,128]{2,1,0:T(8,128)(2,1)S(1)} %get-tuple-element.27), channel_id=1, replica_groups={{0,64,128,192,224,160,96,32},{1,65,129,193,225,161,97,33},{2,66,130,194..., dimensions={0} | all-to-all | bytes 294912 | tf_op jit(solution)/shard_map/all_to_all | solution.py:295
  131.8 9.3 %all_to_all.51.pair_ref = bf16[2,2,2,32,1152]{4,3,2,1,0:T(8,128)(2,1)S(1)} all-to-all(bf16[2,2,2,32,1152]{4,3,2,1,0:T(8,128)(2,1)S(1)} %shard_map.77), channel_id=1, replica_groups=mesh['seq'=2,'head'=8,'dp'=32] {'seq'}, dimensions={0} | all-to-all | bytes 1179648 | tf_op jit(solution)/shard_map/all_to_all | solution.py:299
  142.1 8.0 %shard_map.78 = (bf16[2,2,2,32,1152]{4,3,2,1,0:T(8,128)(2,1)S(1)}, bf16[1152,1152]{1,0:T(8,128)(2,1)}, bf16[1152,1152]{1,0:T(8,128)(2,1)}) custom-call(s32[2]{0:T(128)S(1)} %pad_add_fusion.at_ref.core_ref, bf16[2,2,2,32,1152]{4,3,2,1,0:T(8,128)(2,1)S(1)} %all_to_all.51.pair_ref, bf16[576,1152]{1,0:T(8,128)(2,1)S(1)} %bitcast.33, ...), custom_call_target="tpu_custom_call" | custom-call | tf_op jit(solution)/shard_map/pallas_call | solution.py:284
  150.2 4.6 %collective-permute-start.5 = (bf16[1152,1152]{1,0:T(8,128)(2,1)}, bf16[1152,1152]{1,0:T(8,128)(2,1)S(1)}, u32[]{:S(2)}, u32[]{:S(2)}) collective-permute-start(bf16[1152,1152]{1,0:T(8,128)(2,1)} %get-tuple-element.41), channel_id=1, source_target_pairs={{0,1},{1,0},{2,3},{3,2},{4,5},{5,4},{6,7},{7,6},{8,9},{9,8},{10,11... | collective-permute-start | bytes 7962632 | tf_op jit(solution)/shard_map/ppermute | solution.py:303
  154.8 4.8 %collective-permute-done.5 = bf16[1152,1152]{1,0:T(8,128)(2,1)S(1)} collective-permute-done((bf16[1152,1152]{1,0:T(8,128)(2,1)}, bf16[1152,1152]{1,0:T(8,128)(2,1)S(1)}, u32[]{:S(2)}, u32[]{:S(2)}) %collective-permute-start.5) | collective-permute-done | bytes 2654240 | tf_op jit(solution)/shard_map/ppermute | solution.py:303
  163.6 10.8 %all_to_all.52.back_ref = bf16[2,2,2,32,1152]{4,3,2,1,0:T(8,128)(2,1)S(1)} all-to-all(bf16[2,2,2,32,1152]{4,3,2,1,0:T(8,128)(2,1)S(1)} %get-tuple-element.30), channel_id=1, replica_groups=mesh['seq'=2,'head'=8,'dp'=32] {'seq'}, dimensions={0} | all-to-all | bytes 1179648 | tf_op jit(solution)/shard_map/all_to_all | solution.py:299
  178.4 10.4 %all_to_all.53.gh_ref = bf16[8,72,128]{2,1,0:T(8,128)(2,1)S(1)} all-to-all(bf16[8,72,128]{2,1,0:T(8,128)(2,1)S(1)} %get-tuple-element.33), channel_id=1, replica_groups={{0,64,128,192,224,160,96,32},{1,65,129,193,225,161,97,33},{2,66,130,194..., dimensions={0} | all-to-all | bytes 294912 | tf_op jit(solution)/shard_map/all_to_all | solution.py:295
  188.9 5.2 %all-to-all-start.6 = ((bf16[8,72,1152]{2,1,0:T(8,128)(2,1)}), bf16[8,72,1152]{2,1,0:T(8,128)(2,1)S(1)}, u32[]{:S(2)}, u32[]{:S(2)}) async-start(bf16[8,72,1152]{2,1,0:T(8,128)(2,1)} %copy-done.8), calls=%async_computation.6 | async-start | bytes 2654208 | tf_op jit(solution)/shard_map/all_to_all | solution.py:295
  195.1 5.5 %shard_map.80 = (bf16[8,128,1152]{2,1,0:T(8,128)(2,1)S(1)}, bf16[216,1152]{1,0:T(8,128)(2,1)S(1)}) custom-call(bf16[2,216,512]{2,1,0:T(8,128)(2,1)S(1)} %copy-done.10, bf16[8,72,128]{2,1,0:T(8,128)(2,1)S(1)} %all_to_all.53.gh_ref, bf16[8,128,1152]{2,1,0:T(8,128)(2,1)} %all-to-all-done.hidden_ref, bf16[216,1152]{1,0:T(8,128)(2,1)S(1)} %bitcast.20), custom_call_target="tpu_custom_call" | custom-call | tf_op jit(solution)/shard_map/pallas_call | solution.py:284
  202.0 17.1 %all-to-all-done.6.parts_ref = bf16[8,72,1152]{2,1,0:T(8,128)(2,1)S(1)} async-done(((bf16[8,72,1152]{2,1,0:T(8,128)(2,1)}), bf16[8,72,1152]{2,1,0:T(8,128)(2,1)S(1)}, u32[]{:S(2)}, u32[]{:S(2)}) %all-to-all-start.6) | async-done | bytes 1327136 | tf_op jit(solution)/shard_map/all_to_all | solution.py:295
  220.1 5.3 %all-to-all-start.5 = ((bf16[8,128,1152]{2,1,0:T(8,128)(2,1)}), bf16[8,128,1152]{2,1,0:T(8,128)(2,1)S(1)}, u32[]{:S(2)}, u32[]{:S(2)}) async-start(bf16[8,128,1152]{2,1,0:T(8,128)(2,1)} %copy-done.4), calls=%async_computation.5 | async-start | bytes 4718592 | tf_op jit(solution)/shard_map/all_to_all | solution.py:295
  227.6 5.3 %collective-permute-start.4 = (bf16[144,1152]{1,0:T(8,128)(2,1)S(1)}, bf16[144,1152]{1,0:T(8,128)(2,1)S(1)}, u32[]{:S(2)}, u32[]{:S(2)}) collective-permute-start(bf16[144,1152]{1,0:T(8,128)(2,1)S(1)} %get-tuple-element.39), channel_id=1, source_target_pairs={{0,1},{1,0},{2,3},{3,2},{4,5},{5,4},{6,7},{7,6},{8,9},{9,8},{10,11... | collective-permute-start | bytes 995336 | tf_op jit(solution)/shard_map/ppermute | solution.py:303
  234.2 22.8 %all-to-all-done.5.terms_ref = bf16[8,128,1152]{2,1,0:T(8,128)(2,1)S(1)} async-done(((bf16[8,128,1152]{2,1,0:T(8,128)(2,1)}), bf16[8,128,1152]{2,1,0:T(8,128)(2,1)S(1)}, u32[]{:S(2)}, u32[]{:S(2)}) %all-to-all-start.5) | async-done | bytes 2359328 | tf_op jit(solution)/shard_map/all_to_all | solution.py:295
  260.4 23.9 %all_to_all.54 = bf16[8,40,1152]{2,1,0:T(8,128)(2,1)S(1)} all-to-all(bf16[8,40,1152]{2,1,0:T(8,128)(2,1)S(1)} %get-tuple-element.43), channel_id=1, replica_groups={{0,2,4,6,256,258,260,262},{1,3,5,7,257,259,261,263},{8,10,12,14,264,266..., dimensions={0} | all-to-all | bytes 1474560 | tf_op jit(solution)/shard_map/all_to_all | solution.py:322
  284.5 29.2 %all_to_all.55 = bf16[4,40,1152]{2,1,0:T(8,128)(2,1)S(1)} all-to-all(bf16[4,40,1152]{2,1,0:T(8,128)(2,1)S(1)} %broadcast_in_dim.8), channel_id=1, replica_groups={{0,8,16,24},{1,9,17,25},{2,10,18,26},{3,11,19,27},{4,12,20,28},{5,13,21..., dimensions={0} | all-to-all | bytes 737280 | tf_op jit(solution)/shard_map/all_to_all | solution.py:330
  313.8 23.0 %all_to_all.56 = bf16[8,40,1152]{2,1,0:T(8,128)(2,1)S(1)} all-to-all(bf16[8,40,1152]{2,1,0:T(8,128)(2,1)S(1)} %broadcast_in_dim.9), channel_id=1, replica_groups={{0,2,4,6,256,258,260,262},{1,3,5,7,257,259,261,263},{8,10,12,14,264,266..., dimensions={0} | all-to-all | bytes 1474560 | tf_op jit(solution)/shard_map/all_to_all | solution.py:336
  336.8 4.9 %collective-permute-start.6 = (bf16[320,1152]{1,0:T(8,128)(2,1)S(1)}, bf16[320,1152]{1,0:T(8,128)(2,1)S(1)}, u32[]{:S(2)}, u32[]{:S(2)}) collective-permute-start(bf16[320,1152]{1,0:T(8,128)(2,1)S(1)} %bitcast.24), channel_id=1, source_target_pairs={{0,1},{1,0},{2,3},{3,2},{4,5},{5,4},{6,7},{7,6},{8,9},{9,8},{10,11... | collective-permute-start | bytes 2211848 | tf_op jit(solution)/shard_map/ppermute | solution.py:303
  (59 shorter events, 38.3 us)
Async XLA Ops:
  7.2 67.2 %all-gather.3.cloned.1.call-start = ((), (), s32[]{:S(2)}) async-start(), calls=%async_computation.12 | async-start | bytes 2322432 | tf_op jit(solution)/shard_map/all_gather | solution.py:357
  8.3 1.2 copy-start.5
  12.9 7.0 %copy-start.6 = (bf16[2,1,3,72,1152]{4,3,2,1,0:T(8,128)(2,1)S(1)}, bf16[2,1,3,72,1152]{4,3,2,1,0:T(8,128)(2,1)}, u32[]{:S(2)}) copy-start(bf16[2,1,3,72,1152]{4,3,2,1,0:T(8,128)(2,1)} %param.6) | copy-start | bytes 2985988
  12.9 36.5 %all-to-all-start = ((bf16[8,128,1152]{2,1,0:T(8,128)(2,1)}), bf16[8,128,1152]{2,1,0:T(8,128)(2,1)}, u32[]{:S(2)}, u32[]{:S(2)}) async-start(bf16[8,128,1152]{2,1,0:T(8,128)(2,1)} %get-tuple-element.25), calls=%async_computation | async-start | bytes 4718592 | tf_op jit(solution)/shard_map/all_to_all | solution.py:295
  19.9 237.1 %reduce-scatter.2.cloned.1.call-start = ((), (), s32[]{:S(2)}) async-start(), calls=%async_computation.11 | async-start | bytes 2985984 | tf_op jit(solution)/shard_map/reduce_scatter | solution.py:394
  74.3 1.6 copy-start.7
  75.9 54.7 %copy-start.3 = (bf16[1,2,64,1152]{3,2,1,0:T(8,128)(2,1)S(1)}, bf16[1,2,64,1152]{3,2,1,0:T(8,128)(2,1)}, u32[]{:S(2)}) copy-start(bf16[1,2,64,1152]{3,2,1,0:T(8,128)(2,1)} %param.4) | copy-start | bytes 884740
  75.9 54.7 %copy-start.13 = (bf16[1,2,64,1152]{3,2,1,0:T(8,128)(2,1)S(1)}, bf16[1,2,64,1152]{3,2,1,0:T(8,128)(2,1)}, u32[]{:S(2)}) copy-start(bf16[1,2,64,1152]{3,2,1,0:T(8,128)(2,1)} %param.5) | copy-start | bytes 884740
  80.0 70.1 %copy-start.9 = (bf16[2,216,512]{2,1,0:T(8,128)(2,1)}, bf16[2,216,512]{2,1,0:T(8,128)(2,1)S(1)}, u32[]{:S(2)}) copy-start(bf16[2,216,512]{2,1,0:T(8,128)(2,1)S(1)} %get-tuple-element.32.qkv_ref) | copy-start | bytes 1327108
  80.0 31.0 %collective-permute-start.1 = (bf16[576,1152]{1,0:T(8,128)(2,1)S(1)}, bf16[576,1152]{1,0:T(8,128)(2,1)S(1)}, u32[]{:S(2)}, u32[]{:S(2)}) collective-permute-start(bf16[576,1152]{1,0:T(8,128)(2,1)S(1)} %bitcast.31), channel_id=1, source_target_pairs={{0,2},{1,3},{2,0},{3,1},{4,6},{5,7},{6,4},{7,5},{8,10},{9,11},{10,... | collective-permute-start | bytes 3981320 | tf_op jit(solution)/shard_map/ppermute | solution.py:303
  86.6 54.5 %collective-permute-start.2 = (bf16[576,1152]{1,0:T(8,128)(2,1)S(1)}, bf16[576,1152]{1,0:T(8,128)(2,1)S(1)}, u32[]{:S(2)}, u32[]{:S(2)}) collective-permute-start(bf16[576,1152]{1,0:T(8,128)(2,1)S(1)} %bitcast.32), channel_id=1, source_target_pairs={{0,1},{1,0},{2,3},{3,2},{4,5},{5,4},{6,7},{7,6},{8,9},{9,8},{10,11... | collective-permute-start | bytes 3981320 | tf_op jit(solution)/shard_map/ppermute | solution.py:303
  111.0 30.1 %collective-permute-start.3 = (bf16[576,1152]{1,0:T(8,128)(2,1)S(1)}, bf16[576,1152]{1,0:T(8,128)(2,1)S(1)}, u32[]{:S(2)}, u32[]{:S(2)}) collective-permute-start(bf16[576,1152]{1,0:T(8,128)(2,1)S(1)} %collective-permute-done.1.z_ref), channel_id=1, source_target_pairs={{0,1},{1,0},{2,3},{3,2},{4,5},{5,4},{6,7},{7,6},{8,9},{9,8},{10,11... | collective-permute-start | bytes 3981320 | tf_op jit(solution)/shard_map/ppermute | solution.py:303
  118.6 12.1 %collective-permute-start = (bf16[320,1152]{1,0:T(8,128)(2,1)S(1)}, bf16[320,1152]{1,0:T(8,128)(2,1)S(1)}, u32[]{:S(2)}, u32[]{:S(2)}) collective-permute-start(bf16[320,1152]{1,0:T(8,128)(2,1)S(1)} %bitcast.21), channel_id=1, source_target_pairs={{0,1},{1,0},{2,3},{3,2},{4,5},{5,4},{6,7},{7,6},{8,9},{9,8},{10,11... | collective-permute-start | bytes 2211848 | tf_op jit(solution)/shard_map/ppermute | solution.py:303
  141.1 1.1 copy-start.16
  150.2 9.4 %collective-permute-start.5 = (bf16[1152,1152]{1,0:T(8,128)(2,1)}, bf16[1152,1152]{1,0:T(8,128)(2,1)S(1)}, u32[]{:S(2)}, u32[]{:S(2)}) collective-permute-start(bf16[1152,1152]{1,0:T(8,128)(2,1)} %get-tuple-element.41), channel_id=1, source_target_pairs={{0,1},{1,0},{2,3},{3,2},{4,5},{5,4},{6,7},{7,6},{8,9},{9,8},{10,11... | collective-permute-start | bytes 7962632 | tf_op jit(solution)/shard_map/ppermute | solution.py:303
  176.6 1.1 copy-start.8
  188.9 30.2 %all-to-all-start.6 = ((bf16[8,72,1152]{2,1,0:T(8,128)(2,1)}), bf16[8,72,1152]{2,1,0:T(8,128)(2,1)S(1)}, u32[]{:S(2)}, u32[]{:S(2)}) async-start(bf16[8,72,1152]{2,1,0:T(8,128)(2,1)} %copy-done.8), calls=%async_computation.6 | async-start | bytes 2654208 | tf_op jit(solution)/shard_map/all_to_all | solution.py:295
  194.0 1.0 copy-start.10
  200.5 1.4 copy-start.4
  219.0 1.1 copy-start
  220.1 37.0 %all-to-all-start.5 = ((bf16[8,128,1152]{2,1,0:T(8,128)(2,1)}), bf16[8,128,1152]{2,1,0:T(8,128)(2,1)S(1)}, u32[]{:S(2)}, u32[]{:S(2)}) async-start(bf16[8,128,1152]{2,1,0:T(8,128)(2,1)} %copy-done.4), calls=%async_computation.5 | async-start | bytes 4718592 | tf_op jit(solution)/shard_map/all_to_all | solution.py:295
  225.4 1.3 copy-start.1
  227.6 6.6 %collective-permute-start.4 = (bf16[144,1152]{1,0:T(8,128)(2,1)S(1)}, bf16[144,1152]{1,0:T(8,128)(2,1)S(1)}, u32[]{:S(2)}, u32[]{:S(2)}) collective-permute-start(bf16[144,1152]{1,0:T(8,128)(2,1)S(1)} %get-tuple-element.39), channel_id=1, source_target_pairs={{0,1},{1,0},{2,3},{3,2},{4,5},{5,4},{6,7},{7,6},{8,9},{9,8},{10,11... | collective-permute-start | bytes 995336 | tf_op jit(solution)/shard_map/ppermute | solution.py:303
  336.8 6.7 %collective-permute-start.6 = (bf16[320,1152]{1,0:T(8,128)(2,1)S(1)}, bf16[320,1152]{1,0:T(8,128)(2,1)S(1)}, u32[]{:S(2)}, u32[]{:S(2)}) collective-permute-start(bf16[320,1152]{1,0:T(8,128)(2,1)S(1)} %bitcast.24), channel_id=1, source_target_pairs={{0,1},{1,0},{2,3},{3,2},{4,5},{5,4},{6,7},{7,6},{8,9},{9,8},{10,11... | collective-permute-start | bytes 2211848 | tf_op jit(solution)/shard_map/ppermute | solution.py:303
  (5 other events, 4.6 us)
Sparse Core Ops, SparseCore 0:
  13.0 61.2 all-gather.2
  163.7 63.0 reduce-scatter.1

commit v4 on v3

--- a/solution.py
+++ b/solution.py
@@ -48,17 +48,17 @@
     )
 
 
-def norm_kernel(at_ref, x_ref, wq_ref, wo_ref, out_ref, own_ref, parts_ref):
-    hidden = normalize(x_ref[...])[0].astype(BF)
+def norm_kernel(at_ref, x_ref, wq_ref, wo_ref, out_ref, own_ref):
+    core = at_ref[0]
+    wide = wo_ref[0].astype(F32)
+    half = jnp.where(core == 0, wide[:40], wide[32:])
+    hidden = normalize(x_ref[...])[0]
+    block = jnp.concatenate([hidden, half], axis=0).astype(BF)
     for j in range(8):
-        out_ref[j] = hidden
-    for i in range(3):
-        parts_ref[i] = wq_ref[1, i].astype(F32)
-    parts_ref[3] = wo_ref[1].astype(F32)
-    first = wo_ref[0].astype(F32)
-    half = jnp.where(at_ref[0] == 0, first[:40], first[32:])
-    part = parts_ref[2 * at_ref[0] + at_ref[1]]
-    own_ref[...] = jnp.concatenate([part, half], axis=0).astype(BF)
+        out_ref[j] = block
+    qk = jnp.concatenate([wq_ref[1, 0].astype(F32), wq_ref[1, 1].astype(F32)], axis=0)
+    vo = jnp.concatenate([wq_ref[1, 2].astype(F32), wo_ref[1].astype(F32)], axis=0)
+    own_ref[...] = jnp.where(core == 0, qk, vo).astype(BF)
 
 
 def frame_rows(hidden_ref, f):
@@ -74,11 +74,9 @@
     return tuple(stacked[i * E : (i + 1) * E].astype(BF) for i in range(3))
 
 
-def spatial_kernel(hidden_ref, w_ref, all_ref, heads_ref, qkv_ref, two_ref, one_ref):
+def spatial_kernel(hidden_ref, w_ref, heads_ref, qkv_ref, one_ref):
     for h in range(8):
-        both = all_ref[h].astype(F32)
-        two_ref[h] = both[:E].astype(BF)
-        one_ref[h] = both[E:].astype(BF)
+        one_ref[h] = hidden_ref[h].astype(F32)[128:].astype(BF)
     outs = []
     for f in range(2):
         qkv = nt(w_ref[...], frame_rows(hidden_ref, f))
@@ -93,7 +91,9 @@
         heads_ref[2 * m + 1] = b.astype(BF)
 
 
-def middle_kernel(core_ref, x_ref, g_ref, heads_ref, mine_ref, other_ref, out_ref, split_ref):
+def middle_kernel(
+    core_ref, x_ref, g_ref, heads_ref, mine_ref, other_ref, pass_ref, out_ref, same_ref, split_ref
+):
     core = core_ref[0]
     for h in range(8):
         heads = heads_ref[h].astype(F32)
@@ -111,17 +111,14 @@
 
 
 def temporal_kernel(
-    at_ref, pair_ref, own_ref, z_ref, core_ref, both_ref,
+    core_ref, pair_ref, mine_ref, other_ref,
     back_ref, keep_ref, send_ref,
-    w_ref, gw_ref, in_ref, grads_ref, sems,
+    w_ref, gw_ref, qk_ref, vg_ref, g0_ref, g1_ref, sems,
 ):
-    core, odd = at_ref[0], at_ref[1]
-    here, there = 2 * core, 2 * (1 - core)
+    core = core_ref[0]
     loads = (
-        pltpu.make_async_copy(own_ref, w_ref.at[here + odd], sems.at[0]),
-        pltpu.make_async_copy(z_ref, w_ref.at[here + 1 - odd], sems.at[1]),
-        pltpu.make_async_copy(core_ref, w_ref.at[there + odd], sems.at[2]),
-        pltpu.make_async_copy(both_ref, w_ref.at[there + 1 - odd], sems.at[3]),
+        pltpu.make_async_copy(mine_ref, w_ref.at[core], sems.at[0]),
+        pltpu.make_async_copy(other_ref, w_ref.at[1 - core], sems.at[1]),
     )
     for load in loads:
         load.start()
@@ -130,10 +127,11 @@
     grad = jnp.concatenate([pair_ref[s, 1, f] for s in range(2) for f in range(2)], axis=0)
     normed, inverse = normalize(rows)
     hidden = normed.astype(BF)
+    both = jnp.concatenate([hidden, grad], axis=0)
     for load in loads:
         load.wait()
-    for i in range(4):
-        in_ref[i] = nt(w_ref[i], grad if i == 3 else hidden)
+    qk_ref[...] = nt(w_ref[0], hidden)
+    vg_ref[...] = nt(w_ref[1], both)
 
     def rounded(value):
         return value.astype(BF).astype(F32)
@@ -144,9 +142,13 @@
     def behind(value, r):
         return pltpu.roll(value, 32 * r, 1) if r else value
 
+    zeros = jnp.zeros((E, 128), F32)
     for h in range(8):
-        span = slice(h * E, (h + 1) * E)
-        q, k, v, gh = (rounded(in_ref[i, span]) for i in range(4))
+        base = h * 2 * E
+        q = rounded(qk_ref[base : base + E])
+        k = rounded(qk_ref[base + E : base + 2 * E])
+        v = rounded(vg_ref[base : base + E, :128])
+        gh = rounded(vg_ref[base + E : base + 2 * E, 128:])
         ks = [ahead(k, r) for r in range(4)]
         vs = [ahead(v, r) for r in range(4)]
         exps = [jnp.exp(jnp.sum(q * kr, axis=0, keepdims=True) * SCALE) for kr in ks]
@@ -160,22 +162,22 @@
         gq = sum(sg * kr for sg, kr in zip(sgs, ks))
         gk = sum(behind(sg * q, r) for r, sg in enumerate(sgs))
         gv = sum(behind(w * gh, r) for r, w in enumerate(weights))
-        for i, grads in enumerate((gq, gk, gv, heads)):
-            grads_ref[i, span] = grads
-        wide = slice(h * 2 * E, (h + 1) * 2 * E)
-        qk_grads = jnp.concatenate([gq, gk], axis=0).astype(BF)
-        gw_ref[0, wide] = nn(qk_grads, hidden).astype(BF)
-        vo_grads = [nn(gv.astype(BF), hidden), nn(heads.astype(BF), grad)]
-        gw_ref[1, wide] = jnp.concatenate(vo_grads, axis=0).astype(BF)
+        g0_ref[base : base + 2 * E] = jnp.concatenate([gq, gk], axis=0).astype(BF)
+        g1_ref[base : base + 2 * E, :128] = jnp.concatenate([gv, zeros], axis=0).astype(BF)
+        g1_ref[base : base + 2 * E, 128:] = jnp.concatenate([zeros, heads], axis=0).astype(BF)
+    for h in range(8):
+        span = slice(h * 2 * E, (h + 1) * 2 * E)
+        gw_ref[0, span] = nn(g0_ref[span], hidden).astype(BF)
+        gw_ref[1, span] = nn(g1_ref[span], both).astype(BF)
     stores = (
         pltpu.make_async_copy(gw_ref.at[core], keep_ref, sems.at[0]),
         pltpu.make_async_copy(gw_ref.at[1 - core], send_ref, sems.at[1]),
     )
     for store in stores:
         store.start()
-    sums = [tn(grads_ref[i].astype(BF), w_ref[i]) for i in range(4)]
-    normed_grads = sums[0] + sums[1] + sums[2]
-    result = (rows.astype(F32) + sums[3]).astype(BF)
+    mixed = tn(g1_ref[...], w_ref[1])
+    normed_grads = tn(g0_ref[...], w_ref[0]) + mixed[:128]
+    result = (rows.astype(F32) + mixed[128:]).astype(BF)
     total_grad = normalize_back(grad, inverse, normed, normed_grads).astype(BF)
     for s in range(2):
         for f in range(2):
@@ -186,13 +188,17 @@
         store.wait()
 
 
+def halves(rows, size):
+    return rows[:size], rows[rows.shape[0] - size :]
+
+
 def local_rows(pair_ref, which):
     return jnp.concatenate([pair_ref[s, which, f] for f in range(2) for s in range(2)], axis=0)
 
 
 def turn_kernel(
     core_ref, back_ref, heads_ref, mine_ref, other_ref,
-    gh_ref, gw_ref, out_ref, grad_ref, split_ref,
+    gh_ref, keep_ref, send_ref, out_ref, grad_ref, split_ref,
 ):
     core = core_ref[0]
     out_ref[...] = local_rows(back_ref, 0)
@@ -204,10 +210,18 @@
         at = h * 40
         pieces = [split_ref[0, at : at + 40], split_ref[1, at + 8 : at + 40]]
         gh_ref[h] = jnp.concatenate(pieces, axis=0).astype(BF)
-        gw_ref[h] = nn(heads_ref[h], grad).astype(BF)
-
-
-def spatial_back_kernel(qkv_ref, gh_ref, hidden_ref, w_ref, terms_ref, gw_ref):
+        low, high = halves(nn(heads_ref[h], grad), 40)
+        keep_ref[h] = jnp.where(core == 0, low, high).astype(BF)
+        send_ref[h] = jnp.where(core == 0, high, low).astype(BF)
+
+
+def spatial_back_kernel(
+    core_ref, qkv_ref, gh_ref, hidden_ref, w_ref, mine_ref, recv_ref, terms_ref, keep_ref, send_ref
+):
+    for j in range(8):
+        part = mine_ref[j].astype(F32) + recv_ref[j].astype(F32)
+        low = jnp.zeros((8, part.shape[1]), F32)
+        terms_ref[j, 128:176, :] = jnp.concatenate([part, low], axis=0).astype(BF)
     frames = ([], [])
     for m in range(4):
         pair = regroup(gh_ref[2 * m].astype(F32), gh_ref[2 * m + 1].astype(F32))
@@ -228,46 +242,39 @@
         terms = tn(grads, w_ref[...]).astype(BF)
         for j in range(8):
             terms_ref[j, f * 64 : (f + 1) * 64, :] = terms[j * 64 : (j + 1) * 64]
-    gw_ref[...] = total.astype(BF)
-
-
-def gather_kernel(core_ref, parts_ref, qkv_ref, keep_ref, send_ref, halves_ref):
+    low, high = halves(total, 112)
+    keep_ref[...] = jnp.where(core_ref[0] == 0, low, high).astype(BF)
+    send_ref[...] = jnp.where(core_ref[0] == 0, high, low).astype(BF)
+
+
+def result_kernel(core_ref, mine_ref, other_ref, qkv_ref, out_ref, both_ref):
     core = core_ref[0]
-    total = parts_ref[0].astype(F32)
-    for j in range(1, 8):
-        total = total + parts_ref[j].astype(F32)
-    qkv = qkv_ref[...].astype(F32)
-    halves_ref[0] = qkv[: 2 * E]
-    halves_ref[1] = jnp.concatenate([qkv[2 * E :], total], axis=0)
-    keep_ref[...] = halves_ref[core].astype(BF)
-    send_ref[...] = halves_ref[1 - core].astype(BF)
-
-
-def result_kernel(core_ref, mine_ref, other_ref, qkv_ref, out_ref, halves_ref):
-    core = core_ref[0]
-    halves_ref[core] = mine_ref[...].astype(F32)
-    halves_ref[1 - core] = other_ref[...].astype(F32)
-    for b in range(2):
-        at = b * 2 * E
-        qkv_ref[b, 0] = halves_ref[0, at : at + E]
-        qkv_ref[b, 1] = halves_ref[0, at + E : at + 2 * E]
-        qkv_ref[b, 2] = halves_ref[1, at : at + E]
-        out_ref[b] = halves_ref[1, at + E : at + 2 * E]
+    both_ref[core] = mine_ref[...].astype(F32)
+    both_ref[1 - core] = other_ref[...].astype(F32)
+    qkv = jnp.concatenate([both_ref[0, :112], both_ref[1, 8:112]], axis=0)
+    for i in range(3):
+        qkv_ref[0, i] = qkv[i * E : (i + 1) * E]
+    out_ref[0] = jnp.concatenate([both_ref[0, 112:152], both_ref[1, 120:152]], axis=0)
+    qkv_ref[1, 0] = both_ref[0, 152 : 152 + E]
+    qkv_ref[1, 1] = both_ref[0, 152 + E : 152 + 2 * E]
+    qkv_ref[1, 2] = both_ref[1, 152 : 152 + E]
+    out_ref[1] = both_ref[1, 152 + E : 152 + 2 * E]
 
 
 def last_kernel(
     terms_ref, x_ref, g_ref, keep_ref, recv_ref, two_ref, out_ref, chain_ref, rows_ref
 ):
-    rows_ref[: 2 * E] = keep_ref[...].astype(F32) + recv_ref[...].astype(F32)
-    rows_ref[2 * E : 4 * E] = two_ref[...].astype(F32)
-    rows_ref[4 * E :] = jnp.zeros_like(rows_ref[4 * E :])
+    rows_ref[:112] = keep_ref[...].astype(F32) + recv_ref[...].astype(F32)
+    total = terms_ref[0].astype(F32)
+    for j in range(1, 8):
+        total = total + terms_ref[j].astype(F32)
+    rows_ref[112:152] = total[128:168]
+    rows_ref[152:296] = two_ref[...].astype(F32)
+    rows_ref[296:] = jnp.zeros_like(rows_ref[296:])
     for i in range(8):
         chain_ref[i] = rows_ref[i * 40 : (i + 1) * 40].astype(BF)
     normed, inverse = normalize(x_ref[...])
-    normed_grads = terms_ref[0].astype(F32)
-    for j in range(1, 8):
-        normed_grads = normed_grads + terms_ref[j].astype(F32)
-    out_ref[...] = normalize_back(g_ref[...], inverse, normed, normed_grads).astype(BF)
+    out_ref[...] = normalize_back(g_ref[...], inverse, normed, total[:128]).astype(BF)
 
 
 VMEM = pl.BlockSpec(memory_space=pltpu.VMEM)
@@ -287,6 +294,7 @@
         in_specs=more.pop("in_specs", [VMEM] * len(args)),
         out_specs=more.pop("out_specs", jax.tree.map(lambda _: VMEM, outs)),
         compiler_params=PARAMS,
+        cost_estimate=pl.CostEstimate(flops=0, bytes_accessed=0, transcendentals=0),
         **more,
     )(*args)
 
@@ -341,52 +349,51 @@
 
 def on_device(n_dp, latents, cotangent, w_qkv, w_out):
     depth = latents.shape[-1]
-    index = lax.axis_index("dp")
-    at = jnp.stack([index % 2, index // 2 % 2]).astype(jnp.int32)
+    at = (lax.axis_index("dp") % 2).reshape(1).astype(jnp.int32)
     near, far = groups_of(n_dp)
     x = latents.reshape(128, depth)
     g = cotangent.reshape(128, depth)
     w_own = w_qkv[0].reshape(3 * E, depth)
 
     hidden, own = call(
-        norm_kernel, (shape(8, 128, depth), shape(E + 40, depth)),
+        norm_kernel, (shape(8, 168, depth), shape(2 * E, depth)),
         at, x, w_qkv.reshape(2, 3, E, depth), w_out.reshape(2, E, depth),
         in_specs=[SMEM] + [VMEM] * 3,
-        scratch_shapes=[pltpu.VMEM((4, E, depth), F32)],
-    )
-    parts = lax.all_gather(own, "head", axis_index_groups=RING)
+    )
+    mine_two = lax.all_gather(own, "head", axis_index_groups=RING).reshape(16 * E, depth)
     hidden = over_head(hidden)
-    heads, qkv, own, mine_one = call(
+    heads, qkv, mine_one = call(
         spatial_kernel,
-        (shape(8, E, 128), shape(2, 3 * E, 512), shape(8, E, depth), shape(8, 40, depth)),
-        hidden, w_own, parts,
+        (shape(8, E, 128), shape(2, 3 * E, 512), shape(8, 40, depth)), hidden, w_own,
     )
     heads = over_head(heads)
     mine_one = mine_one.reshape(320, depth)
     other_one = swap_cores(mine_one, n_dp)
-    own = own.reshape(8 * E, depth)
-    from_z = swap_cores(own, n_dp, 2)
-    from_core = swap_cores(own, n_dp)
-    from_both = swap_cores(from_z, n_dp)
-    pair = call(
-        middle_kernel, shape(2, 2, 2, 32, depth), at, x, g, heads, mine_one, other_one,
-        in_specs=[SMEM] + [VMEM] * 5,
+    big = shape(16 * E, depth)
+    pair, mine_two = call(
+        middle_kernel, (shape(2, 2, 2, 32, depth), big),
+        at, x, g, heads, mine_one, other_one, mine_two,
+        in_specs=[SMEM] + [VMEM] * 5 + [ANY],
+        out_specs=(VMEM, ANY),
+        input_output_aliases={6: 1},
         scratch_shapes=[pltpu.VMEM((2, 320, 128), F32)],
     )
     pair = over_seq(pair)
-    big = shape(16 * E, depth)
+    other_two = swap_cores(mine_two, n_dp)
     back, keep, send = call(
         temporal_kernel,
         (shape(2, 2, 2, 32, depth), big, big),
-        at, pair, own, from_z, from_core, from_both,
-        in_specs=[SMEM, VMEM] + [ANY] * 4,
+        at, pair, mine_two, other_two,
+        in_specs=[SMEM, VMEM, ANY, ANY],
         out_specs=(VMEM, ANY, ANY),
         scratch_shapes=[
-            pltpu.VMEM((4, 8 * E, depth), BF),
             pltpu.VMEM((2, 16 * E, depth), BF),
-            pltpu.VMEM((4, 8 * E, 128), F32),
-            pltpu.VMEM((4, 8 * E, 128), F32),
-            pltpu.SemaphoreType.DMA((4,)),
+            pltpu.VMEM((2, 16 * E, depth), BF),
+            pltpu.VMEM((16 * E, 128), F32),
+            pltpu.VMEM((16 * E, 256), F32),
+            pltpu.VMEM((16 * E, 128), BF),
+            pltpu.VMEM((16 * E, 256), BF),
+            pltpu.SemaphoreType.DMA((2,)),
         ],
     )
     back = over_seq(back)
@@ -394,23 +401,20 @@
     two = lax.psum_scatter(
         two, "head", scatter_dimension=0, tiled=True, axis_index_groups=RING
     )
-    gh, parts, output, grad_one = call(
+    half = shape(8, 40, depth)
+    gh, keep, send, output, grad_one = call(
         turn_kernel,
-        (shape(8, E, 128), shape(8, E, depth), shape(128, depth), shape(128, depth)),
+        (shape(8, E, 128), half, half, shape(128, depth), shape(128, depth)),
         at, back, heads, mine_one, other_one,
         in_specs=[SMEM] + [VMEM] * 4,
         scratch_shapes=[pltpu.VMEM((2, 320, 128), F32)],
     )
     gh = over_head(gh)
-    parts = over_head(parts)
-    terms, qkv_one = call(
-        spatial_back_kernel, (shape(8, 128, depth), shape(3 * E, depth)), qkv, gh, hidden, w_own
-    )
-    half = shape(2 * E, depth)
-    keep, send = call(
-        gather_kernel, (half, half), at, parts, qkv_one,
-        in_specs=[SMEM, VMEM, VMEM],
-        scratch_shapes=[pltpu.VMEM((2, 2 * E, depth), F32)],
+    half = shape(112, depth)
+    terms, keep, send = call(
+        spatial_back_kernel, (shape(8, 176, depth), half, half),
+        at, qkv, gh, hidden, w_own, keep, swap_cores(send, n_dp),
+        in_specs=[SMEM] + [VMEM] * 6,
     )
     n_near = len(near[0])
     latent_grads, chain = call(

time: 358 us -> 338 us (0.944); the launches traced: 353 us -> 336 us
  waiting for transfers between devices: 119 us -> 97.4 us
  starting transfers between devices: 55.6 us -> 37.8 us
  blocking collectives: 117 us -> 134 us
  local copies, waits for them, and re-layouts: 14.5 us -> 27.3 us
  Pallas kernels: 28 us -> 23.1 us
    all_gather x1, waiting for transfers between devices: 24.9 us -> 0.01 us  [on_device(): lax.all_gather(own, 'head', axis_index_groups=RING).reshape(16 * E, depth)]
    all_to_all x3 -> x2, waiting for transfers between devices: 69.3 us -> 89.5 us  [over_head(): lax.all_to_all(blocks, 'head', 0, 0, tiled=True, axis_index_groups=RING)]
    ppermute x7 -> x6, waiting for transfers between devices: 25 us -> 7.94 us  [swap_cores(): return lax.ppermute(value, 'dp', [(i, i ^ bit) for i in range(n_dp)])]
    ppermute x7 -> x6, starting transfers between devices: 38.1 us -> 25.5 us  [swap_cores(): return lax.ppermute(value, 'dp', [(i, i ^ bit) for i in range(n_dp)])]
    unnamed x34 -> x56, local copies, waits for them, and re-layouts: 14.3 us -> 25.3 us
    all_to_all x2, blocking collectives: 20.2 us -> 28.9 us  [over_seq(): return lax.all_to_all(blocks, 'seq', 0, 0, tiled=True)]
    all_to_all x3 -> x2, starting transfers between devices: 17.5 us -> 12.2 us  [over_head(): lax.all_to_all(blocks, 'head', 0, 0, tiled=True, axis_index_groups=RING)]
    pallas_call x9 -> x8, Pallas kernels: 28 us -> 23.1 us  [call(): pl.pallas_call(kernel, out_shape=outs, in_specs=more.pop('in_specs', [VME...]
  transfers between devices with their start and end apart: 12 -> 10, of which waited for: 8 -> 5; matrix products, arithmetic and copies ran while one was open for 0% -> 1% of each run, Pallas kernels for 3% -> 3%
where the time goes in v4:
time: 338 us; the launch traced here: 336 us
  blocking collectives  134 us (40%)
  waiting for transfers between devices  97.4 us (29%)
  starting transfers between devices  37.8 us (11%)
  local copies, waits for them, and re-layouts  27.3 us (8%)
  Pallas kernels  23.1 us (7%)
  between operations  14.2 us (4%)
    all_to_all x2, waiting for transfers between devices, over_head(): lax.all_to_all(blocks, 'head', 0, 0, tiled=True, axis_index_groups=RING)  89.5 us
    all_to_all x1, blocking collectives, sum_far(): lax.all_to_all(copies, 'dp', 0, 0, tiled=True, axis_index_groups=far)  31.1 us
    all_to_all x2, blocking collectives, over_seq(): return lax.all_to_all(blocks, 'seq', 0, 0, tiled=True)  28.9 us
    all_to_all x1, blocking collectives, spread(): lax.all_to_all(copies, ('seq', 'dp'), 0, 0, tiled=True, axis_index_groups...  25.5 us
    ppermute x6, starting transfers between devices, swap_cores(): return lax.ppermute(value, 'dp', [(i, i ^ bit) for i in range(n_dp)])  25.5 us
    unnamed x56, local copies, waits for them, and re-layouts  25.3 us
    all_to_all x1, blocking collectives, sum_near(): lax.all_to_all(grads, ('seq', 'dp'), 0, 0, tiled=True, axis_index_groups=...  24.5 us
    all_to_all x2, blocking collectives, over_head(): lax.all_to_all(blocks, 'head', 0, 0, tiled=True, axis_index_groups=RING)  24.2 us
  transfers between devices with their start and end apart: 10, of which 5 were waited for; matrix products, arithmetic and copies ran while one was open for 1% of the time, Pallas kernels for 3%

profile of v4, /device:TPU:7, one launch (start us, length us, event | category | flops | bytes accessed | tf_op | source)
XLA Modules:
  0.0 336.4 jit_solution(4572809593215165777)
XLA Ops:
  13.3 6.9 %all-to-all-start = ((bf16[8,168,1152]{2,1,0:T(8,128)(2,1)}), bf16[8,168,1152]{2,1,0:T(8,128)(2,1)S(1)}, u32[]{:S(2)}, u32[]{:S(2)}) async-start(bf16[8,168,1152]{2,1,0:T(8,128)(2,1)} %copy-done.4), calls=%async_computation | async-start | bytes 6193152 | tf_op jit(solution)/shard_map/all_to_all | solution.py:303
  20.2 1.9 slice.3
  22.0 41.8 %all-to-all-done.hidden_ref = bf16[8,168,1152]{2,1,0:T(8,128)(2,1)S(1)} async-done(((bf16[8,168,1152]{2,1,0:T(8,128)(2,1)}), bf16[8,168,1152]{2,1,0:T(8,128)(2,1)S(1)}, u32[]{:S(2)}, u32[]{:S(2)}) %all-to-all-start) | async-done | bytes 3096608 | tf_op jit(solution)/shard_map/all_to_all | solution.py:303
  64.8 2.3 shard_map.76
  67.9 8.2 %collective-permute-start = (bf16[320,1152]{1,0:T(8,128)(2,1)S(1)}, bf16[320,1152]{1,0:T(8,128)(2,1)S(1)}, u32[]{:S(2)}, u32[]{:S(2)}) collective-permute-start(bf16[320,1152]{1,0:T(8,128)(2,1)S(1)} %bitcast.18), channel_id=1, source_target_pairs={{0,1},{1,0},{2,3},{3,2},{4,5},{5,4},{6,7},{7,6},{8,9},{9,8},{10,11... | collective-permute-start | bytes 2211848 | tf_op jit(solution)/shard_map/ppermute | solution.py:311
  77.0 13.0 %all_to_all.45.heads_ref = bf16[8,72,128]{2,1,0:T(8,128)(2,1)S(1)} all-to-all(bf16[8,72,128]{2,1,0:T(8,128)(2,1)S(1)} %get-tuple-element.27), channel_id=1, replica_groups={{0,64,128,192,224,160,96,32},{1,65,129,193,225,161,97,33},{2,66,130,194..., dimensions={0} | all-to-all | bytes 294912 | tf_op jit(solution)/shard_map/all_to_all | solution.py:303
  97.9 3.3 collective-permute-start.1
  101.3 16.8 %all_to_all.46.pair_ref = bf16[2,2,2,32,1152]{4,3,2,1,0:T(8,128)(2,1)S(1)} all-to-all(bf16[2,2,2,32,1152]{4,3,2,1,0:T(8,128)(2,1)S(1)} %get-tuple-element.30), channel_id=1, replica_groups=mesh['seq'=2,'head'=8,'dp'=32] {'seq'}, dimensions={0} | all-to-all | bytes 1179648 | tf_op jit(solution)/shard_map/all_to_all | solution.py:307
  119.6 8.5 %shard_map.78 = (bf16[2,2,2,32,1152]{4,3,2,1,0:T(8,128)(2,1)S(1)}, bf16[1152,1152]{1,0:T(8,128)(2,1)S(1)}, bf16[1152,1152]{1,0:T(8,128)(2,1)}) custom-call(s32[1]{0:T(128)} %bitcast.at_ref.core_ref, bf16[2,2,2,32,1152]{4,3,2,1,0:T(8,128)(2,1)S(1)} %all_to_all.46.pair_ref, bf16[1152,1152]{1,0:T(8,128)(2,1)} %copy-done.1, bf16[1152,1152]{1,0:T(8,128)(2,1)} %copy-done.27), custom_call_target="tpu_custom_call" | custom-call | tf_op jit(solution)/shard_map/pallas_call | solution.py:291
  128.9 3.0 collective-permute-start.4
  132.0 4.8 %collective-permute-done.4 = bf16[1152,1152]{1,0:T(8,128)(2,1)S(1)} collective-permute-done((bf16[1152,1152]{1,0:T(8,128)(2,1)}, bf16[1152,1152]{1,0:T(8,128)(2,1)S(1)}, u32[]{:S(2)}, u32[]{:S(2)}) %collective-permute-start.4) | collective-permute-done | bytes 2654240 | tf_op jit(solution)/shard_map/ppermute | solution.py:311
  136.7 2.2 add_convert_fusion
  139.0 12.1 %all_to_all.47.back_ref = bf16[2,2,2,32,1152]{4,3,2,1,0:T(8,128)(2,1)S(1)} all-to-all(bf16[2,2,2,32,1152]{4,3,2,1,0:T(8,128)(2,1)} %copy-done.14), channel_id=1, replica_groups=mesh['seq'=2,'head'=8,'dp'=32] {'seq'}, dimensions={0} | all-to-all | bytes 1179648 | tf_op jit(solution)/shard_map/all_to_all | solution.py:307
  154.9 3.1 collective-permute-start.2
  158.0 11.2 %all_to_all.48.gh_ref = bf16[8,72,128]{2,1,0:T(8,128)(2,1)S(1)} all-to-all(bf16[8,72,128]{2,1,0:T(8,128)(2,1)S(1)} %get-tuple-element.35), channel_id=1, replica_groups={{0,64,128,192,224,160,96,32},{1,65,129,193,225,161,97,33},{2,66,130,194..., dimensions={0} | all-to-all | bytes 294912 | tf_op jit(solution)/shard_map/all_to_all | solution.py:303
  169.2 5.6 %shard_map.80 = (bf16[8,176,1152]{2,1,0:T(8,128)(2,1)}, bf16[112,1152]{1,0:T(8,128)(2,1)S(1)}, bf16[112,1152]{1,0:T(8,128)(2,1)S(1)}) custom-call(s32[1]{0:T(128)} %bitcast.at_ref.core_ref, bf16[2,216,512]{2,1,0:T(8,128)(2,1)S(1)} %copy-done.16, bf16[8,72,128]{2,1,0:T(8,128)(2,1)S(1)} %all_to_all.48.gh_ref, ...), custom_call_target="tpu_custom_call" | custom-call | tf_op jit(solution)/shard_map/pallas_call | solution.py:291
  176.2 5.4 %all-to-all-start.5 = ((bf16[8,176,1152]{2,1,0:T(8,128)(2,1)}), bf16[8,176,1152]{2,1,0:T(8,128)(2,1)S(1)}, u32[]{:S(2)}, u32[]{:S(2)}) async-start(bf16[8,176,1152]{2,1,0:T(8,128)(2,1)} %get-tuple-element.38), calls=%async_computation.5 | async-start | bytes 6488064 | tf_op jit(solution)/shard_map/all_to_all | solution.py:303
  181.6 3.4 %collective-permute-start.3 = (bf16[112,1152]{1,0:T(8,128)(2,1)}, bf16[112,1152]{1,0:T(8,128)(2,1)S(1)}, u32[]{:S(2)}, u32[]{:S(2)}) collective-permute-start(bf16[112,1152]{1,0:T(8,128)(2,1)} %copy-done.26), channel_id=1, source_target_pairs={{0,1},{1,0},{2,3},{3,2},{4,5},{5,4},{6,7},{7,6},{8,9},{9,8},{10,11... | collective-permute-start | bytes 774152 | tf_op jit(solution)/shard_map/ppermute | solution.py:311
  187.0 47.7 %all-to-all-done.5.terms_ref = bf16[8,176,1152]{2,1,0:T(8,128)(2,1)S(1)} async-done(((bf16[8,176,1152]{2,1,0:T(8,128)(2,1)}), bf16[8,176,1152]{2,1,0:T(8,128)(2,1)S(1)}, u32[]{:S(2)}, u32[]{:S(2)}) %all-to-all-start.5) | async-done | bytes 3244064 | tf_op jit(solution)/shard_map/all_to_all | solution.py:303
  240.0 24.5 %all_to_all.49 = bf16[8,40,1152]{2,1,0:T(8,128)(2,1)S(1)} all-to-all(bf16[8,40,1152]{2,1,0:T(8,128)(2,1)S(1)} %get-tuple-element.45), channel_id=1, replica_groups={{0,2,4,6,256,258,260,262},{1,3,5,7,257,259,261,263},{8,10,12,14,264,266..., dimensions={0} | all-to-all | bytes 1474560 | tf_op jit(solution)/shard_map/all_to_all | solution.py:330
  264.7 31.1 %all_to_all.50 = bf16[4,40,1152]{2,1,0:T(8,128)(2,1)S(1)} all-to-all(bf16[4,40,1152]{2,1,0:T(8,128)(2,1)S(1)} %broadcast_in_dim.8), channel_id=1, replica_groups={{0,8,16,24},{1,9,17,25},{2,10,18,26},{3,11,19,27},{4,12,20,28},{5,13,21..., dimensions={0} | all-to-all | bytes 737280 | tf_op jit(solution)/shard_map/all_to_all | solution.py:338
  296.0 25.5 %all_to_all.51 = bf16[8,40,1152]{2,1,0:T(8,128)(2,1)S(1)} all-to-all(bf16[8,40,1152]{2,1,0:T(8,128)(2,1)S(1)} %broadcast_in_dim.9), channel_id=1, replica_groups={{0,2,4,6,256,258,260,262},{1,3,5,7,257,259,261,263},{8,10,12,14,264,266..., dimensions={0} | all-to-all | bytes 1474560 | tf_op jit(solution)/shard_map/all_to_all | solution.py:344
  321.5 4.4 %collective-permute-start.5 = (bf16[320,1152]{1,0:T(8,128)(2,1)S(1)}, bf16[320,1152]{1,0:T(8,128)(2,1)S(1)}, u32[]{:S(2)}, u32[]{:S(2)}) collective-permute-start(bf16[320,1152]{1,0:T(8,128)(2,1)S(1)} %bitcast.21), channel_id=1, source_target_pairs={{0,1},{1,0},{2,3},{3,2},{4,5},{5,4},{6,7},{7,6},{8,9},{9,8},{10,11... | collective-permute-start | bytes 2211848 | tf_op jit(solution)/shard_map/ppermute | solution.py:311
  327.7 1.8 shard_map.82
  (75 shorter events, 33.7 us)
Async XLA Ops:
  7.2 83.8 %all-gather.3.cloned.1.call-start = ((), (), s32[]{:S(2)}) async-start(), calls=%async_computation.11 | async-start | bytes 2985984 | tf_op jit(solution)/shard_map/all_gather | solution.py:363
  8.2 1.2 copy-start.13
  11.6 1.6 copy-start.4
  13.3 50.5 %all-to-all-start = ((bf16[8,168,1152]{2,1,0:T(8,128)(2,1)}), bf16[8,168,1152]{2,1,0:T(8,128)(2,1)S(1)}, u32[]{:S(2)}, u32[]{:S(2)}) async-start(bf16[8,168,1152]{2,1,0:T(8,128)(2,1)} %copy-done.4), calls=%async_computation | async-start | bytes 6193152 | tf_op jit(solution)/shard_map/all_to_all | solution.py:303
  20.1 70.8 %copy-start.12 = (bf16[1,2,64,1152]{3,2,1,0:T(8,128)(2,1)S(1)}, bf16[1,2,64,1152]{3,2,1,0:T(8,128)(2,1)}, u32[]{:S(2)}) copy-start(bf16[1,2,64,1152]{3,2,1,0:T(8,128)(2,1)} %param.4) | copy-start | bytes 884740
  20.1 214.6 %reduce-scatter.2.cloned.1.call-start = ((), (), s32[]{:S(2)}) async-start(), calls=%async_computation.10 | async-start | bytes 2985984 | tf_op jit(solution)/shard_map/reduce_scatter | solution.py:401
  63.8 1.0 copy-start.2
  67.9 22.1 %collective-permute-start = (bf16[320,1152]{1,0:T(8,128)(2,1)S(1)}, bf16[320,1152]{1,0:T(8,128)(2,1)S(1)}, u32[]{:S(2)}, u32[]{:S(2)}) collective-permute-start(bf16[320,1152]{1,0:T(8,128)(2,1)S(1)} %bitcast.18), channel_id=1, source_target_pairs={{0,1},{1,0},{2,3},{3,2},{4,5},{5,4},{6,7},{7,6},{8,9},{9,8},{10,11... | collective-permute-start | bytes 2211848 | tf_op jit(solution)/shard_map/ppermute | solution.py:311
  90.9 1.8 copy-start
  92.7 1.1 copy-start.6
  93.8 1.1 copy-start.9
  96.4 1.5 copy-start.1
  97.9 20.2 %collective-permute-start.1 = (bf16[1152,1152]{1,0:T(8,128)(2,1)S(1)}, bf16[1152,1152]{1,0:T(8,128)(2,1)S(1)}, u32[]{:S(2)}, u32[]{:S(2)}) collective-permute-start(bf16[1152,1152]{1,0:T(8,128)(2,1)S(1)} %get-tuple-element.31.mine_ref), channel_id=1, source_target_pairs={{0,1},{1,0},{2,3},{3,2},{4,5},{5,4},{6,7},{7,6},{8,9},{9,8},{10,11... | collective-permute-start | bytes 7962632 | tf_op jit(solution)/shard_map/ppermute | solution.py:311
  118.1 1.5 copy-start.27
  128.9 7.8 %collective-permute-start.4 = (bf16[1152,1152]{1,0:T(8,128)(2,1)}, bf16[1152,1152]{1,0:T(8,128)(2,1)S(1)}, u32[]{:S(2)}, u32[]{:S(2)}) collective-permute-start(bf16[1152,1152]{1,0:T(8,128)(2,1)} %get-tuple-element.43), channel_id=1, source_target_pairs={{0,1},{1,0},{2,3},{3,2},{4,5},{5,4},{6,7},{7,6},{8,9},{9,8},{10,11... | collective-permute-start | bytes 7962632 | tf_op jit(solution)/shard_map/ppermute | solution.py:311
  138.9 30.3 %copy-start.3 = (bf16[1,1,3,72,1152]{4,3,2,1,0:T(8,128)(2,1)S(1)}, bf16[1,1,3,72,1152]{4,3,2,1,0:T(8,128)(2,1)}, u32[]{:S(2)}) copy-start(bf16[1,1,3,72,1152]{4,3,2,1,0:T(8,128)(2,1)} %slice.3) | copy-start | bytes 1492996
  139.0 30.2 %copy-start.16 = (bf16[2,216,512]{2,1,0:T(8,128)(2,1)S(1)}, bf16[2,216,512]{2,1,0:T(8,128)(2,1)}, u32[]{:S(2)}) copy-start(bf16[2,216,512]{2,1,0:T(8,128)(2,1)} %copy-done.15) | copy-start | bytes 1327108
  151.0 1.1 copy-start.7
  152.1 1.1 copy-start.10
  154.9 19.9 %copy-start.20 = (bf16[128,1152]{1,0:T(8,128)(2,1)}, bf16[128,1152]{1,0:T(8,128)(2,1)S(1)}, u32[]{:S(2)}) copy-start(bf16[128,1152]{1,0:T(8,128)(2,1)S(1)} %get-tuple-element.39.g_ref) | copy-start | bytes 884740
  154.9 14.3 %collective-permute-start.2 = (bf16[8,40,1152]{2,1,0:T(8,128)(2,1)S(1)}, bf16[8,40,1152]{2,1,0:T(8,128)(2,1)S(1)}, u32[]{:S(2)}, u32[]{:S(2)}) collective-permute-start(bf16[8,40,1152]{2,1,0:T(8,128)(2,1)S(1)} %get-tuple-element.37), channel_id=1, source_target_pairs={{0,1},{1,0},{2,3},{3,2},{4,5},{5,4},{6,7},{7,6},{8,9},{9,8},{10,11... | collective-permute-start | bytes 2211848 | tf_op jit(solution)/shard_map/ppermute | solution.py:311
  176.2 58.6 %all-to-all-start.5 = ((bf16[8,176,1152]{2,1,0:T(8,128)(2,1)}), bf16[8,176,1152]{2,1,0:T(8,128)(2,1)S(1)}, u32[]{:S(2)}, u32[]{:S(2)}) async-start(bf16[8,176,1152]{2,1,0:T(8,128)(2,1)} %get-tuple-element.38), calls=%async_computation.5 | async-start | bytes 6488064 | tf_op jit(solution)/shard_map/all_to_all | solution.py:303
  181.6 4.8 %collective-permute-start.3 = (bf16[112,1152]{1,0:T(8,128)(2,1)}, bf16[112,1152]{1,0:T(8,128)(2,1)S(1)}, u32[]{:S(2)}, u32[]{:S(2)}) collective-permute-start(bf16[112,1152]{1,0:T(8,128)(2,1)} %copy-done.26), channel_id=1, source_target_pairs={{0,1},{1,0},{2,3},{3,2},{4,5},{5,4},{6,7},{7,6},{8,9},{9,8},{10,11... | collective-permute-start | bytes 774152 | tf_op jit(solution)/shard_map/ppermute | solution.py:311
  321.5 6.2 %collective-permute-start.5 = (bf16[320,1152]{1,0:T(8,128)(2,1)S(1)}, bf16[320,1152]{1,0:T(8,128)(2,1)S(1)}, u32[]{:S(2)}, u32[]{:S(2)}) collective-permute-start(bf16[320,1152]{1,0:T(8,128)(2,1)S(1)} %bitcast.21), channel_id=1, source_target_pairs={{0,1},{1,0},{2,3},{3,2},{4,5},{5,4},{6,7},{7,6},{8,9},{9,8},{10,11... | collective-permute-start | bytes 2211848 | tf_op jit(solution)/shard_map/ppermute | solution.py:311
  (14 other events, 12.2 us)
Sparse Core Ops, SparseCore 0:
  13.4 73.7 all-gather.2
  139.1 52.2 reduce-scatter.1

commit v5 on v4

--- a/solution.py
+++ b/solution.py
@@ -48,17 +48,17 @@
     )
 
 
-def norm_kernel(at_ref, x_ref, wq_ref, wo_ref, out_ref, own_ref):
-    core = at_ref[0]
+def norm_kernel(at_ref, x_ref, wq_ref, wo_ref, out_ref, own_ref, parts_ref):
     wide = wo_ref[0].astype(F32)
-    half = jnp.where(core == 0, wide[:40], wide[32:])
+    half = jnp.where(at_ref[0] == 0, wide[:40], wide[32:])
     hidden = normalize(x_ref[...])[0]
     block = jnp.concatenate([hidden, half], axis=0).astype(BF)
     for j in range(8):
         out_ref[j] = block
-    qk = jnp.concatenate([wq_ref[1, 0].astype(F32), wq_ref[1, 1].astype(F32)], axis=0)
-    vo = jnp.concatenate([wq_ref[1, 2].astype(F32), wo_ref[1].astype(F32)], axis=0)
-    own_ref[...] = jnp.where(core == 0, qk, vo).astype(BF)
+    for i in range(3):
+        parts_ref[i] = wq_ref[1, i].astype(F32)
+    parts_ref[3] = wo_ref[1].astype(F32)
+    own_ref[...] = parts_ref[2 * at_ref[0] + at_ref[1]].astype(BF)
 
 
 def frame_rows(hidden_ref, f):
@@ -111,14 +111,17 @@
 
 
 def temporal_kernel(
-    core_ref, pair_ref, mine_ref, other_ref,
+    at_ref, pair_ref, own_ref, z_ref, core_ref, both_ref,
     back_ref, keep_ref, send_ref,
-    w_ref, gw_ref, qk_ref, vg_ref, g0_ref, g1_ref, sems,
+    w_ref, gw_ref, in_ref, grads_ref, sems,
 ):
-    core = core_ref[0]
+    core, odd = at_ref[0], at_ref[1]
+    here, there = 2 * core, 2 * (1 - core)
     loads = (
-        pltpu.make_async_copy(mine_ref, w_ref.at[core], sems.at[0]),
-        pltpu.make_async_copy(other_ref, w_ref.at[1 - core], sems.at[1]),
+        pltpu.make_async_copy(own_ref, w_ref.at[here + odd], sems.at[0]),
+        pltpu.make_async_copy(z_ref, w_ref.at[here + 1 - odd], sems.at[1]),
+        pltpu.make_async_copy(core_ref, w_ref.at[there + odd], sems.at[2]),
+        pltpu.make_async_copy(both_ref, w_ref.at[there + 1 - odd], sems.at[3]),
     )
     for load in loads:
         load.start()
@@ -127,11 +130,10 @@
     grad = jnp.concatenate([pair_ref[s, 1, f] for s in range(2) for f in range(2)], axis=0)
     normed, inverse = normalize(rows)
     hidden = normed.astype(BF)
-    both = jnp.concatenate([hidden, grad], axis=0)
     for load in loads:
         load.wait()
-    qk_ref[...] = nt(w_ref[0], hidden)
-    vg_ref[...] = nt(w_ref[1], both)
+    for i in range(4):
+        in_ref[i] = nt(w_ref[i], grad if i == 3 else hidden)
 
     def rounded(value):
         return value.astype(BF).astype(F32)
@@ -142,13 +144,9 @@
     def behind(value, r):
         return pltpu.roll(value, 32 * r, 1) if r else value
 
-    zeros = jnp.zeros((E, 128), F32)
     for h in range(8):
-        base = h * 2 * E
-        q = rounded(qk_ref[base : base + E])
-        k = rounded(qk_ref[base + E : base + 2 * E])
-        v = rounded(vg_ref[base : base + E, :128])
-        gh = rounded(vg_ref[base + E : base + 2 * E, 128:])
+        span = slice(h * E, (h + 1) * E)
+        q, k, v, gh = (rounded(in_ref[i, span]) for i in range(4))
         ks = [ahead(k, r) for r in range(4)]
         vs = [ahead(v, r) for r in range(4)]
         exps = [jnp.exp(jnp.sum(q * kr, axis=0, keepdims=True) * SCALE) for kr in ks]
@@ -162,22 +160,22 @@
         gq = sum(sg * kr for sg, kr in zip(sgs, ks))
         gk = sum(behind(sg * q, r) for r, sg in enumerate(sgs))
         gv = sum(behind(w * gh, r) for r, w in enumerate(weights))
-        g0_ref[base : base + 2 * E] = jnp.concatenate([gq, gk], axis=0).astype(BF)
-        g1_ref[base : base + 2 * E, :128] = jnp.concatenate([gv, zeros], axis=0).astype(BF)
-        g1_ref[base : base + 2 * E, 128:] = jnp.concatenate([zeros, heads], axis=0).astype(BF)
-    for h in range(8):
-        span = slice(h * 2 * E, (h + 1) * 2 * E)
-        gw_ref[0, span] = nn(g0_ref[span], hidden).astype(BF)
-        gw_ref[1, span] = nn(g1_ref[span], both).astype(BF)
+        for i, grads in enumerate((gq, gk, gv, heads)):
+            grads_ref[i, span] = grads
+        wide = slice(h * 2 * E, (h + 1) * 2 * E)
+        qk_grads = jnp.concatenate([gq, gk], axis=0).astype(BF)
+        gw_ref[0, wide] = nn(qk_grads, hidden).astype(BF)
+        vo_grads = [nn(gv.astype(BF), hidden), nn(heads.astype(BF), grad)]
+        gw_ref[1, wide] = jnp.concatenate(vo_grads, axis=0).astype(BF)
     stores = (
         pltpu.make_async_copy(gw_ref.at[core], keep_ref, sems.at[0]),
         pltpu.make_async_copy(gw_ref.at[1 - core], send_ref, sems.at[1]),
     )
     for store in stores:
         store.start()
-    mixed = tn(g1_ref[...], w_ref[1])
-    normed_grads = tn(g0_ref[...], w_ref[0]) + mixed[:128]
-    result = (rows.astype(F32) + mixed[128:]).astype(BF)
+    sums = [tn(grads_ref[i].astype(BF), w_ref[i]) for i in range(4)]
+    normed_grads = sums[0] + sums[1] + sums[2]
+    result = (rows.astype(F32) + sums[3]).astype(BF)
     total_grad = normalize_back(grad, inverse, normed, normed_grads).astype(BF)
     for s in range(2):
         for f in range(2):
@@ -280,20 +278,20 @@
 VMEM = pl.BlockSpec(memory_space=pltpu.VMEM)
 SMEM = pl.BlockSpec(memory_space=pltpu.SMEM)
 ANY = pl.BlockSpec(memory_space=pl.ANY)
-PARAMS = pltpu.CompilerParams(vmem_limit_bytes=48 * 1024 * 1024)
+MIB = 1024 * 1024
 
 
 def shape(*dims):
     return jax.ShapeDtypeStruct(dims, BF)
 
 
-def call(kernel, outs, *args, **more):
+def call(kernel, outs, *args, mib=24, **more):
     return pl.pallas_call(
         kernel,
         out_shape=outs,
         in_specs=more.pop("in_specs", [VMEM] * len(args)),
         out_specs=more.pop("out_specs", jax.tree.map(lambda _: VMEM, outs)),
-        compiler_params=PARAMS,
+        compiler_params=pltpu.CompilerParams(vmem_limit_bytes=mib * MIB),
         cost_estimate=pl.CostEstimate(flops=0, bytes_accessed=0, transcendentals=0),
         **more,
     )(*args)
@@ -349,18 +347,20 @@
 
 def on_device(n_dp, latents, cotangent, w_qkv, w_out):
     depth = latents.shape[-1]
-    at = (lax.axis_index("dp") % 2).reshape(1).astype(jnp.int32)
+    index = lax.axis_index("dp")
+    at = jnp.stack([index % 2, index // 2 % 2]).astype(jnp.int32)
     near, far = groups_of(n_dp)
     x = latents.reshape(128, depth)
     g = cotangent.reshape(128, depth)
     w_own = w_qkv[0].reshape(3 * E, depth)
 
     hidden, own = call(
-        norm_kernel, (shape(8, 168, depth), shape(2 * E, depth)),
+        norm_kernel, (shape(8, 168, depth), shape(E, depth)),
         at, x, w_qkv.reshape(2, 3, E, depth), w_out.reshape(2, E, depth),
         in_specs=[SMEM] + [VMEM] * 3,
-    )
-    mine_two = lax.all_gather(own, "head", axis_index_groups=RING).reshape(16 * E, depth)
+        scratch_shapes=[pltpu.VMEM((4, E, depth), F32)],
+    )
+    own = lax.all_gather(own, "head", axis_index_groups=RING).reshape(8 * E, depth)
     hidden = over_head(hidden)
     heads, qkv, mine_one = call(
         spatial_kernel,
@@ -369,32 +369,33 @@
     heads = over_head(heads)
     mine_one = mine_one.reshape(320, depth)
     other_one = swap_cores(mine_one, n_dp)
+    from_z = swap_cores(own, n_dp, 2)
+    from_core = swap_cores(own, n_dp)
     big = shape(16 * E, depth)
-    pair, mine_two = call(
-        middle_kernel, (shape(2, 2, 2, 32, depth), big),
-        at, x, g, heads, mine_one, other_one, mine_two,
+    pair, from_z = call(
+        middle_kernel, (shape(2, 2, 2, 32, depth), shape(8 * E, depth)),
+        at, x, g, heads, mine_one, other_one, from_z,
         in_specs=[SMEM] + [VMEM] * 5 + [ANY],
         out_specs=(VMEM, ANY),
         input_output_aliases={6: 1},
         scratch_shapes=[pltpu.VMEM((2, 320, 128), F32)],
     )
     pair = over_seq(pair)
-    other_two = swap_cores(mine_two, n_dp)
+    from_both = swap_cores(from_z, n_dp)
     back, keep, send = call(
         temporal_kernel,
         (shape(2, 2, 2, 32, depth), big, big),
-        at, pair, mine_two, other_two,
-        in_specs=[SMEM, VMEM, ANY, ANY],
+        at, pair, own, from_z, from_core, from_both,
+        in_specs=[SMEM, VMEM] + [ANY] * 4,
         out_specs=(VMEM, ANY, ANY),
         scratch_shapes=[
+            pltpu.VMEM((4, 8 * E, depth), BF),
             pltpu.VMEM((2, 16 * E, depth), BF),
-            pltpu.VMEM((2, 16 * E, depth), BF),
-            pltpu.VMEM((16 * E, 128), F32),
-            pltpu.VMEM((16 * E, 256), F32),
-            pltpu.VMEM((16 * E, 128), BF),
-            pltpu.VMEM((16 * E, 256), BF),
-            pltpu.SemaphoreType.DMA((2,)),
+            pltpu.VMEM((4, 8 * E, 128), F32),
+            pltpu.VMEM((4, 8 * E, 128), F32),
+            pltpu.SemaphoreType.DMA((4,)),
         ],
+        mib=40,
     )
     back = over_seq(back)
     two = (keep.astype(F32) + swap_cores(send, n_dp).astype(F32)).astype(BF)

time: 338 us -> 357 us (1.056)
  waiting for transfers between devices: 97.4 us -> 132 us
  blocking collectives: 134 us -> 103 us
  starting transfers between devices: 37.8 us -> 53.5 us
  local copies, waits for them, and re-layouts: 27.3 us -> 21.4 us
    all_gather x1, waiting for transfers between devices: 0.01 us -> 61.8 us  [on_device(): lax.all_gather(own, 'head', axis_index_groups=RING).reshape(8 * E, depth)]
    all_to_all x2 -> x3, waiting for transfers between devices: 89.5 us -> 50.7 us  [over_head(): lax.all_to_all(blocks, 'head', 0, 0, tiled=True, axis_index_groups=RING)]
    all_to_all x2 -> x1, blocking collectives: 28.9 us -> 12.1 us  [over_seq(): return lax.all_to_all(blocks, 'seq', 0, 0, tiled=True)]
    all_to_all x2 -> x1, blocking collectives: 24.2 us -> 11.2 us  [over_head(): lax.all_to_all(blocks, 'head', 0, 0, tiled=True, axis_index_groups=RING)]
    all_to_all x0 -> x1, waiting for transfers between devices: none -> 8.86 us  [over_seq(): return lax.all_to_all(blocks, 'seq', 0, 0, tiled=True)]
    all_to_all x2 -> x3, starting transfers between devices: 12.2 us -> 19.3 us  [over_head(): lax.all_to_all(blocks, 'head', 0, 0, tiled=True, axis_index_groups=RING)]
    unnamed x56 -> x46, local copies, waits for them, and re-layouts: 25.3 us -> 19.4 us
    ppermute x6 -> x8, starting transfers between devices: 25.5 us -> 29.9 us  [swap_cores(): return lax.ppermute(value, 'dp', [(i, i ^ bit) for i in range(n_dp)])]
  transfers between devices with their start and end apart: 10 -> 14, of which waited for: 5 -> 8; matrix products, arithmetic and copies ran while one was open for 1% -> 1% of each run, Pallas kernels for 3% -> 4%
where the time goes in v5:
time: 357 us; the launch traced here: 354 us
  waiting for transfers between devices  132 us (37%)
  blocking collectives  103 us (29%)
  starting transfers between devices  53.5 us (15%)
  Pallas kernels  26.6 us (7%)
  local copies, waits for them, and re-layouts  21.4 us (6%)
  between operations  14.3 us (4%)
    all_gather x1, waiting for transfers between devices, on_device(): lax.all_gather(own, 'head', axis_index_groups=RING).reshape(8 * E, depth)  61.8 us
    all_to_all x3, waiting for transfers between devices, over_head(): lax.all_to_all(blocks, 'head', 0, 0, tiled=True, axis_index_groups=RING)  50.7 us
    all_to_all x1, blocking collectives, sum_far(): lax.all_to_all(copies, 'dp', 0, 0, tiled=True, axis_index_groups=far)  30.6 us
    ppermute x8, starting transfers between devices, swap_cores(): return lax.ppermute(value, 'dp', [(i, i ^ bit) for i in range(n_dp)])  29.9 us
    pallas_call x8, Pallas kernels, call(): pl.pallas_call(kernel, out_shape=outs, in_specs=more.pop('in_specs', [VME...  26.6 us
    all_to_all x1, blocking collectives, spread(): lax.all_to_all(copies, ('seq', 'dp'), 0, 0, tiled=True, axis_index_groups...  25.7 us
    all_to_all x1, blocking collectives, sum_near(): lax.all_to_all(grads, ('seq', 'dp'), 0, 0, tiled=True, axis_index_groups=...  23.3 us
    unnamed x46, local copies, waits for them, and re-layouts  19.4 us
  transfers between devices with their start and end apart: 14, of which 8 were waited for; matrix products, arithmetic and copies ran while one was open for 1% of the time, Pallas kernels for 4%

profile of v5, /device:TPU:7, one launch (start us, length us, event | category | flops | bytes accessed | tf_op | source)
XLA Modules:
  0.0 353.6 jit_solution(13514777922229853579)
XLA Ops:
  13.8 6.9 %all-to-all-start = ((bf16[8,168,1152]{2,1,0:T(8,128)(2,1)}), bf16[8,168,1152]{2,1,0:T(8,128)(2,1)S(1)}, u32[]{:S(2)}, u32[]{:S(2)}) async-start(bf16[8,168,1152]{2,1,0:T(8,128)(2,1)} %copy-done.3), calls=%async_computation | async-start | bytes 6193152 | tf_op jit(solution)/shard_map/all_to_all | solution.py:301
  20.7 61.8 %all-gather.3.cloned.1.call-done.own_ref = bf16[576,1152]{1,0:T(8,128)(2,1)} async-done(((bf16[72,1152]{1,0:T(8,128)(2,1)}), bf16[576,1152]{1,0:T(8,128)(2,1)}) %all-gather.3.cloned.1.call-update) | async-done | bytes 1327120 | tf_op jit(solution)/shard_map/all_gather | solution.py:363
  82.5 4.8 %collective-permute-start.1 = (bf16[576,1152]{1,0:T(8,128)(2,1)}, bf16[576,1152]{1,0:T(8,128)(2,1)}, u32[]{:S(2)}, u32[]{:S(2)}) collective-permute-start(bf16[576,1152]{1,0:T(8,128)(2,1)} %all-gather.3.cloned.1.call-done.own_ref), channel_id=1, source_target_pairs={{0,2},{1,3},{2,0},{3,1},{4,6},{5,7},{6,4},{7,5},{8,10},{9,11},{10,... | collective-permute-start | bytes 3981320 | tf_op jit(solution)/shard_map/ppermute | solution.py:309
  90.2 3.0 shard_map.76
  94.7 4.4 %collective-permute-start = (bf16[320,1152]{1,0:T(8,128)(2,1)}, bf16[320,1152]{1,0:T(8,128)(2,1)}, u32[]{:S(2)}, u32[]{:S(2)}) collective-permute-start(bf16[320,1152]{1,0:T(8,128)(2,1)} %bitcast.7.mine_ref), channel_id=1, source_target_pairs={{0,1},{1,0},{2,3},{3,2},{4,5},{5,4},{6,7},{7,6},{8,9},{9,8},{10,11... | collective-permute-start | bytes 2211848 | tf_op jit(solution)/shard_map/ppermute | solution.py:309
  99.2 6.9 %all-to-all-start.1 = ((bf16[8,72,128]{2,1,0:T(8,128)(2,1)}), bf16[8,72,128]{2,1,0:T(8,128)(2,1)S(1)}, u32[]{:S(2)}, u32[]{:S(2)}) async-start(bf16[8,72,128]{2,1,0:T(8,128)(2,1)} %copy-done.21), calls=%async_computation.1 | async-start | bytes 294912 | tf_op jit(solution)/shard_map/all_to_all | solution.py:301
  111.5 3.3 collective-permute-done.1.pass_ref
  118.5 4.8 %collective-permute-start.3 = (bf16[576,1152]{1,0:T(8,128)(2,1)}, bf16[576,1152]{1,0:T(8,128)(2,1)}, u32[]{:S(2)}, u32[]{:S(2)}) collective-permute-start(bf16[576,1152]{1,0:T(8,128)(2,1)} %get-tuple-element.31.z_ref), channel_id=1, source_target_pairs={{0,1},{1,0},{2,3},{3,2},{4,5},{5,4},{6,7},{7,6},{8,9},{9,8},{10,11... | collective-permute-start | bytes 3981320 | tf_op jit(solution)/shard_map/ppermute | solution.py:309
  123.3 4.2 %all-to-all-start.2 = ((bf16[2,2,2,32,1152]{4,3,2,1,0:T(8,128)(2,1)}), bf16[2,2,2,32,1152]{4,3,2,1,0:T(8,128)(2,1)}, u32[]{:S(2)}, u32[]{:S(2)}) async-start(bf16[2,2,2,32,1152]{4,3,2,1,0:T(8,128)(2,1)} %copy-done.9), calls=%async_computation.2 | async-start | bytes 1179648 | tf_op jit(solution)/shard_map/all_to_all | solution.py:305
  127.6 8.9 %all-to-all-done.2.pair_ref = bf16[2,2,2,32,1152]{4,3,2,1,0:T(8,128)(2,1)} async-done(((bf16[2,2,2,32,1152]{4,3,2,1,0:T(8,128)(2,1)}), bf16[2,2,2,32,1152]{4,3,2,1,0:T(8,128)(2,1)}, u32[]{:S(2)}, u32[]{:S(2)}) %all-to-all-start.2) | async-done | bytes 589856 | tf_op jit(solution)/shard_map/all_to_all | solution.py:305
  137.8 8.7 %shard_map.78 = (bf16[2,2,2,32,1152]{4,3,2,1,0:T(8,128)(2,1)S(1)}, bf16[1152,1152]{1,0:T(8,128)(2,1)S(1)}, bf16[1152,1152]{1,0:T(8,128)(2,1)S(1)}) custom-call(s32[2]{0:T(128)S(1)} %pad_add_fusion.at_ref.core_ref, bf16[2,2,2,32,1152]{4,3,2,1,0:T(8,128)(2,1)} %all-to-all-done.2.pair_ref, bf16[576,1152]{1,0:T(8,128)(2,1)S(1)} %copy-done.7, ...), custom_call_target="tpu_custom_call" | custom-call | tf_op jit(solution)/shard_map/pallas_call | solution.py:289
  150.0 4.6 %collective-permute-done.6 = bf16[1152,1152]{1,0:T(8,128)(2,1)S(1)} collective-permute-done((bf16[1152,1152]{1,0:T(8,128)(2,1)S(1)}, bf16[1152,1152]{1,0:T(8,128)(2,1)S(1)}, u32[]{:S(2)}, u32[]{:S(2)}) %collective-permute-start.6) | collective-permute-done | bytes 2654240 | tf_op jit(solution)/shard_map/ppermute | solution.py:309
  156.8 12.1 %all_to_all.45.back_ref = bf16[2,2,2,32,1152]{4,3,2,1,0:T(8,128)(2,1)S(1)} all-to-all(bf16[2,2,2,32,1152]{4,3,2,1,0:T(8,128)(2,1)} %copy-done.8), channel_id=1, replica_groups=mesh['seq'=2,'head'=8,'dp'=32] {'seq'}, dimensions={0} | all-to-all | bytes 1179648 | tf_op jit(solution)/shard_map/all_to_all | solution.py:305
  168.9 3.0 shard_map.79
  172.6 3.1 collective-permute-start.4
  175.7 11.2 %all_to_all.46.gh_ref = bf16[8,72,128]{2,1,0:T(8,128)(2,1)S(1)} all-to-all(bf16[8,72,128]{2,1,0:T(8,128)(2,1)S(1)} %get-tuple-element.35), channel_id=1, replica_groups={{0,64,128,192,224,160,96,32},{1,65,129,193,225,161,97,33},{2,66,130,194..., dimensions={0} | all-to-all | bytes 294912 | tf_op jit(solution)/shard_map/all_to_all | solution.py:301
  186.9 4.5 %shard_map.80 = (bf16[8,176,1152]{2,1,0:T(8,128)(2,1)S(1)}, bf16[112,1152]{1,0:T(8,128)(2,1)S(1)}, bf16[112,1152]{1,0:T(8,128)(2,1)S(1)}) custom-call(s32[2]{0:T(128)S(1)} %pad_add_fusion.at_ref.core_ref, bf16[2,216,512]{2,1,0:T(8,128)(2,1)S(1)} %copy-done.11, bf16[8,72,128]{2,1,0:T(8,128)(2,1)S(1)} %all_to_all.46.gh_ref, ...), custom_call_target="tpu_custom_call" | custom-call | tf_op jit(solution)/shard_map/pallas_call | solution.py:289
  194.5 5.5 %all-to-all-start.5 = ((bf16[8,176,1152]{2,1,0:T(8,128)(2,1)}), bf16[8,176,1152]{2,1,0:T(8,128)(2,1)S(1)}, u32[]{:S(2)}, u32[]{:S(2)}) async-start(bf16[8,176,1152]{2,1,0:T(8,128)(2,1)} %copy-done.2), calls=%async_computation.5 | async-start | bytes 6488064 | tf_op jit(solution)/shard_map/all_to_all | solution.py:301
  200.0 3.2 collective-permute-start.5
  205.3 47.8 %all-to-all-done.5.terms_ref = bf16[8,176,1152]{2,1,0:T(8,128)(2,1)S(1)} async-done(((bf16[8,176,1152]{2,1,0:T(8,128)(2,1)}), bf16[8,176,1152]{2,1,0:T(8,128)(2,1)S(1)}, u32[]{:S(2)}, u32[]{:S(2)}) %all-to-all-start.5) | async-done | bytes 3244064 | tf_op jit(solution)/shard_map/all_to_all | solution.py:301
  258.4 23.3 %all_to_all.47 = bf16[8,40,1152]{2,1,0:T(8,128)(2,1)S(1)} all-to-all(bf16[8,40,1152]{2,1,0:T(8,128)(2,1)S(1)} %get-tuple-element.45), channel_id=1, replica_groups={{0,2,4,6,256,258,260,262},{1,3,5,7,257,259,261,263},{8,10,12,14,264,266..., dimensions={0} | all-to-all | bytes 1474560 | tf_op jit(solution)/shard_map/all_to_all | solution.py:328
  281.8 30.6 %all_to_all.48 = bf16[4,40,1152]{2,1,0:T(8,128)(2,1)S(1)} all-to-all(bf16[4,40,1152]{2,1,0:T(8,128)(2,1)S(1)} %broadcast_in_dim.8), channel_id=1, replica_groups={{0,8,16,24},{1,9,17,25},{2,10,18,26},{3,11,19,27},{4,12,20,28},{5,13,21..., dimensions={0} | all-to-all | bytes 737280 | tf_op jit(solution)/shard_map/all_to_all | solution.py:336
  312.5 25.7 %all_to_all.49 = bf16[8,40,1152]{2,1,0:T(8,128)(2,1)S(1)} all-to-all(bf16[8,40,1152]{2,1,0:T(8,128)(2,1)S(1)} %broadcast_in_dim.9), channel_id=1, replica_groups={{0,2,4,6,256,258,260,262},{1,3,5,7,257,259,261,263},{8,10,12,14,264,266..., dimensions={0} | all-to-all | bytes 1474560 | tf_op jit(solution)/shard_map/all_to_all | solution.py:342
  338.2 4.4 %collective-permute-start.7 = (bf16[320,1152]{1,0:T(8,128)(2,1)S(1)}, bf16[320,1152]{1,0:T(8,128)(2,1)S(1)}, u32[]{:S(2)}, u32[]{:S(2)}) collective-permute-start(bf16[320,1152]{1,0:T(8,128)(2,1)S(1)} %bitcast.19), channel_id=1, source_target_pairs={{0,1},{1,0},{2,3},{3,2},{4,5},{5,4},{6,7},{7,6},{8,9},{9,8},{10,11... | collective-permute-start | bytes 2211848 | tf_op jit(solution)/shard_map/ppermute | solution.py:309
  (72 shorter events, 42.6 us)
Async XLA Ops:
  7.2 75.4 %all-gather.3.cloned.1.call-start = ((), (), s32[]{:S(2)}) async-start(), calls=%async_computation.11 | async-start | bytes 1492992 | tf_op jit(solution)/shard_map/all_gather | solution.py:363
  8.3 1.2 copy-start.6
  9.5 1.0 copy-start.12
  12.2 1.6 copy-start.3
  13.8 75.4 %all-to-all-start = ((bf16[8,168,1152]{2,1,0:T(8,128)(2,1)}), bf16[8,168,1152]{2,1,0:T(8,128)(2,1)S(1)}, u32[]{:S(2)}, u32[]{:S(2)}) async-start(bf16[8,168,1152]{2,1,0:T(8,128)(2,1)} %copy-done.3), calls=%async_computation | async-start | bytes 6193152 | tf_op jit(solution)/shard_map/all_to_all | solution.py:301
  20.7 94.1 %copy-start.5 = (bf16[1,2,64,1152]{3,2,1,0:T(8,128)(2,1)S(1)}, bf16[1,2,64,1152]{3,2,1,0:T(8,128)(2,1)}, u32[]{:S(2)}) copy-start(bf16[1,2,64,1152]{3,2,1,0:T(8,128)(2,1)} %param.4) | copy-start | bytes 884740
  82.5 32.3 %collective-permute-start.1 = (bf16[576,1152]{1,0:T(8,128)(2,1)}, bf16[576,1152]{1,0:T(8,128)(2,1)}, u32[]{:S(2)}, u32[]{:S(2)}) collective-permute-start(bf16[576,1152]{1,0:T(8,128)(2,1)} %all-gather.3.cloned.1.call-done.own_ref), channel_id=1, source_target_pairs={{0,2},{1,3},{2,0},{3,1},{4,6},{5,7},{6,4},{7,5},{8,10},{9,11},{10,... | collective-permute-start | bytes 3981320 | tf_op jit(solution)/shard_map/ppermute | solution.py:309
  89.2 1.0 copy-start
  94.7 16.7 %collective-permute-start = (bf16[320,1152]{1,0:T(8,128)(2,1)}, bf16[320,1152]{1,0:T(8,128)(2,1)}, u32[]{:S(2)}, u32[]{:S(2)}) collective-permute-start(bf16[320,1152]{1,0:T(8,128)(2,1)} %bitcast.7.mine_ref), channel_id=1, source_target_pairs={{0,1},{1,0},{2,3},{3,2},{4,5},{5,4},{6,7},{7,6},{8,9},{9,8},{10,11... | collective-permute-start | bytes 2211848 | tf_op jit(solution)/shard_map/ppermute | solution.py:309
  99.2 12.3 %all-to-all-start.1 = ((bf16[8,72,128]{2,1,0:T(8,128)(2,1)}), bf16[8,72,128]{2,1,0:T(8,128)(2,1)S(1)}, u32[]{:S(2)}, u32[]{:S(2)}) async-start(bf16[8,72,128]{2,1,0:T(8,128)(2,1)} %copy-done.21), calls=%async_computation.1 | async-start | bytes 294912 | tf_op jit(solution)/shard_map/all_to_all | solution.py:301
  106.1 21.5 %collective-permute-start.2 = (bf16[576,1152]{1,0:T(8,128)(2,1)}, bf16[576,1152]{1,0:T(8,128)(2,1)}, u32[]{:S(2)}, u32[]{:S(2)}) collective-permute-start(bf16[576,1152]{1,0:T(8,128)(2,1)} %all-gather.3.cloned.1.call-done.own_ref), channel_id=1, source_target_pairs={{0,1},{1,0},{2,3},{3,2},{4,5},{5,4},{6,7},{7,6},{8,9},{9,8},{10,11... | collective-permute-start | bytes 3981320 | tf_op jit(solution)/shard_map/ppermute | solution.py:309
  118.5 18.0 %collective-permute-start.3 = (bf16[576,1152]{1,0:T(8,128)(2,1)}, bf16[576,1152]{1,0:T(8,128)(2,1)}, u32[]{:S(2)}, u32[]{:S(2)}) collective-permute-start(bf16[576,1152]{1,0:T(8,128)(2,1)} %get-tuple-element.31.z_ref), channel_id=1, source_target_pairs={{0,1},{1,0},{2,3},{3,2},{4,5},{5,4},{6,7},{7,6},{8,9},{9,8},{10,11... | collective-permute-start | bytes 3981320 | tf_op jit(solution)/shard_map/ppermute | solution.py:309
  123.3 13.2 %all-to-all-start.2 = ((bf16[2,2,2,32,1152]{4,3,2,1,0:T(8,128)(2,1)}), bf16[2,2,2,32,1152]{4,3,2,1,0:T(8,128)(2,1)}, u32[]{:S(2)}, u32[]{:S(2)}) async-start(bf16[2,2,2,32,1152]{4,3,2,1,0:T(8,128)(2,1)} %copy-done.9), calls=%async_computation.2 | async-start | bytes 1179648 | tf_op jit(solution)/shard_map/all_to_all | solution.py:305
  127.5 125.6 %reduce-scatter.2.cloned.1.call-start = ((), (), s32[]{:S(2)}) async-start(), calls=%async_computation.10 | async-start | bytes 2985984 | tf_op jit(solution)/shard_map/reduce_scatter | solution.py:402
  136.5 1.3 copy-start.7
  147.3 7.2 %collective-permute-start.6 = (bf16[1152,1152]{1,0:T(8,128)(2,1)S(1)}, bf16[1152,1152]{1,0:T(8,128)(2,1)S(1)}, u32[]{:S(2)}, u32[]{:S(2)}) collective-permute-start(bf16[1152,1152]{1,0:T(8,128)(2,1)S(1)} %get-tuple-element.43), channel_id=1, source_target_pairs={{0,1},{1,0},{2,3},{3,2},{4,5},{5,4},{6,7},{7,6},{8,9},{9,8},{10,11... | collective-permute-start | bytes 7962632 | tf_op jit(solution)/shard_map/ppermute | solution.py:309
  156.8 30.1 %copy-start.1 = (bf16[1,1,3,72,1152]{4,3,2,1,0:T(8,128)(2,1)S(1)}, bf16[1,1,3,72,1152]{4,3,2,1,0:T(8,128)(2,1)}, u32[]{:S(2)}) copy-start(bf16[1,1,3,72,1152]{4,3,2,1,0:T(8,128)(2,1)} %slice.3) | copy-start | bytes 1492996
  156.8 30.1 %copy-start.11 = (bf16[2,216,512]{2,1,0:T(8,128)(2,1)S(1)}, bf16[2,216,512]{2,1,0:T(8,128)(2,1)}, u32[]{:S(2)}) copy-start(bf16[2,216,512]{2,1,0:T(8,128)(2,1)} %copy-done.10) | copy-start | bytes 1327108
  172.6 14.3 %collective-permute-start.4 = (bf16[8,40,1152]{2,1,0:T(8,128)(2,1)S(1)}, bf16[8,40,1152]{2,1,0:T(8,128)(2,1)S(1)}, u32[]{:S(2)}, u32[]{:S(2)}) collective-permute-start(bf16[8,40,1152]{2,1,0:T(8,128)(2,1)S(1)} %get-tuple-element.37), channel_id=1, source_target_pairs={{0,1},{1,0},{2,3},{3,2},{4,5},{5,4},{6,7},{7,6},{8,9},{9,8},{10,11... | collective-permute-start | bytes 2211848 | tf_op jit(solution)/shard_map/ppermute | solution.py:309
  191.4 1.7 copy-start.2
  194.5 58.7 %all-to-all-start.5 = ((bf16[8,176,1152]{2,1,0:T(8,128)(2,1)}), bf16[8,176,1152]{2,1,0:T(8,128)(2,1)S(1)}, u32[]{:S(2)}, u32[]{:S(2)}) async-start(bf16[8,176,1152]{2,1,0:T(8,128)(2,1)} %copy-done.2), calls=%async_computation.5 | async-start | bytes 6488064 | tf_op jit(solution)/shard_map/all_to_all | solution.py:301
  200.0 4.6 %collective-permute-start.5 = (bf16[112,1152]{1,0:T(8,128)(2,1)}, bf16[112,1152]{1,0:T(8,128)(2,1)S(1)}, u32[]{:S(2)}, u32[]{:S(2)}) collective-permute-start(bf16[112,1152]{1,0:T(8,128)(2,1)} %copy-done.22), channel_id=1, source_target_pairs={{0,1},{1,0},{2,3},{3,2},{4,5},{5,4},{6,7},{7,6},{8,9},{9,8},{10,11... | collective-permute-start | bytes 774152 | tf_op jit(solution)/shard_map/ppermute | solution.py:309
  253.1 1.0 copy-start.13
  338.2 6.2 %collective-permute-start.7 = (bf16[320,1152]{1,0:T(8,128)(2,1)S(1)}, bf16[320,1152]{1,0:T(8,128)(2,1)S(1)}, u32[]{:S(2)}, u32[]{:S(2)}) collective-permute-start(bf16[320,1152]{1,0:T(8,128)(2,1)S(1)} %bitcast.19), channel_id=1, source_target_pairs={{0,1},{1,0},{2,3},{3,2},{4,5},{5,4},{6,7},{7,6},{8,9},{9,8},{10,11... | collective-permute-start | bytes 2211848 | tf_op jit(solution)/shard_map/ppermute | solution.py:309
  (13 other events, 10.7 us)
Sparse Core Ops, SparseCore 0:
  13.9 68.5 all-gather.2
  156.9 49.7 reduce-scatter.1

commit v6 on v4

--- a/solution.py
+++ b/solution.py
@@ -48,17 +48,17 @@
     )
 
 
-def norm_kernel(at_ref, x_ref, wq_ref, wo_ref, out_ref, own_ref):
+def norm_kernel(at_ref, x_ref, wq_ref, wo_ref, out_ref):
     core = at_ref[0]
     wide = wo_ref[0].astype(F32)
     half = jnp.where(core == 0, wide[:40], wide[32:])
+    qk = jnp.concatenate([wq_ref[1, 0].astype(F32), wq_ref[1, 1].astype(F32)], axis=0)
+    vo = jnp.concatenate([wq_ref[1, 2].astype(F32), wo_ref[1].astype(F32)], axis=0)
     hidden = normalize(x_ref[...])[0]
-    block = jnp.concatenate([hidden, half], axis=0).astype(BF)
+    block = [hidden, jnp.where(core == 0, qk, vo), half, jnp.zeros_like(half[:8])]
+    block = jnp.concatenate(block, axis=0).astype(BF)
     for j in range(8):
         out_ref[j] = block
-    qk = jnp.concatenate([wq_ref[1, 0].astype(F32), wq_ref[1, 1].astype(F32)], axis=0)
-    vo = jnp.concatenate([wq_ref[1, 2].astype(F32), wo_ref[1].astype(F32)], axis=0)
-    own_ref[...] = jnp.where(core == 0, qk, vo).astype(BF)
 
 
 def frame_rows(hidden_ref, f):
@@ -74,9 +74,10 @@
     return tuple(stacked[i * E : (i + 1) * E].astype(BF) for i in range(3))
 
 
-def spatial_kernel(hidden_ref, w_ref, heads_ref, qkv_ref, one_ref):
+def spatial_kernel(hidden_ref, w_ref, heads_ref, qkv_ref, one_ref, two_ref):
     for h in range(8):
-        one_ref[h] = hidden_ref[h].astype(F32)[128:].astype(BF)
+        two_ref[h * 2 * E : (h + 1) * 2 * E] = hidden_ref[h, 128 : 128 + 2 * E]
+        one_ref[h] = hidden_ref[h, 272:320].astype(F32)[:40].astype(BF)
     outs = []
     for f in range(2):
         qkv = nt(w_ref[...], frame_rows(hidden_ref, f))
@@ -92,7 +93,7 @@
 
 
 def middle_kernel(
-    core_ref, x_ref, g_ref, heads_ref, mine_ref, other_ref, pass_ref, out_ref, same_ref, split_ref
+    core_ref, x_ref, g_ref, heads_ref, mine_ref, other_ref, out_ref, split_ref
 ):
     core = core_ref[0]
     for h in range(8):
@@ -280,20 +281,46 @@
 VMEM = pl.BlockSpec(memory_space=pltpu.VMEM)
 SMEM = pl.BlockSpec(memory_space=pltpu.SMEM)
 ANY = pl.BlockSpec(memory_space=pl.ANY)
-PARAMS = pltpu.CompilerParams(vmem_limit_bytes=48 * 1024 * 1024)
+MIB = 1024 * 1024
 
 
 def shape(*dims):
     return jax.ShapeDtypeStruct(dims, BF)
 
 
-def call(kernel, outs, *args, **more):
+def call(kernel, outs, *args, mib=24, fetch=False, in_specs=None, scratch_shapes=(), **more):
+    specs = list(in_specs or [VMEM] * len(args))
+    scratch = list(scratch_shapes)
+    moved = [i for i, spec in enumerate(specs) if spec is VMEM] if fetch else []
+    n_in, n_out, n_own = len(args), len(jax.tree.leaves(outs)), len(scratch)
+
+    def fetching(*refs):
+        ins = list(refs[:n_in])
+        rest = refs[n_in : n_in + n_out + n_own]
+        held, sems = refs[n_in + n_out + n_own : -1], refs[-1]
+        copies = [
+            pltpu.make_async_copy(ins[i], to, sems.at[k])
+            for k, (i, to) in enumerate(zip(moved, held))
+        ]
+        for copy in copies:
+            copy.start()
+        for copy in copies:
+            copy.wait()
+        for i, to in zip(moved, held):
+            ins[i] = to
+        kernel(*ins, *rest)
+
+    if moved:
+        scratch += [pltpu.VMEM(args[i].shape, args[i].dtype) for i in moved]
+        scratch.append(pltpu.SemaphoreType.DMA((len(moved),)))
+        specs = [ANY if i in moved else spec for i, spec in enumerate(specs)]
     return pl.pallas_call(
-        kernel,
+        fetching if moved else kernel,
         out_shape=outs,
-        in_specs=more.pop("in_specs", [VMEM] * len(args)),
+        in_specs=specs,
         out_specs=more.pop("out_specs", jax.tree.map(lambda _: VMEM, outs)),
-        compiler_params=PARAMS,
+        scratch_shapes=scratch,
+        compiler_params=pltpu.CompilerParams(vmem_limit_bytes=mib * MIB),
         cost_estimate=pl.CostEstimate(flops=0, bytes_accessed=0, transcendentals=0),
         **more,
     )(*args)
@@ -355,31 +382,27 @@
     g = cotangent.reshape(128, depth)
     w_own = w_qkv[0].reshape(3 * E, depth)
 
-    hidden, own = call(
-        norm_kernel, (shape(8, 168, depth), shape(2 * E, depth)),
+    hidden = call(
+        norm_kernel, shape(8, 320, depth),
         at, x, w_qkv.reshape(2, 3, E, depth), w_out.reshape(2, E, depth),
-        in_specs=[SMEM] + [VMEM] * 3,
-    )
-    mine_two = lax.all_gather(own, "head", axis_index_groups=RING).reshape(16 * E, depth)
+        in_specs=[SMEM] + [VMEM] * 3, fetch=True,
+    )
     hidden = over_head(hidden)
-    heads, qkv, mine_one = call(
+    big = shape(16 * E, depth)
+    heads, qkv, mine_one, mine_two = call(
         spatial_kernel,
-        (shape(8, E, 128), shape(2, 3 * E, 512), shape(8, 40, depth)), hidden, w_own,
+        (shape(8, E, 128), shape(2, 3 * E, 512), shape(8, 40, depth), big), hidden, w_own, mib=32,
     )
     heads = over_head(heads)
     mine_one = mine_one.reshape(320, depth)
     other_one = swap_cores(mine_one, n_dp)
-    big = shape(16 * E, depth)
-    pair, mine_two = call(
-        middle_kernel, (shape(2, 2, 2, 32, depth), big),
-        at, x, g, heads, mine_one, other_one, mine_two,
-        in_specs=[SMEM] + [VMEM] * 5 + [ANY],
-        out_specs=(VMEM, ANY),
-        input_output_aliases={6: 1},
+    other_two = swap_cores(mine_two, n_dp)
+    pair = call(
+        middle_kernel, shape(2, 2, 2, 32, depth), at, x, g, heads, mine_one, other_one,
+        in_specs=[SMEM] + [VMEM] * 5, fetch=True,
         scratch_shapes=[pltpu.VMEM((2, 320, 128), F32)],
     )
     pair = over_seq(pair)
-    other_two = swap_cores(mine_two, n_dp)
     back, keep, send = call(
         temporal_kernel,
         (shape(2, 2, 2, 32, depth), big, big),
@@ -395,6 +418,7 @@
             pltpu.VMEM((16 * E, 256), BF),
             pltpu.SemaphoreType.DMA((2,)),
         ],
+        mib=40,
     )
     back = over_seq(back)
     two = (keep.astype(F32) + swap_cores(send, n_dp).astype(F32)).astype(BF)
@@ -406,7 +430,7 @@
         turn_kernel,
         (shape(8, E, 128), half, half, shape(128, depth), shape(128, depth)),
         at, back, heads, mine_one, other_one,
-        in_specs=[SMEM] + [VMEM] * 4,
+        in_specs=[SMEM] + [VMEM] * 4, fetch=True,
         scratch_shapes=[pltpu.VMEM((2, 320, 128), F32)],
     )
     gh = over_head(gh)
@@ -414,13 +438,13 @@
     terms, keep, send = call(
         spatial_back_kernel, (shape(8, 176, depth), half, half),
         at, qkv, gh, hidden, w_own, keep, swap_cores(send, n_dp),
-        in_specs=[SMEM] + [VMEM] * 6,
+        in_specs=[SMEM] + [VMEM] * 6, mib=32,
     )
     n_near = len(near[0])
     latent_grads, chain = call(
         last_kernel, (shape(128, depth), shape(n_near, 320 // n_near, depth)),
         over_head(terms), x, grad_one, keep, swap_cores(send, n_dp), two,
-        scratch_shapes=[pltpu.VMEM((320, depth), F32)],
+        scratch_shapes=[pltpu.VMEM((320, depth), F32)], fetch=True,
     )
     part = sum_near(chain, near)
     mine = spread(sum_far(part, far), near)

time: 338 us -> 363 us (1.074)
  waiting for transfers between devices: 97.4 us -> 136 us
  local copies, waits for them, and re-layouts: 27.3 us -> 13.4 us
  Pallas kernels: 23.1 us -> 28.6 us
    all_to_all x2, waiting for transfers between devices: 89.5 us -> 129 us  [over_head(): lax.all_to_all(blocks, 'head', 0, 0, tiled=True, axis_index_groups=RING)]
    unnamed x56 -> x32, local copies, waits for them, and re-layouts: 25.3 us -> 13.3 us
    pallas_call x8, Pallas kernels: 23.1 us -> 28.6 us  [call(): pl.pallas_call(fetching if moved else kernel, out_shape=outs, in_specs=sp...]
  transfers between devices with their start and end apart: 10 -> 9, of which waited for: 5 -> 5; matrix products, arithmetic and copies ran while one was open for 1% -> 0% of each run, Pallas kernels for 3% -> 3%
where the time goes in v6:
time: 363 us; the launch traced here: 362 us
  waiting for transfers between devices  136 us (37%)
  blocking collectives  133 us (37%)
  starting transfers between devices  34.3 us (9%)
  Pallas kernels  28.6 us (8%)
  between operations  14.2 us (4%)
  local copies, waits for them, and re-layouts  13.4 us (4%)
    all_to_all x2, waiting for transfers between devices, over_head(): lax.all_to_all(blocks, 'head', 0, 0, tiled=True, axis_index_groups=RING)  129 us
    all_to_all x1, blocking collectives, sum_far(): lax.all_to_all(copies, 'dp', 0, 0, tiled=True, axis_index_groups=far)  30.8 us
    all_to_all x2, blocking collectives, over_seq(): return lax.all_to_all(blocks, 'seq', 0, 0, tiled=True)  29.5 us
    pallas_call x8, Pallas kernels, call(): pl.pallas_call(fetching if moved else kernel, out_shape=outs, in_specs=sp...  28.6 us
    all_to_all x1, blocking collectives, spread(): lax.all_to_all(copies, ('seq', 'dp'), 0, 0, tiled=True, axis_index_groups...  25.8 us
    all_to_all x1, blocking collectives, sum_near(): lax.all_to_all(grads, ('seq', 'dp'), 0, 0, tiled=True, axis_index_groups=...  23.8 us
    all_to_all x2, blocking collectives, over_head(): lax.all_to_all(blocks, 'head', 0, 0, tiled=True, axis_index_groups=RING)  22.7 us
    ppermute x6, starting transfers between devices, swap_cores(): return lax.ppermute(value, 'dp', [(i, i ^ bit) for i in range(n_dp)])  22.2 us
  transfers between devices with their start and end apart: 9, of which 5 were waited for; matrix products, arithmetic and copies ran while one was open for 0% of the time, Pallas kernels for 3%

profile of v6, /device:TPU:7, one launch (start us, length us, event | category | flops | bytes accessed | tf_op | source)
XLA Modules:
  0.0 361.9 jit_solution(1437560488050518437)
XLA Ops:
  11.6 2.5 copy-done
  14.1 7.0 %all-to-all-start = ((bf16[8,320,1152]{2,1,0:T(8,128)(2,1)}), bf16[8,320,1152]{2,1,0:T(8,128)(2,1)}, u32[]{:S(2)}, u32[]{:S(2)}) async-start(bf16[8,320,1152]{2,1,0:T(8,128)(2,1)} %copy-done), calls=%async_computation | async-start | bytes 11796480 | tf_op jit(solution)/shard_map/all_to_all | solution.py:330
  21.1 81.2 %all-to-all-done.hidden_ref = bf16[8,320,1152]{2,1,0:T(8,128)(2,1)} async-done(((bf16[8,320,1152]{2,1,0:T(8,128)(2,1)}), bf16[8,320,1152]{2,1,0:T(8,128)(2,1)}, u32[]{:S(2)}, u32[]{:S(2)}) %all-to-all-start) | async-done | bytes 5898272 | tf_op jit(solution)/shard_map/all_to_all | solution.py:330
  102.3 5.2 %shard_map.76 = (bf16[8,72,128]{2,1,0:T(8,128)(2,1)S(1)}, bf16[2,216,512]{2,1,0:T(8,128)(2,1)S(1)}, bf16[8,40,1152]{2,1,0:T(8,128)(2,1)S(1)}, bf16[1152,1152]{1,0:T(8,128)(2,1)S(1)}) custom-call(bf16[8,320,1152]{2,1,0:T(8,128)(2,1)} %all-to-all-done.hidden_ref, bf16[216,1152]{1,0:T(8,128)(2,1)S(1)} %bitcast.16), custom_call_target="tpu_custom_call" | custom-call | tf_op jit(solution)/shard_map/pallas_call | solution.py:317
  107.5 4.4 %collective-permute-start.1 = (bf16[1152,1152]{1,0:T(8,128)(2,1)S(1)}, bf16[1152,1152]{1,0:T(8,128)(2,1)S(1)}, u32[]{:S(2)}, u32[]{:S(2)}) collective-permute-start(bf16[1152,1152]{1,0:T(8,128)(2,1)S(1)} %get-tuple-element.25.mine_ref), channel_id=1, source_target_pairs={{0,1},{1,0},{2,3},{3,2},{4,5},{5,4},{6,7},{7,6},{8,9},{9,8},{10,11... | collective-permute-start | bytes 7962632 | tf_op jit(solution)/shard_map/ppermute | solution.py:338
  113.8 11.1 %all_to_all.45.refs_3_.refs_2_ = bf16[8,72,128]{2,1,0:T(8,128)(2,1)S(1)} all-to-all(bf16[8,72,128]{2,1,0:T(8,128)(2,1)S(1)} %get-tuple-element.23), channel_id=1, replica_groups={{0,64,128,192,224,160,96,32},{1,65,129,193,225,161,97,33},{2,66,130,194..., dimensions={0} | all-to-all | bytes 294912 | tf_op jit(solution)/shard_map/all_to_all | solution.py:330
  126.5 18.6 %all_to_all.46.pair_ref = bf16[2,2,2,32,1152]{4,3,2,1,0:T(8,128)(2,1)S(1)} all-to-all(bf16[2,2,2,32,1152]{4,3,2,1,0:T(8,128)(2,1)S(1)} %shard_map.77), channel_id=1, replica_groups=mesh['seq'=2,'head'=8,'dp'=32] {'seq'}, dimensions={0} | all-to-all | bytes 1179648 | tf_op jit(solution)/shard_map/all_to_all | solution.py:334
  145.1 6.6 %shard_map.78 = (bf16[2,2,2,32,1152]{4,3,2,1,0:T(8,128)(2,1)S(1)}, bf16[1152,1152]{1,0:T(8,128)(2,1)S(1)}, bf16[1152,1152]{1,0:T(8,128)(2,1)S(1)}) custom-call(s32[1]{0:T(128)} %bitcast.refs_0_.core_ref, bf16[2,2,2,32,1152]{4,3,2,1,0:T(8,128)(2,1)S(1)} %all_to_all.46.pair_ref, bf16[1152,1152]{1,0:T(8,128)(2,1)S(1)} %get-tuple-element.25.mine_ref, ...), custom_call_target="tpu_custom_call" | custom-call | tf_op jit(solution)/shard_map/pallas_call | solution.py:317
  151.7 4.9 %collective-permute-start.4 = (bf16[1152,1152]{1,0:T(8,128)(2,1)S(1)}, bf16[1152,1152]{1,0:T(8,128)(2,1)S(1)}, u32[]{:S(2)}, u32[]{:S(2)}) collective-permute-start(bf16[1152,1152]{1,0:T(8,128)(2,1)S(1)} %get-tuple-element.37), channel_id=1, source_target_pairs={{0,1},{1,0},{2,3},{3,2},{4,5},{5,4},{6,7},{7,6},{8,9},{9,8},{10,11... | collective-permute-start | bytes 7962632 | tf_op jit(solution)/shard_map/ppermute | solution.py:338
  156.6 4.6 %collective-permute-done.4 = bf16[1152,1152]{1,0:T(8,128)(2,1)S(1)} collective-permute-done((bf16[1152,1152]{1,0:T(8,128)(2,1)S(1)}, bf16[1152,1152]{1,0:T(8,128)(2,1)S(1)}, u32[]{:S(2)}, u32[]{:S(2)}) %collective-permute-start.4) | collective-permute-done | bytes 2654240 | tf_op jit(solution)/shard_map/ppermute | solution.py:338
  161.2 2.2 add_convert_fusion
  163.4 10.8 %all_to_all.47.refs_1_ = bf16[2,2,2,32,1152]{4,3,2,1,0:T(8,128)(2,1)S(1)} all-to-all(bf16[2,2,2,32,1152]{4,3,2,1,0:T(8,128)(2,1)S(1)} %get-tuple-element.26), channel_id=1, replica_groups=mesh['seq'=2,'head'=8,'dp'=32] {'seq'}, dimensions={0} | all-to-all | bytes 1179648 | tf_op jit(solution)/shard_map/all_to_all | solution.py:334
  174.3 2.6 shard_map.79
  176.9 3.1 collective-permute-start.2
  180.0 11.6 %all_to_all.48.gh_ref = bf16[8,72,128]{2,1,0:T(8,128)(2,1)S(1)} all-to-all(bf16[8,72,128]{2,1,0:T(8,128)(2,1)S(1)} %get-tuple-element.29), channel_id=1, replica_groups={{0,64,128,192,224,160,96,32},{1,65,129,193,225,161,97,33},{2,66,130,194..., dimensions={0} | all-to-all | bytes 294912 | tf_op jit(solution)/shard_map/all_to_all | solution.py:330
  191.6 6.7 %shard_map.80 = (bf16[8,176,1152]{2,1,0:T(8,128)(2,1)S(1)}, bf16[112,1152]{1,0:T(8,128)(2,1)S(1)}, bf16[112,1152]{1,0:T(8,128)(2,1)S(1)}) custom-call(s32[1]{0:T(128)} %bitcast.refs_0_.core_ref, bf16[2,216,512]{2,1,0:T(8,128)(2,1)S(1)} %get-tuple-element.28.qkv_ref, bf16[8,72,128]{2,1,0:T(8,128)(2,1)S(1)} %all_to_all.48.gh_ref, ...), custom_call_target="tpu_custom_call" | custom-call | tf_op jit(solution)/shard_map/pallas_call | solution.py:317
  201.4 5.2 %all-to-all-start.5 = ((bf16[8,176,1152]{2,1,0:T(8,128)(2,1)}), bf16[8,176,1152]{2,1,0:T(8,128)(2,1)S(1)}, u32[]{:S(2)}, u32[]{:S(2)}) async-start(bf16[8,176,1152]{2,1,0:T(8,128)(2,1)} %copy-done.1), calls=%async_computation.5 | async-start | bytes 6488064 | tf_op jit(solution)/shard_map/all_to_all | solution.py:330
  206.5 3.5 collective-permute-start.3
  212.1 47.5 %all-to-all-done.5.refs_0_ = bf16[8,176,1152]{2,1,0:T(8,128)(2,1)S(1)} async-done(((bf16[8,176,1152]{2,1,0:T(8,128)(2,1)}), bf16[8,176,1152]{2,1,0:T(8,128)(2,1)S(1)}, u32[]{:S(2)}, u32[]{:S(2)}) %all-to-all-start.5) | async-done | bytes 3244064 | tf_op jit(solution)/shard_map/all_to_all | solution.py:330
  263.4 2.9 shard_map.81
  266.3 23.8 %all_to_all.49 = bf16[8,40,1152]{2,1,0:T(8,128)(2,1)S(1)} all-to-all(bf16[8,40,1152]{2,1,0:T(8,128)(2,1)S(1)} %get-tuple-element.39), channel_id=1, replica_groups={{0,2,4,6,256,258,260,262},{1,3,5,7,257,259,261,263},{8,10,12,14,264,266..., dimensions={0} | all-to-all | bytes 1474560 | tf_op jit(solution)/shard_map/all_to_all | solution.py:357
  290.3 30.8 %all_to_all.50 = bf16[4,40,1152]{2,1,0:T(8,128)(2,1)S(1)} all-to-all(bf16[4,40,1152]{2,1,0:T(8,128)(2,1)S(1)} %broadcast_in_dim.8), channel_id=1, replica_groups={{0,8,16,24},{1,9,17,25},{2,10,18,26},{3,11,19,27},{4,12,20,28},{5,13,21..., dimensions={0} | all-to-all | bytes 737280 | tf_op jit(solution)/shard_map/all_to_all | solution.py:365
  321.2 25.8 %all_to_all.51 = bf16[8,40,1152]{2,1,0:T(8,128)(2,1)S(1)} all-to-all(bf16[8,40,1152]{2,1,0:T(8,128)(2,1)S(1)} %broadcast_in_dim.9), channel_id=1, replica_groups={{0,2,4,6,256,258,260,262},{1,3,5,7,257,259,261,263},{8,10,12,14,264,266..., dimensions={0} | all-to-all | bytes 1474560 | tf_op jit(solution)/shard_map/all_to_all | solution.py:371
  347.0 4.4 %collective-permute-start.5 = (bf16[320,1152]{1,0:T(8,128)(2,1)S(1)}, bf16[320,1152]{1,0:T(8,128)(2,1)S(1)}, u32[]{:S(2)}, u32[]{:S(2)}) collective-permute-start(bf16[320,1152]{1,0:T(8,128)(2,1)S(1)} %bitcast.21), channel_id=1, source_target_pairs={{0,1},{1,0},{2,3},{3,2},{4,5},{5,4},{6,7},{7,6},{8,9},{9,8},{10,11... | collective-permute-start | bytes 2211848 | tf_op jit(solution)/shard_map/ppermute | solution.py:338
  (48 shorter events, 20.8 us)
Async XLA Ops:
  7.2 1.0 copy-start.2
  8.1 1.2 copy-start.4
  9.3 1.0 copy-start.6
  11.6 2.5 copy-start
  14.1 7.0 %copy-start.5 = (bf16[2,1,3,72,1152]{4,3,2,1,0:T(8,128)(2,1)S(1)}, bf16[2,1,3,72,1152]{4,3,2,1,0:T(8,128)(2,1)}, u32[]{:S(2)}) copy-start(bf16[2,1,3,72,1152]{4,3,2,1,0:T(8,128)(2,1)} %param.6) | copy-start | bytes 2985988
  14.1 88.2 %all-to-all-start = ((bf16[8,320,1152]{2,1,0:T(8,128)(2,1)}), bf16[8,320,1152]{2,1,0:T(8,128)(2,1)}, u32[]{:S(2)}, u32[]{:S(2)}) async-start(bf16[8,320,1152]{2,1,0:T(8,128)(2,1)} %copy-done), calls=%async_computation | async-start | bytes 11796480 | tf_op jit(solution)/shard_map/all_to_all | solution.py:330
  21.1 238.5 %reduce-scatter.2.cloned.1.call-start = ((), (), s32[]{:S(2)}) async-start(), calls=%async_computation.10 | async-start | bytes 2985984 | tf_op jit(solution)/shard_map/reduce_scatter | solution.py:425
  102.3 22.6 %copy-start.3 = (bf16[1,2,64,1152]{3,2,1,0:T(8,128)(2,1)S(1)}, bf16[1,2,64,1152]{3,2,1,0:T(8,128)(2,1)}, u32[]{:S(2)}) copy-start(bf16[1,2,64,1152]{3,2,1,0:T(8,128)(2,1)} %param.4) | copy-start | bytes 884740
  102.3 22.6 %copy-start.8 = (bf16[1,2,64,1152]{3,2,1,0:T(8,128)(2,1)S(1)}, bf16[1,2,64,1152]{3,2,1,0:T(8,128)(2,1)}, u32[]{:S(2)}) copy-start(bf16[1,2,64,1152]{3,2,1,0:T(8,128)(2,1)} %param.5) | copy-start | bytes 884740
  107.5 37.6 %collective-permute-start.1 = (bf16[1152,1152]{1,0:T(8,128)(2,1)S(1)}, bf16[1152,1152]{1,0:T(8,128)(2,1)S(1)}, u32[]{:S(2)}, u32[]{:S(2)}) collective-permute-start(bf16[1152,1152]{1,0:T(8,128)(2,1)S(1)} %get-tuple-element.25.mine_ref), channel_id=1, source_target_pairs={{0,1},{1,0},{2,3},{3,2},{4,5},{5,4},{6,7},{7,6},{8,9},{9,8},{10,11... | collective-permute-start | bytes 7962632 | tf_op jit(solution)/shard_map/ppermute | solution.py:338
  111.9 13.0 %collective-permute-start = (bf16[320,1152]{1,0:T(8,128)(2,1)S(1)}, bf16[320,1152]{1,0:T(8,128)(2,1)S(1)}, u32[]{:S(2)}, u32[]{:S(2)}) collective-permute-start(bf16[320,1152]{1,0:T(8,128)(2,1)S(1)} %bitcast.18), channel_id=1, source_target_pairs={{0,1},{1,0},{2,3},{3,2},{4,5},{5,4},{6,7},{7,6},{8,9},{9,8},{10,11... | collective-permute-start | bytes 2211848 | tf_op jit(solution)/shard_map/ppermute | solution.py:338
  151.7 9.5 %collective-permute-start.4 = (bf16[1152,1152]{1,0:T(8,128)(2,1)S(1)}, bf16[1152,1152]{1,0:T(8,128)(2,1)S(1)}, u32[]{:S(2)}, u32[]{:S(2)}) collective-permute-start(bf16[1152,1152]{1,0:T(8,128)(2,1)S(1)} %get-tuple-element.37), channel_id=1, source_target_pairs={{0,1},{1,0},{2,3},{3,2},{4,5},{5,4},{6,7},{7,6},{8,9},{9,8},{10,11... | collective-permute-start | bytes 7962632 | tf_op jit(solution)/shard_map/ppermute | solution.py:338
  176.9 14.7 %copy-start.9 = (bf16[128,1152]{1,0:T(8,128)(2,1)}, bf16[128,1152]{1,0:T(8,128)(2,1)S(1)}, u32[]{:S(2)}) copy-start(bf16[128,1152]{1,0:T(8,128)(2,1)S(1)} %get-tuple-element.33.refs_2_) | copy-start | bytes 884740
  176.9 14.7 %collective-permute-start.2 = (bf16[8,40,1152]{2,1,0:T(8,128)(2,1)S(1)}, bf16[8,40,1152]{2,1,0:T(8,128)(2,1)S(1)}, u32[]{:S(2)}, u32[]{:S(2)}) collective-permute-start(bf16[8,40,1152]{2,1,0:T(8,128)(2,1)S(1)} %get-tuple-element.31), channel_id=1, source_target_pairs={{0,1},{1,0},{2,3},{3,2},{4,5},{5,4},{6,7},{7,6},{8,9},{9,8},{10,11... | collective-permute-start | bytes 2211848 | tf_op jit(solution)/shard_map/ppermute | solution.py:338
  198.3 1.7 copy-start.1
  200.0 0.7 copy-start.11
  200.7 0.7 copy-start.15
  201.4 58.2 %all-to-all-start.5 = ((bf16[8,176,1152]{2,1,0:T(8,128)(2,1)}), bf16[8,176,1152]{2,1,0:T(8,128)(2,1)S(1)}, u32[]{:S(2)}, u32[]{:S(2)}) async-start(bf16[8,176,1152]{2,1,0:T(8,128)(2,1)} %copy-done.1), calls=%async_computation.5 | async-start | bytes 6488064 | tf_op jit(solution)/shard_map/all_to_all | solution.py:330
  206.5 4.9 %collective-permute-start.3 = (bf16[112,1152]{1,0:T(8,128)(2,1)}, bf16[112,1152]{1,0:T(8,128)(2,1)S(1)}, u32[]{:S(2)}, u32[]{:S(2)}) collective-permute-start(bf16[112,1152]{1,0:T(8,128)(2,1)} %copy-done.15), channel_id=1, source_target_pairs={{0,1},{1,0},{2,3},{3,2},{4,5},{5,4},{6,7},{7,6},{8,9},{9,8},{10,11... | collective-permute-start | bytes 774152 | tf_op jit(solution)/shard_map/ppermute | solution.py:338
  259.5 1.0 copy-start.7
  260.5 1.0 copy-start.10
  261.5 0.9 copy-start.12
  262.4 0.9 copy-start.14
  347.0 6.2 %collective-permute-start.5 = (bf16[320,1152]{1,0:T(8,128)(2,1)S(1)}, bf16[320,1152]{1,0:T(8,128)(2,1)S(1)}, u32[]{:S(2)}, u32[]{:S(2)}) collective-permute-start(bf16[320,1152]{1,0:T(8,128)(2,1)S(1)} %bitcast.21), channel_id=1, source_target_pairs={{0,1},{1,0},{2,3},{3,2},{4,5},{5,4},{6,7},{7,6},{8,9},{9,8},{10,11... | collective-permute-start | bytes 2211848 | tf_op jit(solution)/shard_map/ppermute | solution.py:338
  (1 other events, 0.7 us)
Sparse Core Ops, SparseCore 0:
  163.6 51.1 reduce-scatter.1

commit v7 on v6

--- a/solution.py
+++ b/solution.py
@@ -48,17 +48,17 @@
     )
 
 
-def norm_kernel(at_ref, x_ref, wq_ref, wo_ref, out_ref):
+def norm_kernel(at_ref, x_ref, wq_ref, wo_ref, out_ref, own_ref):
     core = at_ref[0]
     wide = wo_ref[0].astype(F32)
     half = jnp.where(core == 0, wide[:40], wide[32:])
+    hidden = normalize(x_ref[...])[0]
+    block = jnp.concatenate([hidden, half], axis=0).astype(BF)
+    for j in range(8):
+        out_ref[j] = block
     qk = jnp.concatenate([wq_ref[1, 0].astype(F32), wq_ref[1, 1].astype(F32)], axis=0)
     vo = jnp.concatenate([wq_ref[1, 2].astype(F32), wo_ref[1].astype(F32)], axis=0)
-    hidden = normalize(x_ref[...])[0]
-    block = [hidden, jnp.where(core == 0, qk, vo), half, jnp.zeros_like(half[:8])]
-    block = jnp.concatenate(block, axis=0).astype(BF)
-    for j in range(8):
-        out_ref[j] = block
+    own_ref[...] = jnp.where(core == 0, qk, vo).astype(BF)
 
 
 def frame_rows(hidden_ref, f):
@@ -74,10 +74,9 @@
     return tuple(stacked[i * E : (i + 1) * E].astype(BF) for i in range(3))
 
 
-def spatial_kernel(hidden_ref, w_ref, heads_ref, qkv_ref, one_ref, two_ref):
+def spatial_kernel(hidden_ref, w_ref, heads_ref, qkv_ref, one_ref):
     for h in range(8):
-        two_ref[h * 2 * E : (h + 1) * 2 * E] = hidden_ref[h, 128 : 128 + 2 * E]
-        one_ref[h] = hidden_ref[h, 272:320].astype(F32)[:40].astype(BF)
+        one_ref[h] = hidden_ref[h].astype(F32)[128:].astype(BF)
     outs = []
     for f in range(2):
         qkv = nt(w_ref[...], frame_rows(hidden_ref, f))
@@ -93,7 +92,7 @@
 
 
 def middle_kernel(
-    core_ref, x_ref, g_ref, heads_ref, mine_ref, other_ref, out_ref, split_ref
+    core_ref, x_ref, g_ref, heads_ref, mine_ref, other_ref, pass_ref, out_ref, same_ref, split_ref
 ):
     core = core_ref[0]
     for h in range(8):
@@ -198,8 +197,8 @@
 
 
 def turn_kernel(
-    core_ref, back_ref, heads_ref, mine_ref, other_ref,
-    gh_ref, keep_ref, send_ref, out_ref, grad_ref, split_ref,
+    core_ref, back_ref, heads_ref, mine_ref, other_ref, two_ref, recv_ref,
+    gh_ref, keep_ref, send_ref, out_ref, grad_ref, sum_ref, split_ref,
 ):
     core = core_ref[0]
     out_ref[...] = local_rows(back_ref, 0)
@@ -214,6 +213,8 @@
         low, high = halves(nn(heads_ref[h], grad), 40)
         keep_ref[h] = jnp.where(core == 0, low, high).astype(BF)
         send_ref[h] = jnp.where(core == 0, high, low).astype(BF)
+        span = slice(h * 2 * E, (h + 1) * 2 * E)
+        sum_ref[span] = (two_ref[span].astype(F32) + recv_ref[span].astype(F32)).astype(BF)
 
 
 def spatial_back_kernel(
@@ -382,27 +383,31 @@
     g = cotangent.reshape(128, depth)
     w_own = w_qkv[0].reshape(3 * E, depth)
 
-    hidden = call(
-        norm_kernel, shape(8, 320, depth),
+    hidden, own = call(
+        norm_kernel, (shape(8, 168, depth), shape(2 * E, depth)),
         at, x, w_qkv.reshape(2, 3, E, depth), w_out.reshape(2, E, depth),
         in_specs=[SMEM] + [VMEM] * 3, fetch=True,
     )
+    mine_two = lax.all_gather(own, "head", axis_index_groups=RING).reshape(16 * E, depth)
     hidden = over_head(hidden)
-    big = shape(16 * E, depth)
-    heads, qkv, mine_one, mine_two = call(
+    heads, qkv, mine_one = call(
         spatial_kernel,
-        (shape(8, E, 128), shape(2, 3 * E, 512), shape(8, 40, depth), big), hidden, w_own, mib=32,
+        (shape(8, E, 128), shape(2, 3 * E, 512), shape(8, 40, depth)), hidden, w_own,
     )
     heads = over_head(heads)
     mine_one = mine_one.reshape(320, depth)
     other_one = swap_cores(mine_one, n_dp)
+    big = shape(16 * E, depth)
+    pair, mine_two = call(
+        middle_kernel, (shape(2, 2, 2, 32, depth), big),
+        at, x, g, heads, mine_one, other_one, mine_two,
+        in_specs=[SMEM] + [VMEM] * 5 + [ANY], fetch=True,
+        out_specs=(VMEM, ANY),
+        input_output_aliases={6: 1},
+        scratch_shapes=[pltpu.VMEM((2, 320, 128), F32)],
+    )
+    pair = over_seq(pair)
     other_two = swap_cores(mine_two, n_dp)
-    pair = call(
-        middle_kernel, shape(2, 2, 2, 32, depth), at, x, g, heads, mine_one, other_one,
-        in_specs=[SMEM] + [VMEM] * 5, fetch=True,
-        scratch_shapes=[pltpu.VMEM((2, 320, 128), F32)],
-    )
-    pair = over_seq(pair)
     back, keep, send = call(
         temporal_kernel,
         (shape(2, 2, 2, 32, depth), big, big),
@@ -421,17 +426,16 @@
         mib=40,
     )
     back = over_seq(back)
-    two = (keep.astype(F32) + swap_cores(send, n_dp).astype(F32)).astype(BF)
+    half = shape(8, 40, depth)
+    gh, keep, send, output, grad_one, two = call(
+        turn_kernel,
+        (shape(8, E, 128), half, half, shape(128, depth), shape(128, depth), big),
+        at, back, heads, mine_one, other_one, keep, swap_cores(send, n_dp),
+        in_specs=[SMEM] + [VMEM] * 6, fetch=True,
+        scratch_shapes=[pltpu.VMEM((2, 320, 128), F32)],
+    )
     two = lax.psum_scatter(
         two, "head", scatter_dimension=0, tiled=True, axis_index_groups=RING
-    )
-    half = shape(8, 40, depth)
-    gh, keep, send, output, grad_one = call(
-        turn_kernel,
-        (shape(8, E, 128), half, half, shape(128, depth), shape(128, depth)),
-        at, back, heads, mine_one, other_one,
-        in_specs=[SMEM] + [VMEM] * 4, fetch=True,
-        scratch_shapes=[pltpu.VMEM((2, 320, 128), F32)],
     )
     gh = over_head(gh)
     half = shape(112, depth)

time: 363 us -> 345 us (0.950)
  waiting for transfers between devices: 136 us -> 100 us
  local copies, waits for them, and re-layouts: 13.4 us -> 33.8 us
    all_to_all x2, waiting for transfers between devices: 129 us -> 97 us  [over_head(): lax.all_to_all(blocks, 'head', 0, 0, tiled=True, axis_index_groups=RING)]
    unnamed x32 -> x68, local copies, waits for them, and re-layouts: 13.3 us -> 31.9 us
    ppermute x6, waiting for transfers between devices: 7.73 us -> 3.17 us  [swap_cores(): return lax.ppermute(value, 'dp', [(i, i ^ bit) for i in range(n_dp)])]
  transfers between devices with their start and end apart: 9 -> 10, of which waited for: 5 -> 4; matrix products, arithmetic and copies ran while one was open for 0% -> 1% of each run, Pallas kernels for 3% -> 2%
where the time goes in v7:
time: 345 us; the launch traced here: 342 us
  blocking collectives  131 us (38%)
  waiting for transfers between devices  100 us (29%)
  starting transfers between devices  37.5 us (11%)
  local copies, waits for them, and re-layouts  33.8 us (10%)
  Pallas kernels  25.1 us (7%)
  between operations  14.3 us (4%)
    all_to_all x2, waiting for transfers between devices, over_head(): lax.all_to_all(blocks, 'head', 0, 0, tiled=True, axis_index_groups=RING)  97 us
    unnamed x68, local copies, waits for them, and re-layouts  31.9 us
    all_to_all x1, blocking collectives, sum_far(): lax.all_to_all(copies, 'dp', 0, 0, tiled=True, axis_index_groups=far)  30.9 us
    all_to_all x2, blocking collectives, over_seq(): return lax.all_to_all(blocks, 'seq', 0, 0, tiled=True)  28.1 us
    all_to_all x1, blocking collectives, spread(): lax.all_to_all(copies, ('seq', 'dp'), 0, 0, tiled=True, axis_index_groups...  25.6 us
    ppermute x6, starting transfers between devices, swap_cores(): return lax.ppermute(value, 'dp', [(i, i ^ bit) for i in range(n_dp)])  25.5 us
    pallas_call x8, Pallas kernels, call(): pl.pallas_call(fetching if moved else kernel, out_shape=outs, in_specs=sp...  25.1 us
    all_to_all x1, blocking collectives, sum_near(): lax.all_to_all(grads, ('seq', 'dp'), 0, 0, tiled=True, axis_index_groups=...  23.1 us
  transfers between devices with their start and end apart: 10, of which 4 were waited for; matrix products, arithmetic and copies ran while one was open for 1% of the time, Pallas kernels for 2%

profile of v7, /device:TPU:7, one launch (start us, length us, event | category | flops | bytes accessed | tf_op | source)
XLA Modules:
  0.0 341.8 jit_solution(10650769585197055722)
XLA Ops:
  13.8 6.9 %all-to-all-start = ((bf16[8,168,1152]{2,1,0:T(8,128)(2,1)}), bf16[8,168,1152]{2,1,0:T(8,128)(2,1)S(1)}, u32[]{:S(2)}, u32[]{:S(2)}) async-start(bf16[8,168,1152]{2,1,0:T(8,128)(2,1)} %copy-done.6), calls=%async_computation | async-start | bytes 6193152 | tf_op jit(solution)/shard_map/all_to_all | solution.py:331
  20.7 1.9 slice.3
  22.6 41.8 %all-to-all-done.hidden_ref = bf16[8,168,1152]{2,1,0:T(8,128)(2,1)S(1)} async-done(((bf16[8,168,1152]{2,1,0:T(8,128)(2,1)}), bf16[8,168,1152]{2,1,0:T(8,128)(2,1)S(1)}, u32[]{:S(2)}, u32[]{:S(2)}) %all-to-all-start) | async-done | bytes 3096608 | tf_op jit(solution)/shard_map/all_to_all | solution.py:331
  65.4 2.3 shard_map.76
  68.5 8.2 %collective-permute-start = (bf16[320,1152]{1,0:T(8,128)(2,1)S(1)}, bf16[320,1152]{1,0:T(8,128)(2,1)S(1)}, u32[]{:S(2)}, u32[]{:S(2)}) collective-permute-start(bf16[320,1152]{1,0:T(8,128)(2,1)S(1)} %bitcast.18), channel_id=1, source_target_pairs={{0,1},{1,0},{2,3},{3,2},{4,5},{5,4},{6,7},{7,6},{8,9},{9,8},{10,11... | collective-permute-start | bytes 2211848 | tf_op jit(solution)/shard_map/ppermute | solution.py:339
  77.5 13.0 %all_to_all.45.refs_3_.refs_2_ = bf16[8,72,128]{2,1,0:T(8,128)(2,1)S(1)} all-to-all(bf16[8,72,128]{2,1,0:T(8,128)(2,1)S(1)} %get-tuple-element.28), channel_id=1, replica_groups={{0,64,128,192,224,160,96,32},{1,65,129,193,225,161,97,33},{2,66,130,194..., dimensions={0} | all-to-all | bytes 294912 | tf_op jit(solution)/shard_map/all_to_all | solution.py:331
  97.9 3.4 collective-permute-start.1
  102.8 16.8 %all_to_all.46.pair_ref = bf16[2,2,2,32,1152]{4,3,2,1,0:T(8,128)(2,1)S(1)} all-to-all(bf16[2,2,2,32,1152]{4,3,2,1,0:T(8,128)(2,1)S(1)} %get-tuple-element.31), channel_id=1, replica_groups=mesh['seq'=2,'head'=8,'dp'=32] {'seq'}, dimensions={0} | all-to-all | bytes 1179648 | tf_op jit(solution)/shard_map/all_to_all | solution.py:335
  121.3 6.6 %shard_map.78 = (bf16[2,2,2,32,1152]{4,3,2,1,0:T(8,128)(2,1)S(1)}, bf16[1152,1152]{1,0:T(8,128)(2,1)S(1)}, bf16[1152,1152]{1,0:T(8,128)(2,1)S(1)}) custom-call(s32[1]{0:T(128)} %bitcast.refs_0_.core_ref, bf16[2,2,2,32,1152]{4,3,2,1,0:T(8,128)(2,1)S(1)} %all_to_all.46.pair_ref, bf16[1152,1152]{1,0:T(8,128)(2,1)S(1)} %copy-done.2, ...), custom_call_target="tpu_custom_call" | custom-call | tf_op jit(solution)/shard_map/pallas_call | solution.py:318
  127.9 3.0 collective-permute-start.2
  130.9 11.3 %all_to_all.47.refs_1_ = bf16[2,2,2,32,1152]{4,3,2,1,0:T(8,128)(2,1)S(1)} all-to-all(bf16[2,2,2,32,1152]{4,3,2,1,0:T(8,128)(2,1)S(1)} %get-tuple-element.33), channel_id=1, replica_groups=mesh['seq'=2,'head'=8,'dp'=32] {'seq'}, dimensions={0} | all-to-all | bytes 1179648 | tf_op jit(solution)/shard_map/all_to_all | solution.py:335
  142.2 4.3 %shard_map.79 = (bf16[8,72,128]{2,1,0:T(8,128)(2,1)S(1)}, bf16[8,40,1152]{2,1,0:T(8,128)(2,1)S(1)}, bf16[8,40,1152]{2,1,0:T(8,128)(2,1)S(1)}, bf16[128,1152]{1,0...) custom-call(s32[1]{0:T(128)} %bitcast.refs_0_.core_ref, ...), custom_call_target="tpu_custom_call" | custom-call | tf_op jit(solution)/shard_map/pallas_call | solution.py:318
  151.1 2.8 collective-permute-start.3
  154.0 10.1 %all_to_all.48.gh_ref = bf16[8,72,128]{2,1,0:T(8,128)(2,1)S(1)} all-to-all(bf16[8,72,128]{2,1,0:T(8,128)(2,1)S(1)} %copy-done.31), channel_id=1, replica_groups={{0,64,128,192,224,160,96,32},{1,65,129,193,225,161,97,33},{2,66,130,194..., dimensions={0} | all-to-all | bytes 294912 | tf_op jit(solution)/shard_map/all_to_all | solution.py:331
  167.2 3.9 %shard_map.80 = (bf16[8,176,1152]{2,1,0:T(8,128)(2,1)S(1)}, bf16[112,1152]{1,0:T(8,128)(2,1)S(1)}, bf16[112,1152]{1,0:T(8,128)(2,1)S(1)}) custom-call(s32[1]{0:T(128)} %bitcast.refs_0_.core_ref, bf16[2,216,512]{2,1,0:T(8,128)(2,1)S(1)} %copy-done.20, bf16[8,72,128]{2,1,0:T(8,128)(2,1)S(1)} %all_to_all.48.gh_ref, ...), custom_call_target="tpu_custom_call" | custom-call | tf_op jit(solution)/shard_map/pallas_call | solution.py:318
  174.2 5.2 %all-to-all-start.5 = ((bf16[8,176,1152]{2,1,0:T(8,128)(2,1)}), bf16[8,176,1152]{2,1,0:T(8,128)(2,1)S(1)}, u32[]{:S(2)}, u32[]{:S(2)}) async-start(bf16[8,176,1152]{2,1,0:T(8,128)(2,1)} %copy-done.5), calls=%async_computation.5 | async-start | bytes 6488064 | tf_op jit(solution)/shard_map/all_to_all | solution.py:331
  179.4 3.7 %collective-permute-start.4 = (bf16[112,1152]{1,0:T(8,128)(2,1)}, bf16[112,1152]{1,0:T(8,128)(2,1)S(1)}, u32[]{:S(2)}, u32[]{:S(2)}) collective-permute-start(bf16[112,1152]{1,0:T(8,128)(2,1)} %copy-done.33), channel_id=1, source_target_pairs={{0,1},{1,0},{2,3},{3,2},{4,5},{5,4},{6,7},{7,6},{8,9},{9,8},{10,11... | collective-permute-start | bytes 774152 | tf_op jit(solution)/shard_map/ppermute | solution.py:339
  185.1 55.2 %all-to-all-done.5.refs_0_ = bf16[8,176,1152]{2,1,0:T(8,128)(2,1)S(1)} async-done(((bf16[8,176,1152]{2,1,0:T(8,128)(2,1)}), bf16[8,176,1152]{2,1,0:T(8,128)(2,1)S(1)}, u32[]{:S(2)}, u32[]{:S(2)}) %all-to-all-start.5) | async-done | bytes 3244064 | tf_op jit(solution)/shard_map/all_to_all | solution.py:331
  244.2 2.9 shard_map.81
  247.1 23.1 %all_to_all.49 = bf16[8,40,1152]{2,1,0:T(8,128)(2,1)S(1)} all-to-all(bf16[8,40,1152]{2,1,0:T(8,128)(2,1)S(1)} %get-tuple-element.47), channel_id=1, replica_groups={{0,2,4,6,256,258,260,262},{1,3,5,7,257,259,261,263},{8,10,12,14,264,266..., dimensions={0} | all-to-all | bytes 1474560 | tf_op jit(solution)/shard_map/all_to_all | solution.py:358
  270.4 30.9 %all_to_all.50 = bf16[4,40,1152]{2,1,0:T(8,128)(2,1)S(1)} all-to-all(bf16[4,40,1152]{2,1,0:T(8,128)(2,1)S(1)} %broadcast_in_dim.8), channel_id=1, replica_groups={{0,8,16,24},{1,9,17,25},{2,10,18,26},{3,11,19,27},{4,12,20,28},{5,13,21..., dimensions={0} | all-to-all | bytes 737280 | tf_op jit(solution)/shard_map/all_to_all | solution.py:366
  301.3 25.6 %all_to_all.51 = bf16[8,40,1152]{2,1,0:T(8,128)(2,1)S(1)} all-to-all(bf16[8,40,1152]{2,1,0:T(8,128)(2,1)S(1)} %broadcast_in_dim.9), channel_id=1, replica_groups={{0,2,4,6,256,258,260,262},{1,3,5,7,257,259,261,263},{8,10,12,14,264,266..., dimensions={0} | all-to-all | bytes 1474560 | tf_op jit(solution)/shard_map/all_to_all | solution.py:372
  327.0 4.4 %collective-permute-start.5 = (bf16[320,1152]{1,0:T(8,128)(2,1)S(1)}, bf16[320,1152]{1,0:T(8,128)(2,1)S(1)}, u32[]{:S(2)}, u32[]{:S(2)}) collective-permute-start(bf16[320,1152]{1,0:T(8,128)(2,1)S(1)} %bitcast.21), channel_id=1, source_target_pairs={{0,1},{1,0},{2,3},{3,2},{4,5},{5,4},{6,7},{7,6},{8,9},{9,8},{10,11... | collective-permute-start | bytes 2211848 | tf_op jit(solution)/shard_map/ppermute | solution.py:339
  333.2 1.8 shard_map.82
  (86 shorter events, 38.7 us)
Async XLA Ops:
  7.2 84.2 %all-gather.3.cloned.1.call-start = ((), (), s32[]{:S(2)}) async-start(), calls=%async_computation.11 | async-start | bytes 2985984 | tf_op jit(solution)/shard_map/all_gather | solution.py:391
  8.2 1.2 copy-start.16
  12.2 1.7 copy-start.6
  13.8 50.5 %all-to-all-start = ((bf16[8,168,1152]{2,1,0:T(8,128)(2,1)}), bf16[8,168,1152]{2,1,0:T(8,128)(2,1)S(1)}, u32[]{:S(2)}, u32[]{:S(2)}) async-start(bf16[8,168,1152]{2,1,0:T(8,128)(2,1)} %copy-done.6), calls=%async_computation | async-start | bytes 6193152 | tf_op jit(solution)/shard_map/all_to_all | solution.py:331
  20.7 70.7 %copy-start.15 = (bf16[1,2,64,1152]{3,2,1,0:T(8,128)(2,1)S(1)}, bf16[1,2,64,1152]{3,2,1,0:T(8,128)(2,1)}, u32[]{:S(2)}) copy-start(bf16[1,2,64,1152]{3,2,1,0:T(8,128)(2,1)} %param.4) | copy-start | bytes 884740
  20.7 219.6 %reduce-scatter.2.cloned.1.call-start = ((), (), s32[]{:S(2)}) async-start(), calls=%async_computation.10 | async-start | bytes 2985984 | tf_op jit(solution)/shard_map/reduce_scatter | solution.py:437
  68.5 22.1 %collective-permute-start = (bf16[320,1152]{1,0:T(8,128)(2,1)S(1)}, bf16[320,1152]{1,0:T(8,128)(2,1)S(1)}, u32[]{:S(2)}, u32[]{:S(2)}) collective-permute-start(bf16[320,1152]{1,0:T(8,128)(2,1)S(1)} %bitcast.18), channel_id=1, source_target_pairs={{0,1},{1,0},{2,3},{3,2},{4,5},{5,4},{6,7},{7,6},{8,9},{9,8},{10,11... | collective-permute-start | bytes 2211848 | tf_op jit(solution)/shard_map/ppermute | solution.py:339
  91.4 1.8 copy-start
  93.2 1.1 copy-start.8
  94.3 1.1 copy-start.11
  97.9 21.7 %collective-permute-start.1 = (bf16[1152,1152]{1,0:T(8,128)(2,1)S(1)}, bf16[1152,1152]{1,0:T(8,128)(2,1)S(1)}, u32[]{:S(2)}, u32[]{:S(2)}) collective-permute-start(bf16[1152,1152]{1,0:T(8,128)(2,1)S(1)} %get-tuple-element.32.mine_ref), channel_id=1, source_target_pairs={{0,1},{1,0},{2,3},{3,2},{4,5},{5,4},{6,7},{7,6},{8,9},{9,8},{10,11... | collective-permute-start | bytes 7962632 | tf_op jit(solution)/shard_map/ppermute | solution.py:339
  101.3 1.5 copy-start.1
  119.6 1.8 copy-start.2
  121.3 20.9 %copy-start.9 = (bf16[8,40,1152]{2,1,0:T(8,128)(2,1)S(1)}, bf16[8,40,1152]{2,1,0:T(8,128)(2,1)}, u32[]{:S(2)}) copy-start(bf16[8,40,1152]{2,1,0:T(8,128)(2,1)} %copy-done.7) | copy-start | bytes 2211844
  121.3 20.9 %copy-start.12 = (bf16[320,1152]{1,0:T(8,128)(2,1)S(1)}, bf16[320,1152]{1,0:T(8,128)(2,1)}, u32[]{:S(2)}) copy-start(bf16[320,1152]{1,0:T(8,128)(2,1)} %copy-done.10) | copy-start | bytes 2211844
  127.9 14.3 %collective-permute-start.2 = (bf16[1152,1152]{1,0:T(8,128)(2,1)S(1)}, bf16[1152,1152]{1,0:T(8,128)(2,1)S(1)}, u32[]{:S(2)}, u32[]{:S(2)}) collective-permute-start(bf16[1152,1152]{1,0:T(8,128)(2,1)S(1)} %get-tuple-element.35), channel_id=1, source_target_pairs={{0,1},{1,0},{2,3},{3,2},{4,5},{5,4},{6,7},{7,6},{8,9},{9,8},{10,11... | collective-permute-start | bytes 7962632 | tf_op jit(solution)/shard_map/ppermute | solution.py:339
  146.5 1.5 copy-start.13
  151.1 2.9 copy-start.31
  151.1 12.9 %collective-permute-start.3 = (bf16[8,40,1152]{2,1,0:T(8,128)(2,1)}, bf16[8,40,1152]{2,1,0:T(8,128)(2,1)S(1)}, u32[]{:S(2)}, u32[]{:S(2)}) collective-permute-start(bf16[8,40,1152]{2,1,0:T(8,128)(2,1)} %copy-done.32), channel_id=1, source_target_pairs={{0,1},{1,0},{2,3},{3,2},{4,5},{5,4},{6,7},{7,6},{8,9},{9,8},{10,11... | collective-permute-start | bytes 2211848 | tf_op jit(solution)/shard_map/ppermute | solution.py:339
  165.1 1.1 copy-start.18
  171.1 1.7 copy-start.5
  174.2 66.1 %all-to-all-start.5 = ((bf16[8,176,1152]{2,1,0:T(8,128)(2,1)}), bf16[8,176,1152]{2,1,0:T(8,128)(2,1)S(1)}, u32[]{:S(2)}, u32[]{:S(2)}) async-start(bf16[8,176,1152]{2,1,0:T(8,128)(2,1)} %copy-done.5), calls=%async_computation.5 | async-start | bytes 6488064 | tf_op jit(solution)/shard_map/all_to_all | solution.py:331
  179.4 5.1 %collective-permute-start.4 = (bf16[112,1152]{1,0:T(8,128)(2,1)}, bf16[112,1152]{1,0:T(8,128)(2,1)S(1)}, u32[]{:S(2)}, u32[]{:S(2)}) collective-permute-start(bf16[112,1152]{1,0:T(8,128)(2,1)} %copy-done.33), channel_id=1, source_target_pairs={{0,1},{1,0},{2,3},{3,2},{4,5},{5,4},{6,7},{7,6},{8,9},{9,8},{10,11... | collective-permute-start | bytes 774152 | tf_op jit(solution)/shard_map/ppermute | solution.py:339
  327.0 6.2 %collective-permute-start.5 = (bf16[320,1152]{1,0:T(8,128)(2,1)S(1)}, bf16[320,1152]{1,0:T(8,128)(2,1)S(1)}, u32[]{:S(2)}, u32[]{:S(2)}) collective-permute-start(bf16[320,1152]{1,0:T(8,128)(2,1)S(1)} %bitcast.21), channel_id=1, source_target_pairs={{0,1},{1,0},{2,3},{3,2},{4,5},{5,4},{6,7},{7,6},{8,9},{9,8},{10,11... | collective-permute-start | bytes 2211848 | tf_op jit(solution)/shard_map/ppermute | solution.py:339
  (20 other events, 17.5 us)
Sparse Core Ops, SparseCore 0:
  14.0 73.7 all-gather.2
  151.2 88.4 reduce-scatter.1

commit v8 on v5

--- a/solution.py
+++ b/solution.py
@@ -48,17 +48,17 @@
     )
 
 
-def norm_kernel(at_ref, x_ref, wq_ref, wo_ref, out_ref, own_ref, parts_ref):
+def norm_kernel(at_ref, x_ref, wq_ref, wo_ref, out_ref, parts_ref):
     wide = wo_ref[0].astype(F32)
     half = jnp.where(at_ref[0] == 0, wide[:40], wide[32:])
-    hidden = normalize(x_ref[...])[0]
-    block = jnp.concatenate([hidden, half], axis=0).astype(BF)
-    for j in range(8):
-        out_ref[j] = block
     for i in range(3):
         parts_ref[i] = wq_ref[1, i].astype(F32)
     parts_ref[3] = wo_ref[1].astype(F32)
-    own_ref[...] = parts_ref[2 * at_ref[0] + at_ref[1]].astype(BF)
+    part = parts_ref[2 * at_ref[0] + at_ref[1]]
+    hidden = normalize(x_ref[...])[0]
+    block = jnp.concatenate([hidden, part, half], axis=0).astype(BF)
+    for j in range(8):
+        out_ref[j] = block
 
 
 def frame_rows(hidden_ref, f):
@@ -74,9 +74,11 @@
     return tuple(stacked[i * E : (i + 1) * E].astype(BF) for i in range(3))
 
 
-def spatial_kernel(hidden_ref, w_ref, heads_ref, qkv_ref, one_ref):
+def spatial_kernel(hidden_ref, w_ref, heads_ref, qkv_ref, two_ref, one_ref):
     for h in range(8):
-        one_ref[h] = hidden_ref[h].astype(F32)[128:].astype(BF)
+        both = hidden_ref[h, 128:240].astype(F32)
+        two_ref[h] = both[:E].astype(BF)
+        one_ref[h] = both[E:].astype(BF)
     outs = []
     for f in range(2):
         qkv = nt(w_ref[...], frame_rows(hidden_ref, f))
@@ -285,12 +287,38 @@
     return jax.ShapeDtypeStruct(dims, BF)
 
 
-def call(kernel, outs, *args, mib=24, **more):
+def call(kernel, outs, *args, mib=24, fetch=False, in_specs=None, scratch_shapes=(), **more):
+    specs = list(in_specs or [VMEM] * len(args))
+    scratch = list(scratch_shapes)
+    moved = [i for i, spec in enumerate(specs) if spec is VMEM] if fetch else []
+    n_in, n_out, n_own = len(args), len(jax.tree.leaves(outs)), len(scratch)
+
+    def fetching(*refs):
+        ins = list(refs[:n_in])
+        rest = refs[n_in : n_in + n_out + n_own]
+        held, sems = refs[n_in + n_out + n_own : -1], refs[-1]
+        copies = [
+            pltpu.make_async_copy(ins[i], to, sems.at[k])
+            for k, (i, to) in enumerate(zip(moved, held))
+        ]
+        for copy in copies:
+            copy.start()
+        for copy in copies:
+            copy.wait()
+        for i, to in zip(moved, held):
+            ins[i] = to
+        kernel(*ins, *rest)
+
+    if moved:
+        scratch += [pltpu.VMEM(args[i].shape, args[i].dtype) for i in moved]
+        scratch.append(pltpu.SemaphoreType.DMA((len(moved),)))
+        specs = [ANY if i in moved else spec for i, spec in enumerate(specs)]
     return pl.pallas_call(
-        kernel,
+        fetching if moved else kernel,
         out_shape=outs,
-        in_specs=more.pop("in_specs", [VMEM] * len(args)),
+        in_specs=specs,
         out_specs=more.pop("out_specs", jax.tree.map(lambda _: VMEM, outs)),
+        scratch_shapes=scratch,
         compiler_params=pltpu.CompilerParams(vmem_limit_bytes=mib * MIB),
         cost_estimate=pl.CostEstimate(flops=0, bytes_accessed=0, transcendentals=0),
         **more,
@@ -354,18 +382,19 @@
     g = cotangent.reshape(128, depth)
     w_own = w_qkv[0].reshape(3 * E, depth)
 
-    hidden, own = call(
-        norm_kernel, (shape(8, 168, depth), shape(E, depth)),
+    hidden = call(
+        norm_kernel, shape(8, 240, depth),
         at, x, w_qkv.reshape(2, 3, E, depth), w_out.reshape(2, E, depth),
-        in_specs=[SMEM] + [VMEM] * 3,
+        in_specs=[SMEM] + [VMEM] * 3, fetch=True,
         scratch_shapes=[pltpu.VMEM((4, E, depth), F32)],
     )
-    own = lax.all_gather(own, "head", axis_index_groups=RING).reshape(8 * E, depth)
     hidden = over_head(hidden)
-    heads, qkv, mine_one = call(
+    heads, qkv, own, mine_one = call(
         spatial_kernel,
-        (shape(8, E, 128), shape(2, 3 * E, 512), shape(8, 40, depth)), hidden, w_own,
-    )
+        (shape(8, E, 128), shape(2, 3 * E, 512), shape(8, E, depth), shape(8, 40, depth)),
+        hidden, w_own,
+    )
+    own = own.reshape(8 * E, depth)
     heads = over_head(heads)
     mine_one = mine_one.reshape(320, depth)
     other_one = swap_cores(mine_one, n_dp)
@@ -375,7 +404,7 @@
     pair, from_z = call(
         middle_kernel, (shape(2, 2, 2, 32, depth), shape(8 * E, depth)),
         at, x, g, heads, mine_one, other_one, from_z,
-        in_specs=[SMEM] + [VMEM] * 5 + [ANY],
+        in_specs=[SMEM] + [VMEM] * 5 + [ANY], fetch=True,
         out_specs=(VMEM, ANY),
         input_output_aliases={6: 1},
         scratch_shapes=[pltpu.VMEM((2, 320, 128), F32)],
@@ -407,7 +436,7 @@
         turn_kernel,
         (shape(8, E, 128), half, half, shape(128, depth), shape(128, depth)),
         at, back, heads, mine_one, other_one,
-        in_specs=[SMEM] + [VMEM] * 4,
+        in_specs=[SMEM] + [VMEM] * 4, fetch=True,
         scratch_shapes=[pltpu.VMEM((2, 320, 128), F32)],
     )
     gh = over_head(gh)
@@ -415,13 +444,13 @@
     terms, keep, send = call(
         spatial_back_kernel, (shape(8, 176, depth), half, half),
         at, qkv, gh, hidden, w_own, keep, swap_cores(send, n_dp),
-        in_specs=[SMEM] + [VMEM] * 6,
+        in_specs=[SMEM] + [VMEM] * 6, mib=32,
     )
     n_near = len(near[0])
     latent_grads, chain = call(
         last_kernel, (shape(128, depth), shape(n_near, 320 // n_near, depth)),
         over_head(terms), x, grad_one, keep, swap_cores(send, n_dp), two,
-        scratch_shapes=[pltpu.VMEM((320, depth), F32)],
+        scratch_shapes=[pltpu.VMEM((320, depth), F32)], fetch=True,
     )
     part = sum_near(chain, near)
     mine = spread(sum_far(part, far), near)

time: 357 us -> 366 us (1.025)
  waiting for transfers between devices: 132 us -> 139 us
  Pallas kernels: 26.6 us -> 32.6 us
  starting transfers between devices: 53.5 us -> 58.7 us
  blocking collectives: 103 us -> 98.5 us
    all_gather x1 -> x0, waiting for transfers between devices: 61.8 us -> none  [on_device(): lax.all_gather(own, 'head', axis_index_groups=RING).reshape(8 * E, depth)]
    all_to_all x3, waiting for transfers between devices: 50.7 us -> 110 us  [over_head(): lax.all_to_all(blocks, 'head', 0, 0, tiled=True, axis_index_groups=RING)]
    ppermute x8, waiting for transfers between devices: 11 us -> 20.2 us  [swap_cores(): return lax.ppermute(value, 'dp', [(i, i ^ bit) for i in range(n_dp)])]
    ppermute x8, starting transfers between devices: 29.9 us -> 35.9 us  [swap_cores(): return lax.ppermute(value, 'dp', [(i, i ^ bit) for i in range(n_dp)])]
    pallas_call x8, Pallas kernels: 26.6 us -> 32.6 us  [call(): pl.pallas_call(fetching if moved else kernel, out_shape=outs, in_specs=sp...]
  transfers between devices with their start and end apart: 14 -> 13, of which waited for: 8 -> 8; matrix products, arithmetic and copies ran while one was open for 1% -> 0% of each run, Pallas kernels for 4% -> 3%
where the time goes in v8:
time: 366 us; the launch traced here: 365 us
  waiting for transfers between devices  139 us (38%)
  blocking collectives  98.5 us (27%)
  starting transfers between devices  58.7 us (16%)
  Pallas kernels  32.6 us (9%)
  local copies, waits for them, and re-layouts  19 us (5%)
  between operations  14.3 us (4%)
    all_to_all x3, waiting for transfers between devices, over_head(): lax.all_to_all(blocks, 'head', 0, 0, tiled=True, axis_index_groups=RING)  110 us
    ppermute x8, starting transfers between devices, swap_cores(): return lax.ppermute(value, 'dp', [(i, i ^ bit) for i in range(n_dp)])  35.9 us
    pallas_call x8, Pallas kernels, call(): pl.pallas_call(fetching if moved else kernel, out_shape=outs, in_specs=sp...  32.6 us
    all_to_all x1, blocking collectives, sum_far(): lax.all_to_all(copies, 'dp', 0, 0, tiled=True, axis_index_groups=far)  29.7 us
    all_to_all x1, blocking collectives, spread(): lax.all_to_all(copies, ('seq', 'dp'), 0, 0, tiled=True, axis_index_groups...  23 us
    all_to_all x1, blocking collectives, sum_near(): lax.all_to_all(grads, ('seq', 'dp'), 0, 0, tiled=True, axis_index_groups=...  22.6 us
    ppermute x8, waiting for transfers between devices, swap_cores(): return lax.ppermute(value, 'dp', [(i, i ^ bit) for i in range(n_dp)])  20.2 us
    unnamed x46, local copies, waits for them, and re-layouts  18.9 us
  transfers between devices with their start and end apart: 13, of which 8 were waited for; matrix products, arithmetic and copies ran while one was open for 0% of the time, Pallas kernels for 3%

profile of v8, /device:TPU:7, one launch (start us, length us, event | category | flops | bytes accessed | tf_op | source)
XLA Modules:
  0.0 364.8 jit_solution(14225080766731063663)
XLA Ops:
  14.1 7.0 %all-to-all-start = ((bf16[8,240,1152]{2,1,0:T(8,128)(2,1)}), bf16[8,240,1152]{2,1,0:T(8,128)(2,1)}, u32[]{:S(2)}, u32[]{:S(2)}) async-start(bf16[8,240,1152]{2,1,0:T(8,128)(2,1)} %copy-done), calls=%async_computation | async-start | bytes 8847360 | tf_op jit(solution)/shard_map/all_to_all | solution.py:329
  21.2 60.4 %all-to-all-done.hidden_ref = bf16[8,240,1152]{2,1,0:T(8,128)(2,1)} async-done(((bf16[8,240,1152]{2,1,0:T(8,128)(2,1)}), bf16[8,240,1152]{2,1,0:T(8,128)(2,1)}, u32[]{:S(2)}, u32[]{:S(2)}) %all-to-all-start) | async-done | bytes 4423712 | tf_op jit(solution)/shard_map/all_to_all | solution.py:329
  81.6 5.6 %shard_map.76 = (bf16[8,72,128]{2,1,0:T(8,128)(2,1)S(1)}, bf16[2,216,512]{2,1,0:T(8,128)(2,1)S(1)}, bf16[8,72,1152]{2,1,0:T(8,128)(2,1)}, bf16[8,40,1152]{2,1,0:T(8,128)(2,1)S(1)}) custom-call(bf16[8,240,1152]{2,1,0:T(8,128)(2,1)} %all-to-all-done.hidden_ref, bf16[216,1152]{1,0:T(8,128)(2,1)S(1)} %bitcast.18), custom_call_target="tpu_custom_call" | custom-call | tf_op jit(solution)/shard_map/pallas_call | solution.py:316
  88.7 10.9 %collective-permute-start.1 = (bf16[576,1152]{1,0:T(8,128)(2,1)}, bf16[576,1152]{1,0:T(8,128)(2,1)S(1)}, u32[]{:S(2)}, u32[]{:S(2)}) collective-permute-start(bf16[576,1152]{1,0:T(8,128)(2,1)} %bitcast.8.own_ref), channel_id=1, source_target_pairs={{0,2},{1,3},{2,0},{3,1},{4,6},{5,7},{6,4},{7,5},{8,10},{9,11},{10,... | collective-permute-start | bytes 3981320 | tf_op jit(solution)/shard_map/ppermute | solution.py:337
  99.6 4.1 %collective-permute-start = (bf16[320,1152]{1,0:T(8,128)(2,1)S(1)}, bf16[320,1152]{1,0:T(8,128)(2,1)S(1)}, u32[]{:S(2)}, u32[]{:S(2)}) collective-permute-start(bf16[320,1152]{1,0:T(8,128)(2,1)S(1)} %bitcast.22), channel_id=1, source_target_pairs={{0,1},{1,0},{2,3},{3,2},{4,5},{5,4},{6,7},{7,6},{8,9},{9,8},{10,11... | collective-permute-start | bytes 2211848 | tf_op jit(solution)/shard_map/ppermute | solution.py:337
  103.6 5.9 %all-to-all-start.1 = ((bf16[8,72,128]{2,1,0:T(8,128)(2,1)}), bf16[8,72,128]{2,1,0:T(8,128)(2,1)S(1)}, u32[]{:S(2)}, u32[]{:S(2)}) async-start(bf16[8,72,128]{2,1,0:T(8,128)(2,1)} %copy-done.21), calls=%async_computation.1 | async-start | bytes 294912 | tf_op jit(solution)/shard_map/all_to_all | solution.py:329
  114.9 12.4 %collective-permute-done.1.refs_6_ = bf16[576,1152]{1,0:T(8,128)(2,1)S(1)} collective-permute-done((bf16[576,1152]{1,0:T(8,128)(2,1)}, bf16[576,1152]{1,0:T(8,128)(2,1)S(1)}, u32[]{:S(2)}, u32[]{:S(2)}) %collective-permute-start.1) | collective-permute-done | bytes 1327136 | tf_op jit(solution)/shard_map/ppermute | solution.py:337
  132.2 4.4 %collective-permute-start.3 = (bf16[576,1152]{1,0:T(8,128)(2,1)S(1)}, bf16[576,1152]{1,0:T(8,128)(2,1)}, u32[]{:S(2)}, u32[]{:S(2)}) collective-permute-start(bf16[576,1152]{1,0:T(8,128)(2,1)S(1)} %get-tuple-element.29.z_ref), channel_id=1, source_target_pairs={{0,1},{1,0},{2,3},{3,2},{4,5},{5,4},{6,7},{7,6},{8,9},{9,8},{10,11... | collective-permute-start | bytes 3981320 | tf_op jit(solution)/shard_map/ppermute | solution.py:337
  136.6 4.3 %all-to-all-start.2 = ((bf16[2,2,2,32,1152]{4,3,2,1,0:T(8,128)(2,1)}), bf16[2,2,2,32,1152]{4,3,2,1,0:T(8,128)(2,1)}, u32[]{:S(2)}, u32[]{:S(2)}) async-start(bf16[2,2,2,32,1152]{4,3,2,1,0:T(8,128)(2,1)} %copy-done.9), calls=%async_computation.2 | async-start | bytes 1179648 | tf_op jit(solution)/shard_map/all_to_all | solution.py:333
  140.9 8.9 %all-to-all-done.2.pair_ref = bf16[2,2,2,32,1152]{4,3,2,1,0:T(8,128)(2,1)} async-done(((bf16[2,2,2,32,1152]{4,3,2,1,0:T(8,128)(2,1)}), bf16[2,2,2,32,1152]{4,3,2,1,0:T(8,128)(2,1)}, u32[]{:S(2)}, u32[]{:S(2)}) %all-to-all-start.2) | async-done | bytes 589856 | tf_op jit(solution)/shard_map/all_to_all | solution.py:333
  149.8 8.6 %shard_map.78 = (bf16[2,2,2,32,1152]{4,3,2,1,0:T(8,128)(2,1)S(1)}, bf16[1152,1152]{1,0:T(8,128)(2,1)S(1)}, bf16[1152,1152]{1,0:T(8,128)(2,1)S(1)}) custom-call(s32[2]{0:T(128)S(1)} %pad_add_fusion.refs_0_.at_ref.core_ref, bf16[2,2,2,32,1152]{4,3,2,1,0:T(8,128)(2,1)} %all-to-all-done.2.pair_ref, bf16[576,1152]{1,0:T(8,128)(2,1)} %bitcast.8.own_ref, ...), custom_call_target="tpu_custom_call" | custom-call | tf_op jit(solution)/shard_map/pallas_call | solution.py:316
  161.9 4.6 %collective-permute-done.6 = bf16[1152,1152]{1,0:T(8,128)(2,1)S(1)} collective-permute-done((bf16[1152,1152]{1,0:T(8,128)(2,1)S(1)}, bf16[1152,1152]{1,0:T(8,128)(2,1)S(1)}, u32[]{:S(2)}, u32[]{:S(2)}) %collective-permute-start.6) | collective-permute-done | bytes 2654240 | tf_op jit(solution)/shard_map/ppermute | solution.py:337
  169.8 10.8 %all_to_all.45.refs_1_ = bf16[2,2,2,32,1152]{4,3,2,1,0:T(8,128)(2,1)S(1)} all-to-all(bf16[2,2,2,32,1152]{4,3,2,1,0:T(8,128)(2,1)S(1)} %copy-done.8), channel_id=1, replica_groups=mesh['seq'=2,'head'=8,'dp'=32] {'seq'}, dimensions={0} | all-to-all | bytes 1179648 | tf_op jit(solution)/shard_map/all_to_all | solution.py:333
  180.6 3.2 shard_map.79
  183.8 3.1 collective-permute-start.4
  186.9 12.4 %all_to_all.46.gh_ref = bf16[8,72,128]{2,1,0:T(8,128)(2,1)S(1)} all-to-all(bf16[8,72,128]{2,1,0:T(8,128)(2,1)S(1)} %get-tuple-element.33), channel_id=1, replica_groups={{0,64,128,192,224,160,96,32},{1,65,129,193,225,161,97,33},{2,66,130,194..., dimensions={0} | all-to-all | bytes 294912 | tf_op jit(solution)/shard_map/all_to_all | solution.py:329
  199.3 6.3 %shard_map.80 = (bf16[8,176,1152]{2,1,0:T(8,128)(2,1)S(1)}, bf16[112,1152]{1,0:T(8,128)(2,1)S(1)}, bf16[112,1152]{1,0:T(8,128)(2,1)S(1)}) custom-call(s32[2]{0:T(128)S(1)} %pad_add_fusion.refs_0_.at_ref.core_ref, bf16[2,216,512]{2,1,0:T(8,128)(2,1)S(1)} %copy-done.11, bf16[8,72,128]{2,1,0:T(8,128)(2,1)S(1)} %all_to_all.46.gh_ref, ...), custom_call_target="tpu_custom_call" | custom-call | tf_op jit(solution)/shard_map/pallas_call | solution.py:316
  208.6 5.7 %all-to-all-start.5 = ((bf16[8,176,1152]{2,1,0:T(8,128)(2,1)}), bf16[8,176,1152]{2,1,0:T(8,128)(2,1)S(1)}, u32[]{:S(2)}, u32[]{:S(2)}) async-start(bf16[8,176,1152]{2,1,0:T(8,128)(2,1)} %copy-done.1), calls=%async_computation.5 | async-start | bytes 6488064 | tf_op jit(solution)/shard_map/all_to_all | solution.py:329
  214.3 3.4 collective-permute-start.5
  219.7 46.8 %all-to-all-done.5.refs_0_ = bf16[8,176,1152]{2,1,0:T(8,128)(2,1)S(1)} async-done(((bf16[8,176,1152]{2,1,0:T(8,128)(2,1)}), bf16[8,176,1152]{2,1,0:T(8,128)(2,1)S(1)}, u32[]{:S(2)}, u32[]{:S(2)}) %all-to-all-start.5) | async-done | bytes 3244064 | tf_op jit(solution)/shard_map/all_to_all | solution.py:329
  273.3 22.6 %all_to_all.47 = bf16[8,40,1152]{2,1,0:T(8,128)(2,1)S(1)} all-to-all(bf16[8,40,1152]{2,1,0:T(8,128)(2,1)S(1)} %get-tuple-element.43), channel_id=1, replica_groups={{0,2,4,6,256,258,260,262},{1,3,5,7,257,259,261,263},{8,10,12,14,264,266..., dimensions={0} | all-to-all | bytes 1474560 | tf_op jit(solution)/shard_map/all_to_all | solution.py:356
  296.1 29.7 %all_to_all.48 = bf16[4,40,1152]{2,1,0:T(8,128)(2,1)S(1)} all-to-all(bf16[4,40,1152]{2,1,0:T(8,128)(2,1)S(1)} %broadcast_in_dim.8), channel_id=1, replica_groups={{0,8,16,24},{1,9,17,25},{2,10,18,26},{3,11,19,27},{4,12,20,28},{5,13,21..., dimensions={0} | all-to-all | bytes 737280 | tf_op jit(solution)/shard_map/all_to_all | solution.py:364
  325.9 23.0 %all_to_all.49 = bf16[8,40,1152]{2,1,0:T(8,128)(2,1)S(1)} all-to-all(bf16[8,40,1152]{2,1,0:T(8,128)(2,1)S(1)} %broadcast_in_dim.9), channel_id=1, replica_groups={{0,2,4,6,256,258,260,262},{1,3,5,7,257,259,261,263},{8,10,12,14,264,266..., dimensions={0} | all-to-all | bytes 1474560 | tf_op jit(solution)/shard_map/all_to_all | solution.py:370
  348.9 4.9 %collective-permute-start.7 = (bf16[320,1152]{1,0:T(8,128)(2,1)S(1)}, bf16[320,1152]{1,0:T(8,128)(2,1)S(1)}, u32[]{:S(2)}, u32[]{:S(2)}) collective-permute-start(bf16[320,1152]{1,0:T(8,128)(2,1)S(1)} %bitcast.20), channel_id=1, source_target_pairs={{0,1},{1,0},{2,3},{3,2},{4,5},{5,4},{6,7},{7,6},{8,9},{9,8},{10,11... | collective-permute-start | bytes 2211848 | tf_op jit(solution)/shard_map/ppermute | solution.py:337
  (69 shorter events, 41.8 us)
Async XLA Ops:
  8.2 1.2 copy-start.5
  9.4 1.0 copy-start.12
  12.1 2.1 copy-start
  14.1 7.0 %copy-start.6 = (bf16[2,1,3,72,1152]{4,3,2,1,0:T(8,128)(2,1)S(1)}, bf16[2,1,3,72,1152]{4,3,2,1,0:T(8,128)(2,1)}, u32[]{:S(2)}) copy-start(bf16[2,1,3,72,1152]{4,3,2,1,0:T(8,128)(2,1)} %param.6) | copy-start | bytes 2985988
  14.1 67.4 %all-to-all-start = ((bf16[8,240,1152]{2,1,0:T(8,128)(2,1)}), bf16[8,240,1152]{2,1,0:T(8,128)(2,1)}, u32[]{:S(2)}, u32[]{:S(2)}) async-start(bf16[8,240,1152]{2,1,0:T(8,128)(2,1)} %copy-done), calls=%async_computation | async-start | bytes 8847360 | tf_op jit(solution)/shard_map/all_to_all | solution.py:329
  88.7 38.7 %collective-permute-start.1 = (bf16[576,1152]{1,0:T(8,128)(2,1)}, bf16[576,1152]{1,0:T(8,128)(2,1)S(1)}, u32[]{:S(2)}, u32[]{:S(2)}) collective-permute-start(bf16[576,1152]{1,0:T(8,128)(2,1)} %bitcast.8.own_ref), channel_id=1, source_target_pairs={{0,2},{1,3},{2,0},{3,1},{4,6},{5,7},{6,4},{7,5},{8,10},{9,11},{10,... | collective-permute-start | bytes 3981320 | tf_op jit(solution)/shard_map/ppermute | solution.py:337
  99.6 15.3 %collective-permute-start = (bf16[320,1152]{1,0:T(8,128)(2,1)S(1)}, bf16[320,1152]{1,0:T(8,128)(2,1)S(1)}, u32[]{:S(2)}, u32[]{:S(2)}) collective-permute-start(bf16[320,1152]{1,0:T(8,128)(2,1)S(1)} %bitcast.22), channel_id=1, source_target_pairs={{0,1},{1,0},{2,3},{3,2},{4,5},{5,4},{6,7},{7,6},{8,9},{9,8},{10,11... | collective-permute-start | bytes 2211848 | tf_op jit(solution)/shard_map/ppermute | solution.py:337
  103.6 11.3 %all-to-all-start.1 = ((bf16[8,72,128]{2,1,0:T(8,128)(2,1)}), bf16[8,72,128]{2,1,0:T(8,128)(2,1)S(1)}, u32[]{:S(2)}, u32[]{:S(2)}) async-start(bf16[8,72,128]{2,1,0:T(8,128)(2,1)} %copy-done.21), calls=%async_computation.1 | async-start | bytes 294912 | tf_op jit(solution)/shard_map/all_to_all | solution.py:329
  109.5 31.4 %collective-permute-start.2 = (bf16[576,1152]{1,0:T(8,128)(2,1)}, bf16[576,1152]{1,0:T(8,128)(2,1)}, u32[]{:S(2)}, u32[]{:S(2)}) collective-permute-start(bf16[576,1152]{1,0:T(8,128)(2,1)} %bitcast.8.own_ref), channel_id=1, source_target_pairs={{0,1},{1,0},{2,3},{3,2},{4,5},{5,4},{6,7},{7,6},{8,9},{9,8},{10,11... | collective-permute-start | bytes 3981320 | tf_op jit(solution)/shard_map/ppermute | solution.py:337
  127.3 1.0 copy-start.3
  132.2 17.6 %collective-permute-start.3 = (bf16[576,1152]{1,0:T(8,128)(2,1)S(1)}, bf16[576,1152]{1,0:T(8,128)(2,1)}, u32[]{:S(2)}, u32[]{:S(2)}) collective-permute-start(bf16[576,1152]{1,0:T(8,128)(2,1)S(1)} %get-tuple-element.29.z_ref), channel_id=1, source_target_pairs={{0,1},{1,0},{2,3},{3,2},{4,5},{5,4},{6,7},{7,6},{8,9},{9,8},{10,11... | collective-permute-start | bytes 3981320 | tf_op jit(solution)/shard_map/ppermute | solution.py:337
  136.6 13.2 %all-to-all-start.2 = ((bf16[2,2,2,32,1152]{4,3,2,1,0:T(8,128)(2,1)}), bf16[2,2,2,32,1152]{4,3,2,1,0:T(8,128)(2,1)}, u32[]{:S(2)}, u32[]{:S(2)}) async-start(bf16[2,2,2,32,1152]{4,3,2,1,0:T(8,128)(2,1)} %copy-done.9), calls=%async_computation.2 | async-start | bytes 1179648 | tf_op jit(solution)/shard_map/all_to_all | solution.py:333
  140.9 125.6 %reduce-scatter.2.cloned.1.call-start = ((), (), s32[]{:S(2)}) async-start(), calls=%async_computation.10 | async-start | bytes 2985984 | tf_op jit(solution)/shard_map/reduce_scatter | solution.py:431
  159.2 7.3 %collective-permute-start.6 = (bf16[1152,1152]{1,0:T(8,128)(2,1)S(1)}, bf16[1152,1152]{1,0:T(8,128)(2,1)S(1)}, u32[]{:S(2)}, u32[]{:S(2)}) collective-permute-start(bf16[1152,1152]{1,0:T(8,128)(2,1)S(1)} %get-tuple-element.41), channel_id=1, source_target_pairs={{0,1},{1,0},{2,3},{3,2},{4,5},{5,4},{6,7},{7,6},{8,9},{9,8},{10,11... | collective-permute-start | bytes 7962632 | tf_op jit(solution)/shard_map/ppermute | solution.py:337
  168.7 1.1 copy-start.8
  168.7 30.6 %copy-start.11 = (bf16[2,216,512]{2,1,0:T(8,128)(2,1)S(1)}, bf16[2,216,512]{2,1,0:T(8,128)(2,1)}, u32[]{:S(2)}) copy-start(bf16[2,216,512]{2,1,0:T(8,128)(2,1)} %copy-done.10) | copy-start | bytes 1327108
  183.8 15.5 %copy-start.15 = (bf16[128,1152]{1,0:T(8,128)(2,1)}, bf16[128,1152]{1,0:T(8,128)(2,1)S(1)}, u32[]{:S(2)}) copy-start(bf16[128,1152]{1,0:T(8,128)(2,1)S(1)} %get-tuple-element.37.refs_2_) | copy-start | bytes 884740
  183.8 15.5 %collective-permute-start.4 = (bf16[8,40,1152]{2,1,0:T(8,128)(2,1)S(1)}, bf16[8,40,1152]{2,1,0:T(8,128)(2,1)S(1)}, u32[]{:S(2)}, u32[]{:S(2)}) collective-permute-start(bf16[8,40,1152]{2,1,0:T(8,128)(2,1)S(1)} %get-tuple-element.35), channel_id=1, source_target_pairs={{0,1},{1,0},{2,3},{3,2},{4,5},{5,4},{6,7},{7,6},{8,9},{9,8},{10,11... | collective-permute-start | bytes 2211848 | tf_op jit(solution)/shard_map/ppermute | solution.py:337
  205.5 1.7 copy-start.1
  208.6 57.9 %copy-start.4 = (bf16[1,2,64,1152]{3,2,1,0:T(8,128)(2,1)S(1)}, bf16[1,2,64,1152]{3,2,1,0:T(8,128)(2,1)}, u32[]{:S(2)}) copy-start(bf16[1,2,64,1152]{3,2,1,0:T(8,128)(2,1)} %param.4) | copy-start | bytes 884740
  208.6 57.9 %all-to-all-start.5 = ((bf16[8,176,1152]{2,1,0:T(8,128)(2,1)}), bf16[8,176,1152]{2,1,0:T(8,128)(2,1)S(1)}, u32[]{:S(2)}, u32[]{:S(2)}) async-start(bf16[8,176,1152]{2,1,0:T(8,128)(2,1)} %copy-done.1), calls=%async_computation.5 | async-start | bytes 6488064 | tf_op jit(solution)/shard_map/all_to_all | solution.py:329
  214.3 4.7 %collective-permute-start.5 = (bf16[112,1152]{1,0:T(8,128)(2,1)}, bf16[112,1152]{1,0:T(8,128)(2,1)S(1)}, u32[]{:S(2)}, u32[]{:S(2)}) collective-permute-start(bf16[112,1152]{1,0:T(8,128)(2,1)} %copy-done.22), channel_id=1, source_target_pairs={{0,1},{1,0},{2,3},{3,2},{4,5},{5,4},{6,7},{7,6},{8,9},{9,8},{10,11... | collective-permute-start | bytes 774152 | tf_op jit(solution)/shard_map/ppermute | solution.py:337
  266.5 1.0 copy-start.13
  348.9 6.7 %collective-permute-start.7 = (bf16[320,1152]{1,0:T(8,128)(2,1)S(1)}, bf16[320,1152]{1,0:T(8,128)(2,1)S(1)}, u32[]{:S(2)}, u32[]{:S(2)}) collective-permute-start(bf16[320,1152]{1,0:T(8,128)(2,1)S(1)} %bitcast.20), channel_id=1, source_target_pairs={{0,1},{1,0},{2,3},{3,2},{4,5},{5,4},{6,7},{7,6},{8,9},{9,8},{10,11... | collective-permute-start | bytes 2211848 | tf_op jit(solution)/shard_map/ppermute | solution.py:337
  (12 other events, 10.0 us)
Sparse Core Ops, SparseCore 0:
  168.9 50.2 reduce-scatter.1

commit v9 on v4

--- a/solution.py
+++ b/solution.py
@@ -11,6 +11,7 @@
 E = 72
 SCALE = E ** (-0.5)
 RING = [[0, 2, 4, 6, 7, 5, 3, 1]]
+ALONG_X = [[0, 2, 4, 6], [1, 3, 5, 7]]
 BF = jnp.bfloat16
 F32 = jnp.float32
 
@@ -48,21 +49,27 @@
     )
 
 
-def norm_kernel(at_ref, x_ref, wq_ref, wo_ref, out_ref, own_ref):
+def norm_kernel(at_ref, x_ref, wq_ref, wo_ref, out_ref, row_ref, own_ref):
     core = at_ref[0]
     wide = wo_ref[0].astype(F32)
     half = jnp.where(core == 0, wide[:40], wide[32:])
     hidden = normalize(x_ref[...])[0]
     block = jnp.concatenate([hidden, half], axis=0).astype(BF)
-    for j in range(8):
+    row_ref[...] = block
+    for j in range(4):
         out_ref[j] = block
     qk = jnp.concatenate([wq_ref[1, 0].astype(F32), wq_ref[1, 1].astype(F32)], axis=0)
     vo = jnp.concatenate([wq_ref[1, 2].astype(F32), wo_ref[1].astype(F32)], axis=0)
     own_ref[...] = jnp.where(core == 0, qk, vo).astype(BF)
 
 
-def frame_rows(hidden_ref, f):
-    return hidden_ref[:, f * 64 : (f + 1) * 64, :].reshape(512, hidden_ref.shape[2])
+def frame_rows(near_ref, far_ref, f):
+    rows = [ref[:, f * 64 : (f + 1) * 64, :].reshape(256, ref.shape[2]) for ref in (near_ref, far_ref)]
+    return jnp.concatenate(rows, axis=0)
+
+
+def head_at(at_ref, slot):
+    return 2 * (slot % 4) + (at_ref[1] if slot < 4 else 1 - at_ref[1])
 
 
 def softmax(queries, key_rows):
@@ -74,12 +81,13 @@
     return tuple(stacked[i * E : (i + 1) * E].astype(BF) for i in range(3))
 
 
-def spatial_kernel(hidden_ref, w_ref, heads_ref, qkv_ref, one_ref):
-    for h in range(8):
-        one_ref[h] = hidden_ref[h].astype(F32)[128:].astype(BF)
+def spatial_kernel(at_ref, near_ref, far_ref, w_ref, heads_ref, qkv_ref, one_ref):
+    for i in range(8):
+        block = (near_ref if i < 4 else far_ref)[i % 4].astype(F32)
+        one_ref[head_at(at_ref, i)] = block[128:].astype(BF)
     outs = []
     for f in range(2):
-        qkv = nt(w_ref[...], frame_rows(hidden_ref, f))
+        qkv = nt(w_ref[...], frame_rows(near_ref, far_ref, f))
         qkv_ref[f] = qkv.astype(BF)
         q, k, v = split3(qkv)
         weights = softmax(q, k).astype(BF)
@@ -87,8 +95,8 @@
     for m in range(4):
         lanes = slice(m * 128, (m + 1) * 128)
         a, b = regroup(outs[0][:, lanes], outs[1][:, lanes])
-        heads_ref[2 * m] = a.astype(BF)
-        heads_ref[2 * m + 1] = b.astype(BF)
+        heads_ref[head_at(at_ref, 2 * m)] = a.astype(BF)
+        heads_ref[head_at(at_ref, 2 * m + 1)] = b.astype(BF)
 
 
 def middle_kernel(
@@ -216,15 +224,18 @@
 
 
 def spatial_back_kernel(
-    core_ref, qkv_ref, gh_ref, hidden_ref, w_ref, mine_ref, recv_ref, terms_ref, keep_ref, send_ref
+    at_ref, qkv_ref, gh_ref, near_ref, far_ref, w_ref, mine_ref, recv_ref,
+    first_ref, second_ref, keep_ref, send_ref,
 ):
-    for j in range(8):
+    terms_refs = [second_ref] * 4 + [first_ref] * 4
+    for i in range(8):
+        j = head_at(at_ref, i)
         part = mine_ref[j].astype(F32) + recv_ref[j].astype(F32)
         low = jnp.zeros((8, part.shape[1]), F32)
-        terms_ref[j, 128:176, :] = jnp.concatenate([part, low], axis=0).astype(BF)
+        terms_refs[i][i % 4, 128:176, :] = jnp.concatenate([part, low], axis=0).astype(BF)
     frames = ([], [])
     for m in range(4):
-        pair = regroup(gh_ref[2 * m].astype(F32), gh_ref[2 * m + 1].astype(F32))
+        pair = regroup(*(gh_ref[head_at(at_ref, 2 * m + i)].astype(F32) for i in range(2)))
         for f in range(2):
             frames[f].append(pair[f])
     total = None
@@ -237,14 +248,14 @@
         inner = jnp.sum(probs * gp, axis=1, keepdims=True)
         sg = (probs * (gp - inner) * SCALE).astype(BF)
         grads = jnp.concatenate([nt(k, sg), nn(q, sg), gv], axis=0).astype(BF)
-        gw = nn(grads, frame_rows(hidden_ref, f))
+        gw = nn(grads, frame_rows(near_ref, far_ref, f))
         total = gw if total is None else total + gw
         terms = tn(grads, w_ref[...]).astype(BF)
         for j in range(8):
-            terms_ref[j, f * 64 : (f + 1) * 64, :] = terms[j * 64 : (j + 1) * 64]
+            terms_refs[j][j % 4, f * 64 : (f + 1) * 64, :] = terms[j * 64 : (j + 1) * 64]
     low, high = halves(total, 112)
-    keep_ref[...] = jnp.where(core_ref[0] == 0, low, high).astype(BF)
-    send_ref[...] = jnp.where(core_ref[0] == 0, high, low).astype(BF)
+    keep_ref[...] = jnp.where(at_ref[0] == 0, low, high).astype(BF)
+    send_ref[...] = jnp.where(at_ref[0] == 0, high, low).astype(BF)
 
 
 def result_kernel(core_ref, mine_ref, other_ref, qkv_ref, out_ref, both_ref):
@@ -261,12 +272,19 @@
     out_ref[1] = both_ref[1, 152 + E : 152 + 2 * E]
 
 
+def half_sum_kernel(terms_ref, pass_ref, out_ref, same_ref):
+    total = terms_ref[0].astype(F32)
+    for j in range(1, 4):
+        total = total + terms_ref[j].astype(F32)
+    out_ref[...] = total.astype(BF)
+
+
 def last_kernel(
-    terms_ref, x_ref, g_ref, keep_ref, recv_ref, two_ref, out_ref, chain_ref, rows_ref
+    terms_ref, half_ref, x_ref, g_ref, keep_ref, recv_ref, two_ref, out_ref, chain_ref, rows_ref
 ):
     rows_ref[:112] = keep_ref[...].astype(F32) + recv_ref[...].astype(F32)
-    total = terms_ref[0].astype(F32)
-    for j in range(1, 8):
+    total = half_ref[...].astype(F32)
+    for j in range(4):
         total = total + terms_ref[j].astype(F32)
     rows_ref[112:152] = total[128:168]
     rows_ref[152:296] = two_ref[...].astype(F32)
@@ -300,7 +318,15 @@
 
 
 def over_head(blocks):
-    return lax.all_to_all(blocks, "head", 0, 0, tiled=True, axis_index_groups=RING)
+    return lax.all_to_all(blocks, "head", 0, 0, tiled=True)
+
+
+def over_x(blocks):
+    return lax.all_to_all(blocks, "head", 0, 0, tiled=True, axis_index_groups=ALONG_X)
+
+
+def swap_y(value):
+    return lax.ppermute(value, "head", [(i, i ^ 1) for i in range(8)])
 
 
 def over_seq(blocks):
@@ -349,22 +375,25 @@
 
 def on_device(n_dp, latents, cotangent, w_qkv, w_out):
     depth = latents.shape[-1]
-    at = (lax.axis_index("dp") % 2).reshape(1).astype(jnp.int32)
+    at = jnp.stack([lax.axis_index("dp") % 2, lax.axis_index("head") % 2]).astype(jnp.int32)
     near, far = groups_of(n_dp)
     x = latents.reshape(128, depth)
     g = cotangent.reshape(128, depth)
     w_own = w_qkv[0].reshape(3 * E, depth)
 
-    hidden, own = call(
-        norm_kernel, (shape(8, 168, depth), shape(2 * E, depth)),
+    hidden, row, own = call(
+        norm_kernel, (shape(4, 168, depth), shape(168, depth), shape(2 * E, depth)),
         at, x, w_qkv.reshape(2, 3, E, depth), w_out.reshape(2, E, depth),
         in_specs=[SMEM] + [VMEM] * 3,
     )
     mine_two = lax.all_gather(own, "head", axis_index_groups=RING).reshape(16 * E, depth)
-    hidden = over_head(hidden)
+    hidden = over_x(hidden)
+    partner = over_x(jnp.broadcast_to(swap_y(row)[None], (4, 168, depth)))
     heads, qkv, mine_one = call(
         spatial_kernel,
-        (shape(8, E, 128), shape(2, 3 * E, 512), shape(8, 40, depth)), hidden, w_own,
+        (shape(8, E, 128), shape(2, 3 * E, 512), shape(8, 40, depth)),
+        at, hidden, partner, w_own,
+        in_specs=[SMEM] + [VMEM] * 3,
     )
     heads = over_head(heads)
     mine_one = mine_one.reshape(320, depth)
@@ -411,15 +440,22 @@
     )
     gh = over_head(gh)
     half = shape(112, depth)
-    terms, keep, send = call(
-        spatial_back_kernel, (shape(8, 176, depth), half, half),
-        at, qkv, gh, hidden, w_own, keep, swap_cores(send, n_dp),
-        in_specs=[SMEM] + [VMEM] * 6,
+    terms = shape(4, 176, depth)
+    first, second, keep, send = call(
+        spatial_back_kernel, (terms, terms, half, half),
+        at, qkv, gh, hidden, partner, w_own, keep, swap_cores(send, n_dp),
+        in_specs=[SMEM] + [VMEM] * 7,
+    )
+    half_sum, second = call(
+        half_sum_kernel, (shape(176, depth), terms), over_x(first), second,
+        in_specs=[VMEM, ANY],
+        out_specs=(VMEM, ANY),
+        input_output_aliases={1: 1},
     )
     n_near = len(near[0])
     latent_grads, chain = call(
         last_kernel, (shape(128, depth), shape(n_near, 320 // n_near, depth)),
-        over_head(terms), x, grad_one, keep, swap_cores(send, n_dp), two,
+        over_x(second), swap_y(half_sum), x, grad_one, keep, swap_cores(send, n_dp), two,
         scratch_shapes=[pltpu.VMEM((320, depth), F32)],
     )
     part = sum_near(chain, near)

time: 338 us -> 328 us (0.970)
  waiting for transfers between devices: 97.4 us -> 56.1 us
  blocking collectives: 134 us -> 150 us
  starting transfers between devices: 37.8 us -> 52.1 us
  local copies, waits for them, and re-layouts: 27.3 us -> 22 us
  Pallas kernels: 23.1 us -> 27.3 us
    all_to_all x2 -> x3, waiting for transfers between devices: 89.5 us -> 38.1 us  [over_x(): lax.all_to_all(blocks, 'head', 0, 0, tiled=True, axis_index_groups=ALONG_X)]
    all_to_all x2 -> x3, blocking collectives: 24.2 us -> 52.3 us  [the longest x1 28.9 us: over_x(): lax.all_to_all(blocks, 'head', 0, 0, tiled=True, axis_index_groups=ALONG_X)]
    ppermute x0 -> x2, waiting for transfers between devices: none -> 10.1 us  [swap_y(): return lax.ppermute(value, 'head', [(i, i ^ 1) for i in range(8)])]
    ppermute x0 -> x2, starting transfers between devices: none -> 7.78 us  [swap_y(): return lax.ppermute(value, 'head', [(i, i ^ 1) for i in range(8)])]
    unnamed x56 -> x50, local copies, waits for them, and re-layouts: 25.3 us -> 18.7 us
    all_to_all x2, blocking collectives: 28.9 us -> 23.3 us  [over_seq(): return lax.all_to_all(blocks, 'seq', 0, 0, tiled=True)]
    pallas_call x8 -> x9, Pallas kernels: 23.1 us -> 27.3 us  [call(): pl.pallas_call(kernel, out_shape=outs, in_specs=more.pop('in_specs', [VME...]
    ppermute x6, starting transfers between devices: 25.5 us -> 28.9 us  [swap_cores(): return lax.ppermute(value, 'dp', [(i, i ^ bit) for i in range(n_dp)])]
  transfers between devices with their start and end apart: 10 -> 13, of which waited for: 5 -> 8; matrix products, arithmetic and copies ran while one was open for 1% -> 1% of each run, Pallas kernels for 3% -> 3%
where the time goes in v9:
time: 328 us; the launch traced here: 324 us
  blocking collectives  150 us (46%)
  waiting for transfers between devices  56.1 us (17%)
  starting transfers between devices  52.1 us (16%)
  Pallas kernels  27.3 us (8%)
  local copies, waits for them, and re-layouts  22 us (7%)
  between operations  14.3 us (4%)
    all_to_all x3, waiting for transfers between devices, over_x(): lax.all_to_all(blocks, 'head', 0, 0, tiled=True, axis_index_groups=ALONG_X)  38.1 us
    all_to_all x1, blocking collectives, sum_far(): lax.all_to_all(copies, 'dp', 0, 0, tiled=True, axis_index_groups=far)  29.1 us
    all_to_all x1, blocking collectives, over_x(): lax.all_to_all(blocks, 'head', 0, 0, tiled=True, axis_index_groups=ALONG_X)  28.9 us
    ppermute x6, starting transfers between devices, swap_cores(): return lax.ppermute(value, 'dp', [(i, i ^ bit) for i in range(n_dp)])  28.9 us
    pallas_call x9, Pallas kernels, call(): pl.pallas_call(kernel, out_shape=outs, in_specs=more.pop('in_specs', [VME...  27.3 us
    all_to_all x2, blocking collectives, over_head(): return lax.all_to_all(blocks, 'head', 0, 0, tiled=True)  23.4 us
    all_to_all x2, blocking collectives, over_seq(): return lax.all_to_all(blocks, 'seq', 0, 0, tiled=True)  23.3 us
    all_to_all x1, blocking collectives, spread(): lax.all_to_all(copies, ('seq', 'dp'), 0, 0, tiled=True, axis_index_groups...  22.9 us
  transfers between devices with their start and end apart: 13, of which 8 were waited for; matrix products, arithmetic and copies ran while one was open for 1% of the time, Pallas kernels for 3%

profile of v9, /device:TPU:7, one launch (start us, length us, event | category | flops | bytes accessed | tf_op | source)
XLA Modules:
  0.0 324.4 jit_solution(8666615761924823433)
XLA Ops:
  12.6 4.2 %all-to-all-start = ((bf16[4,168,1152]{2,1,0:T(8,128)(2,1)}), bf16[4,168,1152]{2,1,0:T(8,128)(2,1)S(1)}, u32[]{:S(2)}, u32[]{:S(2)}) async-start(bf16[4,168,1152]{2,1,0:T(8,128)(2,1)} %get-tuple-element.30), calls=%async_computation | async-start | bytes 3096576 | tf_op jit(solution)/shard_map/all_to_all | solution.py:325
  16.8 4.8 %collective-permute-start = (bf16[168,1152]{1,0:T(8,128)(2,1)S(1)}, bf16[168,1152]{1,0:T(8,128)(2,1)S(1)}, u32[]{:S(2)}, u32[]{:S(2)}) collective-permute-start(bf16[168,1152]{1,0:T(8,128)(2,1)S(1)} %get-tuple-element.31), channel_id=1, source_target_pairs={{0,32},{32,0},{64,96},{96,64},{128,160},{160,128},{192,224},{224,1... | collective-permute-start | bytes 1161224 | tf_op jit(solution)/shard_map/ppermute | solution.py:329
  21.6 5.6 %collective-permute-done = bf16[168,1152]{1,0:T(8,128)(2,1)S(1)} collective-permute-done((bf16[168,1152]{1,0:T(8,128)(2,1)S(1)}, bf16[168,1152]{1,0:T(8,128)(2,1)S(1)}, u32[]{:S(2)}, u32[]{:S(2)}) %collective-permute-start) | collective-permute-done | bytes 387104 | tf_op jit(solution)/shard_map/ppermute | solution.py:329
  31.2 5.3 %all-to-all-start.1 = ((bf16[4,168,1152]{2,1,0:T(8,128)(2,1)}), bf16[4,168,1152]{2,1,0:T(8,128)(2,1)S(1)}, u32[]{:S(2)}, u32[]{:S(2)}) async-start(bf16[4,168,1152]{2,1,0:T(8,128)(2,1)} %broadcast_in_dim.10), calls=%async_computation.1 | async-start | bytes 3096576 | tf_op jit(solution)/shard_map/all_to_all | solution.py:325
  38.4 29.8 %all-to-all-done.1.far_ref = bf16[4,168,1152]{2,1,0:T(8,128)(2,1)S(1)} async-done(((bf16[4,168,1152]{2,1,0:T(8,128)(2,1)}), bf16[4,168,1152]{2,1,0:T(8,128)(2,1)S(1)}, u32[]{:S(2)}, u32[]{:S(2)}) %all-to-all-start.1) | async-done | bytes 1548320 | tf_op jit(solution)/shard_map/all_to_all | solution.py:325
  72.9 11.1 %collective-permute-start.1 = (bf16[320,1152]{1,0:T(8,128)(2,1)S(1)}, bf16[320,1152]{1,0:T(8,128)(2,1)S(1)}, u32[]{:S(2)}, u32[]{:S(2)}) collective-permute-start(bf16[320,1152]{1,0:T(8,128)(2,1)S(1)} %bitcast.19), channel_id=1, source_target_pairs={{0,1},{1,0},{2,3},{3,2},{4,5},{5,4},{6,7},{7,6},{8,9},{9,8},{10,11... | collective-permute-start | bytes 2211848 | tf_op jit(solution)/shard_map/ppermute | solution.py:337
  84.9 12.7 %all_to_all.55.heads_ref = bf16[8,72,128]{2,1,0:T(8,128)(2,1)S(1)} all-to-all(bf16[8,72,128]{2,1,0:T(8,128)(2,1)S(1)} %get-tuple-element.32), channel_id=1, replica_groups=mesh['seq'=2,'head'=8,'dp'=32] {'head'}, dimensions={0} | all-to-all | bytes 294912 | tf_op jit(solution)/shard_map/all_to_all | solution.py:321
  106.1 3.3 %collective-permute-start.2 = (bf16[1152,1152]{1,0:T(8,128)(2,1)S(1)}, bf16[1152,1152]{1,0:T(8,128)(2,1)S(1)}, u32[]{:S(2)}, u32[]{:S(2)}) collective-permute-start(bf16[1152,1152]{1,0:T(8,128)(2,1)S(1)} %get-tuple-element.36.mine_ref), channel_id=1, source_target_pairs={{0,1},{1,0},{2,3},{3,2},{4,5},{5,4},{6,7},{7,6},{8,9},{9,8},{10,11... | collective-permute-start | bytes 7962632 | tf_op jit(solution)/shard_map/ppermute | solution.py:337
  109.3 11.3 %all_to_all.56.pair_ref = bf16[2,2,2,32,1152]{4,3,2,1,0:T(8,128)(2,1)S(1)} all-to-all(bf16[2,2,2,32,1152]{4,3,2,1,0:T(8,128)(2,1)S(1)} %get-tuple-element.35), channel_id=1, replica_groups=mesh['seq'=2,'head'=8,'dp'=32] {'seq'}, dimensions={0} | all-to-all | bytes 1179648 | tf_op jit(solution)/shard_map/all_to_all | solution.py:333
  122.1 9.1 %shard_map.78 = (bf16[2,2,2,32,1152]{4,3,2,1,0:T(8,128)(2,1)S(1)}, bf16[1152,1152]{1,0:T(8,128)(2,1)S(1)}, bf16[1152,1152]{1,0:T(8,128)(2,1)}) custom-call(s32[2]{0:T(128)S(1)} %pad_add_fusion.at_ref.core_ref, bf16[2,2,2,32,1152]{4,3,2,1,0:T(8,128)(2,1)S(1)} %all_to_all.56.pair_ref, bf16[1152,1152]{1,0:T(8,128)(2,1)} %copy-done.1, bf16[1152,1152]{1,0:T(8,128)(2,1)} %copy-done.24), custom_call_target="tpu_custom_call" | custom-call | tf_op jit(solution)/shard_map/pallas_call | solution.py:309
  134.7 4.8 %collective-permute-done.6 = bf16[1152,1152]{1,0:T(8,128)(2,1)S(1)} collective-permute-done((bf16[1152,1152]{1,0:T(8,128)(2,1)}, bf16[1152,1152]{1,0:T(8,128)(2,1)S(1)}, u32[]{:S(2)}, u32[]{:S(2)}) %collective-permute-start.6) | collective-permute-done | bytes 2654240 | tf_op jit(solution)/shard_map/ppermute | solution.py:337
  141.7 12.1 %all_to_all.57.back_ref = bf16[2,2,2,32,1152]{4,3,2,1,0:T(8,128)(2,1)S(1)} all-to-all(bf16[2,2,2,32,1152]{4,3,2,1,0:T(8,128)(2,1)} %copy-done.13), channel_id=1, replica_groups=mesh['seq'=2,'head'=8,'dp'=32] {'seq'}, dimensions={0} | all-to-all | bytes 1179648 | tf_op jit(solution)/shard_map/all_to_all | solution.py:333
  158.1 3.1 collective-permute-start.3
  161.2 10.7 %all_to_all.58.gh_ref = bf16[8,72,128]{2,1,0:T(8,128)(2,1)S(1)} all-to-all(bf16[8,72,128]{2,1,0:T(8,128)(2,1)S(1)} %get-tuple-element.40), channel_id=1, replica_groups=mesh['seq'=2,'head'=8,'dp'=32] {'head'}, dimensions={0} | all-to-all | bytes 294912 | tf_op jit(solution)/shard_map/all_to_all | solution.py:321
  172.0 6.1 %shard_map.80 = (bf16[4,176,1152]{2,1,0:T(8,128)(2,1)}, bf16[4,176,1152]{2,1,0:T(8,128)(2,1)}, bf16[112,1152]{1,0:T(8,128)(2,1)S(1)}, bf16[112,1152]{1,0:T(8,128)(2,1)S(1)}) custom-call(s32[2]{0:T(128)S(1)} %pad_add_fusion.at_ref.core_ref, bf16[2,216,512]{2,1,0:T(8,128)(2,1)S(1)} %copy-done.15, bf16[8,72,128]{2,1,0:T(8,128)(2,1)S(1)} %all_to_all.58.gh_ref, ...), custom_call_target="tpu_custom_call" | custom-call | tf_op jit(solution)/shard_map/pallas_call | solution.py:309
  178.1 28.9 %all_to_all.59.terms_ref = bf16[4,176,1152]{2,1,0:T(8,128)(2,1)S(1)} all-to-all(bf16[4,176,1152]{2,1,0:T(8,128)(2,1)} %get-tuple-element.43), channel_id=1, replica_groups={{0,64,128,192},{32,96,160,224},{1,65,129,193},{33,97,161,225},{2,66,130..., dimensions={0} | all-to-all | bytes 3244032 | tf_op jit(solution)/shard_map/all_to_all | solution.py:325
  207.2 5.8 %all-to-all-start.7 = ((bf16[4,176,1152]{2,1,0:T(8,128)(2,1)}), bf16[4,176,1152]{2,1,0:T(8,128)(2,1)S(1)}, u32[]{:S(2)}, u32[]{:S(2)}) async-start(bf16[4,176,1152]{2,1,0:T(8,128)(2,1)} %get-tuple-element.45), calls=%async_computation.7 | async-start | bytes 3244032 | tf_op jit(solution)/shard_map/all_to_all | solution.py:325
  216.1 3.8 %collective-permute-start.5 = (bf16[112,1152]{1,0:T(8,128)(2,1)}, bf16[112,1152]{1,0:T(8,128)(2,1)S(1)}, u32[]{:S(2)}, u32[]{:S(2)}) collective-permute-start(bf16[112,1152]{1,0:T(8,128)(2,1)} %copy-done.23), channel_id=1, source_target_pairs={{0,1},{1,0},{2,3},{3,2},{4,5},{5,4},{6,7},{7,6},{8,9},{9,8},{10,11... | collective-permute-start | bytes 774152 | tf_op jit(solution)/shard_map/ppermute | solution.py:337
  221.2 4.5 %collective-permute-done.4.half_ref = bf16[176,1152]{1,0:T(8,128)(2,1)S(1)} collective-permute-done((bf16[176,1152]{1,0:T(8,128)(2,1)S(1)}, bf16[176,1152]{1,0:T(8,128)(2,1)S(1)}, u32[]{:S(2)}, u32[]{:S(2)}) %collective-permute-start.4) | collective-permute-done | bytes 405536 | tf_op jit(solution)/shard_map/ppermute | solution.py:329
  225.7 5.5 %all-to-all-done.7.terms_ref = bf16[4,176,1152]{2,1,0:T(8,128)(2,1)S(1)} async-done(((bf16[4,176,1152]{2,1,0:T(8,128)(2,1)}), bf16[4,176,1152]{2,1,0:T(8,128)(2,1)S(1)}, u32[]{:S(2)}, u32[]{:S(2)}) %all-to-all-start.7) | async-done | bytes 1622048 | tf_op jit(solution)/shard_map/all_to_all | solution.py:325
  233.5 22.7 %all_to_all.60 = bf16[8,40,1152]{2,1,0:T(8,128)(2,1)S(1)} all-to-all(bf16[8,40,1152]{2,1,0:T(8,128)(2,1)S(1)} %get-tuple-element.53), channel_id=1, replica_groups={{0,2,4,6,256,258,260,262},{1,3,5,7,257,259,261,263},{8,10,12,14,264,266..., dimensions={0} | all-to-all | bytes 1474560 | tf_op jit(solution)/shard_map/all_to_all | solution.py:356
  256.4 29.1 %all_to_all.61 = bf16[4,40,1152]{2,1,0:T(8,128)(2,1)S(1)} all-to-all(bf16[4,40,1152]{2,1,0:T(8,128)(2,1)S(1)} %broadcast_in_dim.11), channel_id=1, replica_groups={{0,8,16,24},{1,9,17,25},{2,10,18,26},{3,11,19,27},{4,12,20,28},{5,13,21..., dimensions={0} | all-to-all | bytes 737280 | tf_op jit(solution)/shard_map/all_to_all | solution.py:364
  285.6 22.9 %all_to_all.62 = bf16[8,40,1152]{2,1,0:T(8,128)(2,1)S(1)} all-to-all(bf16[8,40,1152]{2,1,0:T(8,128)(2,1)S(1)} %broadcast_in_dim.12), channel_id=1, replica_groups={{0,2,4,6,256,258,260,262},{1,3,5,7,257,259,261,263},{8,10,12,14,264,266..., dimensions={0} | all-to-all | bytes 1474560 | tf_op jit(solution)/shard_map/all_to_all | solution.py:370
  308.5 4.9 %collective-permute-start.7 = (bf16[320,1152]{1,0:T(8,128)(2,1)S(1)}, bf16[320,1152]{1,0:T(8,128)(2,1)S(1)}, u32[]{:S(2)}, u32[]{:S(2)}) collective-permute-start(bf16[320,1152]{1,0:T(8,128)(2,1)S(1)} %bitcast.22), channel_id=1, source_target_pairs={{0,1},{1,0},{2,3},{3,2},{4,5},{5,4},{6,7},{7,6},{8,9},{9,8},{10,11... | collective-permute-start | bytes 2211848 | tf_op jit(solution)/shard_map/ppermute | solution.py:337
  (79 shorter events, 48.1 us)
Async XLA Ops:
  7.2 91.4 %all-gather.3.cloned.1.call-start = ((), (), s32[]{:S(2)}) async-start(), calls=%async_computation.13 | async-start | bytes 2985984 | tf_op jit(solution)/shard_map/all_gather | solution.py:389
  12.6 17.4 %all-to-all-start = ((bf16[4,168,1152]{2,1,0:T(8,128)(2,1)}), bf16[4,168,1152]{2,1,0:T(8,128)(2,1)S(1)}, u32[]{:S(2)}, u32[]{:S(2)}) async-start(bf16[4,168,1152]{2,1,0:T(8,128)(2,1)} %get-tuple-element.30), calls=%async_computation | async-start | bytes 3096576 | tf_op jit(solution)/shard_map/all_to_all | solution.py:325
  16.8 10.4 %collective-permute-start = (bf16[168,1152]{1,0:T(8,128)(2,1)S(1)}, bf16[168,1152]{1,0:T(8,128)(2,1)S(1)}, u32[]{:S(2)}, u32[]{:S(2)}) collective-permute-start(bf16[168,1152]{1,0:T(8,128)(2,1)S(1)} %get-tuple-element.31), channel_id=1, source_target_pairs={{0,32},{32,0},{64,96},{96,64},{128,160},{160,128},{192,224},{224,1... | collective-permute-start | bytes 1161224 | tf_op jit(solution)/shard_map/ppermute | solution.py:329
  31.2 37.1 %all-to-all-start.1 = ((bf16[4,168,1152]{2,1,0:T(8,128)(2,1)}), bf16[4,168,1152]{2,1,0:T(8,128)(2,1)S(1)}, u32[]{:S(2)}, u32[]{:S(2)}) async-start(bf16[4,168,1152]{2,1,0:T(8,128)(2,1)} %broadcast_in_dim.10), calls=%async_computation.1 | async-start | bytes 3096576 | tf_op jit(solution)/shard_map/all_to_all | solution.py:325
  36.5 62.0 %copy-start.11 = (bf16[1,2,64,1152]{3,2,1,0:T(8,128)(2,1)S(1)}, bf16[1,2,64,1152]{3,2,1,0:T(8,128)(2,1)}, u32[]{:S(2)}) copy-start(bf16[1,2,64,1152]{3,2,1,0:T(8,128)(2,1)} %param.4) | copy-start | bytes 884740
  36.5 194.7 %reduce-scatter.2.cloned.1.call-start = ((), (), s32[]{:S(2)}) async-start(), calls=%async_computation.12 | async-start | bytes 2985984 | tf_op jit(solution)/shard_map/reduce_scatter | solution.py:430
  72.9 24.7 %collective-permute-start.1 = (bf16[320,1152]{1,0:T(8,128)(2,1)S(1)}, bf16[320,1152]{1,0:T(8,128)(2,1)S(1)}, u32[]{:S(2)}, u32[]{:S(2)}) collective-permute-start(bf16[320,1152]{1,0:T(8,128)(2,1)S(1)} %bitcast.19), channel_id=1, source_target_pairs={{0,1},{1,0},{2,3},{3,2},{4,5},{5,4},{6,7},{7,6},{8,9},{9,8},{10,11... | collective-permute-start | bytes 2211848 | tf_op jit(solution)/shard_map/ppermute | solution.py:337
  98.5 1.8 copy-start
  104.6 1.5 copy-start.1
  106.1 14.5 %collective-permute-start.2 = (bf16[1152,1152]{1,0:T(8,128)(2,1)S(1)}, bf16[1152,1152]{1,0:T(8,128)(2,1)S(1)}, u32[]{:S(2)}, u32[]{:S(2)}) collective-permute-start(bf16[1152,1152]{1,0:T(8,128)(2,1)S(1)} %get-tuple-element.36.mine_ref), channel_id=1, source_target_pairs={{0,1},{1,0},{2,3},{3,2},{4,5},{5,4},{6,7},{7,6},{8,9},{9,8},{10,11... | collective-permute-start | bytes 7962632 | tf_op jit(solution)/shard_map/ppermute | solution.py:337
  120.6 1.5 copy-start.24
  132.0 7.5 %collective-permute-start.6 = (bf16[1152,1152]{1,0:T(8,128)(2,1)}, bf16[1152,1152]{1,0:T(8,128)(2,1)S(1)}, u32[]{:S(2)}, u32[]{:S(2)}) collective-permute-start(bf16[1152,1152]{1,0:T(8,128)(2,1)} %get-tuple-element.51), channel_id=1, source_target_pairs={{0,1},{1,0},{2,3},{3,2},{4,5},{5,4},{6,7},{7,6},{8,9},{9,8},{10,11... | collective-permute-start | bytes 7962632 | tf_op jit(solution)/shard_map/ppermute | solution.py:337
  141.6 30.4 %copy-start.3 = (bf16[1,1,3,72,1152]{4,3,2,1,0:T(8,128)(2,1)S(1)}, bf16[1,1,3,72,1152]{4,3,2,1,0:T(8,128)(2,1)}, u32[]{:S(2)}) copy-start(bf16[1,1,3,72,1152]{4,3,2,1,0:T(8,128)(2,1)} %slice.3) | copy-start | bytes 1492996
  141.7 30.3 %copy-start.15 = (bf16[2,216,512]{2,1,0:T(8,128)(2,1)S(1)}, bf16[2,216,512]{2,1,0:T(8,128)(2,1)}, u32[]{:S(2)}) copy-start(bf16[2,216,512]{2,1,0:T(8,128)(2,1)} %copy-done.14) | copy-start | bytes 1327108
  158.1 20.0 %copy-start.19 = (bf16[128,1152]{1,0:T(8,128)(2,1)}, bf16[128,1152]{1,0:T(8,128)(2,1)S(1)}, u32[]{:S(2)}) copy-start(bf16[128,1152]{1,0:T(8,128)(2,1)S(1)} %get-tuple-element.47.g_ref) | copy-start | bytes 884740
  158.1 13.9 %collective-permute-start.3 = (bf16[8,40,1152]{2,1,0:T(8,128)(2,1)S(1)}, bf16[8,40,1152]{2,1,0:T(8,128)(2,1)S(1)}, u32[]{:S(2)}, u32[]{:S(2)}) collective-permute-start(bf16[8,40,1152]{2,1,0:T(8,128)(2,1)S(1)} %get-tuple-element.42), channel_id=1, source_target_pairs={{0,1},{1,0},{2,3},{3,2},{4,5},{5,4},{6,7},{7,6},{8,9},{9,8},{10,11... | collective-permute-start | bytes 2211848 | tf_op jit(solution)/shard_map/ppermute | solution.py:337
  178.1 28.9 %copy-start.21 = (bf16[112,1152]{1,0:T(8,128)(2,1)}, bf16[112,1152]{1,0:T(8,128)(2,1)S(1)}, u32[]{:S(2)}) copy-start(bf16[112,1152]{1,0:T(8,128)(2,1)S(1)} %get-tuple-element.48.keep_ref) | copy-start | bytes 774148
  178.1 29.1 %copy-start.23 = (bf16[112,1152]{1,0:T(8,128)(2,1)}, bf16[112,1152]{1,0:T(8,128)(2,1)S(1)}, u32[]{:S(2)}) copy-start(bf16[112,1152]{1,0:T(8,128)(2,1)S(1)} %get-tuple-element.49) | copy-start | bytes 774148
  207.0 24.2 %copy-start.20 = (bf16[128,1152]{1,0:T(8,128)(2,1)S(1)}, bf16[128,1152]{1,0:T(8,128)(2,1)}, u32[]{:S(2)}) copy-start(bf16[128,1152]{1,0:T(8,128)(2,1)} %copy-done.19) | copy-start | bytes 884740
  207.0 24.2 %copy-start.22 = (bf16[112,1152]{1,0:T(8,128)(2,1)S(1)}, bf16[112,1152]{1,0:T(8,128)(2,1)}, u32[]{:S(2)}) copy-start(bf16[112,1152]{1,0:T(8,128)(2,1)} %copy-done.21) | copy-start | bytes 774148
  207.2 24.0 %all-to-all-start.7 = ((bf16[4,176,1152]{2,1,0:T(8,128)(2,1)}), bf16[4,176,1152]{2,1,0:T(8,128)(2,1)S(1)}, u32[]{:S(2)}, u32[]{:S(2)}) async-start(bf16[4,176,1152]{2,1,0:T(8,128)(2,1)} %get-tuple-element.45), calls=%async_computation.7 | async-start | bytes 3244032 | tf_op jit(solution)/shard_map/all_to_all | solution.py:325
  213.1 12.6 %collective-permute-start.4 = (bf16[176,1152]{1,0:T(8,128)(2,1)S(1)}, bf16[176,1152]{1,0:T(8,128)(2,1)S(1)}, u32[]{:S(2)}, u32[]{:S(2)}) collective-permute-start(bf16[176,1152]{1,0:T(8,128)(2,1)S(1)} %get-tuple-element.46), channel_id=1, source_target_pairs={{0,32},{32,0},{64,96},{96,64},{128,160},{160,128},{192,224},{224,1... | collective-permute-start | bytes 1216520 | tf_op jit(solution)/shard_map/ppermute | solution.py:329
  216.1 5.2 %collective-permute-start.5 = (bf16[112,1152]{1,0:T(8,128)(2,1)}, bf16[112,1152]{1,0:T(8,128)(2,1)S(1)}, u32[]{:S(2)}, u32[]{:S(2)}) collective-permute-start(bf16[112,1152]{1,0:T(8,128)(2,1)} %copy-done.23), channel_id=1, source_target_pairs={{0,1},{1,0},{2,3},{3,2},{4,5},{5,4},{6,7},{7,6},{8,9},{9,8},{10,11... | collective-permute-start | bytes 774152 | tf_op jit(solution)/shard_map/ppermute | solution.py:337
  308.5 6.7 %collective-permute-start.7 = (bf16[320,1152]{1,0:T(8,128)(2,1)S(1)}, bf16[320,1152]{1,0:T(8,128)(2,1)S(1)}, u32[]{:S(2)}, u32[]{:S(2)}) collective-permute-start(bf16[320,1152]{1,0:T(8,128)(2,1)S(1)} %bitcast.22), channel_id=1, source_target_pairs={{0,1},{1,0},{2,3},{3,2},{4,5},{5,4},{6,7},{7,6},{8,9},{9,8},{10,11... | collective-permute-start | bytes 2211848 | tf_op jit(solution)/shard_map/ppermute | solution.py:337
  (14 other events, 14.0 us)
Sparse Core Ops, SparseCore 0:
  12.7 64.7 all-gather.2
  141.8 51.5 reduce-scatter.1

commit v10 on v9

--- a/solution.py
+++ b/solution.py
@@ -224,15 +224,9 @@
 
 
 def spatial_back_kernel(
-    at_ref, qkv_ref, gh_ref, near_ref, far_ref, w_ref, mine_ref, recv_ref,
-    first_ref, second_ref, keep_ref, send_ref,
+    at_ref, qkv_ref, gh_ref, near_ref, far_ref, w_ref,
+    a0_ref, a1_ref, a2_ref, a3_ref, b0_ref, b1_ref, b2_ref, b3_ref, keep_ref, send_ref, rows_ref,
 ):
-    terms_refs = [second_ref] * 4 + [first_ref] * 4
-    for i in range(8):
-        j = head_at(at_ref, i)
-        part = mine_ref[j].astype(F32) + recv_ref[j].astype(F32)
-        low = jnp.zeros((8, part.shape[1]), F32)
-        terms_refs[i][i % 4, 128:176, :] = jnp.concatenate([part, low], axis=0).astype(BF)
     frames = ([], [])
     for m in range(4):
         pair = regroup(*(gh_ref[head_at(at_ref, 2 * m + i)].astype(F32) for i in range(2)))
@@ -252,7 +246,12 @@
         total = gw if total is None else total + gw
         terms = tn(grads, w_ref[...]).astype(BF)
         for j in range(8):
-            terms_refs[j][j % 4, f * 64 : (f + 1) * 64, :] = terms[j * 64 : (j + 1) * 64]
+            rows_ref[j, f * 64 : (f + 1) * 64, :] = terms[j * 64 : (j + 1) * 64]
+    ahead = ((a0_ref, b0_ref), (a1_ref, b1_ref), (a2_ref, b2_ref), (a3_ref, b3_ref))
+    for k, (other_ref, own_ref) in enumerate(ahead):
+        x_at = lax.rem(at_ref[2] + k, 4)
+        own_ref[...] = rows_ref[x_at]
+        other_ref[...] = rows_ref[4 + x_at]
     low, high = halves(total, 112)
     keep_ref[...] = jnp.where(at_ref[0] == 0, low, high).astype(BF)
     send_ref[...] = jnp.where(at_ref[0] == 0, high, low).astype(BF)
@@ -272,27 +271,48 @@
     out_ref[1] = both_ref[1, 152 + E : 152 + 2 * E]
 
 
-def half_sum_kernel(terms_ref, pass_ref, out_ref, same_ref):
-    total = terms_ref[0].astype(F32)
-    for j in range(1, 4):
-        total = total + terms_ref[j].astype(F32)
-    out_ref[...] = total.astype(BF)
-
-
-def last_kernel(
-    terms_ref, half_ref, x_ref, g_ref, keep_ref, recv_ref, two_ref, out_ref, chain_ref, rows_ref
-):
+def chain_kernel(keep_ref, recv_ref, parts_ref, two_ref, chain_ref, rows_ref):
     rows_ref[:112] = keep_ref[...].astype(F32) + recv_ref[...].astype(F32)
-    total = half_ref[...].astype(F32)
-    for j in range(4):
-        total = total + terms_ref[j].astype(F32)
-    rows_ref[112:152] = total[128:168]
+    rows_ref[112:152] = block_sum(parts_ref)
     rows_ref[152:296] = two_ref[...].astype(F32)
     rows_ref[296:] = jnp.zeros_like(rows_ref[296:])
-    for i in range(8):
-        chain_ref[i] = rows_ref[i * 40 : (i + 1) * 40].astype(BF)
+    n, size = chain_ref.shape[:2]
+    for i in range(n):
+        chain_ref[i] = rows_ref[i * size : (i + 1) * size].astype(BF)
+
+
+def block_sum(ref):
+    total = ref[0].astype(F32)
+    for j in range(1, ref.shape[0]):
+        total = total + ref[j].astype(F32)
+    return total
+
+
+def copy_sum(blocks_ref, out_ref):
+    total = block_sum(blocks_ref).astype(BF)
+    for i in range(out_ref.shape[0]):
+        out_ref[i] = total
+
+
+def half_sum_kernel(t0_ref, t1_ref, t2_ref, t3_ref, grads_ref, out_ref, copies_ref):
+    out_ref[...] = row_sum(t0_ref, t1_ref, t2_ref, t3_ref).astype(BF)
+    copy_sum(grads_ref, copies_ref)
+
+
+def row_sum(*refs):
+    total = refs[0][...].astype(F32)
+    for ref in refs[1:]:
+        total = total + ref[...].astype(F32)
+    return total
+
+
+def last_kernel(
+    t0_ref, t1_ref, t2_ref, t3_ref, half_ref, x_ref, g_ref, grads_ref, out_ref, copies_ref
+):
+    copy_sum(grads_ref, copies_ref)
+    total = row_sum(t0_ref, t1_ref, t2_ref, t3_ref, half_ref)
     normed, inverse = normalize(x_ref[...])
-    out_ref[...] = normalize_back(g_ref[...], inverse, normed, total[:128]).astype(BF)
+    out_ref[...] = normalize_back(g_ref[...], inverse, normed, total).astype(BF)
 
 
 VMEM = pl.BlockSpec(memory_space=pltpu.VMEM)
@@ -323,6 +343,12 @@
 
 def over_x(blocks):
     return lax.all_to_all(blocks, "head", 0, 0, tiled=True, axis_index_groups=ALONG_X)
+
+
+def shift_x(blocks):
+    perms = [[(i, (i + 2 * k) % 8) for i in range(8)] for k in range(4)]
+    moved = [lax.ppermute(blocks[k], "head", perms[k]) for k in (2, 1, 3)]
+    return [blocks[0], *moved]
 
 
 def swap_y(value):
@@ -352,30 +378,14 @@
     return near, far
 
 
-def sum_near(grads, near):
-    parts = lax.all_to_all(grads, ("seq", "dp"), 0, 0, tiled=True, axis_index_groups=near)
-    return jnp.sum(parts.astype(F32), axis=0).astype(BF)
-
-
-def sum_far(part, far):
-    if len(far[0]) == 1:
-        return part
-    copies = jnp.broadcast_to(part[None], (len(far[0]), *part.shape))
-    parts = lax.all_to_all(copies, "dp", 0, 0, tiled=True, axis_index_groups=far)
-    return jnp.sum(parts.astype(F32), axis=0).astype(BF)
-
-
-def spread(part, near):
-    copies = jnp.broadcast_to(part[None], (len(near[0]), *part.shape))
-    whole = lax.all_to_all(
-        copies, ("seq", "dp"), 0, 0, tiled=True, axis_index_groups=near
-    )
-    return whole.reshape(len(near[0]) * part.shape[0], part.shape[1])
+def over_near(blocks, near):
+    return lax.all_to_all(blocks, ("seq", "dp"), 0, 0, tiled=True, axis_index_groups=near)
 
 
 def on_device(n_dp, latents, cotangent, w_qkv, w_out):
     depth = latents.shape[-1]
-    at = jnp.stack([lax.axis_index("dp") % 2, lax.axis_index("head") % 2]).astype(jnp.int32)
+    index = lax.axis_index("head")
+    at = jnp.stack([lax.axis_index("dp") % 2, index % 2, index // 2]).astype(jnp.int32)
     near, far = groups_of(n_dp)
     x = latents.reshape(128, depth)
     g = cotangent.reshape(128, depth)
@@ -439,27 +449,30 @@
         scratch_shapes=[pltpu.VMEM((2, 320, 128), F32)],
     )
     gh = over_head(gh)
-    half = shape(112, depth)
-    terms = shape(4, 176, depth)
-    first, second, keep, send = call(
-        spatial_back_kernel, (terms, terms, half, half),
-        at, qkv, gh, hidden, partner, w_own, keep, swap_cores(send, n_dp),
-        in_specs=[SMEM] + [VMEM] * 7,
-    )
-    half_sum, second = call(
-        half_sum_kernel, (shape(176, depth), terms), over_x(first), second,
-        in_specs=[VMEM, ANY],
-        out_specs=(VMEM, ANY),
-        input_output_aliases={1: 1},
-    )
-    n_near = len(near[0])
-    latent_grads, chain = call(
-        last_kernel, (shape(128, depth), shape(n_near, 320 // n_near, depth)),
-        over_x(second), swap_y(half_sum), x, grad_one, keep, swap_cores(send, n_dp), two,
+    parts = over_head((keep.astype(F32) + swap_cores(send, n_dp).astype(F32)).astype(BF))
+    half, row = shape(112, depth), shape(128, depth)
+    *terms, keep, send = call(
+        spatial_back_kernel, (*[row] * 8, half, half),
+        at, qkv, gh, hidden, partner, w_own,
+        in_specs=[SMEM] + [VMEM] * 5,
+        scratch_shapes=[pltpu.VMEM((8, 128, depth), BF)],
+    )
+    n_near, n_far = len(near[0]), len(far[0])
+    size = 320 // n_near
+    chain = call(
+        chain_kernel, shape(n_near, size, depth), keep, swap_cores(send, n_dp), parts, two,
         scratch_shapes=[pltpu.VMEM((320, depth), F32)],
     )
-    part = sum_near(chain, near)
-    mine = spread(sum_far(part, far), near)
+    half, copies = call(
+        half_sum_kernel, (row, shape(n_far, size, depth)),
+        *shift_x(terms[:4]), over_near(chain, near),
+    )
+    summed = lax.all_to_all(copies, "dp", 0, 0, tiled=True, axis_index_groups=far)
+    latent_grads, copies = call(
+        last_kernel, (shape(128, depth), shape(n_near, size, depth)),
+        *shift_x(terms[4:]), swap_y(half), x, grad_one, summed,
+    )
+    mine = over_near(copies, near).reshape(320, depth)
     grad_qkv, grad_out = call(
         result_kernel,
         (

time: 328 us -> 303 us (0.924)
  blocking collectives: 150 us -> 58.9 us
  starting transfers between devices: 52.1 us -> 92.5 us
  waiting for transfers between devices: 56.1 us -> 68.6 us
  local copies, waits for them, and re-layouts: 22 us -> 30.4 us
    all_to_all x4 -> x1, blocking collectives: 104 us -> 22.9 us  [over_near(): lax.all_to_all(blocks, ('seq', 'dp'), 0, 0, tiled=True, axis_index_groups...]
    all_to_all x0 -> x4, starting transfers between devices: none -> 28.1 us  [the longest x1 12.5 us: on_device(): lax.all_to_all(copies, 'dp', 0, 0, tiled=True, axis_index_groups=far)]
    ppermute x0 -> x6, starting transfers between devices: none -> 15.6 us  [shift_x(): moved = [lax.ppermute(blocks[k], 'head', perms[k]) for k in (2, 1, 3)]]
    ppermute x0 -> x6, waiting for transfers between devices: none -> 11.6 us  [shift_x(): moved = [lax.ppermute(blocks[k], 'head', perms[k]) for k in (2, 1, 3)]]
    all_to_all x2 -> x1, blocking collectives: 23.4 us -> 12.7 us  [over_head(): return lax.all_to_all(blocks, 'head', 0, 0, tiled=True)]
    unnamed x50 -> x82, local copies, waits for them, and re-layouts: 18.7 us -> 27.2 us
    all_to_all x0 -> x4, waiting for transfers between devices: none -> 7.09 us  [the longest x2 5.64 us: over_head(): return lax.all_to_all(blocks, 'head', 0, 0, tiled=True)]
    all_to_all x3 -> x2, starting transfers between devices: 15.4 us -> 9.55 us  [over_x(): lax.all_to_all(blocks, 'head', 0, 0, tiled=True, axis_index_groups=ALONG_X)]
  transfers between devices with their start and end apart: 13 -> 22, of which waited for: 8 -> 16; matrix products, arithmetic and copies ran while one was open for 1% -> 2% of each run, Pallas kernels for 3% -> 4%
where the time goes in v10:
time: 303 us; the launch traced here: 299 us
  starting transfers between devices  92.5 us (31%)
  waiting for transfers between devices  68.6 us (23%)
  blocking collectives  58.9 us (19%)
  local copies, waits for them, and re-layouts  30.4 us (10%)
  Pallas kernels  29.5 us (10%)
  between operations  14.3 us (5%)
  other arithmetic  4.46 us (1%)
    all_to_all x2, waiting for transfers between devices, over_x(): lax.all_to_all(blocks, 'head', 0, 0, tiled=True, axis_index_groups=ALONG_X)  32.6 us
    pallas_call x10, Pallas kernels, call(): pl.pallas_call(kernel, out_shape=outs, in_specs=more.pop('in_specs', [VME...  29.5 us
    ppermute x6, starting transfers between devices, swap_cores(): return lax.ppermute(value, 'dp', [(i, i ^ bit) for i in range(n_dp)])  28.5 us
    unnamed x82, local copies, waits for them, and re-layouts  27.2 us
    all_to_all x2, blocking collectives, over_seq(): return lax.all_to_all(blocks, 'seq', 0, 0, tiled=True)  23.3 us
    all_to_all x1, blocking collectives, over_near(): lax.all_to_all(blocks, ('seq', 'dp'), 0, 0, tiled=True, axis_index_groups...  22.9 us
    ppermute x6, starting transfers between devices, shift_x(): moved = [lax.ppermute(blocks[k], 'head', perms[k]) for k in (2, 1, 3)]  15.6 us
    all_to_all x1, blocking collectives, over_head(): return lax.all_to_all(blocks, 'head', 0, 0, tiled=True)  12.7 us
  transfers between devices with their start and end apart: 22, of which 16 were waited for; matrix products, arithmetic and copies ran while one was open for 2% of the time, Pallas kernels for 4%

profile of v10, /device:TPU:7, one launch (start us, length us, event | category | flops | bytes accessed | tf_op | source)
XLA Modules:
  0.0 298.7 jit_solution(953361761898909487)
XLA Ops:
  12.6 4.2 %all-to-all-start = ((bf16[4,168,1152]{2,1,0:T(8,128)(2,1)}), bf16[4,168,1152]{2,1,0:T(8,128)(2,1)S(1)}, u32[]{:S(2)}, u32[]{:S(2)}) async-start(bf16[4,168,1152]{2,1,0:T(8,128)(2,1)} %get-tuple-element.36), calls=%async_computation | async-start | bytes 3096576 | tf_op jit(solution)/shard_map/all_to_all | solution.py:345
  16.8 4.8 %collective-permute-start = (bf16[168,1152]{1,0:T(8,128)(2,1)S(1)}, bf16[168,1152]{1,0:T(8,128)(2,1)S(1)}, u32[]{:S(2)}, u32[]{:S(2)}) collective-permute-start(bf16[168,1152]{1,0:T(8,128)(2,1)S(1)} %get-tuple-element.37), channel_id=1, source_target_pairs={{0,32},{32,0},{64,96},{96,64},{128,160},{160,128},{192,224},{224,1... | collective-permute-start | bytes 1161224 | tf_op jit(solution)/shard_map/ppermute | solution.py:355
  21.6 5.6 %collective-permute-done = bf16[168,1152]{1,0:T(8,128)(2,1)S(1)} collective-permute-done((bf16[168,1152]{1,0:T(8,128)(2,1)S(1)}, bf16[168,1152]{1,0:T(8,128)(2,1)S(1)}, u32[]{:S(2)}, u32[]{:S(2)}) %collective-permute-start) | collective-permute-done | bytes 387104 | tf_op jit(solution)/shard_map/ppermute | solution.py:355
  31.2 5.3 %all-to-all-start.1 = ((bf16[4,168,1152]{2,1,0:T(8,128)(2,1)}), bf16[4,168,1152]{2,1,0:T(8,128)(2,1)S(1)}, u32[]{:S(2)}, u32[]{:S(2)}) async-start(bf16[4,168,1152]{2,1,0:T(8,128)(2,1)} %broadcast_in_dim.12), calls=%async_computation.1 | async-start | bytes 3096576 | tf_op jit(solution)/shard_map/all_to_all | solution.py:345
  38.5 29.8 %all-to-all-done.1.far_ref = bf16[4,168,1152]{2,1,0:T(8,128)(2,1)S(1)} async-done(((bf16[4,168,1152]{2,1,0:T(8,128)(2,1)}), bf16[4,168,1152]{2,1,0:T(8,128)(2,1)S(1)}, u32[]{:S(2)}, u32[]{:S(2)}) %all-to-all-start.1) | async-done | bytes 1548320 | tf_op jit(solution)/shard_map/all_to_all | solution.py:345
  73.3 11.1 %collective-permute-start.1 = (bf16[320,1152]{1,0:T(8,128)(2,1)S(1)}, bf16[320,1152]{1,0:T(8,128)(2,1)S(1)}, u32[]{:S(2)}, u32[]{:S(2)}) collective-permute-start(bf16[320,1152]{1,0:T(8,128)(2,1)S(1)} %bitcast.20), channel_id=1, source_target_pairs={{0,1},{1,0},{2,3},{3,2},{4,5},{5,4},{6,7},{7,6},{8,9},{9,8},{10,11... | collective-permute-start | bytes 2211848 | tf_op jit(solution)/shard_map/ppermute | solution.py:363
  85.2 12.7 %all_to_all.50.heads_ref = bf16[8,72,128]{2,1,0:T(8,128)(2,1)S(1)} all-to-all(bf16[8,72,128]{2,1,0:T(8,128)(2,1)S(1)} %get-tuple-element.38), channel_id=1, replica_groups=mesh['seq'=2,'head'=8,'dp'=32] {'head'}, dimensions={0} | all-to-all | bytes 294912 | tf_op jit(solution)/shard_map/all_to_all | solution.py:341
  107.0 3.2 %collective-permute-start.2 = (bf16[1152,1152]{1,0:T(8,128)(2,1)S(1)}, bf16[1152,1152]{1,0:T(8,128)(2,1)S(1)}, u32[]{:S(2)}, u32[]{:S(2)}) collective-permute-start(bf16[1152,1152]{1,0:T(8,128)(2,1)S(1)} %get-tuple-element.42.mine_ref), channel_id=1, source_target_pairs={{0,1},{1,0},{2,3},{3,2},{4,5},{5,4},{6,7},{7,6},{8,9},{9,8},{10,11... | collective-permute-start | bytes 7962632 | tf_op jit(solution)/shard_map/ppermute | solution.py:363
  110.2 11.3 %all_to_all.51.pair_ref = bf16[2,2,2,32,1152]{4,3,2,1,0:T(8,128)(2,1)S(1)} all-to-all(bf16[2,2,2,32,1152]{4,3,2,1,0:T(8,128)(2,1)S(1)} %get-tuple-element.41), channel_id=1, replica_groups=mesh['seq'=2,'head'=8,'dp'=32] {'seq'}, dimensions={0} | all-to-all | bytes 1179648 | tf_op jit(solution)/shard_map/all_to_all | solution.py:359
  123.0 9.1 %shard_map.78 = (bf16[2,2,2,32,1152]{4,3,2,1,0:T(8,128)(2,1)S(1)}, bf16[1152,1152]{1,0:T(8,128)(2,1)S(1)}, bf16[1152,1152]{1,0:T(8,128)(2,1)}) custom-call(s32[3]{0:T(128)S(1)} %pad_add_fusion.at_ref.core_ref, bf16[2,2,2,32,1152]{4,3,2,1,0:T(8,128)(2,1)S(1)} %all_to_all.51.pair_ref, bf16[1152,1152]{1,0:T(8,128)(2,1)} %copy-done.2, bf16[1152,1152]{1,0:T(8,128)(2,1)} %copy-done.40), custom_call_target="tpu_custom_call" | custom-call | tf_op jit(solution)/shard_map/pallas_call | solution.py:329
  135.6 4.8 %collective-permute-done.11 = bf16[1152,1152]{1,0:T(8,128)(2,1)S(1)} collective-permute-done((bf16[1152,1152]{1,0:T(8,128)(2,1)}, bf16[1152,1152]{1,0:T(8,128)(2,1)S(1)}, u32[]{:S(2)}, u32[]{:S(2)}) %collective-permute-start.11) | collective-permute-done | bytes 2654240 | tf_op jit(solution)/shard_map/ppermute | solution.py:363
  142.6 12.1 %all_to_all.52.back_ref = bf16[2,2,2,32,1152]{4,3,2,1,0:T(8,128)(2,1)S(1)} all-to-all(bf16[2,2,2,32,1152]{4,3,2,1,0:T(8,128)(2,1)} %copy-done.18), channel_id=1, replica_groups=mesh['seq'=2,'head'=8,'dp'=32] {'seq'}, dimensions={0} | all-to-all | bytes 1179648 | tf_op jit(solution)/shard_map/all_to_all | solution.py:359
  163.5 5.4 %all-to-all-start.5 = ((bf16[8,72,128]{2,1,0:T(8,128)(2,1)}), bf16[8,72,128]{2,1,0:T(8,128)(2,1)S(1)}, u32[]{:S(2)}, u32[]{:S(2)}) async-start(bf16[8,72,128]{2,1,0:T(8,128)(2,1)} %copy-done.32), calls=%async_computation.5 | async-start | bytes 294912 | tf_op jit(solution)/shard_map/all_to_all | solution.py:341
  171.1 4.3 %all-to-all-done.5.gh_ref = bf16[8,72,128]{2,1,0:T(8,128)(2,1)S(1)} async-done(((bf16[8,72,128]{2,1,0:T(8,128)(2,1)}), bf16[8,72,128]{2,1,0:T(8,128)(2,1)S(1)}, u32[]{:S(2)}, u32[]{:S(2)}) %all-to-all-start.5) | async-done | bytes 147488 | tf_op jit(solution)/shard_map/all_to_all | solution.py:341
  175.4 5.3 %all-to-all-start.6 = ((bf16[8,40,1152]{2,1,0:T(8,128)(2,1)}), bf16[8,40,1152]{2,1,0:T(8,128)(2,1)S(1)}, u32[]{:S(2)}, u32[]{:S(2)}) async-start(bf16[8,40,1152]{2,1,0:T(8,128)(2,1)} %add_convert_fusion.1), calls=%async_computation.6 | async-start | bytes 1474560 | tf_op jit(solution)/shard_map/all_to_all | solution.py:341
  180.7 6.4 %shard_map.80 = (bf16[128,1152]{1,0:T(8,128)(2,1)S(1)}, bf16[128,1152]{1,0:T(8,128)(2,1)}, bf16[128,1152]{1,0:T(8,128)(2,1)}, bf16[128,1152]{1,0:T(8,128)(2,1)S(...) custom-call(s32[3]{0:T(128)S(1)} %pad_add_fusion.at_ref.core_ref, ...), custom_call_target="tpu_custom_call" | custom-call | tf_op jit(solution)/shard_map/pallas_call | solution.py:329
  192.1 3.3 %collective-permute-start.9 = (bf16[112,1152]{1,0:T(8,128)(2,1)S(1)}, bf16[112,1152]{1,0:T(8,128)(2,1)S(1)}, u32[]{:S(2)}, u32[]{:S(2)}) collective-permute-start(bf16[112,1152]{1,0:T(8,128)(2,1)S(1)} %get-tuple-element.56), channel_id=1, source_target_pairs={{0,1},{1,0},{2,3},{3,2},{4,5},{5,4},{6,7},{7,6},{8,9},{9,8},{10,11... | collective-permute-start | bytes 774152 | tf_op jit(solution)/shard_map/ppermute | solution.py:363
  203.3 4.9 %all-to-all-start.7 = ((bf16[8,40,1152]{2,1,0:T(8,128)(2,1)}), bf16[8,40,1152]{2,1,0:T(8,128)(2,1)S(1)}, u32[]{:S(2)}, u32[]{:S(2)}) async-start(bf16[8,40,1152]{2,1,0:T(8,128)(2,1)} %shard_map.81), calls=%async_computation.8 | async-start | bytes 1474560 | tf_op jit(solution)/shard_map/all_to_all | solution.py:382
  217.4 4.8 %collective-permute-done.7.t2_ref = bf16[128,1152]{1,0:T(8,128)(2,1)S(1)} collective-permute-done((bf16[128,1152]{1,0:T(8,128)(2,1)}, bf16[128,1152]{1,0:T(8,128)(2,1)S(1)}, u32[]{:S(2)}, u32[]{:S(2)}) %collective-permute-start.7) | collective-permute-done | bytes 294944 | tf_op jit(solution)/shard_map/ppermute | solution.py:350
  225.6 12.5 %all-to-all-start.8 = ((bf16[4,40,1152]{2,1,0:T(8,128)(2,1)}), bf16[4,40,1152]{2,1,0:T(8,128)(2,1)S(1)}, u32[]{:S(2)}, u32[]{:S(2)}) async-start(bf16[4,40,1152]{2,1,0:T(8,128)(2,1)} %get-tuple-element.63), calls=%async_computation.9 | async-start | bytes 737280 | tf_op jit(solution)/shard_map/all_to_all | solution.py:470
  240.5 4.1 %collective-permute-start.4 = (bf16[128,1152]{1,0:T(8,128)(2,1)S(1)}, bf16[128,1152]{1,0:T(8,128)(2,1)S(1)}, u32[]{:S(2)}, u32[]{:S(2)}) collective-permute-start(bf16[128,1152]{1,0:T(8,128)(2,1)S(1)} %copy-done.36), channel_id=1, source_target_pairs={{0,64},{32,96},{64,128},{96,160},{128,192},{160,224},{192,0},{224,... | collective-permute-start | bytes 884744 | tf_op jit(solution)/shard_map/ppermute | solution.py:350
  246.6 5.9 %collective-permute-start.12 = (bf16[128,1152]{1,0:T(8,128)(2,1)}, bf16[128,1152]{1,0:T(8,128)(2,1)S(1)}, u32[]{:S(2)}, u32[]{:S(2)}) collective-permute-start(bf16[128,1152]{1,0:T(8,128)(2,1)} %copy-done.39), channel_id=1, source_target_pairs={{0,32},{32,0},{64,96},{96,64},{128,160},{160,128},{192,224},{224,1... | collective-permute-start | bytes 884744 | tf_op jit(solution)/shard_map/ppermute | solution.py:355
  259.9 22.9 %all_to_all.53 = bf16[8,40,1152]{2,1,0:T(8,128)(2,1)S(1)} all-to-all(bf16[8,40,1152]{2,1,0:T(8,128)(2,1)S(1)} %get-tuple-element.65), channel_id=1, replica_groups={{0,2,4,6,256,258,260,262},{1,3,5,7,257,259,261,263},{8,10,12,14,264,266..., dimensions={0} | all-to-all | bytes 1474560 | tf_op jit(solution)/shard_map/all_to_all | solution.py:382
  282.8 4.9 %collective-permute-start.13 = (bf16[320,1152]{1,0:T(8,128)(2,1)S(1)}, bf16[320,1152]{1,0:T(8,128)(2,1)S(1)}, u32[]{:S(2)}, u32[]{:S(2)}) collective-permute-start(bf16[320,1152]{1,0:T(8,128)(2,1)S(1)} %bitcast.23), channel_id=1, source_target_pairs={{0,1},{1,0},{2,3},{3,2},{4,5},{5,4},{6,7},{7,6},{8,9},{9,8},{10,11... | collective-permute-start | bytes 2211848 | tf_op jit(solution)/shard_map/ppermute | solution.py:363
  (123 shorter events, 85.6 us)
Async XLA Ops:
  7.2 91.6 %all-gather.3.cloned.1.call-start = ((), (), s32[]{:S(2)}) async-start(), calls=%async_computation.12 | async-start | bytes 2985984 | tf_op jit(solution)/shard_map/all_gather | solution.py:399
  12.6 17.4 %all-to-all-start = ((bf16[4,168,1152]{2,1,0:T(8,128)(2,1)}), bf16[4,168,1152]{2,1,0:T(8,128)(2,1)S(1)}, u32[]{:S(2)}, u32[]{:S(2)}) async-start(bf16[4,168,1152]{2,1,0:T(8,128)(2,1)} %get-tuple-element.36), calls=%async_computation | async-start | bytes 3096576 | tf_op jit(solution)/shard_map/all_to_all | solution.py:345
  16.8 10.4 %collective-permute-start = (bf16[168,1152]{1,0:T(8,128)(2,1)S(1)}, bf16[168,1152]{1,0:T(8,128)(2,1)S(1)}, u32[]{:S(2)}, u32[]{:S(2)}) collective-permute-start(bf16[168,1152]{1,0:T(8,128)(2,1)S(1)} %get-tuple-element.37), channel_id=1, source_target_pairs={{0,32},{32,0},{64,96},{96,64},{128,160},{160,128},{192,224},{224,1... | collective-permute-start | bytes 1161224 | tf_op jit(solution)/shard_map/ppermute | solution.py:355
  31.2 37.1 %all-to-all-start.1 = ((bf16[4,168,1152]{2,1,0:T(8,128)(2,1)}), bf16[4,168,1152]{2,1,0:T(8,128)(2,1)S(1)}, u32[]{:S(2)}, u32[]{:S(2)}) async-start(bf16[4,168,1152]{2,1,0:T(8,128)(2,1)} %broadcast_in_dim.12), calls=%async_computation.1 | async-start | bytes 3096576 | tf_op jit(solution)/shard_map/all_to_all | solution.py:345
  36.5 62.2 %copy-start.12 = (bf16[1,2,64,1152]{3,2,1,0:T(8,128)(2,1)S(1)}, bf16[1,2,64,1152]{3,2,1,0:T(8,128)(2,1)}, u32[]{:S(2)}) copy-start(bf16[1,2,64,1152]{3,2,1,0:T(8,128)(2,1)} %param.4) | copy-start | bytes 884740
  36.5 163.8 %reduce-scatter.2.cloned.1.call-start = ((), (), s32[]{:S(2)}) async-start(), calls=%async_computation.11 | async-start | bytes 2985984 | tf_op jit(solution)/shard_map/reduce_scatter | solution.py:440
  73.3 24.6 %collective-permute-start.1 = (bf16[320,1152]{1,0:T(8,128)(2,1)S(1)}, bf16[320,1152]{1,0:T(8,128)(2,1)S(1)}, u32[]{:S(2)}, u32[]{:S(2)}) collective-permute-start(bf16[320,1152]{1,0:T(8,128)(2,1)S(1)} %bitcast.20), channel_id=1, source_target_pairs={{0,1},{1,0},{2,3},{3,2},{4,5},{5,4},{6,7},{7,6},{8,9},{9,8},{10,11... | collective-permute-start | bytes 2211848 | tf_op jit(solution)/shard_map/ppermute | solution.py:363
  107.0 14.5 %collective-permute-start.2 = (bf16[1152,1152]{1,0:T(8,128)(2,1)S(1)}, bf16[1152,1152]{1,0:T(8,128)(2,1)S(1)}, u32[]{:S(2)}, u32[]{:S(2)}) collective-permute-start(bf16[1152,1152]{1,0:T(8,128)(2,1)S(1)} %get-tuple-element.42.mine_ref), channel_id=1, source_target_pairs={{0,1},{1,0},{2,3},{3,2},{4,5},{5,4},{6,7},{7,6},{8,9},{9,8},{10,11... | collective-permute-start | bytes 7962632 | tf_op jit(solution)/shard_map/ppermute | solution.py:363
  132.9 7.5 %collective-permute-start.11 = (bf16[1152,1152]{1,0:T(8,128)(2,1)}, bf16[1152,1152]{1,0:T(8,128)(2,1)S(1)}, u32[]{:S(2)}, u32[]{:S(2)}) collective-permute-start(bf16[1152,1152]{1,0:T(8,128)(2,1)} %get-tuple-element.60), channel_id=1, source_target_pairs={{0,1},{1,0},{2,3},{3,2},{4,5},{5,4},{6,7},{7,6},{8,9},{9,8},{10,11... | collective-permute-start | bytes 7962632 | tf_op jit(solution)/shard_map/ppermute | solution.py:363
  160.3 8.6 %collective-permute-start.10 = (bf16[8,40,1152]{2,1,0:T(8,128)(2,1)}, bf16[8,40,1152]{2,1,0:T(8,128)(2,1)S(1)}, u32[]{:S(2)}, u32[]{:S(2)}) collective-permute-start(bf16[8,40,1152]{2,1,0:T(8,128)(2,1)} %get-tuple-element.58), channel_id=1, source_target_pairs={{0,1},{1,0},{2,3},{3,2},{4,5},{5,4},{6,7},{7,6},{8,9},{9,8},{10,11... | collective-permute-start | bytes 2211848 | tf_op jit(solution)/shard_map/ppermute | solution.py:363
  163.5 11.9 %all-to-all-start.5 = ((bf16[8,72,128]{2,1,0:T(8,128)(2,1)}), bf16[8,72,128]{2,1,0:T(8,128)(2,1)S(1)}, u32[]{:S(2)}, u32[]{:S(2)}) async-start(bf16[8,72,128]{2,1,0:T(8,128)(2,1)} %copy-done.32), calls=%async_computation.5 | async-start | bytes 294912 | tf_op jit(solution)/shard_map/all_to_all | solution.py:341
  175.4 22.5 %all-to-all-start.6 = ((bf16[8,40,1152]{2,1,0:T(8,128)(2,1)}), bf16[8,40,1152]{2,1,0:T(8,128)(2,1)S(1)}, u32[]{:S(2)}, u32[]{:S(2)}) async-start(bf16[8,40,1152]{2,1,0:T(8,128)(2,1)} %add_convert_fusion.1), calls=%async_computation.6 | async-start | bytes 1474560 | tf_op jit(solution)/shard_map/all_to_all | solution.py:341
  192.1 4.5 %collective-permute-start.9 = (bf16[112,1152]{1,0:T(8,128)(2,1)S(1)}, bf16[112,1152]{1,0:T(8,128)(2,1)S(1)}, u32[]{:S(2)}, u32[]{:S(2)}) collective-permute-start(bf16[112,1152]{1,0:T(8,128)(2,1)S(1)} %get-tuple-element.56), channel_id=1, source_target_pairs={{0,1},{1,0},{2,3},{3,2},{4,5},{5,4},{6,7},{7,6},{8,9},{9,8},{10,11... | collective-permute-start | bytes 774152 | tf_op jit(solution)/shard_map/ppermute | solution.py:363
  203.3 55.3 %copy-start.27 = (bf16[128,1152]{1,0:T(8,128)(2,1)S(1)}, bf16[128,1152]{1,0:T(8,128)(2,1)}, u32[]{:S(2)}) copy-start(bf16[128,1152]{1,0:T(8,128)(2,1)} %copy-done.26) | copy-start | bytes 884740
  203.3 20.7 %all-to-all-start.7 = ((bf16[8,40,1152]{2,1,0:T(8,128)(2,1)}), bf16[8,40,1152]{2,1,0:T(8,128)(2,1)S(1)}, u32[]{:S(2)}, u32[]{:S(2)}) async-start(bf16[8,40,1152]{2,1,0:T(8,128)(2,1)} %shard_map.81), calls=%async_computation.8 | async-start | bytes 1474560 | tf_op jit(solution)/shard_map/all_to_all | solution.py:382
  208.2 9.2 %collective-permute-start.6 = (bf16[128,1152]{1,0:T(8,128)(2,1)}, bf16[128,1152]{1,0:T(8,128)(2,1)S(1)}, u32[]{:S(2)}, u32[]{:S(2)}) collective-permute-start(bf16[128,1152]{1,0:T(8,128)(2,1)} %get-tuple-element.52), channel_id=1, source_target_pairs={{0,128},{32,160},{64,192},{96,224},{128,0},{160,32},{192,64},{224,... | collective-permute-start | bytes 884744 | tf_op jit(solution)/shard_map/ppermute | solution.py:350
  210.2 12.1 %collective-permute-start.7 = (bf16[128,1152]{1,0:T(8,128)(2,1)}, bf16[128,1152]{1,0:T(8,128)(2,1)S(1)}, u32[]{:S(2)}, u32[]{:S(2)}) collective-permute-start(bf16[128,1152]{1,0:T(8,128)(2,1)} %get-tuple-element.53), channel_id=1, source_target_pairs={{0,64},{32,96},{64,128},{96,160},{128,192},{160,224},{192,0},{224,... | collective-permute-start | bytes 884744 | tf_op jit(solution)/shard_map/ppermute | solution.py:350
  213.4 10.6 %collective-permute-start.8 = (bf16[128,1152]{1,0:T(8,128)(2,1)}, bf16[128,1152]{1,0:T(8,128)(2,1)S(1)}, u32[]{:S(2)}, u32[]{:S(2)}) collective-permute-start(bf16[128,1152]{1,0:T(8,128)(2,1)} %copy-done.38), channel_id=1, source_target_pairs={{0,192},{32,224},{64,0},{96,32},{128,64},{160,96},{192,128},{224,1... | collective-permute-start | bytes 884744 | tf_op jit(solution)/shard_map/ppermute | solution.py:350
  225.6 33.0 %all-to-all-start.8 = ((bf16[4,40,1152]{2,1,0:T(8,128)(2,1)}), bf16[4,40,1152]{2,1,0:T(8,128)(2,1)S(1)}, u32[]{:S(2)}, u32[]{:S(2)}) async-start(bf16[4,40,1152]{2,1,0:T(8,128)(2,1)} %get-tuple-element.63), calls=%async_computation.9 | async-start | bytes 737280 | tf_op jit(solution)/shard_map/all_to_all | solution.py:470
  238.1 14.4 %collective-permute-start.3 = (bf16[128,1152]{1,0:T(8,128)(2,1)}, bf16[128,1152]{1,0:T(8,128)(2,1)S(1)}, u32[]{:S(2)}, u32[]{:S(2)}) collective-permute-start(bf16[128,1152]{1,0:T(8,128)(2,1)} %copy-done.37), channel_id=1, source_target_pairs={{0,128},{32,160},{64,192},{96,224},{128,0},{160,32},{192,64},{224,... | collective-permute-start | bytes 884744 | tf_op jit(solution)/shard_map/ppermute | solution.py:350
  240.5 12.7 %collective-permute-start.4 = (bf16[128,1152]{1,0:T(8,128)(2,1)S(1)}, bf16[128,1152]{1,0:T(8,128)(2,1)S(1)}, u32[]{:S(2)}, u32[]{:S(2)}) collective-permute-start(bf16[128,1152]{1,0:T(8,128)(2,1)S(1)} %copy-done.36), channel_id=1, source_target_pairs={{0,64},{32,96},{64,128},{96,160},{128,192},{160,224},{192,0},{224,... | collective-permute-start | bytes 884744 | tf_op jit(solution)/shard_map/ppermute | solution.py:350
  244.6 11.0 %collective-permute-start.5 = (bf16[128,1152]{1,0:T(8,128)(2,1)S(1)}, bf16[128,1152]{1,0:T(8,128)(2,1)S(1)}, u32[]{:S(2)}, u32[]{:S(2)}) collective-permute-start(bf16[128,1152]{1,0:T(8,128)(2,1)S(1)} %copy-done.34), channel_id=1, source_target_pairs={{0,192},{32,224},{64,0},{96,32},{128,64},{160,96},{192,128},{224,1... | collective-permute-start | bytes 884744 | tf_op jit(solution)/shard_map/ppermute | solution.py:350
  246.6 10.5 %collective-permute-start.12 = (bf16[128,1152]{1,0:T(8,128)(2,1)}, bf16[128,1152]{1,0:T(8,128)(2,1)S(1)}, u32[]{:S(2)}, u32[]{:S(2)}) collective-permute-start(bf16[128,1152]{1,0:T(8,128)(2,1)} %copy-done.39), channel_id=1, source_target_pairs={{0,32},{32,0},{64,96},{96,64},{128,160},{160,128},{192,224},{224,1... | collective-permute-start | bytes 884744 | tf_op jit(solution)/shard_map/ppermute | solution.py:355
  282.8 6.7 %collective-permute-start.13 = (bf16[320,1152]{1,0:T(8,128)(2,1)S(1)}, bf16[320,1152]{1,0:T(8,128)(2,1)S(1)}, u32[]{:S(2)}, u32[]{:S(2)}) collective-permute-start(bf16[320,1152]{1,0:T(8,128)(2,1)S(1)} %bitcast.23), channel_id=1, source_target_pairs={{0,1},{1,0},{2,3},{3,2},{4,5},{5,4},{6,7},{7,6},{8,9},{9,8},{10,11... | collective-permute-start | bytes 2211848 | tf_op jit(solution)/shard_map/ppermute | solution.py:363
  (39 other events, 345.5 us)
Sparse Core Ops, SparseCore 0:
  12.7 64.7 all-gather.2
  142.7 57.5 reduce-scatter.1

commit v11 on v10

--- a/solution.py
+++ b/solution.py
@@ -225,7 +225,7 @@
 
 def spatial_back_kernel(
     at_ref, qkv_ref, gh_ref, near_ref, far_ref, w_ref,
-    a0_ref, a1_ref, a2_ref, a3_ref, b0_ref, b1_ref, b2_ref, b3_ref, keep_ref, send_ref, rows_ref,
+    a0_ref, a1_ref, a2_ref, a3_ref, b0_ref, b1_ref, b2_ref, b3_ref, keep_ref, send_ref, rows_ref, sems,
 ):
     frames = ([], [])
     for m in range(4):
@@ -247,14 +247,19 @@
         terms = tn(grads, w_ref[...]).astype(BF)
         for j in range(8):
             rows_ref[j, f * 64 : (f + 1) * 64, :] = terms[j * 64 : (j + 1) * 64]
+    copies = []
     ahead = ((a0_ref, b0_ref), (a1_ref, b1_ref), (a2_ref, b2_ref), (a3_ref, b3_ref))
     for k, (other_ref, own_ref) in enumerate(ahead):
         x_at = lax.rem(at_ref[2] + k, 4)
-        own_ref[...] = rows_ref[x_at]
-        other_ref[...] = rows_ref[4 + x_at]
+        copies.append(pltpu.make_async_copy(rows_ref.at[x_at], own_ref, sems.at[k]))
+        copies.append(pltpu.make_async_copy(rows_ref.at[4 + x_at], other_ref, sems.at[4 + k]))
+    for copy in copies:
+        copy.start()
     low, high = halves(total, 112)
     keep_ref[...] = jnp.where(at_ref[0] == 0, low, high).astype(BF)
     send_ref[...] = jnp.where(at_ref[0] == 0, high, low).astype(BF)
+    for copy in copies:
+        copy.wait()
 
 
 def result_kernel(core_ref, mine_ref, other_ref, qkv_ref, out_ref, both_ref):
@@ -317,21 +322,47 @@
 
 VMEM = pl.BlockSpec(memory_space=pltpu.VMEM)
 SMEM = pl.BlockSpec(memory_space=pltpu.SMEM)
-ANY = pl.BlockSpec(memory_space=pl.ANY)
-PARAMS = pltpu.CompilerParams(vmem_limit_bytes=48 * 1024 * 1024)
+HBM = pl.BlockSpec(memory_space=pltpu.HBM)
+MIB = 1024 * 1024
 
 
 def shape(*dims):
     return jax.ShapeDtypeStruct(dims, BF)
 
 
-def call(kernel, outs, *args, **more):
+def call(kernel, outs, *args, mib=48, fetch=(), in_specs=None, scratch_shapes=(), **more):
+    specs = list(in_specs or [VMEM] * len(args))
+    scratch = list(scratch_shapes)
+    moved = list(fetch)
+    n_in, n_out, n_own = len(args), len(jax.tree.leaves(outs)), len(scratch)
+
+    def fetching(*refs):
+        ins = list(refs[:n_in])
+        rest = refs[n_in : n_in + n_out + n_own]
+        held, sems = refs[n_in + n_out + n_own : -1], refs[-1]
+        copies = [
+            pltpu.make_async_copy(ins[i], to, sems.at[k])
+            for k, (i, to) in enumerate(zip(moved, held))
+        ]
+        for copy in copies:
+            copy.start()
+        for copy in copies:
+            copy.wait()
+        for i, to in zip(moved, held):
+            ins[i] = to
+        kernel(*ins, *rest)
+
+    if moved:
+        scratch += [pltpu.VMEM(args[i].shape, args[i].dtype) for i in moved]
+        scratch.append(pltpu.SemaphoreType.DMA((len(moved),)))
+        specs = [HBM if i in moved else spec for i, spec in enumerate(specs)]
     return pl.pallas_call(
-        kernel,
+        fetching if moved else kernel,
         out_shape=outs,
-        in_specs=more.pop("in_specs", [VMEM] * len(args)),
+        in_specs=specs,
         out_specs=more.pop("out_specs", jax.tree.map(lambda _: VMEM, outs)),
-        compiler_params=PARAMS,
+        scratch_shapes=scratch,
+        compiler_params=pltpu.CompilerParams(vmem_limit_bytes=mib * MIB),
         cost_estimate=pl.CostEstimate(flops=0, bytes_accessed=0, transcendentals=0),
         **more,
     )(*args)
@@ -394,7 +425,7 @@
     hidden, row, own = call(
         norm_kernel, (shape(4, 168, depth), shape(168, depth), shape(2 * E, depth)),
         at, x, w_qkv.reshape(2, 3, E, depth), w_out.reshape(2, E, depth),
-        in_specs=[SMEM] + [VMEM] * 3,
+        in_specs=[SMEM] + [VMEM] * 3, fetch=(1, 2, 3), mib=60,
     )
     mine_two = lax.all_gather(own, "head", axis_index_groups=RING).reshape(16 * E, depth)
     hidden = over_x(hidden)
@@ -412,8 +443,8 @@
     pair, mine_two = call(
         middle_kernel, (shape(2, 2, 2, 32, depth), big),
         at, x, g, heads, mine_one, other_one, mine_two,
-        in_specs=[SMEM] + [VMEM] * 5 + [ANY],
-        out_specs=(VMEM, ANY),
+        in_specs=[SMEM] + [VMEM] * 5 + [HBM], fetch=(1, 2, 3, 4, 5), mib=62,
+        out_specs=(VMEM, HBM),
         input_output_aliases={6: 1},
         scratch_shapes=[pltpu.VMEM((2, 320, 128), F32)],
     )
@@ -423,8 +454,8 @@
         temporal_kernel,
         (shape(2, 2, 2, 32, depth), big, big),
         at, pair, mine_two, other_two,
-        in_specs=[SMEM, VMEM, ANY, ANY],
-        out_specs=(VMEM, ANY, ANY),
+        in_specs=[SMEM, VMEM, HBM, HBM],
+        out_specs=(VMEM, HBM, HBM),
         scratch_shapes=[
             pltpu.VMEM((2, 16 * E, depth), BF),
             pltpu.VMEM((2, 16 * E, depth), BF),
@@ -454,8 +485,9 @@
     *terms, keep, send = call(
         spatial_back_kernel, (*[row] * 8, half, half),
         at, qkv, gh, hidden, partner, w_own,
-        in_specs=[SMEM] + [VMEM] * 5,
-        scratch_shapes=[pltpu.VMEM((8, 128, depth), BF)],
+        in_specs=[SMEM] + [VMEM] * 5, fetch=(1, 2, 3, 4, 5), mib=62,
+        out_specs=(*[HBM] * 8, VMEM, VMEM),
+        scratch_shapes=[pltpu.VMEM((8, 128, depth), BF), pltpu.SemaphoreType.DMA((8,))],
     )
     n_near, n_far = len(near[0]), len(far[0])
     size = 320 // n_near
@@ -471,6 +503,7 @@
     latent_grads, copies = call(
         last_kernel, (shape(128, depth), shape(n_near, size, depth)),
         *shift_x(terms[4:]), swap_y(half), x, grad_one, summed,
+        fetch=(0, 1, 2, 3, 4, 5, 6, 7), mib=60,
     )
     mine = over_near(copies, near).reshape(320, depth)
     grad_qkv, grad_out = call(

time: 303 us -> 299 us (0.987)
  local copies, waits for them, and re-layouts: 30.4 us -> 8.93 us
  waiting for transfers between devices: 68.6 us -> 79.5 us
  Pallas kernels: 29.5 us -> 39 us
  blocking collectives: 58.9 us -> 63.1 us
  starting transfers between devices: 92.5 us -> 88.4 us
    unnamed x82 -> x56, local copies, waits for them, and re-layouts: 27.2 us -> 7.54 us
    pallas_call x10, Pallas kernels: 29.5 us -> 39 us  [call(): pl.pallas_call(fetching if moved else kernel, out_shape=outs, in_specs=sp...]
    all_to_all x1, blocking collectives: 22.9 us -> 27.8 us  [over_near(): lax.all_to_all(blocks, ('seq', 'dp'), 0, 0, tiled=True, axis_index_groups...]
    ppermute x6, waiting for transfers between devices: 11.6 us -> 15.7 us  [shift_x(): moved = [lax.ppermute(blocks[k], 'head', perms[k]) for k in (2, 1, 3)]]
    all_to_all x2, waiting for transfers between devices: 5.64 us -> 9.14 us  [over_head(): return lax.all_to_all(blocks, 'head', 0, 0, tiled=True)]
  transfers between devices with their start and end apart: 22 -> 22, of which waited for: 16 -> 15; matrix products, arithmetic and copies ran while one was open for 2% -> 1% of each run, Pallas kernels for 4% -> 5%
where the time goes in v11:
time: 299 us; the launch traced here: 297 us
  starting transfers between devices  88.4 us (30%)
  waiting for transfers between devices  79.5 us (27%)
  blocking collectives  63.1 us (21%)
  Pallas kernels  39 us (13%)
  between operations  14.4 us (5%)
  local copies, waits for them, and re-layouts  8.93 us (3%)
  other arithmetic  3.87 us (1%)
    pallas_call x10, Pallas kernels, call(): pl.pallas_call(fetching if moved else kernel, out_shape=outs, in_specs=sp...  39 us
    all_to_all x2, waiting for transfers between devices, over_x(): lax.all_to_all(blocks, 'head', 0, 0, tiled=True, axis_index_groups=ALONG_X)  35.1 us
    all_to_all x1, blocking collectives, over_near(): lax.all_to_all(blocks, ('seq', 'dp'), 0, 0, tiled=True, axis_index_groups...  27.8 us
    ppermute x6, starting transfers between devices, swap_cores(): return lax.ppermute(value, 'dp', [(i, i ^ bit) for i in range(n_dp)])  27.7 us
    all_to_all x2, blocking collectives, over_seq(): return lax.all_to_all(blocks, 'seq', 0, 0, tiled=True)  23.3 us
    ppermute x6, starting transfers between devices, shift_x(): moved = [lax.ppermute(blocks[k], 'head', perms[k]) for k in (2, 1, 3)]  16.8 us
    ppermute x6, waiting for transfers between devices, shift_x(): moved = [lax.ppermute(blocks[k], 'head', perms[k]) for k in (2, 1, 3)]  15.7 us
    all_to_all x1, blocking collectives, over_head(): return lax.all_to_all(blocks, 'head', 0, 0, tiled=True)  11.9 us
  transfers between devices with their start and end apart: 22, of which 15 were waited for; matrix products, arithmetic and copies ran while one was open for 1% of the time, Pallas kernels for 5%

profile of v11, /device:TPU:7, one launch (start us, length us, event | category | flops | bytes accessed | tf_op | source)
XLA Modules:
  0.0 297.1 jit_solution(10665274306059091158)
XLA Ops:
  11.7 4.4 %all-to-all-start = ((bf16[4,168,1152]{2,1,0:T(8,128)(2,1)}), bf16[4,168,1152]{2,1,0:T(8,128)(2,1)S(1)}, u32[]{:S(2)}, u32[]{:S(2)}) async-start(bf16[4,168,1152]{2,1,0:T(8,128)(2,1)} %get-tuple-element.36), calls=%async_computation | async-start | bytes 3096576 | tf_op jit(solution)/shard_map/all_to_all | solution.py:376
  16.1 4.9 %collective-permute-start = (bf16[168,1152]{1,0:T(8,128)(2,1)S(1)}, bf16[168,1152]{1,0:T(8,128)(2,1)S(1)}, u32[]{:S(2)}, u32[]{:S(2)}) collective-permute-start(bf16[168,1152]{1,0:T(8,128)(2,1)S(1)} %copy-done.23), channel_id=1, source_target_pairs={{0,32},{32,0},{64,96},{96,64},{128,160},{160,128},{192,224},{224,1... | collective-permute-start | bytes 1161224 | tf_op jit(solution)/shard_map/ppermute | solution.py:386
  21.0 5.6 %collective-permute-done = bf16[168,1152]{1,0:T(8,128)(2,1)S(1)} collective-permute-done((bf16[168,1152]{1,0:T(8,128)(2,1)S(1)}, bf16[168,1152]{1,0:T(8,128)(2,1)S(1)}, u32[]{:S(2)}, u32[]{:S(2)}) %collective-permute-start) | collective-permute-done | bytes 387104 | tf_op jit(solution)/shard_map/ppermute | solution.py:386
  30.5 6.1 %all-to-all-start.1 = ((bf16[4,168,1152]{2,1,0:T(8,128)(2,1)}), bf16[4,168,1152]{2,1,0:T(8,128)(2,1)}, u32[]{:S(2)}, u32[]{:S(2)}) async-start(bf16[4,168,1152]{2,1,0:T(8,128)(2,1)} %broadcast_in_dim.12), calls=%async_computation.1 | async-start | bytes 3096576 | tf_op jit(solution)/shard_map/all_to_all | solution.py:376
  36.7 32.6 %all-to-all-done.1.far_ref.refs_4_ = bf16[4,168,1152]{2,1,0:T(8,128)(2,1)} async-done(((bf16[4,168,1152]{2,1,0:T(8,128)(2,1)}), bf16[4,168,1152]{2,1,0:T(8,128)(2,1)}, u32[]{:S(2)}, u32[]{:S(2)}) %all-to-all-start.1) | async-done | bytes 1548320 | tf_op jit(solution)/shard_map/all_to_all | solution.py:376
  74.7 10.3 %collective-permute-start.1 = (bf16[320,1152]{1,0:T(8,128)(2,1)S(1)}, bf16[320,1152]{1,0:T(8,128)(2,1)S(1)}, u32[]{:S(2)}, u32[]{:S(2)}) collective-permute-start(bf16[320,1152]{1,0:T(8,128)(2,1)S(1)} %bitcast.20), channel_id=1, source_target_pairs={{0,1},{1,0},{2,3},{3,2},{4,5},{5,4},{6,7},{7,6},{8,9},{9,8},{10,11... | collective-permute-start | bytes 2211848 | tf_op jit(solution)/shard_map/ppermute | solution.py:394
  85.0 11.9 %all_to_all.50.refs_3_.heads_ref = bf16[8,72,128]{2,1,0:T(8,128)(2,1)} all-to-all(bf16[8,72,128]{2,1,0:T(8,128)(2,1)S(1)} %get-tuple-element.38), channel_id=1, replica_groups=mesh['seq'=2,'head'=8,'dp'=32] {'head'}, dimensions={0} | all-to-all | bytes 294912 | tf_op jit(solution)/shard_map/all_to_all | solution.py:372
  104.8 12.3 %all_to_all.51.pair_ref = bf16[2,2,2,32,1152]{4,3,2,1,0:T(8,128)(2,1)S(1)} all-to-all(bf16[2,2,2,32,1152]{4,3,2,1,0:T(8,128)(2,1)} %get-tuple-element.41), channel_id=1, replica_groups=mesh['seq'=2,'head'=8,'dp'=32] {'seq'}, dimensions={0} | all-to-all | bytes 1179648 | tf_op jit(solution)/shard_map/all_to_all | solution.py:390
  118.7 9.1 %shard_map.78 = (bf16[2,2,2,32,1152]{4,3,2,1,0:T(8,128)(2,1)S(1)}, bf16[1152,1152]{1,0:T(8,128)(2,1)S(1)}, bf16[1152,1152]{1,0:T(8,128)(2,1)}) custom-call(s32[3]{0:T(128)S(1)} %copy-done.13, bf16[2,2,2,32,1152]{4,3,2,1,0:T(8,128)(2,1)S(1)} %all_to_all.51.pair_ref, bf16[1152,1152]{1,0:T(8,128)(2,1)} %get-tuple-element.42.mine_ref, bf16[1152,1152]{1,0:T(8,128)(2,1)} %copy-done.15), custom_call_target="tpu_custom_call" | custom-call | tf_op jit(solution)/shard_map/pallas_call | solution.py:359
  130.5 4.8 %collective-permute-done.11 = bf16[1152,1152]{1,0:T(8,128)(2,1)S(1)} collective-permute-done((bf16[1152,1152]{1,0:T(8,128)(2,1)}, bf16[1152,1152]{1,0:T(8,128)(2,1)S(1)}, u32[]{:S(2)}, u32[]{:S(2)}) %collective-permute-start.11) | collective-permute-done | bytes 2654240 | tf_op jit(solution)/shard_map/ppermute | solution.py:394
  137.5 11.0 %all_to_all.52.back_ref = bf16[2,2,2,32,1152]{4,3,2,1,0:T(8,128)(2,1)S(1)} all-to-all(bf16[2,2,2,32,1152]{4,3,2,1,0:T(8,128)(2,1)S(1)} %get-tuple-element.43), channel_id=1, replica_groups=mesh['seq'=2,'head'=8,'dp'=32] {'seq'}, dimensions={0} | all-to-all | bytes 1179648 | tf_op jit(solution)/shard_map/all_to_all | solution.py:390
  154.4 5.4 %all-to-all-start.5 = ((bf16[8,72,128]{2,1,0:T(8,128)(2,1)}), bf16[8,72,128]{2,1,0:T(8,128)(2,1)S(1)}, u32[]{:S(2)}, u32[]{:S(2)}) async-start(bf16[8,72,128]{2,1,0:T(8,128)(2,1)} %get-tuple-element.46), calls=%async_computation.5 | async-start | bytes 294912 | tf_op jit(solution)/shard_map/all_to_all | solution.py:372
  160.9 5.1 %all-to-all-done.5.refs_2_ = bf16[8,72,128]{2,1,0:T(8,128)(2,1)S(1)} async-done(((bf16[8,72,128]{2,1,0:T(8,128)(2,1)}), bf16[8,72,128]{2,1,0:T(8,128)(2,1)S(1)}, u32[]{:S(2)}, u32[]{:S(2)}) %all-to-all-start.5) | async-done | bytes 147488 | tf_op jit(solution)/shard_map/all_to_all | solution.py:372
  166.0 5.5 %all-to-all-start.6 = ((bf16[8,40,1152]{2,1,0:T(8,128)(2,1)}), bf16[8,40,1152]{2,1,0:T(8,128)(2,1)S(1)}, u32[]{:S(2)}, u32[]{:S(2)}) async-start(bf16[8,40,1152]{2,1,0:T(8,128)(2,1)} %add_convert_fusion.1), calls=%async_computation.6 | async-start | bytes 1474560 | tf_op jit(solution)/shard_map/all_to_all | solution.py:372
  171.5 9.0 %shard_map.80 = (bf16[128,1152]{1,0:T(8,128)(2,1)}, bf16[128,1152]{1,0:T(8,128)(2,1)}, bf16[128,1152]{1,0:T(8,128)(2,1)}, bf16[128,1152]{1,0:T(8,128)(2,1)}, bf1...) custom-call(s32[3]{0:T(128)} %pad_add_fusion.refs_0_.at_ref.core_ref, ...), custom_call_target="tpu_custom_call" | custom-call | tf_op jit(solution)/shard_map/pallas_call | solution.py:359
  185.3 4.0 %all-to-all-done.6.parts_ref = bf16[8,40,1152]{2,1,0:T(8,128)(2,1)S(1)} async-done(((bf16[8,40,1152]{2,1,0:T(8,128)(2,1)}), bf16[8,40,1152]{2,1,0:T(8,128)(2,1)S(1)}, u32[]{:S(2)}, u32[]{:S(2)}) %all-to-all-start.6) | async-done | bytes 737312 | tf_op jit(solution)/shard_map/all_to_all | solution.py:372
  189.3 5.2 %reduce-scatter.2.cloned.1.call-done.two_ref = bf16[144,1152]{1,0:T(8,128)(2,1)} async-done(((bf16[1152,1152]{1,0:T(8,128)(2,1)}), bf16[144,1152]{1,0:T(8,128)(2,1)}) %reduce-scatter.2.cloned.1.call-update) | async-done | bytes 331792 | tf_op jit(solution)/shard_map/reduce_scatter | solution.py:471
  197.5 4.5 %all-to-all-start.7 = ((bf16[8,40,1152]{2,1,0:T(8,128)(2,1)}), bf16[8,40,1152]{2,1,0:T(8,128)(2,1)S(1)}, u32[]{:S(2)}, u32[]{:S(2)}) async-start(bf16[8,40,1152]{2,1,0:T(8,128)(2,1)} %shard_map.81), calls=%async_computation.8 | async-start | bytes 1474560 | tf_op jit(solution)/shard_map/all_to_all | solution.py:413
  204.2 4.1 %collective-permute-start.7 = (bf16[128,1152]{1,0:T(8,128)(2,1)}, bf16[128,1152]{1,0:T(8,128)(2,1)S(1)}, u32[]{:S(2)}, u32[]{:S(2)}) collective-permute-start(bf16[128,1152]{1,0:T(8,128)(2,1)} %get-tuple-element.53), channel_id=1, source_target_pairs={{0,64},{32,96},{64,128},{96,160},{128,192},{160,224},{192,0},{224,... | collective-permute-start | bytes 884744 | tf_op jit(solution)/shard_map/ppermute | solution.py:381
  211.1 4.7 %collective-permute-done.7.t2_ref = bf16[128,1152]{1,0:T(8,128)(2,1)S(1)} collective-permute-done((bf16[128,1152]{1,0:T(8,128)(2,1)}, bf16[128,1152]{1,0:T(8,128)(2,1)S(1)}, u32[]{:S(2)}, u32[]{:S(2)}) %collective-permute-start.7) | collective-permute-done | bytes 294944 | tf_op jit(solution)/shard_map/ppermute | solution.py:381
  215.8 4.5 %collective-permute-done.8.t3_ref = bf16[128,1152]{1,0:T(8,128)(2,1)S(1)} collective-permute-done((bf16[128,1152]{1,0:T(8,128)(2,1)S(1)}, bf16[128,1152]{1,0:T(8,128)(2,1)S(1)}, u32[]{:S(2)}, u32[]{:S(2)}) %collective-permute-start.8) | collective-permute-done | bytes 294944 | tf_op jit(solution)/shard_map/ppermute | solution.py:381
  221.1 10.2 %all-to-all-start.8 = ((bf16[4,40,1152]{2,1,0:T(8,128)(2,1)}), bf16[4,40,1152]{2,1,0:T(8,128)(2,1)S(1)}, u32[]{:S(2)}, u32[]{:S(2)}) async-start(bf16[4,40,1152]{2,1,0:T(8,128)(2,1)} %get-tuple-element.63), calls=%async_computation.9 | async-start | bytes 737280 | tf_op jit(solution)/shard_map/all_to_all | solution.py:502
  253.3 27.8 %all_to_all.53 = bf16[8,40,1152]{2,1,0:T(8,128)(2,1)S(1)} all-to-all(bf16[8,40,1152]{2,1,0:T(8,128)(2,1)} %get-tuple-element.65), channel_id=1, replica_groups={{0,2,4,6,256,258,260,262},{1,3,5,7,257,259,261,263},{8,10,12,14,264,266..., dimensions={0} | all-to-all | bytes 1474560 | tf_op jit(solution)/shard_map/all_to_all | solution.py:413
  281.1 5.0 %collective-permute-start.13 = (bf16[320,1152]{1,0:T(8,128)(2,1)S(1)}, bf16[320,1152]{1,0:T(8,128)(2,1)S(1)}, u32[]{:S(2)}, u32[]{:S(2)}) collective-permute-start(bf16[320,1152]{1,0:T(8,128)(2,1)S(1)} %bitcast.23), channel_id=1, source_target_pairs={{0,1},{1,0},{2,3},{3,2},{4,5},{5,4},{6,7},{7,6},{8,9},{9,8},{10,11... | collective-permute-start | bytes 2211848 | tf_op jit(solution)/shard_map/ppermute | solution.py:394
  (97 shorter events, 74.8 us)
Async XLA Ops:
  7.2 89.7 %all-gather.3.cloned.1.call-start = ((), (), s32[]{:S(2)}) async-start(), calls=%async_computation.12 | async-start | bytes 2985984 | tf_op jit(solution)/shard_map/all_gather | solution.py:430
  11.7 17.5 %all-to-all-start = ((bf16[4,168,1152]{2,1,0:T(8,128)(2,1)}), bf16[4,168,1152]{2,1,0:T(8,128)(2,1)S(1)}, u32[]{:S(2)}, u32[]{:S(2)}) async-start(bf16[4,168,1152]{2,1,0:T(8,128)(2,1)} %get-tuple-element.36), calls=%async_computation | async-start | bytes 3096576 | tf_op jit(solution)/shard_map/all_to_all | solution.py:376
  16.0 53.2 %copy-start.12 = (s32[3]{0:T(128)S(1)}, s32[3]{0:T(128)}, u32[]{:S(2)}) copy-start(s32[3]{0:T(128)} %pad_add_fusion.refs_0_.at_ref.core_ref) | copy-start | bytes 40
  16.1 10.5 %collective-permute-start = (bf16[168,1152]{1,0:T(8,128)(2,1)S(1)}, bf16[168,1152]{1,0:T(8,128)(2,1)S(1)}, u32[]{:S(2)}, u32[]{:S(2)}) collective-permute-start(bf16[168,1152]{1,0:T(8,128)(2,1)S(1)} %copy-done.23), channel_id=1, source_target_pairs={{0,32},{32,0},{64,96},{96,64},{128,160},{160,128},{192,224},{224,1... | collective-permute-start | bytes 1161224 | tf_op jit(solution)/shard_map/ppermute | solution.py:386
  30.5 38.8 %all-to-all-start.1 = ((bf16[4,168,1152]{2,1,0:T(8,128)(2,1)}), bf16[4,168,1152]{2,1,0:T(8,128)(2,1)}, u32[]{:S(2)}, u32[]{:S(2)}) async-start(bf16[4,168,1152]{2,1,0:T(8,128)(2,1)} %broadcast_in_dim.12), calls=%async_computation.1 | async-start | bytes 3096576 | tf_op jit(solution)/shard_map/all_to_all | solution.py:376
  36.7 157.9 %reduce-scatter.2.cloned.1.call-start = ((), (), s32[]{:S(2)}) async-start(), calls=%async_computation.11 | async-start | bytes 2985984 | tf_op jit(solution)/shard_map/reduce_scatter | solution.py:471
  74.7 22.2 %collective-permute-start.1 = (bf16[320,1152]{1,0:T(8,128)(2,1)S(1)}, bf16[320,1152]{1,0:T(8,128)(2,1)S(1)}, u32[]{:S(2)}, u32[]{:S(2)}) collective-permute-start(bf16[320,1152]{1,0:T(8,128)(2,1)S(1)} %bitcast.20), channel_id=1, source_target_pairs={{0,1},{1,0},{2,3},{3,2},{4,5},{5,4},{6,7},{7,6},{8,9},{9,8},{10,11... | collective-permute-start | bytes 2211848 | tf_op jit(solution)/shard_map/ppermute | solution.py:394
  101.6 15.6 %collective-permute-start.2 = (bf16[1152,1152]{1,0:T(8,128)(2,1)}, bf16[1152,1152]{1,0:T(8,128)(2,1)S(1)}, u32[]{:S(2)}, u32[]{:S(2)}) collective-permute-start(bf16[1152,1152]{1,0:T(8,128)(2,1)} %get-tuple-element.42.mine_ref), channel_id=1, source_target_pairs={{0,1},{1,0},{2,3},{3,2},{4,5},{5,4},{6,7},{7,6},{8,9},{9,8},{10,11... | collective-permute-start | bytes 7962632 | tf_op jit(solution)/shard_map/ppermute | solution.py:394
  127.8 7.5 %collective-permute-start.11 = (bf16[1152,1152]{1,0:T(8,128)(2,1)}, bf16[1152,1152]{1,0:T(8,128)(2,1)S(1)}, u32[]{:S(2)}, u32[]{:S(2)}) collective-permute-start(bf16[1152,1152]{1,0:T(8,128)(2,1)} %get-tuple-element.60), channel_id=1, source_target_pairs={{0,1},{1,0},{2,3},{3,2},{4,5},{5,4},{6,7},{7,6},{8,9},{9,8},{10,11... | collective-permute-start | bytes 7962632 | tf_op jit(solution)/shard_map/ppermute | solution.py:394
  151.3 8.5 %collective-permute-start.10 = (bf16[8,40,1152]{2,1,0:T(8,128)(2,1)S(1)}, bf16[8,40,1152]{2,1,0:T(8,128)(2,1)S(1)}, u32[]{:S(2)}, u32[]{:S(2)}) collective-permute-start(bf16[8,40,1152]{2,1,0:T(8,128)(2,1)S(1)} %get-tuple-element.58), channel_id=1, source_target_pairs={{0,1},{1,0},{2,3},{3,2},{4,5},{5,4},{6,7},{7,6},{8,9},{9,8},{10,11... | collective-permute-start | bytes 2211848 | tf_op jit(solution)/shard_map/ppermute | solution.py:394
  154.4 11.5 %all-to-all-start.5 = ((bf16[8,72,128]{2,1,0:T(8,128)(2,1)}), bf16[8,72,128]{2,1,0:T(8,128)(2,1)S(1)}, u32[]{:S(2)}, u32[]{:S(2)}) async-start(bf16[8,72,128]{2,1,0:T(8,128)(2,1)} %get-tuple-element.46), calls=%async_computation.5 | async-start | bytes 294912 | tf_op jit(solution)/shard_map/all_to_all | solution.py:372
  166.0 23.3 %all-to-all-start.6 = ((bf16[8,40,1152]{2,1,0:T(8,128)(2,1)}), bf16[8,40,1152]{2,1,0:T(8,128)(2,1)S(1)}, u32[]{:S(2)}, u32[]{:S(2)}) async-start(bf16[8,40,1152]{2,1,0:T(8,128)(2,1)} %add_convert_fusion.1), calls=%async_computation.6 | async-start | bytes 1474560 | tf_op jit(solution)/shard_map/all_to_all | solution.py:372
  180.5 4.7 %collective-permute-start.9 = (bf16[112,1152]{1,0:T(8,128)(2,1)}, bf16[112,1152]{1,0:T(8,128)(2,1)S(1)}, u32[]{:S(2)}, u32[]{:S(2)}) collective-permute-start(bf16[112,1152]{1,0:T(8,128)(2,1)} %get-tuple-element.56), channel_id=1, source_target_pairs={{0,1},{1,0},{2,3},{3,2},{4,5},{5,4},{6,7},{7,6},{8,9},{9,8},{10,11... | collective-permute-start | bytes 774152 | tf_op jit(solution)/shard_map/ppermute | solution.py:394
  197.5 22.8 %all-to-all-start.7 = ((bf16[8,40,1152]{2,1,0:T(8,128)(2,1)}), bf16[8,40,1152]{2,1,0:T(8,128)(2,1)S(1)}, u32[]{:S(2)}, u32[]{:S(2)}) async-start(bf16[8,40,1152]{2,1,0:T(8,128)(2,1)} %shard_map.81), calls=%async_computation.8 | async-start | bytes 1474560 | tf_op jit(solution)/shard_map/all_to_all | solution.py:413
  202.0 9.2 %collective-permute-start.6 = (bf16[128,1152]{1,0:T(8,128)(2,1)}, bf16[128,1152]{1,0:T(8,128)(2,1)S(1)}, u32[]{:S(2)}, u32[]{:S(2)}) collective-permute-start(bf16[128,1152]{1,0:T(8,128)(2,1)} %get-tuple-element.52), channel_id=1, source_target_pairs={{0,128},{32,160},{64,192},{96,224},{128,0},{160,32},{192,64},{224,... | collective-permute-start | bytes 884744 | tf_op jit(solution)/shard_map/ppermute | solution.py:381
  204.2 11.7 %collective-permute-start.7 = (bf16[128,1152]{1,0:T(8,128)(2,1)}, bf16[128,1152]{1,0:T(8,128)(2,1)S(1)}, u32[]{:S(2)}, u32[]{:S(2)}) collective-permute-start(bf16[128,1152]{1,0:T(8,128)(2,1)} %get-tuple-element.53), channel_id=1, source_target_pairs={{0,64},{32,96},{64,128},{96,160},{128,192},{160,224},{192,0},{224,... | collective-permute-start | bytes 884744 | tf_op jit(solution)/shard_map/ppermute | solution.py:381
  208.3 12.0 %collective-permute-start.8 = (bf16[128,1152]{1,0:T(8,128)(2,1)S(1)}, bf16[128,1152]{1,0:T(8,128)(2,1)S(1)}, u32[]{:S(2)}, u32[]{:S(2)}) collective-permute-start(bf16[128,1152]{1,0:T(8,128)(2,1)S(1)} %copy-done.27), channel_id=1, source_target_pairs={{0,192},{32,224},{64,0},{96,32},{128,64},{160,96},{192,128},{224,1... | collective-permute-start | bytes 884744 | tf_op jit(solution)/shard_map/ppermute | solution.py:381
  221.1 66.8 %copy-start.14 = (s32[3]{0:T(128)S(1)}, s32[3]{0:T(128)}, u32[]{:S(2)}) copy-start(s32[3]{0:T(128)} %pad_add_fusion.refs_0_.at_ref.core_ref) | copy-start | bytes 40
  221.1 28.1 %all-to-all-start.8 = ((bf16[4,40,1152]{2,1,0:T(8,128)(2,1)}), bf16[4,40,1152]{2,1,0:T(8,128)(2,1)S(1)}, u32[]{:S(2)}, u32[]{:S(2)}) async-start(bf16[4,40,1152]{2,1,0:T(8,128)(2,1)} %get-tuple-element.63), calls=%async_computation.9 | async-start | bytes 737280 | tf_op jit(solution)/shard_map/all_to_all | solution.py:502
  231.3 11.5 %collective-permute-start.3 = (bf16[128,1152]{1,0:T(8,128)(2,1)S(1)}, bf16[128,1152]{1,0:T(8,128)(2,1)S(1)}, u32[]{:S(2)}, u32[]{:S(2)}) collective-permute-start(bf16[128,1152]{1,0:T(8,128)(2,1)S(1)} %copy-done.26), channel_id=1, source_target_pairs={{0,128},{32,160},{64,192},{96,224},{128,0},{160,32},{192,64},{224,... | collective-permute-start | bytes 884744 | tf_op jit(solution)/shard_map/ppermute | solution.py:381
  234.4 10.9 %collective-permute-start.4 = (bf16[128,1152]{1,0:T(8,128)(2,1)S(1)}, bf16[128,1152]{1,0:T(8,128)(2,1)S(1)}, u32[]{:S(2)}, u32[]{:S(2)}) collective-permute-start(bf16[128,1152]{1,0:T(8,128)(2,1)S(1)} %copy-done.25), channel_id=1, source_target_pairs={{0,64},{32,96},{64,128},{96,160},{128,192},{160,224},{192,0},{224,... | collective-permute-start | bytes 884744 | tf_op jit(solution)/shard_map/ppermute | solution.py:381
  238.0 10.4 %collective-permute-start.5 = (bf16[128,1152]{1,0:T(8,128)(2,1)S(1)}, bf16[128,1152]{1,0:T(8,128)(2,1)S(1)}, u32[]{:S(2)}, u32[]{:S(2)}) collective-permute-start(bf16[128,1152]{1,0:T(8,128)(2,1)S(1)} %copy-done.24), channel_id=1, source_target_pairs={{0,192},{32,224},{64,0},{96,32},{128,64},{160,96},{192,128},{224,1... | collective-permute-start | bytes 884744 | tf_op jit(solution)/shard_map/ppermute | solution.py:381
  239.9 9.3 %collective-permute-start.12 = (bf16[128,1152]{1,0:T(8,128)(2,1)S(1)}, bf16[128,1152]{1,0:T(8,128)(2,1)S(1)}, u32[]{:S(2)}, u32[]{:S(2)}) collective-permute-start(bf16[128,1152]{1,0:T(8,128)(2,1)S(1)} %get-tuple-element.61), channel_id=1, source_target_pairs={{0,32},{32,0},{64,96},{96,64},{128,160},{160,128},{192,224},{224,1... | collective-permute-start | bytes 884744 | tf_op jit(solution)/shard_map/ppermute | solution.py:386
  281.1 6.8 %collective-permute-start.13 = (bf16[320,1152]{1,0:T(8,128)(2,1)S(1)}, bf16[320,1152]{1,0:T(8,128)(2,1)S(1)}, u32[]{:S(2)}, u32[]{:S(2)}) collective-permute-start(bf16[320,1152]{1,0:T(8,128)(2,1)S(1)} %bitcast.23), channel_id=1, source_target_pairs={{0,1},{1,0},{2,3},{3,2},{4,5},{5,4},{6,7},{7,6},{8,9},{9,8},{10,11... | collective-permute-start | bytes 2211848 | tf_op jit(solution)/shard_map/ppermute | solution.py:394
  (26 other events, 330.2 us)
Sparse Core Ops, SparseCore 0:
  11.8 64.3 all-gather.2
  137.6 56.9 reduce-scatter.1

commit v12 on v11

--- a/solution.py
+++ b/solution.py
@@ -311,10 +311,11 @@
     return total
 
 
-def last_kernel(
-    t0_ref, t1_ref, t2_ref, t3_ref, half_ref, x_ref, g_ref, grads_ref, out_ref, copies_ref
-):
-    copy_sum(grads_ref, copies_ref)
+def copy_kernel(grads_ref, *refs):
+    copy_sum(grads_ref, refs[4])
+
+
+def last_kernel(t0_ref, t1_ref, t2_ref, t3_ref, half_ref, x_ref, g_ref, out_ref):
     total = row_sum(t0_ref, t1_ref, t2_ref, t3_ref, half_ref)
     normed, inverse = normalize(x_ref[...])
     out_ref[...] = normalize_back(g_ref[...], inverse, normed, total).astype(BF)
@@ -465,6 +466,7 @@
             pltpu.VMEM((16 * E, 256), BF),
             pltpu.SemaphoreType.DMA((2,)),
         ],
+        mib=60,
     )
     back = over_seq(back)
     two = (keep.astype(F32) + swap_cores(send, n_dp).astype(F32)).astype(BF)
@@ -493,6 +495,7 @@
     size = 320 // n_near
     chain = call(
         chain_kernel, shape(n_near, size, depth), keep, swap_cores(send, n_dp), parts, two,
+        fetch=(0, 1, 2, 3), mib=60,
         scratch_shapes=[pltpu.VMEM((320, depth), F32)],
     )
     half, copies = call(
@@ -500,10 +503,15 @@
         *shift_x(terms[:4]), over_near(chain, near),
     )
     summed = lax.all_to_all(copies, "dp", 0, 0, tiled=True, axis_index_groups=far)
-    latent_grads, copies = call(
-        last_kernel, (shape(128, depth), shape(n_near, size, depth)),
-        *shift_x(terms[4:]), swap_y(half), x, grad_one, summed,
-        fetch=(0, 1, 2, 3, 4, 5, 6, 7), mib=60,
+    own, *moved = shift_x(terms[4:])
+    copies, *moved = call(
+        copy_kernel, (shape(n_near, size, depth), *[row] * 4), summed, *moved, swap_y(half),
+        in_specs=[VMEM] + [HBM] * 4,
+        out_specs=(VMEM, *[HBM] * 4),
+        input_output_aliases={i: i for i in range(1, 5)},
+    )
+    latent_grads = call(
+        last_kernel, row, own, *moved, x, grad_one, fetch=(0, 1, 2, 3, 4, 5, 6), mib=60
     )
     mine = over_near(copies, near).reshape(320, depth)
     grad_qkv, grad_out = call(

time: 299 us -> 300 us (level)
  starting transfers between devices: 88.4 us -> 92.3 us
  waiting for transfers between devices: 79.5 us -> 76 us
  blocking collectives: 63.1 us -> 60 us
    all_to_all x1, blocking collectives: 27.8 us -> 24 us  [over_near(): lax.all_to_all(blocks, ('seq', 'dp'), 0, 0, tiled=True, axis_index_groups...]
    all_to_all x1, waiting for transfers between devices: 0.01 us -> 3.29 us  [on_device(): lax.all_to_all(copies, 'dp', 0, 0, tiled=True, axis_index_groups=far)]
    pallas_call x10 -> x11, Pallas kernels: 39 us -> 41.7 us  [call(): pl.pallas_call(fetching if moved else kernel, out_shape=outs, in_specs=sp...]
    unnamed x56 -> x58, local copies, waits for them, and re-layouts: 7.54 us -> 5.9 us
  transfers between devices with their start and end apart: 22 -> 22, of which waited for: 15 -> 14; matrix products, arithmetic and copies ran while one was open for 1% -> 1% of each run, Pallas kernels for 5% -> 6%
where the time goes in v12:
time: 300 us; the launch traced here: 297 us
  starting transfers between devices  92.3 us (31%)
  waiting for transfers between devices  76 us (25%)
  blocking collectives  60 us (20%)
  Pallas kernels  41.7 us (14%)
  between operations  14.5 us (5%)
  local copies, waits for them, and re-layouts  7.27 us (2%)
  other arithmetic  5.64 us (2%)
    pallas_call x11, Pallas kernels, call(): pl.pallas_call(fetching if moved else kernel, out_shape=outs, in_specs=sp...  41.7 us
    all_to_all x2, waiting for transfers between devices, over_x(): lax.all_to_all(blocks, 'head', 0, 0, tiled=True, axis_index_groups=ALONG_X)  35 us
    ppermute x6, starting transfers between devices, swap_cores(): return lax.ppermute(value, 'dp', [(i, i ^ bit) for i in range(n_dp)])  27.7 us
    all_to_all x1, blocking collectives, over_near(): lax.all_to_all(blocks, ('seq', 'dp'), 0, 0, tiled=True, axis_index_groups...  24 us
    all_to_all x2, blocking collectives, over_seq(): return lax.all_to_all(blocks, 'seq', 0, 0, tiled=True)  24 us
    ppermute x6, starting transfers between devices, shift_x(): moved = [lax.ppermute(blocks[k], 'head', perms[k]) for k in (2, 1, 3)]  16 us
    ppermute x6, waiting for transfers between devices, shift_x(): moved = [lax.ppermute(blocks[k], 'head', perms[k]) for k in (2, 1, 3)]  13.8 us
    all_to_all x1, blocking collectives, over_head(): return lax.all_to_all(blocks, 'head', 0, 0, tiled=True)  12 us
  transfers between devices with their start and end apart: 22, of which 14 were waited for; matrix products, arithmetic and copies ran while one was open for 1% of the time, Pallas kernels for 6%

profile of v12, /device:TPU:7, one launch (start us, length us, event | category | flops | bytes accessed | tf_op | source)
XLA Modules:
  0.0 297.3 jit_solution(7404675376536850461)
XLA Ops:
  11.7 4.4 %all-to-all-start = ((bf16[4,168,1152]{2,1,0:T(8,128)(2,1)}), bf16[4,168,1152]{2,1,0:T(8,128)(2,1)S(1)}, u32[]{:S(2)}, u32[]{:S(2)}) async-start(bf16[4,168,1152]{2,1,0:T(8,128)(2,1)} %get-tuple-element.39), calls=%async_computation | async-start | bytes 3096576 | tf_op jit(solution)/shard_map/all_to_all | solution.py:377
  16.0 4.9 %collective-permute-start = (bf16[168,1152]{1,0:T(8,128)(2,1)S(1)}, bf16[168,1152]{1,0:T(8,128)(2,1)S(1)}, u32[]{:S(2)}, u32[]{:S(2)}) collective-permute-start(bf16[168,1152]{1,0:T(8,128)(2,1)S(1)} %copy-done.23), channel_id=1, source_target_pairs={{0,32},{32,0},{64,96},{96,64},{128,160},{160,128},{192,224},{224,1... | collective-permute-start | bytes 1161224 | tf_op jit(solution)/shard_map/ppermute | solution.py:387
  21.0 5.6 %collective-permute-done = bf16[168,1152]{1,0:T(8,128)(2,1)S(1)} collective-permute-done((bf16[168,1152]{1,0:T(8,128)(2,1)S(1)}, bf16[168,1152]{1,0:T(8,128)(2,1)S(1)}, u32[]{:S(2)}, u32[]{:S(2)}) %collective-permute-start) | collective-permute-done | bytes 387104 | tf_op jit(solution)/shard_map/ppermute | solution.py:387
  30.5 6.1 %all-to-all-start.1 = ((bf16[4,168,1152]{2,1,0:T(8,128)(2,1)}), bf16[4,168,1152]{2,1,0:T(8,128)(2,1)}, u32[]{:S(2)}, u32[]{:S(2)}) async-start(bf16[4,168,1152]{2,1,0:T(8,128)(2,1)} %broadcast_in_dim.12), calls=%async_computation.1 | async-start | bytes 3096576 | tf_op jit(solution)/shard_map/all_to_all | solution.py:377
  36.6 32.4 %all-to-all-done.1.far_ref.refs_4_ = bf16[4,168,1152]{2,1,0:T(8,128)(2,1)} async-done(((bf16[4,168,1152]{2,1,0:T(8,128)(2,1)}), bf16[4,168,1152]{2,1,0:T(8,128)(2,1)}, u32[]{:S(2)}, u32[]{:S(2)}) %all-to-all-start.1) | async-done | bytes 1548320 | tf_op jit(solution)/shard_map/all_to_all | solution.py:377
  74.4 10.5 %collective-permute-start.1 = (bf16[320,1152]{1,0:T(8,128)(2,1)S(1)}, bf16[320,1152]{1,0:T(8,128)(2,1)S(1)}, u32[]{:S(2)}, u32[]{:S(2)}) collective-permute-start(bf16[320,1152]{1,0:T(8,128)(2,1)S(1)} %bitcast.20), channel_id=1, source_target_pairs={{0,1},{1,0},{2,3},{3,2},{4,5},{5,4},{6,7},{7,6},{8,9},{9,8},{10,11... | collective-permute-start | bytes 2211848 | tf_op jit(solution)/shard_map/ppermute | solution.py:395
  84.9 12.0 %all_to_all.50.refs_3_.heads_ref = bf16[8,72,128]{2,1,0:T(8,128)(2,1)} all-to-all(bf16[8,72,128]{2,1,0:T(8,128)(2,1)S(1)} %get-tuple-element.41), channel_id=1, replica_groups=mesh['seq'=2,'head'=8,'dp'=32] {'head'}, dimensions={0} | all-to-all | bytes 294912 | tf_op jit(solution)/shard_map/all_to_all | solution.py:373
  104.7 13.2 %all_to_all.51.pair_ref = bf16[2,2,2,32,1152]{4,3,2,1,0:T(8,128)(2,1)} all-to-all(bf16[2,2,2,32,1152]{4,3,2,1,0:T(8,128)(2,1)} %get-tuple-element.44), channel_id=1, replica_groups=mesh['seq'=2,'head'=8,'dp'=32] {'seq'}, dimensions={0} | all-to-all | bytes 1179648 | tf_op jit(solution)/shard_map/all_to_all | solution.py:391
  119.4 10.6 %shard_map.78 = (bf16[2,2,2,32,1152]{4,3,2,1,0:T(8,128)(2,1)}, bf16[1152,1152]{1,0:T(8,128)(2,1)}, bf16[1152,1152]{1,0:T(8,128)(2,1)}) custom-call(s32[3]{0:T(128)} %pad_add_fusion.refs_0_.at_ref.core_ref, bf16[2,2,2,32,1152]{4,3,2,1,0:T(8,128)(2,1)} %all_to_all.51.pair_ref, bf16[1152,1152]{1,0:T(8,128)(2,1)} %get-tuple-element.45.mine_ref, ...), custom_call_target="tpu_custom_call" | custom-call | tf_op jit(solution)/shard_map/pallas_call | solution.py:360
  132.8 4.8 %collective-permute-done.8 = bf16[1152,1152]{1,0:T(8,128)(2,1)S(1)} collective-permute-done((bf16[1152,1152]{1,0:T(8,128)(2,1)}, bf16[1152,1152]{1,0:T(8,128)(2,1)S(1)}, u32[]{:S(2)}, u32[]{:S(2)}) %collective-permute-start.8) | collective-permute-done | bytes 2654240 | tf_op jit(solution)/shard_map/ppermute | solution.py:395
  142.5 10.8 %all_to_all.52.back_ref = bf16[2,2,2,32,1152]{4,3,2,1,0:T(8,128)(2,1)S(1)} all-to-all(bf16[2,2,2,32,1152]{4,3,2,1,0:T(8,128)(2,1)S(1)} %copy-done.21), channel_id=1, replica_groups=mesh['seq'=2,'head'=8,'dp'=32] {'seq'}, dimensions={0} | all-to-all | bytes 1179648 | tf_op jit(solution)/shard_map/all_to_all | solution.py:391
  159.4 5.4 %all-to-all-start.5 = ((bf16[8,72,128]{2,1,0:T(8,128)(2,1)}), bf16[8,72,128]{2,1,0:T(8,128)(2,1)S(1)}, u32[]{:S(2)}, u32[]{:S(2)}) async-start(bf16[8,72,128]{2,1,0:T(8,128)(2,1)} %get-tuple-element.49), calls=%async_computation.5 | async-start | bytes 294912 | tf_op jit(solution)/shard_map/all_to_all | solution.py:373
  165.9 5.1 %all-to-all-done.5.refs_2_ = bf16[8,72,128]{2,1,0:T(8,128)(2,1)S(1)} async-done(((bf16[8,72,128]{2,1,0:T(8,128)(2,1)}), bf16[8,72,128]{2,1,0:T(8,128)(2,1)S(1)}, u32[]{:S(2)}, u32[]{:S(2)}) %all-to-all-start.5) | async-done | bytes 147488 | tf_op jit(solution)/shard_map/all_to_all | solution.py:373
  170.9 5.8 %all-to-all-start.6 = ((bf16[8,40,1152]{2,1,0:T(8,128)(2,1)}), bf16[8,40,1152]{2,1,0:T(8,128)(2,1)S(1)}, u32[]{:S(2)}, u32[]{:S(2)}) async-start(bf16[8,40,1152]{2,1,0:T(8,128)(2,1)} %add_convert_fusion.1), calls=%async_computation.6 | async-start | bytes 1474560 | tf_op jit(solution)/shard_map/all_to_all | solution.py:373
  176.7 9.0 %shard_map.80 = (bf16[128,1152]{1,0:T(8,128)(2,1)}, bf16[128,1152]{1,0:T(8,128)(2,1)}, bf16[128,1152]{1,0:T(8,128)(2,1)}, bf16[128,1152]{1,0:T(8,128)(2,1)}, bf1...) custom-call(s32[3]{0:T(128)} %pad_add_fusion.refs_0_.at_ref.core_ref, ...), custom_call_target="tpu_custom_call" | custom-call | tf_op jit(solution)/shard_map/pallas_call | solution.py:360
  190.4 4.0 %all-to-all-done.6.refs_2_ = bf16[8,40,1152]{2,1,0:T(8,128)(2,1)S(1)} async-done(((bf16[8,40,1152]{2,1,0:T(8,128)(2,1)}), bf16[8,40,1152]{2,1,0:T(8,128)(2,1)S(1)}, u32[]{:S(2)}, u32[]{:S(2)}) %all-to-all-start.6) | async-done | bytes 737312 | tf_op jit(solution)/shard_map/all_to_all | solution.py:373
  200.2 5.9 %all-to-all-start.7 = ((bf16[8,40,1152]{2,1,0:T(8,128)(2,1)}), bf16[8,40,1152]{2,1,0:T(8,128)(2,1)S(1)}, u32[]{:S(2)}, u32[]{:S(2)}) async-start(bf16[8,40,1152]{2,1,0:T(8,128)(2,1)} %shard_map.81), calls=%async_computation.8 | async-start | bytes 1474560 | tf_op jit(solution)/shard_map/all_to_all | solution.py:414
  208.2 4.3 %collective-permute-start.4 = (bf16[128,1152]{1,0:T(8,128)(2,1)S(1)}, bf16[128,1152]{1,0:T(8,128)(2,1)S(1)}, u32[]{:S(2)}, u32[]{:S(2)}) collective-permute-start(bf16[128,1152]{1,0:T(8,128)(2,1)S(1)} %copy-done.28), channel_id=1, source_target_pairs={{0,64},{32,96},{64,128},{96,160},{128,192},{160,224},{192,0},{224,... | collective-permute-start | bytes 884744 | tf_op jit(solution)/shard_map/ppermute | solution.py:382
  215.3 4.8 %collective-permute-done.4.t2_ref = bf16[128,1152]{1,0:T(8,128)(2,1)S(1)} collective-permute-done((bf16[128,1152]{1,0:T(8,128)(2,1)S(1)}, bf16[128,1152]{1,0:T(8,128)(2,1)S(1)}, u32[]{:S(2)}, u32[]{:S(2)}) %collective-permute-start.4) | collective-permute-done | bytes 294944 | tf_op jit(solution)/shard_map/ppermute | solution.py:382
  224.5 11.4 %all-to-all-start.8 = ((bf16[4,40,1152]{2,1,0:T(8,128)(2,1)}), bf16[4,40,1152]{2,1,0:T(8,128)(2,1)S(1)}, u32[]{:S(2)}, u32[]{:S(2)}) async-start(bf16[4,40,1152]{2,1,0:T(8,128)(2,1)} %get-tuple-element.61), calls=%async_computation.9 | async-start | bytes 737280 | tf_op jit(solution)/shard_map/all_to_all | solution.py:505
  243.6 4.7 %collective-permute-start.12 = (bf16[128,1152]{1,0:T(8,128)(2,1)S(1)}, bf16[128,1152]{1,0:T(8,128)(2,1)S(1)}, u32[]{:S(2)}, u32[]{:S(2)}) collective-permute-start(bf16[128,1152]{1,0:T(8,128)(2,1)S(1)} %get-tuple-element.65), channel_id=1, source_target_pairs={{0,32},{32,0},{64,96},{96,64},{128,160},{160,128},{192,224},{224,1... | collective-permute-start | bytes 884744 | tf_op jit(solution)/shard_map/ppermute | solution.py:387
  249.0 4.0 %collective-permute-done.11.refs_2_ = bf16[128,1152]{1,0:T(8,128)(2,1)S(1)} collective-permute-done((bf16[128,1152]{1,0:T(8,128)(2,1)S(1)}, bf16[128,1152]{1,0:T(8,128)(2,1)S(1)}, u32[]{:S(2)}, u32[]{:S(2)}) %collective-permute-start.11) | collective-permute-done | bytes 294944 | tf_op jit(solution)/shard_map/ppermute | solution.py:382
  256.4 24.0 %all_to_all.53 = bf16[8,40,1152]{2,1,0:T(8,128)(2,1)S(1)} all-to-all(bf16[8,40,1152]{2,1,0:T(8,128)(2,1)S(1)} %get-tuple-element.71), channel_id=1, replica_groups={{0,2,4,6,256,258,260,262},{1,3,5,7,257,259,261,263},{8,10,12,14,264,266..., dimensions={0} | all-to-all | bytes 1474560 | tf_op jit(solution)/shard_map/all_to_all | solution.py:414
  280.5 4.7 %collective-permute-start.13 = (bf16[320,1152]{1,0:T(8,128)(2,1)S(1)}, bf16[320,1152]{1,0:T(8,128)(2,1)S(1)}, u32[]{:S(2)}, u32[]{:S(2)}) collective-permute-start(bf16[320,1152]{1,0:T(8,128)(2,1)S(1)} %bitcast.23), channel_id=1, source_target_pairs={{0,1},{1,0},{2,3},{3,2},{4,5},{5,4},{6,7},{7,6},{8,9},{9,8},{10,11... | collective-permute-start | bytes 2211848 | tf_op jit(solution)/shard_map/ppermute | solution.py:395
  (100 shorter events, 74.4 us)
Async XLA Ops:
  7.2 89.7 %all-gather.3.cloned.1.call-start = ((), (), s32[]{:S(2)}) async-start(), calls=%async_computation.12 | async-start | bytes 2985984 | tf_op jit(solution)/shard_map/all_gather | solution.py:431
  11.7 17.5 %all-to-all-start = ((bf16[4,168,1152]{2,1,0:T(8,128)(2,1)}), bf16[4,168,1152]{2,1,0:T(8,128)(2,1)S(1)}, u32[]{:S(2)}, u32[]{:S(2)}) async-start(bf16[4,168,1152]{2,1,0:T(8,128)(2,1)} %get-tuple-element.39), calls=%async_computation | async-start | bytes 3096576 | tf_op jit(solution)/shard_map/all_to_all | solution.py:377
  16.0 53.0 %copy-start.14 = (s32[3]{0:T(128)S(1)}, s32[3]{0:T(128)}, u32[]{:S(2)}) copy-start(s32[3]{0:T(128)} %pad_add_fusion.refs_0_.at_ref.core_ref) | copy-start | bytes 40
  16.0 10.5 %collective-permute-start = (bf16[168,1152]{1,0:T(8,128)(2,1)S(1)}, bf16[168,1152]{1,0:T(8,128)(2,1)S(1)}, u32[]{:S(2)}, u32[]{:S(2)}) collective-permute-start(bf16[168,1152]{1,0:T(8,128)(2,1)S(1)} %copy-done.23), channel_id=1, source_target_pairs={{0,32},{32,0},{64,96},{96,64},{128,160},{160,128},{192,224},{224,1... | collective-permute-start | bytes 1161224 | tf_op jit(solution)/shard_map/ppermute | solution.py:387
  30.5 38.5 %all-to-all-start.1 = ((bf16[4,168,1152]{2,1,0:T(8,128)(2,1)}), bf16[4,168,1152]{2,1,0:T(8,128)(2,1)}, u32[]{:S(2)}, u32[]{:S(2)}) async-start(bf16[4,168,1152]{2,1,0:T(8,128)(2,1)} %broadcast_in_dim.12), calls=%async_computation.1 | async-start | bytes 3096576 | tf_op jit(solution)/shard_map/all_to_all | solution.py:377
  36.6 161.0 %reduce-scatter.2.cloned.1.call-start = ((), (), s32[]{:S(2)}) async-start(), calls=%async_computation.11 | async-start | bytes 2985984 | tf_op jit(solution)/shard_map/reduce_scatter | solution.py:473
  74.4 22.5 %collective-permute-start.1 = (bf16[320,1152]{1,0:T(8,128)(2,1)S(1)}, bf16[320,1152]{1,0:T(8,128)(2,1)S(1)}, u32[]{:S(2)}, u32[]{:S(2)}) collective-permute-start(bf16[320,1152]{1,0:T(8,128)(2,1)S(1)} %bitcast.20), channel_id=1, source_target_pairs={{0,1},{1,0},{2,3},{3,2},{4,5},{5,4},{6,7},{7,6},{8,9},{9,8},{10,11... | collective-permute-start | bytes 2211848 | tf_op jit(solution)/shard_map/ppermute | solution.py:395
  101.4 16.4 %collective-permute-start.2 = (bf16[1152,1152]{1,0:T(8,128)(2,1)}, bf16[1152,1152]{1,0:T(8,128)(2,1)S(1)}, u32[]{:S(2)}, u32[]{:S(2)}) collective-permute-start(bf16[1152,1152]{1,0:T(8,128)(2,1)} %get-tuple-element.45.mine_ref), channel_id=1, source_target_pairs={{0,1},{1,0},{2,3},{3,2},{4,5},{5,4},{6,7},{7,6},{8,9},{9,8},{10,11... | collective-permute-start | bytes 7962632 | tf_op jit(solution)/shard_map/ppermute | solution.py:395
  130.0 7.5 %collective-permute-start.8 = (bf16[1152,1152]{1,0:T(8,128)(2,1)}, bf16[1152,1152]{1,0:T(8,128)(2,1)S(1)}, u32[]{:S(2)}, u32[]{:S(2)}) collective-permute-start(bf16[1152,1152]{1,0:T(8,128)(2,1)} %get-tuple-element.60), channel_id=1, source_target_pairs={{0,1},{1,0},{2,3},{3,2},{4,5},{5,4},{6,7},{7,6},{8,9},{9,8},{10,11... | collective-permute-start | bytes 7962632 | tf_op jit(solution)/shard_map/ppermute | solution.py:395
  156.3 8.5 %collective-permute-start.7 = (bf16[8,40,1152]{2,1,0:T(8,128)(2,1)S(1)}, bf16[8,40,1152]{2,1,0:T(8,128)(2,1)S(1)}, u32[]{:S(2)}, u32[]{:S(2)}) collective-permute-start(bf16[8,40,1152]{2,1,0:T(8,128)(2,1)S(1)} %get-tuple-element.58), channel_id=1, source_target_pairs={{0,1},{1,0},{2,3},{3,2},{4,5},{5,4},{6,7},{7,6},{8,9},{9,8},{10,11... | collective-permute-start | bytes 2211848 | tf_op jit(solution)/shard_map/ppermute | solution.py:395
  159.4 11.5 %all-to-all-start.5 = ((bf16[8,72,128]{2,1,0:T(8,128)(2,1)}), bf16[8,72,128]{2,1,0:T(8,128)(2,1)S(1)}, u32[]{:S(2)}, u32[]{:S(2)}) async-start(bf16[8,72,128]{2,1,0:T(8,128)(2,1)} %get-tuple-element.49), calls=%async_computation.5 | async-start | bytes 294912 | tf_op jit(solution)/shard_map/all_to_all | solution.py:373
  170.9 23.5 %all-to-all-start.6 = ((bf16[8,40,1152]{2,1,0:T(8,128)(2,1)}), bf16[8,40,1152]{2,1,0:T(8,128)(2,1)S(1)}, u32[]{:S(2)}, u32[]{:S(2)}) async-start(bf16[8,40,1152]{2,1,0:T(8,128)(2,1)} %add_convert_fusion.1), calls=%async_computation.6 | async-start | bytes 1474560 | tf_op jit(solution)/shard_map/all_to_all | solution.py:373
  185.7 4.7 %collective-permute-start.6 = (bf16[112,1152]{1,0:T(8,128)(2,1)}, bf16[112,1152]{1,0:T(8,128)(2,1)S(1)}, u32[]{:S(2)}, u32[]{:S(2)}) collective-permute-start(bf16[112,1152]{1,0:T(8,128)(2,1)} %get-tuple-element.56), channel_id=1, source_target_pairs={{0,1},{1,0},{2,3},{3,2},{4,5},{5,4},{6,7},{7,6},{8,9},{9,8},{10,11... | collective-permute-start | bytes 774152 | tf_op jit(solution)/shard_map/ppermute | solution.py:395
  200.2 23.4 %all-to-all-start.7 = ((bf16[8,40,1152]{2,1,0:T(8,128)(2,1)}), bf16[8,40,1152]{2,1,0:T(8,128)(2,1)S(1)}, u32[]{:S(2)}, u32[]{:S(2)}) async-start(bf16[8,40,1152]{2,1,0:T(8,128)(2,1)} %shard_map.81), calls=%async_computation.8 | async-start | bytes 1474560 | tf_op jit(solution)/shard_map/all_to_all | solution.py:414
  206.2 9.2 %collective-permute-start.3 = (bf16[128,1152]{1,0:T(8,128)(2,1)}, bf16[128,1152]{1,0:T(8,128)(2,1)S(1)}, u32[]{:S(2)}, u32[]{:S(2)}) collective-permute-start(bf16[128,1152]{1,0:T(8,128)(2,1)} %get-tuple-element.52), channel_id=1, source_target_pairs={{0,128},{32,160},{64,192},{96,224},{128,0},{160,32},{192,64},{224,... | collective-permute-start | bytes 884744 | tf_op jit(solution)/shard_map/ppermute | solution.py:382
  208.2 12.0 %collective-permute-start.4 = (bf16[128,1152]{1,0:T(8,128)(2,1)S(1)}, bf16[128,1152]{1,0:T(8,128)(2,1)S(1)}, u32[]{:S(2)}, u32[]{:S(2)}) collective-permute-start(bf16[128,1152]{1,0:T(8,128)(2,1)S(1)} %copy-done.28), channel_id=1, source_target_pairs={{0,64},{32,96},{64,128},{96,160},{128,192},{160,224},{192,0},{224,... | collective-permute-start | bytes 884744 | tf_op jit(solution)/shard_map/ppermute | solution.py:382
  212.6 11.1 %collective-permute-start.5 = (bf16[128,1152]{1,0:T(8,128)(2,1)S(1)}, bf16[128,1152]{1,0:T(8,128)(2,1)S(1)}, u32[]{:S(2)}, u32[]{:S(2)}) collective-permute-start(bf16[128,1152]{1,0:T(8,128)(2,1)S(1)} %copy-done.27), channel_id=1, source_target_pairs={{0,192},{32,224},{64,0},{96,32},{128,64},{160,96},{192,128},{224,1... | collective-permute-start | bytes 884744 | tf_op jit(solution)/shard_map/ppermute | solution.py:382
  224.5 31.9 %all-to-all-start.8 = ((bf16[4,40,1152]{2,1,0:T(8,128)(2,1)}), bf16[4,40,1152]{2,1,0:T(8,128)(2,1)S(1)}, u32[]{:S(2)}, u32[]{:S(2)}) async-start(bf16[4,40,1152]{2,1,0:T(8,128)(2,1)} %get-tuple-element.61), calls=%async_computation.9 | async-start | bytes 737280 | tf_op jit(solution)/shard_map/all_to_all | solution.py:505
  235.9 12.5 %collective-permute-start.9 = (bf16[128,1152]{1,0:T(8,128)(2,1)S(1)}, bf16[128,1152]{1,0:T(8,128)(2,1)S(1)}, u32[]{:S(2)}, u32[]{:S(2)}) collective-permute-start(bf16[128,1152]{1,0:T(8,128)(2,1)S(1)} %copy-done.26), channel_id=1, source_target_pairs={{0,128},{32,160},{64,192},{96,224},{128,0},{160,32},{192,64},{224,... | collective-permute-start | bytes 884744 | tf_op jit(solution)/shard_map/ppermute | solution.py:382
  237.9 11.2 %collective-permute-start.10 = (bf16[128,1152]{1,0:T(8,128)(2,1)S(1)}, bf16[128,1152]{1,0:T(8,128)(2,1)S(1)}, u32[]{:S(2)}, u32[]{:S(2)}) collective-permute-start(bf16[128,1152]{1,0:T(8,128)(2,1)S(1)} %copy-done.25), channel_id=1, source_target_pairs={{0,64},{32,96},{64,128},{96,160},{128,192},{160,224},{192,0},{224,... | collective-permute-start | bytes 884744 | tf_op jit(solution)/shard_map/ppermute | solution.py:382
  241.7 11.4 %collective-permute-start.11 = (bf16[128,1152]{1,0:T(8,128)(2,1)S(1)}, bf16[128,1152]{1,0:T(8,128)(2,1)S(1)}, u32[]{:S(2)}, u32[]{:S(2)}) collective-permute-start(bf16[128,1152]{1,0:T(8,128)(2,1)S(1)} %copy-done.24), channel_id=1, source_target_pairs={{0,192},{32,224},{64,0},{96,32},{128,64},{160,96},{192,128},{224,1... | collective-permute-start | bytes 884744 | tf_op jit(solution)/shard_map/ppermute | solution.py:382
  243.6 44.5 %copy-start.16 = (s32[3]{0:T(128)S(1)}, s32[3]{0:T(128)}, u32[]{:S(2)}) copy-start(s32[3]{0:T(128)} %pad_add_fusion.refs_0_.at_ref.core_ref) | copy-start | bytes 40
  243.6 9.4 %collective-permute-start.12 = (bf16[128,1152]{1,0:T(8,128)(2,1)S(1)}, bf16[128,1152]{1,0:T(8,128)(2,1)S(1)}, u32[]{:S(2)}, u32[]{:S(2)}) collective-permute-start(bf16[128,1152]{1,0:T(8,128)(2,1)S(1)} %get-tuple-element.65), channel_id=1, source_target_pairs={{0,32},{32,0},{64,96},{96,64},{128,160},{160,128},{192,224},{224,1... | collective-permute-start | bytes 884744 | tf_op jit(solution)/shard_map/ppermute | solution.py:387
  280.5 7.6 %collective-permute-start.13 = (bf16[320,1152]{1,0:T(8,128)(2,1)S(1)}, bf16[320,1152]{1,0:T(8,128)(2,1)S(1)}, u32[]{:S(2)}, u32[]{:S(2)}) collective-permute-start(bf16[320,1152]{1,0:T(8,128)(2,1)S(1)} %bitcast.23), channel_id=1, source_target_pairs={{0,1},{1,0},{2,3},{3,2},{4,5},{5,4},{6,7},{7,6},{8,9},{9,8},{10,11... | collective-permute-start | bytes 2211848 | tf_op jit(solution)/shard_map/ppermute | solution.py:395
  (27 other events, 495.4 us)
Sparse Core Ops, SparseCore 0:
  11.8 64.3 all-gather.2
  141.6 55.8 reduce-scatter.1

commit v13 on v12

--- a/solution.py
+++ b/solution.py
@@ -466,7 +466,6 @@
             pltpu.VMEM((16 * E, 256), BF),
             pltpu.SemaphoreType.DMA((2,)),
         ],
-        mib=60,
     )
     back = over_seq(back)
     two = (keep.astype(F32) + swap_cores(send, n_dp).astype(F32)).astype(BF)

time: 300 us -> 296 us (0.987)
  starting transfers between devices: 92.3 us -> 88.8 us
  blocking collectives: 60 us -> 63 us
    all_to_all x1, blocking collectives: 24 us -> 27.8 us  [over_near(): lax.all_to_all(blocks, ('seq', 'dp'), 0, 0, tiled=True, axis_index_groups...]
    all_to_all x1, waiting for transfers between devices: 3.29 us -> 0.01 us  [on_device(): lax.all_to_all(copies, 'dp', 0, 0, tiled=True, axis_index_groups=far)]
where the time goes in v13:
time: 296 us; the launch traced here: 294 us
  starting transfers between devices  88.8 us (30%)
  waiting for transfers between devices  77.2 us (26%)
  blocking collectives  63 us (21%)
  Pallas kernels  40.3 us (14%)
  between operations  14.4 us (5%)
  local copies, waits for them, and re-layouts  6.19 us (2%)
  other arithmetic  3.77 us (1%)
    pallas_call x11, Pallas kernels, call(): pl.pallas_call(fetching if moved else kernel, out_shape=outs, in_specs=sp...  40.3 us
    all_to_all x2, waiting for transfers between devices, over_x(): lax.all_to_all(blocks, 'head', 0, 0, tiled=True, axis_index_groups=ALONG_X)  35.2 us
    all_to_all x1, blocking collectives, over_near(): lax.all_to_all(blocks, ('seq', 'dp'), 0, 0, tiled=True, axis_index_groups...  27.8 us
    ppermute x6, starting transfers between devices, swap_cores(): return lax.ppermute(value, 'dp', [(i, i ^ bit) for i in range(n_dp)])  27.7 us
    all_to_all x2, blocking collectives, over_seq(): return lax.all_to_all(blocks, 'seq', 0, 0, tiled=True)  23.3 us
    ppermute x6, starting transfers between devices, shift_x(): moved = [lax.ppermute(blocks[k], 'head', perms[k]) for k in (2, 1, 3)]  16.6 us
    ppermute x6, waiting for transfers between devices, shift_x(): moved = [lax.ppermute(blocks[k], 'head', perms[k]) for k in (2, 1, 3)]  15.4 us
    all_to_all x1, blocking collectives, over_head(): return lax.all_to_all(blocks, 'head', 0, 0, tiled=True)  11.9 us
  transfers between devices with their start and end apart: 22, of which 14 were waited for; matrix products, arithmetic and copies ran while one was open for 1% of the time, Pallas kernels for 6%

profile of v13, /device:TPU:7, one launch (start us, length us, event | category | flops | bytes accessed | tf_op | source)
XLA Modules:
  0.0 293.7 jit_solution(13807066446150453564)
XLA Ops:
  11.6 4.4 %all-to-all-start = ((bf16[4,168,1152]{2,1,0:T(8,128)(2,1)}), bf16[4,168,1152]{2,1,0:T(8,128)(2,1)S(1)}, u32[]{:S(2)}, u32[]{:S(2)}) async-start(bf16[4,168,1152]{2,1,0:T(8,128)(2,1)} %get-tuple-element.39), calls=%async_computation | async-start | bytes 3096576 | tf_op jit(solution)/shard_map/all_to_all | solution.py:377
  15.9 4.9 %collective-permute-start = (bf16[168,1152]{1,0:T(8,128)(2,1)S(1)}, bf16[168,1152]{1,0:T(8,128)(2,1)S(1)}, u32[]{:S(2)}, u32[]{:S(2)}) collective-permute-start(bf16[168,1152]{1,0:T(8,128)(2,1)S(1)} %copy-done.22), channel_id=1, source_target_pairs={{0,32},{32,0},{64,96},{96,64},{128,160},{160,128},{192,224},{224,1... | collective-permute-start | bytes 1161224 | tf_op jit(solution)/shard_map/ppermute | solution.py:387
  20.9 5.6 %collective-permute-done = bf16[168,1152]{1,0:T(8,128)(2,1)S(1)} collective-permute-done((bf16[168,1152]{1,0:T(8,128)(2,1)S(1)}, bf16[168,1152]{1,0:T(8,128)(2,1)S(1)}, u32[]{:S(2)}, u32[]{:S(2)}) %collective-permute-start) | collective-permute-done | bytes 387104 | tf_op jit(solution)/shard_map/ppermute | solution.py:387
  30.4 6.1 %all-to-all-start.1 = ((bf16[4,168,1152]{2,1,0:T(8,128)(2,1)}), bf16[4,168,1152]{2,1,0:T(8,128)(2,1)}, u32[]{:S(2)}, u32[]{:S(2)}) async-start(bf16[4,168,1152]{2,1,0:T(8,128)(2,1)} %broadcast_in_dim.12), calls=%async_computation.1 | async-start | bytes 3096576 | tf_op jit(solution)/shard_map/all_to_all | solution.py:377
  36.6 32.6 %all-to-all-done.1.far_ref.refs_4_ = bf16[4,168,1152]{2,1,0:T(8,128)(2,1)} async-done(((bf16[4,168,1152]{2,1,0:T(8,128)(2,1)}), bf16[4,168,1152]{2,1,0:T(8,128)(2,1)}, u32[]{:S(2)}, u32[]{:S(2)}) %all-to-all-start.1) | async-done | bytes 1548320 | tf_op jit(solution)/shard_map/all_to_all | solution.py:377
  74.6 10.3 %collective-permute-start.1 = (bf16[320,1152]{1,0:T(8,128)(2,1)S(1)}, bf16[320,1152]{1,0:T(8,128)(2,1)S(1)}, u32[]{:S(2)}, u32[]{:S(2)}) collective-permute-start(bf16[320,1152]{1,0:T(8,128)(2,1)S(1)} %bitcast.20), channel_id=1, source_target_pairs={{0,1},{1,0},{2,3},{3,2},{4,5},{5,4},{6,7},{7,6},{8,9},{9,8},{10,11... | collective-permute-start | bytes 2211848 | tf_op jit(solution)/shard_map/ppermute | solution.py:395
  84.9 11.9 %all_to_all.50.refs_3_.heads_ref = bf16[8,72,128]{2,1,0:T(8,128)(2,1)} all-to-all(bf16[8,72,128]{2,1,0:T(8,128)(2,1)S(1)} %get-tuple-element.41), channel_id=1, replica_groups=mesh['seq'=2,'head'=8,'dp'=32] {'head'}, dimensions={0} | all-to-all | bytes 294912 | tf_op jit(solution)/shard_map/all_to_all | solution.py:373
  104.7 12.3 %all_to_all.51.pair_ref = bf16[2,2,2,32,1152]{4,3,2,1,0:T(8,128)(2,1)S(1)} all-to-all(bf16[2,2,2,32,1152]{4,3,2,1,0:T(8,128)(2,1)} %get-tuple-element.44), channel_id=1, replica_groups=mesh['seq'=2,'head'=8,'dp'=32] {'seq'}, dimensions={0} | all-to-all | bytes 1179648 | tf_op jit(solution)/shard_map/all_to_all | solution.py:391
  118.6 9.1 %shard_map.78 = (bf16[2,2,2,32,1152]{4,3,2,1,0:T(8,128)(2,1)S(1)}, bf16[1152,1152]{1,0:T(8,128)(2,1)S(1)}, bf16[1152,1152]{1,0:T(8,128)(2,1)}) custom-call(s32[3]{0:T(128)S(1)} %copy-done.15, bf16[2,2,2,32,1152]{4,3,2,1,0:T(8,128)(2,1)S(1)} %all_to_all.51.pair_ref, bf16[1152,1152]{1,0:T(8,128)(2,1)} %get-tuple-element.45.mine_ref, bf16[1152,1152]{1,0:T(8,128)(2,1)} %copy-done.18), custom_call_target="tpu_custom_call" | custom-call | tf_op jit(solution)/shard_map/pallas_call | solution.py:360
  130.4 4.8 %collective-permute-done.8 = bf16[1152,1152]{1,0:T(8,128)(2,1)S(1)} collective-permute-done((bf16[1152,1152]{1,0:T(8,128)(2,1)}, bf16[1152,1152]{1,0:T(8,128)(2,1)S(1)}, u32[]{:S(2)}, u32[]{:S(2)}) %collective-permute-start.8) | collective-permute-done | bytes 2654240 | tf_op jit(solution)/shard_map/ppermute | solution.py:395
  137.4 11.0 %all_to_all.52.back_ref = bf16[2,2,2,32,1152]{4,3,2,1,0:T(8,128)(2,1)S(1)} all-to-all(bf16[2,2,2,32,1152]{4,3,2,1,0:T(8,128)(2,1)S(1)} %get-tuple-element.46), channel_id=1, replica_groups=mesh['seq'=2,'head'=8,'dp'=32] {'seq'}, dimensions={0} | all-to-all | bytes 1179648 | tf_op jit(solution)/shard_map/all_to_all | solution.py:391
  154.3 5.4 %all-to-all-start.5 = ((bf16[8,72,128]{2,1,0:T(8,128)(2,1)}), bf16[8,72,128]{2,1,0:T(8,128)(2,1)S(1)}, u32[]{:S(2)}, u32[]{:S(2)}) async-start(bf16[8,72,128]{2,1,0:T(8,128)(2,1)} %get-tuple-element.49), calls=%async_computation.5 | async-start | bytes 294912 | tf_op jit(solution)/shard_map/all_to_all | solution.py:373
  160.7 5.1 %all-to-all-done.5.refs_2_ = bf16[8,72,128]{2,1,0:T(8,128)(2,1)S(1)} async-done(((bf16[8,72,128]{2,1,0:T(8,128)(2,1)}), bf16[8,72,128]{2,1,0:T(8,128)(2,1)S(1)}, u32[]{:S(2)}, u32[]{:S(2)}) %all-to-all-start.5) | async-done | bytes 147488 | tf_op jit(solution)/shard_map/all_to_all | solution.py:373
  165.9 5.6 %all-to-all-start.6 = ((bf16[8,40,1152]{2,1,0:T(8,128)(2,1)}), bf16[8,40,1152]{2,1,0:T(8,128)(2,1)S(1)}, u32[]{:S(2)}, u32[]{:S(2)}) async-start(bf16[8,40,1152]{2,1,0:T(8,128)(2,1)} %add_convert_fusion.1), calls=%async_computation.6 | async-start | bytes 1474560 | tf_op jit(solution)/shard_map/all_to_all | solution.py:373
  171.4 9.0 %shard_map.80 = (bf16[128,1152]{1,0:T(8,128)(2,1)}, bf16[128,1152]{1,0:T(8,128)(2,1)}, bf16[128,1152]{1,0:T(8,128)(2,1)}, bf16[128,1152]{1,0:T(8,128)(2,1)}, bf1...) custom-call(s32[3]{0:T(128)} %pad_add_fusion.refs_0_.at_ref.core_ref, ...), custom_call_target="tpu_custom_call" | custom-call | tf_op jit(solution)/shard_map/pallas_call | solution.py:360
  189.1 5.2 %reduce-scatter.2.cloned.1.call-done.refs_3_ = bf16[144,1152]{1,0:T(8,128)(2,1)} async-done(((bf16[1152,1152]{1,0:T(8,128)(2,1)}), bf16[144,1152]{1,0:T(8,128)(2,1)}) %reduce-scatter.2.cloned.1.call-update) | async-done | bytes 331792 | tf_op jit(solution)/shard_map/reduce_scatter | solution.py:472
  196.9 5.0 %all-to-all-start.7 = ((bf16[8,40,1152]{2,1,0:T(8,128)(2,1)}), bf16[8,40,1152]{2,1,0:T(8,128)(2,1)S(1)}, u32[]{:S(2)}, u32[]{:S(2)}) async-start(bf16[8,40,1152]{2,1,0:T(8,128)(2,1)} %shard_map.81), calls=%async_computation.8 | async-start | bytes 1474560 | tf_op jit(solution)/shard_map/all_to_all | solution.py:414
  203.8 4.1 %collective-permute-start.4 = (bf16[128,1152]{1,0:T(8,128)(2,1)}, bf16[128,1152]{1,0:T(8,128)(2,1)S(1)}, u32[]{:S(2)}, u32[]{:S(2)}) collective-permute-start(bf16[128,1152]{1,0:T(8,128)(2,1)} %get-tuple-element.53), channel_id=1, source_target_pairs={{0,64},{32,96},{64,128},{96,160},{128,192},{160,224},{192,0},{224,... | collective-permute-start | bytes 884744 | tf_op jit(solution)/shard_map/ppermute | solution.py:382
  211.0 4.6 %collective-permute-done.4.t2_ref = bf16[128,1152]{1,0:T(8,128)(2,1)S(1)} collective-permute-done((bf16[128,1152]{1,0:T(8,128)(2,1)}, bf16[128,1152]{1,0:T(8,128)(2,1)S(1)}, u32[]{:S(2)}, u32[]{:S(2)}) %collective-permute-start.4) | collective-permute-done | bytes 294944 | tf_op jit(solution)/shard_map/ppermute | solution.py:382
  215.6 4.0 %collective-permute-done.5.t3_ref = bf16[128,1152]{1,0:T(8,128)(2,1)S(1)} collective-permute-done((bf16[128,1152]{1,0:T(8,128)(2,1)S(1)}, bf16[128,1152]{1,0:T(8,128)(2,1)S(1)}, u32[]{:S(2)}, u32[]{:S(2)}) %collective-permute-start.5) | collective-permute-done | bytes 294944 | tf_op jit(solution)/shard_map/ppermute | solution.py:382
  220.5 10.3 %all-to-all-start.8 = ((bf16[4,40,1152]{2,1,0:T(8,128)(2,1)}), bf16[4,40,1152]{2,1,0:T(8,128)(2,1)S(1)}, u32[]{:S(2)}, u32[]{:S(2)}) async-start(bf16[4,40,1152]{2,1,0:T(8,128)(2,1)} %get-tuple-element.61), calls=%async_computation.9 | async-start | bytes 737280 | tf_op jit(solution)/shard_map/all_to_all | solution.py:504
  233.8 3.8 %collective-permute-start.10 = (bf16[128,1152]{1,0:T(8,128)(2,1)S(1)}, bf16[128,1152]{1,0:T(8,128)(2,1)S(1)}, u32[]{:S(2)}, u32[]{:S(2)}) collective-permute-start(bf16[128,1152]{1,0:T(8,128)(2,1)S(1)} %copy-done.24), channel_id=1, source_target_pairs={{0,64},{32,96},{64,128},{96,160},{128,192},{160,224},{192,0},{224,... | collective-permute-start | bytes 884744 | tf_op jit(solution)/shard_map/ppermute | solution.py:382
  248.9 27.8 %all_to_all.53 = bf16[8,40,1152]{2,1,0:T(8,128)(2,1)S(1)} all-to-all(bf16[8,40,1152]{2,1,0:T(8,128)(2,1)S(1)} %get-tuple-element.71), channel_id=1, replica_groups={{0,2,4,6,256,258,260,262},{1,3,5,7,257,259,261,263},{8,10,12,14,264,266..., dimensions={0} | all-to-all | bytes 1474560 | tf_op jit(solution)/shard_map/all_to_all | solution.py:414
  276.7 4.9 %collective-permute-start.13 = (bf16[320,1152]{1,0:T(8,128)(2,1)S(1)}, bf16[320,1152]{1,0:T(8,128)(2,1)S(1)}, u32[]{:S(2)}, u32[]{:S(2)}) collective-permute-start(bf16[320,1152]{1,0:T(8,128)(2,1)S(1)} %bitcast.23), channel_id=1, source_target_pairs={{0,1},{1,0},{2,3},{3,2},{4,5},{5,4},{6,7},{7,6},{8,9},{9,8},{10,11... | collective-permute-start | bytes 2211848 | tf_op jit(solution)/shard_map/ppermute | solution.py:395
  (96 shorter events, 71.6 us)
Async XLA Ops:
  7.2 89.6 %all-gather.3.cloned.1.call-start = ((), (), s32[]{:S(2)}) async-start(), calls=%async_computation.12 | async-start | bytes 2985984 | tf_op jit(solution)/shard_map/all_gather | solution.py:431
  11.6 17.5 %all-to-all-start = ((bf16[4,168,1152]{2,1,0:T(8,128)(2,1)}), bf16[4,168,1152]{2,1,0:T(8,128)(2,1)S(1)}, u32[]{:S(2)}, u32[]{:S(2)}) async-start(bf16[4,168,1152]{2,1,0:T(8,128)(2,1)} %get-tuple-element.39), calls=%async_computation | async-start | bytes 3096576 | tf_op jit(solution)/shard_map/all_to_all | solution.py:377
  15.9 53.3 %copy-start.14 = (s32[3]{0:T(128)S(1)}, s32[3]{0:T(128)}, u32[]{:S(2)}) copy-start(s32[3]{0:T(128)} %pad_add_fusion.refs_0_.at_ref.core_ref) | copy-start | bytes 40
  15.9 10.5 %collective-permute-start = (bf16[168,1152]{1,0:T(8,128)(2,1)S(1)}, bf16[168,1152]{1,0:T(8,128)(2,1)S(1)}, u32[]{:S(2)}, u32[]{:S(2)}) collective-permute-start(bf16[168,1152]{1,0:T(8,128)(2,1)S(1)} %copy-done.22), channel_id=1, source_target_pairs={{0,32},{32,0},{64,96},{96,64},{128,160},{160,128},{192,224},{224,1... | collective-permute-start | bytes 1161224 | tf_op jit(solution)/shard_map/ppermute | solution.py:387
  30.4 38.8 %all-to-all-start.1 = ((bf16[4,168,1152]{2,1,0:T(8,128)(2,1)}), bf16[4,168,1152]{2,1,0:T(8,128)(2,1)}, u32[]{:S(2)}, u32[]{:S(2)}) async-start(bf16[4,168,1152]{2,1,0:T(8,128)(2,1)} %broadcast_in_dim.12), calls=%async_computation.1 | async-start | bytes 3096576 | tf_op jit(solution)/shard_map/all_to_all | solution.py:377
  36.6 157.7 %reduce-scatter.2.cloned.1.call-start = ((), (), s32[]{:S(2)}) async-start(), calls=%async_computation.11 | async-start | bytes 2985984 | tf_op jit(solution)/shard_map/reduce_scatter | solution.py:472
  74.6 22.2 %collective-permute-start.1 = (bf16[320,1152]{1,0:T(8,128)(2,1)S(1)}, bf16[320,1152]{1,0:T(8,128)(2,1)S(1)}, u32[]{:S(2)}, u32[]{:S(2)}) collective-permute-start(bf16[320,1152]{1,0:T(8,128)(2,1)S(1)} %bitcast.20), channel_id=1, source_target_pairs={{0,1},{1,0},{2,3},{3,2},{4,5},{5,4},{6,7},{7,6},{8,9},{9,8},{10,11... | collective-permute-start | bytes 2211848 | tf_op jit(solution)/shard_map/ppermute | solution.py:395
  101.5 15.6 %collective-permute-start.2 = (bf16[1152,1152]{1,0:T(8,128)(2,1)}, bf16[1152,1152]{1,0:T(8,128)(2,1)S(1)}, u32[]{:S(2)}, u32[]{:S(2)}) collective-permute-start(bf16[1152,1152]{1,0:T(8,128)(2,1)} %get-tuple-element.45.mine_ref), channel_id=1, source_target_pairs={{0,1},{1,0},{2,3},{3,2},{4,5},{5,4},{6,7},{7,6},{8,9},{9,8},{10,11... | collective-permute-start | bytes 7962632 | tf_op jit(solution)/shard_map/ppermute | solution.py:395
  127.7 7.5 %collective-permute-start.8 = (bf16[1152,1152]{1,0:T(8,128)(2,1)}, bf16[1152,1152]{1,0:T(8,128)(2,1)S(1)}, u32[]{:S(2)}, u32[]{:S(2)}) collective-permute-start(bf16[1152,1152]{1,0:T(8,128)(2,1)} %get-tuple-element.60), channel_id=1, source_target_pairs={{0,1},{1,0},{2,3},{3,2},{4,5},{5,4},{6,7},{7,6},{8,9},{9,8},{10,11... | collective-permute-start | bytes 7962632 | tf_op jit(solution)/shard_map/ppermute | solution.py:395
  151.2 8.5 %collective-permute-start.7 = (bf16[8,40,1152]{2,1,0:T(8,128)(2,1)S(1)}, bf16[8,40,1152]{2,1,0:T(8,128)(2,1)S(1)}, u32[]{:S(2)}, u32[]{:S(2)}) collective-permute-start(bf16[8,40,1152]{2,1,0:T(8,128)(2,1)S(1)} %get-tuple-element.58), channel_id=1, source_target_pairs={{0,1},{1,0},{2,3},{3,2},{4,5},{5,4},{6,7},{7,6},{8,9},{9,8},{10,11... | collective-permute-start | bytes 2211848 | tf_op jit(solution)/shard_map/ppermute | solution.py:395
  154.3 11.5 %all-to-all-start.5 = ((bf16[8,72,128]{2,1,0:T(8,128)(2,1)}), bf16[8,72,128]{2,1,0:T(8,128)(2,1)S(1)}, u32[]{:S(2)}, u32[]{:S(2)}) async-start(bf16[8,72,128]{2,1,0:T(8,128)(2,1)} %get-tuple-element.49), calls=%async_computation.5 | async-start | bytes 294912 | tf_op jit(solution)/shard_map/all_to_all | solution.py:373
  165.9 23.2 %all-to-all-start.6 = ((bf16[8,40,1152]{2,1,0:T(8,128)(2,1)}), bf16[8,40,1152]{2,1,0:T(8,128)(2,1)S(1)}, u32[]{:S(2)}, u32[]{:S(2)}) async-start(bf16[8,40,1152]{2,1,0:T(8,128)(2,1)} %add_convert_fusion.1), calls=%async_computation.6 | async-start | bytes 1474560 | tf_op jit(solution)/shard_map/all_to_all | solution.py:373
  180.5 4.9 %collective-permute-start.6 = (bf16[112,1152]{1,0:T(8,128)(2,1)}, bf16[112,1152]{1,0:T(8,128)(2,1)S(1)}, u32[]{:S(2)}, u32[]{:S(2)}) collective-permute-start(bf16[112,1152]{1,0:T(8,128)(2,1)} %get-tuple-element.56), channel_id=1, source_target_pairs={{0,1},{1,0},{2,3},{3,2},{4,5},{5,4},{6,7},{7,6},{8,9},{9,8},{10,11... | collective-permute-start | bytes 774152 | tf_op jit(solution)/shard_map/ppermute | solution.py:395
  196.9 22.7 %all-to-all-start.7 = ((bf16[8,40,1152]{2,1,0:T(8,128)(2,1)}), bf16[8,40,1152]{2,1,0:T(8,128)(2,1)S(1)}, u32[]{:S(2)}, u32[]{:S(2)}) async-start(bf16[8,40,1152]{2,1,0:T(8,128)(2,1)} %shard_map.81), calls=%async_computation.8 | async-start | bytes 1474560 | tf_op jit(solution)/shard_map/all_to_all | solution.py:414
  201.9 9.2 %collective-permute-start.3 = (bf16[128,1152]{1,0:T(8,128)(2,1)}, bf16[128,1152]{1,0:T(8,128)(2,1)S(1)}, u32[]{:S(2)}, u32[]{:S(2)}) collective-permute-start(bf16[128,1152]{1,0:T(8,128)(2,1)} %get-tuple-element.52), channel_id=1, source_target_pairs={{0,128},{32,160},{64,192},{96,224},{128,0},{160,32},{192,64},{224,... | collective-permute-start | bytes 884744 | tf_op jit(solution)/shard_map/ppermute | solution.py:382
  203.8 11.8 %collective-permute-start.4 = (bf16[128,1152]{1,0:T(8,128)(2,1)}, bf16[128,1152]{1,0:T(8,128)(2,1)S(1)}, u32[]{:S(2)}, u32[]{:S(2)}) collective-permute-start(bf16[128,1152]{1,0:T(8,128)(2,1)} %get-tuple-element.53), channel_id=1, source_target_pairs={{0,64},{32,96},{64,128},{96,160},{128,192},{160,224},{192,0},{224,... | collective-permute-start | bytes 884744 | tf_op jit(solution)/shard_map/ppermute | solution.py:382
  207.9 11.8 %collective-permute-start.5 = (bf16[128,1152]{1,0:T(8,128)(2,1)S(1)}, bf16[128,1152]{1,0:T(8,128)(2,1)S(1)}, u32[]{:S(2)}, u32[]{:S(2)}) collective-permute-start(bf16[128,1152]{1,0:T(8,128)(2,1)S(1)} %copy-done.26), channel_id=1, source_target_pairs={{0,192},{32,224},{64,0},{96,32},{128,64},{160,96},{192,128},{224,1... | collective-permute-start | bytes 884744 | tf_op jit(solution)/shard_map/ppermute | solution.py:382
  220.5 28.3 %all-to-all-start.8 = ((bf16[4,40,1152]{2,1,0:T(8,128)(2,1)}), bf16[4,40,1152]{2,1,0:T(8,128)(2,1)S(1)}, u32[]{:S(2)}, u32[]{:S(2)}) async-start(bf16[4,40,1152]{2,1,0:T(8,128)(2,1)} %get-tuple-element.61), calls=%async_computation.9 | async-start | bytes 737280 | tf_op jit(solution)/shard_map/all_to_all | solution.py:504
  230.8 11.6 %collective-permute-start.9 = (bf16[128,1152]{1,0:T(8,128)(2,1)S(1)}, bf16[128,1152]{1,0:T(8,128)(2,1)S(1)}, u32[]{:S(2)}, u32[]{:S(2)}) collective-permute-start(bf16[128,1152]{1,0:T(8,128)(2,1)S(1)} %copy-done.25), channel_id=1, source_target_pairs={{0,128},{32,160},{64,192},{96,224},{128,0},{160,32},{192,64},{224,... | collective-permute-start | bytes 884744 | tf_op jit(solution)/shard_map/ppermute | solution.py:382
  233.8 11.3 %collective-permute-start.10 = (bf16[128,1152]{1,0:T(8,128)(2,1)S(1)}, bf16[128,1152]{1,0:T(8,128)(2,1)S(1)}, u32[]{:S(2)}, u32[]{:S(2)}) collective-permute-start(bf16[128,1152]{1,0:T(8,128)(2,1)S(1)} %copy-done.24), channel_id=1, source_target_pairs={{0,64},{32,96},{64,128},{96,160},{128,192},{160,224},{192,0},{224,... | collective-permute-start | bytes 884744 | tf_op jit(solution)/shard_map/ppermute | solution.py:382
  237.6 10.3 %collective-permute-start.11 = (bf16[128,1152]{1,0:T(8,128)(2,1)S(1)}, bf16[128,1152]{1,0:T(8,128)(2,1)S(1)}, u32[]{:S(2)}, u32[]{:S(2)}) collective-permute-start(bf16[128,1152]{1,0:T(8,128)(2,1)S(1)} %copy-done.23), channel_id=1, source_target_pairs={{0,192},{32,224},{64,0},{96,32},{128,64},{160,96},{192,128},{224,1... | collective-permute-start | bytes 884744 | tf_op jit(solution)/shard_map/ppermute | solution.py:382
  239.6 44.9 %copy-start.16 = (s32[3]{0:T(128)S(1)}, s32[3]{0:T(128)}, u32[]{:S(2)}) copy-start(s32[3]{0:T(128)} %pad_add_fusion.refs_0_.at_ref.core_ref) | copy-start | bytes 40
  239.6 9.3 %collective-permute-start.12 = (bf16[128,1152]{1,0:T(8,128)(2,1)S(1)}, bf16[128,1152]{1,0:T(8,128)(2,1)S(1)}, u32[]{:S(2)}, u32[]{:S(2)}) collective-permute-start(bf16[128,1152]{1,0:T(8,128)(2,1)S(1)} %get-tuple-element.65), channel_id=1, source_target_pairs={{0,32},{32,0},{64,96},{96,64},{128,160},{160,128},{192,224},{224,1... | collective-permute-start | bytes 884744 | tf_op jit(solution)/shard_map/ppermute | solution.py:387
  276.7 7.8 %collective-permute-start.13 = (bf16[320,1152]{1,0:T(8,128)(2,1)S(1)}, bf16[320,1152]{1,0:T(8,128)(2,1)S(1)}, u32[]{:S(2)}, u32[]{:S(2)}) collective-permute-start(bf16[320,1152]{1,0:T(8,128)(2,1)S(1)} %bitcast.23), channel_id=1, source_target_pairs={{0,1},{1,0},{2,3},{3,2},{4,5},{5,4},{6,7},{7,6},{8,9},{9,8},{10,11... | collective-permute-start | bytes 2211848 | tf_op jit(solution)/shard_map/ppermute | solution.py:395
  (25 other events, 496.6 us)
Sparse Core Ops, SparseCore 0:
  11.7 64.3 all-gather.2
  137.5 56.7 reduce-scatter.1
